TPU v7x, 32 devices: a whole 2x2x4 slice. The times are simulated.
32 devices in a mesh: rep: 16 (over z, y, core), fsdp: 2 (over x).
Axes of the slice: x: 2, y: 2, z: 4, core: 2. Of those that a mesh axis runs over, the one named last changes fastest.
Arguments:
- tokens: bfloat16 [16384, 896], P(('rep', 'fsdp')), may hold values from -6 to 6
- segments: int32 [16384], P(('rep', 'fsdp')), may hold values from -1 to 3, as said below
- cotangent: bfloat16 [16384, 896], P(('rep', 'fsdp')), may hold values from -6 to 6
- w_query: bfloat16 [896, 896], P('fsdp'), may hold values from -0.1875 to 0.1875
- w_key: bfloat16 [896, 128], P('fsdp'), may hold values from -0.1875 to 0.1875
- w_value: bfloat16 [896, 128], P('fsdp'), may hold values from -0.1875 to 0.1875
- w_output: bfloat16 [896, 896], P('fsdp'), may hold values from -0.75 to 0.75
- w_gate: bfloat16 [896, 4864], P('fsdp'), may hold values from -0.1875 to 0.1875
- w_up: bfloat16 [896, 4864], P('fsdp'), may hold values from -0.1875 to 0.1875
- w_down: bfloat16 [4864, 896], P('fsdp'), may hold values from -0.078125 to 0.078125
- b_query: bfloat16 [896], P('fsdp'), may hold values from -2 to 2
- b_key: bfloat16 [128], P('fsdp'), may hold values from -2 to 2
- b_value: bfloat16 [128], P('fsdp'), may hold values from -2 to 2
- gain_attn: bfloat16 [896], P('fsdp'), may hold values from 0.5 to 1.5
- gain_mlp: bfloat16 [896], P('fsdp'), may hold values from 0.5 to 1.5
Outputs:
- output: bfloat16 [16384, 896], P(('rep', 'fsdp'))
- tokens_grad: float32 [16384, 896], P(('rep', 'fsdp'))
- w_query_grad: float32 [896, 896], P('fsdp')
- w_key_grad: float32 [896, 128], P('fsdp')
- w_value_grad: float32 [896, 128], P('fsdp')
- w_output_grad: float32 [896, 896], P('fsdp')
- w_gate_grad: float32 [896, 4864], P('fsdp')
- w_up_grad: float32 [896, 4864], P('fsdp')
- w_down_grad: float32 [4864, 896], P('fsdp')
- b_query_grad: float32 [896], P('fsdp')
- b_key_grad: float32 [128], P('fsdp')
- b_value_grad: float32 [128], P('fsdp')
- gain_attn_grad: float32 [896], P('fsdp')
- gain_mlp_grad: float32 [896], P('fsdp')
Inputs may be any that keep to these rules, and one draw needn't show every extreme that they name: `segments`: in each device's 512 slots the used slots come first with segment numbers that never fall, the unused ones last; at least 128 slots of every device are used, and on one device all slots hold one sequence.
All inputs are finite; a program needn't handle non-finite values.
Results may differ from a plain program's by a relative error of at most 0.024.
Values may be sent and summed in bfloat16 or wider, within the bound.
No kernel may reach another device: no remote copies, remote signals or barrier semaphores. Data moves between devices by JAX's collectives and lax.ppermute only.
A program may use at most 256 MiB of HBM per device.

v0:
```python
import jax
import jax.numpy as jnp
from jax import lax
from jax.sharding import PartitionSpec as P

HEAD_DIM = 64


EPSILON = 1e-06
THETA = 1000000.0
NEGATIVE = -1e30


def positions(segs):
    length = segs.shape[0]
    index = jnp.arange(length, dtype=jnp.int32)
    before = jnp.concatenate([jnp.full((1,), -2, dtype=jnp.int32), segs[:-1]])
    starts = lax.cummax(jnp.where(segs != before, index, jnp.zeros_like(index)), axis=0)
    return (index - starts).astype(jnp.float32)


def rope_tables(segs, head_dim):
    halfway = head_dim // 2
    inverse = THETA ** (-(jnp.arange(halfway, dtype=jnp.float32) * 2.0 / head_dim))
    angles = positions(segs)[:, None] * inverse[None, :]
    return (jnp.cos(angles), jnp.sin(angles))


def rotate(values, cosine, sine):
    halfway = values.shape[-1] // 2
    first = values[..., :halfway]
    second = values[..., halfway:]
    cosine = cosine[:, None, :]
    sine = sine[:, None, :]
    return jnp.concatenate(
        [first * cosine - second * sine, second * cosine + first * sine], axis=-1
    )


def normed(values, gain):
    scale = lax.rsqrt(jnp.mean(values * values, axis=-1, keepdims=True) + EPSILON)
    return values * scale * gain


def forward_product(left, right):
    return jnp.dot(left, right, preferred_element_type=jnp.float32)


def contract_rows(left, right):
    return lax.dot_general(
        left, right, (((0,), (0,)), ((), ())), preferred_element_type=jnp.float32
    )


def contract_cols(left, right):
    return lax.dot_general(
        left, right, (((1,), (1,)), ((), ())), preferred_element_type=jnp.float32
    )


def block_mask(segs, row_start, block_rows):
    length = segs.shape[0]
    row_index = row_start + jnp.arange(block_rows, dtype=jnp.int32)
    col_index = jnp.arange(length, dtype=jnp.int32)
    return (segs[:, None] == segs[None, :]) & (row_index[:, None] >= col_index[None, :])


def head_forward(queries, keys, values, segs, block_rows):
    length, groups, head_dim = queries.shape
    scale = head_dim ** (-0.5)
    block_count = length // block_rows
    starts = jnp.arange(block_count, dtype=jnp.int32) * block_rows
    blocks = queries.reshape(block_count, block_rows, groups, head_dim)

    def one_block(inputs_blk):
        query_blk, row_start = inputs_blk
        raw = jnp.einsum("tgd,sd->gts", query_blk, keys, preferred_element_type=jnp.float32) * scale
        allowed = block_mask(segs, row_start, block_rows)
        scores = jnp.where(allowed[None], raw, NEGATIVE)
        row_max = jnp.max(scores, axis=-1, keepdims=True)
        exponent = jnp.exp(scores - row_max)
        row_total = jnp.sum(exponent, axis=-1, keepdims=True)
        probs = (exponent / row_total).astype(jnp.bfloat16)
        attended = jnp.einsum("gts,sd->tgd", probs, values, preferred_element_type=jnp.float32)
        return (attended, (row_max + jnp.log(row_total))[..., 0])

    attended_all, log_totals = lax.map(one_block, (blocks, starts))
    return (attended_all.reshape(length, groups, head_dim), log_totals)


def head_backward(queries, keys, values, grad_heads, log_totals, segs, block_rows):
    length, groups, head_dim = queries.shape
    scale = head_dim ** (-0.5)
    block_count = length // block_rows
    starts = jnp.arange(block_count, dtype=jnp.int32) * block_rows
    query_blocks = queries.reshape(block_count, block_rows, groups, head_dim)
    grad_blocks = grad_heads.reshape(block_count, block_rows, groups, head_dim)

    def one_block(carry, inputs_blk):
        key_grad, value_grad = carry
        query_blk, grad_blk, log_blk, row_start = inputs_blk
        raw = jnp.einsum("tgd,sd->gts", query_blk, keys, preferred_element_type=jnp.float32) * scale
        allowed = block_mask(segs, row_start, block_rows)
        scores = jnp.where(allowed[None], raw, NEGATIVE)
        probs = jnp.exp(scores - log_blk[..., None])
        value_grad = value_grad + jnp.einsum(
            "gts,tgd->sd", probs.astype(jnp.bfloat16), grad_blk, preferred_element_type=jnp.float32
        )
        prob_grad = jnp.einsum("tgd,sd->gts", grad_blk, values, preferred_element_type=jnp.float32)
        score_grad = (
            probs * (prob_grad - jnp.sum(prob_grad * probs, axis=-1, keepdims=True))
        ).astype(jnp.bfloat16)
        query_grad = (
            jnp.einsum("gts,sd->tgd", score_grad, keys, preferred_element_type=jnp.float32) * scale
        )
        key_grad = (
            key_grad
            + jnp.einsum("gts,tgd->sd", score_grad, query_blk, preferred_element_type=jnp.float32)
            * scale
        )
        return ((key_grad, value_grad), query_grad)

    zeros_head = jnp.zeros((length, head_dim), jnp.float32)
    (key_grad, value_grad), query_grads = lax.scan(
        one_block, (zeros_head, zeros_head), (query_blocks, grad_blocks, log_totals, starts)
    )
    return (query_grads.reshape(length, groups, head_dim), key_grad, value_grad)


def shards(
    tokens,
    segments,
    cotangent,
    w_query,
    w_key,
    w_value,
    w_output,
    w_gate,
    w_up,
    w_down,
    b_query,
    b_key,
    b_value,
    gain_attn,
    gain_mlp,
):
    (
        full_query,
        full_key,
        full_value,
        full_output,
        full_gate,
        full_up,
        full_down,
        bias_query,
        bias_key,
        bias_value,
        full_gain_attn,
        full_gain_mlp,
    ) = (
        lax.all_gather(w_query, "fsdp", axis=0, tiled=True),
        lax.all_gather(w_key, "fsdp", axis=0, tiled=True),
        lax.all_gather(w_value, "fsdp", axis=0, tiled=True),
        lax.all_gather(w_output, "fsdp", axis=0, tiled=True),
        lax.all_gather(w_gate, "fsdp", axis=0, tiled=True),
        lax.all_gather(w_up, "fsdp", axis=0, tiled=True),
        lax.all_gather(w_down, "fsdp", axis=0, tiled=True),
        lax.all_gather(b_query, "fsdp", axis=0, tiled=True),
        lax.all_gather(b_key, "fsdp", axis=0, tiled=True),
        lax.all_gather(b_value, "fsdp", axis=0, tiled=True),
        lax.all_gather(gain_attn, "fsdp", axis=0, tiled=True),
        lax.all_gather(gain_mlp, "fsdp", axis=0, tiled=True),
    )
    length = tokens.shape[0]
    heads = full_query.shape[1] // HEAD_DIM
    kv_heads = full_key.shape[1] // HEAD_DIM
    groups = heads // kv_heads
    block_rows = min(512, length)
    hidden_in = tokens.astype(jnp.float32)
    live = (segments >= 0).astype(jnp.float32)[:, None]
    cosine, sine = rope_tables(segments, HEAD_DIM)
    normed_low = normed(hidden_in, full_gain_attn.astype(jnp.float32)).astype(jnp.bfloat16)
    query_pre = forward_product(normed_low, full_query) + bias_query.astype(jnp.float32)
    key_pre = forward_product(normed_low, full_key) + bias_key.astype(jnp.float32)
    value_low = (forward_product(normed_low, full_value) + bias_value.astype(jnp.float32)).astype(
        jnp.bfloat16
    )
    query_rot = (
        rotate(query_pre.reshape(length, heads, HEAD_DIM), cosine, sine)
        .astype(jnp.bfloat16)
        .reshape(length, kv_heads, groups, HEAD_DIM)
    )
    key_rot = rotate(key_pre.reshape(length, kv_heads, HEAD_DIM), cosine, sine).astype(jnp.bfloat16)
    value_heads = value_low.reshape(length, kv_heads, HEAD_DIM)
    head_outputs = []
    head_logs = []
    for kv_head in range(kv_heads):
        attended, log_totals = head_forward(
            query_rot[:, kv_head],
            key_rot[:, kv_head],
            value_heads[:, kv_head],
            segments,
            block_rows,
        )
        head_outputs.append(attended)
        head_logs.append(log_totals)
    attended_low = (
        jnp.stack(head_outputs, axis=1).reshape(length, heads * HEAD_DIM).astype(jnp.bfloat16)
    )
    middle = hidden_in + live * forward_product(attended_low, full_output)
    mid_low = normed(middle, full_gain_mlp.astype(jnp.float32)).astype(jnp.bfloat16)
    gate = forward_product(mid_low, full_gate)
    upward = forward_product(mid_low, full_up)
    activ_low = (jax.nn.silu(gate) * upward).astype(jnp.bfloat16)
    output = (middle + live * forward_product(activ_low, full_down)).astype(jnp.bfloat16)
    (
        back_query,
        back_key,
        back_value,
        back_output,
        back_gate,
        back_up,
        back_down,
        back_gain_attn,
        back_gain_mlp,
    ) = (
        lax.all_gather(w_query, "fsdp", axis=0, tiled=True),
        lax.all_gather(w_key, "fsdp", axis=0, tiled=True),
        lax.all_gather(w_value, "fsdp", axis=0, tiled=True),
        lax.all_gather(w_output, "fsdp", axis=0, tiled=True),
        lax.all_gather(w_gate, "fsdp", axis=0, tiled=True),
        lax.all_gather(w_up, "fsdp", axis=0, tiled=True),
        lax.all_gather(w_down, "fsdp", axis=0, tiled=True),
        lax.all_gather(gain_attn, "fsdp", axis=0, tiled=True),
        lax.all_gather(gain_mlp, "fsdp", axis=0, tiled=True),
    )
    grad_in = cotangent.astype(jnp.float32)
    mlp_grad = (live * grad_in).astype(jnp.bfloat16)
    grad_down = contract_rows(activ_low, mlp_grad)
    activ_grad = contract_cols(mlp_grad, back_down)
    sigmoid_gate = jax.nn.sigmoid(gate)
    gate_grad = (activ_grad * upward * sigmoid_gate * (1.0 + gate * (1.0 - sigmoid_gate))).astype(
        jnp.bfloat16
    )
    up_grad = (activ_grad * gate * sigmoid_gate).astype(jnp.bfloat16)
    grad_gate = contract_rows(mid_low, gate_grad)
    grad_up = contract_rows(mid_low, up_grad)
    mid_norm_grad = contract_cols(gate_grad, back_gate) + contract_cols(up_grad, back_up)
    mid_pull = jax.vjp(normed, middle, back_gain_mlp.astype(jnp.float32))[1]
    middle_grad, gain_mlp_grad = mid_pull(mid_norm_grad)
    middle_grad = middle_grad + grad_in
    attn_grad = (live * middle_grad).astype(jnp.bfloat16)
    grad_output = contract_rows(attended_low, attn_grad)
    attended_grad = (
        contract_cols(attn_grad, back_output)
        .astype(jnp.bfloat16)
        .reshape(length, kv_heads, groups, HEAD_DIM)
    )
    query_parts = []
    key_parts = []
    value_parts = []
    for kv_head in range(kv_heads):
        query_part, key_part, value_part = head_backward(
            query_rot[:, kv_head],
            key_rot[:, kv_head],
            value_heads[:, kv_head],
            attended_grad[:, kv_head],
            head_logs[kv_head],
            segments,
            block_rows,
        )
        query_parts.append(query_part)
        key_parts.append(key_part)
        value_parts.append(value_part)
    query_grad_rot = jnp.stack(query_parts, axis=1).reshape(length, heads, HEAD_DIM)
    key_grad_rot = jnp.stack(key_parts, axis=1)
    query_grad = (
        rotate(query_grad_rot, cosine, -sine).reshape(length, heads * HEAD_DIM).astype(jnp.bfloat16)
    )
    key_grad = (
        rotate(key_grad_rot, cosine, -sine)
        .reshape(length, kv_heads * HEAD_DIM)
        .astype(jnp.bfloat16)
    )
    value_grad = (
        jnp.stack(value_parts, axis=1).reshape(length, kv_heads * HEAD_DIM).astype(jnp.bfloat16)
    )
    grad_query = contract_rows(normed_low, query_grad)
    grad_key = contract_rows(normed_low, key_grad)
    grad_value = contract_rows(normed_low, value_grad)
    bias_query_grad = jnp.sum(query_grad.astype(jnp.float32), axis=0)
    bias_key_grad = jnp.sum(key_grad.astype(jnp.float32), axis=0)
    bias_value_grad = jnp.sum(value_grad.astype(jnp.float32), axis=0)
    in_norm_grad = (
        contract_cols(query_grad, back_query)
        + contract_cols(key_grad, back_key)
        + contract_cols(value_grad, back_value)
    )
    in_pull = jax.vjp(normed, hidden_in, back_gain_attn.astype(jnp.float32))[1]
    input_grad, gain_attn_grad = in_pull(in_norm_grad)
    input_grad = input_grad + middle_grad
    (
        shard_query,
        shard_key,
        shard_value,
        shard_output,
        shard_gate,
        shard_up,
        shard_down,
        shard_bias_query,
        shard_bias_key,
        shard_bias_value,
        shard_gain_attn,
        shard_gain_mlp,
    ) = (
        lax.psum_scatter(grad_query, "fsdp", scatter_dimension=0, tiled=True),
        lax.psum_scatter(grad_key, "fsdp", scatter_dimension=0, tiled=True),
        lax.psum_scatter(grad_value, "fsdp", scatter_dimension=0, tiled=True),
        lax.psum_scatter(grad_output, "fsdp", scatter_dimension=0, tiled=True),
        lax.psum_scatter(grad_gate, "fsdp", scatter_dimension=0, tiled=True),
        lax.psum_scatter(grad_up, "fsdp", scatter_dimension=0, tiled=True),
        lax.psum_scatter(grad_down, "fsdp", scatter_dimension=0, tiled=True),
        lax.psum_scatter(bias_query_grad, "fsdp", scatter_dimension=0, tiled=True),
        lax.psum_scatter(bias_key_grad, "fsdp", scatter_dimension=0, tiled=True),
        lax.psum_scatter(bias_value_grad, "fsdp", scatter_dimension=0, tiled=True),
        lax.psum_scatter(gain_attn_grad, "fsdp", scatter_dimension=0, tiled=True),
        lax.psum_scatter(gain_mlp_grad, "fsdp", scatter_dimension=0, tiled=True),
    )
    replicas = lax.psum(
        (
            shard_query,
            shard_key,
            shard_value,
            shard_output,
            shard_gate,
            shard_up,
            shard_down,
            shard_bias_query,
            shard_bias_key,
            shard_bias_value,
            shard_gain_attn,
            shard_gain_mlp,
        ),
        "rep",
    )
    return (output, input_grad) + tuple(replicas)


def solution(mesh):
    placed = (
        P(("rep", "fsdp"), None),
        P(("rep", "fsdp")),
        P(("rep", "fsdp"), None),
        P("fsdp", None),
        P("fsdp", None),
        P("fsdp", None),
        P("fsdp", None),
        P("fsdp", None),
        P("fsdp", None),
        P("fsdp", None),
        P("fsdp"),
        P("fsdp"),
        P("fsdp"),
        P("fsdp"),
        P("fsdp"),
    )
    return jax.shard_map(
        shards,
        mesh=mesh,
        in_specs=placed,
        out_specs=(
            P(("rep", "fsdp"), None),
            P(("rep", "fsdp"), None),
            P("fsdp", None),
            P("fsdp", None),
            P("fsdp", None),
            P("fsdp", None),
            P("fsdp", None),
            P("fsdp", None),
            P("fsdp", None),
            P("fsdp"),
            P("fsdp"),
            P("fsdp"),
            P("fsdp"),
            P("fsdp"),
        ),
        check_vma=False,
    )
```

profile of v0, /device:TPU:1, one launch (start us, length us, event | category | flops | bytes accessed | tf_op | source)
XLA Modules:
  0.0 1752.1 jit_solution(11006961518384839466)
XLA Ops:
  11.9 5.6 all_gather.48
  17.5 0.9 fusion.59
  18.4 7.2 all_gather.46
  28.8 4.7 all-reduce.13
  34.1 1.2 fusion.32
  35.3 6.5 all-gather.6.cloned.1.call-done
  41.8 3.9 convolution_add_fusion
  45.8 1.8 copy.56
  47.9 1.3 fusion.83
  49.2 1.3 fusion.84
  50.5 1.0 fusion.7
  51.6 1.0 fusion.6
  52.6 1.4 fusion.31
  54.7 1.4 fusion.30
  56.0 1.0 pad_maximum_fusion.1
  57.1 14.0 all-gather.8.cloned.1.call-done
  71.0 3.1 multiply_reduce_fusion.2
  74.5 108.3 %all-gather.12.cloned.1.call-done = bf16[896,4864]{1,0:T(8,128)(2,1)} async-done(((bf16[448,4864]{1,0:T(8,128)(2,1)}), bf16[896,4864]{1,0:T(8,128)(2,1)}) %all-gather.12.cloned.1.call-update) | async-done | bytes 8716304 | tf_op jit(solution)/shard_map/all_gather | solution.py:166
  182.7 12.2 fusion.86
  195.0 99.3 %all-gather.10.cloned.1.call-done = bf16[896,4864]{1,0:T(8,128)(2,1)} async-done(((bf16[448,4864]{1,0:T(8,128)(2,1)}), bf16[896,4864]{1,0:T(8,128)(2,1)}) %all-gather.10.cloned.1.call-update) | async-done | bytes 8716304 | tf_op jit(solution)/shard_map/all_gather | solution.py:165
  294.3 11.7 fusion.85
  305.9 99.9 %all-gather.14.cloned.1.call-done = bf16[4864,896]{1,0:T(8,128)(2,1)} async-done(((bf16[2432,896]{1,0:T(8,128)(2,1)}), bf16[4864,896]{1,0:T(8,128)(2,1)}) %all-gather.14.cloned.1.call-update) | async-done | bytes 8716304 | tf_op jit(solution)/shard_map/all_gather | solution.py:167
  405.8 18.0 %multiply_convert_fusion = (bf16[512,4864]{1,0:T(8,128)(2,1)}, bf16[512,4864]{1,0:T(8,128)(2,1)}, bf16[512,4864]{1,0:T(8,128)(2,1)}) fusion(f32[512,4864]{1,0:T(8,128)} %fusion.85, f32[512,4864]{1,0:T(8,128)} %fusion.86, bf16[4864,896]{1,0:T(8,128)(2,1)} %all-gather.14.cloned.1.call-done, bf16[512,896]{1,0:T(8,128)(2,1)} %param.17, f32[512]{0:T(512)S(1)} %compare_convert_fusion), kind=kOutput, calls=%fused_computation | convolution fusion | flops 4503961600 | bytes 44500992 | tf_op jit(solution)/shard_map/dot_general | solution.py:56
  423.8 12.0 fusion.87
  435.8 11.3 multiply_reduce_fusion
  447.8 1.2 copy-done.4
  449.0 2.2 convolution_convert_fusion
  451.2 2.2 copy.59
  453.4 4.5 fusion.36
  458.0 5.6 fusion
  463.6 1.2 fusion.33
  464.8 4.2 fusion.3
  469.8 1.3 fusion.73
  471.4 7.5 fusion.5
  479.0 1.9 fusion.40
  480.9 7.0 fusion.2
  487.9 3.5 fusion.42
  491.6 1.3 fusion.75
  493.0 2.9 fusion.70
  496.0 2.9 fusion.26
  500.6 0.9 copy-done.21
  501.5 3.0 fusion.77
  505.0 11.1 fusion.49
  516.1 13.9 fusion.91
  530.2 13.5 fusion.90
  543.9 10.0 reduce-scatter.14.cloned.1.call-done
  553.9 47.0 %reduce-scatter.8.cloned.1.call-done = f32[448,896]{1,0:T(8,128)} async-done(((f32[896,896]{1,0:T(8,128)}), f32[448,896]{1,0:T(8,128)}) %reduce-scatter.8.cloned.1.call-update) | async-done | bytes 1605648 | tf_op jit(solution)/shard_map/reduce_scatter | solution.py:316
  600.9 198.4 %reduce-scatter.20.cloned.1.call-done = f32[2432,896]{1,0:T(8,128)} async-done(((f32[4864,896]{1,0:T(8,128)}), f32[2432,896]{1,0:T(8,128)}) %reduce-scatter.20.cloned.1.call-update) | async-done | bytes 8716304 | tf_op jit(solution)/shard_map/reduce_scatter | solution.py:322
  799.3 198.6 %reduce-scatter.18.cloned.1.call-done = f32[448,4864]{1,0:T(8,128)} async-done(((f32[896,4864]{1,0:T(8,128)}), f32[448,4864]{1,0:T(8,128)}) %reduce-scatter.18.cloned.1.call-update) | async-done | bytes 8716304 | tf_op jit(solution)/shard_map/reduce_scatter | solution.py:321
  997.9 198.4 %reduce-scatter.16.cloned.1.call-done = f32[448,4864]{1,0:T(8,128)} async-done(((f32[896,4864]{1,0:T(8,128)}), f32[448,4864]{1,0:T(8,128)}) %reduce-scatter.16.cloned.1.call-update) | async-done | bytes 8716304 | tf_op jit(solution)/shard_map/reduce_scatter | solution.py:320
  1198.3 3.0 fusion.88
  1201.4 2.1 fusion.21
  1203.5 5.3 all-reduce.12
  1209.2 34.6 %all-reduce.10 = (f32[448]{0:T(512)}, f32[64]{0:T(128)}, f32[64]{0:T(128)}, f32[448]{0:T(512)}, f32[448]{0:T(512)}) all-reduce(f32[448]{0:T(512)S(1)} %dynamic-slice.6, f32[64]{0:T(128)S(1)} %dynamic-slice.8, f32[64]{0:T(128)S(1)} %dynamic-slice.10, f32[448]{0:T(512)S(1)} %dynamic-slice.12, ...), channel_id=1, replica_groups=mesh['rep'=16,'fsdp'=2] {'rep'}, use_global_device_ids=true, to_apply=%region_28.29 | all-reduce | flops 1472 | bytes 11776 | tf_op jit(solution)/shard_map/psum | solution.py:329
  1243.8 3.4 fusion.23
  1247.2 10.6 add_convert_fusion
  1257.8 463.1 %all-reduce.16.cloned.1.call-done = (f32[448,896]{1,0:T(8,128)}, f32[448,128]{1,0:T(8,128)}, f32[448,128]{1,0:T(8,128)}, f32[448,896]{1,0:T(8,128)}, f32[448,486...) async-done(((f32[448,896]{1,0:T(8,128)}, f32[448,128]{1,0:T(8,128)}, f32[448,128]{1,0:T(8,128)}, f32[448,896]{1,0:T(8,128)}, f32[448,4864]{1,0:T(8,128)}, ...) | async-done | bytes 29818896 | tf_op jit(solution)/shard_map/psum | solution.py:329
  1720.9 2.8 copy.86
  1723.7 1.6 copy.87
  1726.0 1.2 copy.89
  1727.2 8.6 copy.90
  1735.8 4.4 copy.91
  1740.2 1.6 slice-done.7
  1741.9 3.5 copy.92
  (201 shorter events, 14.4 us)
Async XLA Ops:
  7.2 34.6 %all-gather.6.cloned.1.call-start = ((), (), s32[]{:S(2)}) async-start(), calls=%async_computation.7 | async-start | bytes 2408448 | tf_op jit(solution)/shard_map/all_gather | solution.py:161
  7.9 63.1 %all-gather.8.cloned.1.call-start = ((), (), s32[]{:S(2)}) async-start(), calls=%async_computation.8 | async-start | bytes 2408448 | tf_op jit(solution)/shard_map/all_gather | solution.py:164
  8.7 174.1 %all-gather.12.cloned.1.call-start = ((), (), s32[]{:S(2)}) async-start(), calls=%async_computation.10 | async-start | bytes 13074432 | tf_op jit(solution)/shard_map/all_gather | solution.py:166
  9.4 1.3 copy-start.40
  9.4 1.6 copy-start.6
  9.4 284.9 %all-gather.10.cloned.1.call-start = ((), (), s32[]{:S(2)}) async-start(), calls=%async_computation.9 | async-start | bytes 13074432 | tf_op jit(solution)/shard_map/all_gather | solution.py:165
  10.0 1.9 copy-start.38
  10.0 8.4 copy-start.39
  10.0 15.6 copy-start.43
  10.0 17.5 %copy-start.48 = (bf16[64]{0:T(256)(128)(2,1)S(1)}, bf16[64]{0:T(256)(128)(2,1)}, u32[]{:S(2)}) copy-start(bf16[64]{0:T(256)(128)(2,1)} %param.26) | copy-start | bytes 388
  10.0 17.8 %copy-start.49 = (bf16[64]{0:T(256)(128)(2,1)S(1)}, bf16[64]{0:T(256)(128)(2,1)}, u32[]{:S(2)}) copy-start(bf16[64]{0:T(256)(128)(2,1)} %param.27) | copy-start | bytes 388
  10.1 18.0 %copy-start.44 = (bf16[448]{0:T(512)(128)(2,1)S(1)}, bf16[448]{0:T(512)(128)(2,1)}, u32[]{:S(2)}) copy-start(bf16[448]{0:T(512)(128)(2,1)} %param.28) | copy-start | bytes 2692
  10.1 18.3 %copy-start.45 = (bf16[448]{0:T(512)(128)(2,1)S(1)}, bf16[448]{0:T(512)(128)(2,1)}, u32[]{:S(2)}) copy-start(bf16[448]{0:T(512)(128)(2,1)} %param.25) | copy-start | bytes 2692
  10.1 18.5 %copy-start.46 = (bf16[448]{0:T(512)(128)(2,1)S(1)}, bf16[448]{0:T(512)(128)(2,1)}, u32[]{:S(2)}) copy-start(bf16[448]{0:T(512)(128)(2,1)} %param.29) | copy-start | bytes 2692
  10.1 395.7 %all-gather.14.cloned.1.call-start = ((), (), s32[]{:S(2)}) async-start(), calls=%async_computation.11 | async-start | bytes 13074432 | tf_op jit(solution)/shard_map/all_gather | solution.py:167
  10.7 533.2 %reduce-scatter.12.cloned.1.call-start = ((), (), s32[]{:S(2)}) async-start(), calls=%async_computation.14 | async-start | bytes 688128 | tf_op jit(solution)/shard_map/reduce_scatter | solution.py:318
  11.2 6.3 copy-start.41
  17.5 28.3 %copy-start.23 = (bf16[896,128]{1,0:T(8,128)(2,1)}, bf16[896,128]{1,0:T(8,128)(2,1)S(1)}, u32[]{:S(2)}) copy-start(bf16[896,128]{1,0:T(8,128)(2,1)S(1)} %all_gather.48) | copy-start | bytes 688132
  25.7 16.2 copy-start.26
  49.2 3.4 copy-start
  50.5 4.2 copy-start.1
  74.2 373.1 %copy-start.17 = (f32[512,896]{1,0:T(8,128)}, f32[512,896]{1,0:T(8,128)S(1)}, u32[]{:S(2)}) copy-start(f32[512,896]{1,0:T(8,128)S(1)} %get-tuple-element.169) | copy-start | bytes 5505028
  74.4 219.8 %copy-start.11 = (bf16[512,896]{1,0:T(8,128)(2,1)}, bf16[512,896]{1,0:T(8,128)(2,1)S(1)}, u32[]{:S(2)}) copy-start(bf16[512,896]{1,0:T(8,128)(2,1)S(1)} %multiply_convert_fusion.4) | copy-start | bytes 2752516
  423.8 12.0 copy-start.19
  435.8 11.4 copy-start.25
  447.2 1.8 copy-start.47
  449.0 8.9 slice-start
  453.4 4.5 slice-start.1
  453.4 10.1 slice-start.4
  458.0 5.6 slice-start.5
  458.0 5.6 copy-start.12
  464.8 5.0 copy-start.7
  471.1 72.8 %reduce-scatter.10.cloned.1.call-start = ((), (), s32[]{:S(2)}) async-start(), calls=%async_computation.13 | async-start | bytes 688128 | tf_op jit(solution)/shard_map/reduce_scatter | solution.py:317
  471.4 9.4 slice-start.2
  471.4 7.5 copy-start.14
  471.4 7.5 copy-start.16
  471.4 9.4 slice-start.3
  479.0 8.9 copy-start.2
  487.9 3.5 copy-start.28
  487.9 3.5 copy-start.34
  487.9 3.7 copy-start.8
  487.9 5.1 copy-start.5
  491.4 1.6 copy-start.20
  491.6 4.3 copy-start.32
  492.9 61.0 %reduce-scatter.14.cloned.1.call-start = ((), (), s32[]{:S(2)}) async-start(), calls=%async_computation.15 | async-start | bytes 4816896 | tf_op jit(solution)/shard_map/reduce_scatter | solution.py:319
  495.9 105.0 %reduce-scatter.8.cloned.1.call-start = ((), (), s32[]{:S(2)}) async-start(), calls=%async_computation.12 | async-start | bytes 4816896 | tf_op jit(solution)/shard_map/reduce_scatter | solution.py:316
  495.9 3.1 copy-start.3
  499.8 1.7 copy-start.9
  504.5 294.7 %reduce-scatter.20.cloned.1.call-start = ((), (), s32[]{:S(2)}) async-start(), calls=%async_computation.18 | async-start | bytes 26148864 | tf_op jit(solution)/shard_map/reduce_scatter | solution.py:322
  516.1 481.8 %reduce-scatter.18.cloned.1.call-start = ((), (), s32[]{:S(2)}) async-start(), calls=%async_computation.17 | async-start | bytes 26148864 | tf_op jit(solution)/shard_map/reduce_scatter | solution.py:321
  530.1 666.2 %reduce-scatter.16.cloned.1.call-start = ((), (), s32[]{:S(2)}) async-start(), calls=%async_computation.16 | async-start | bytes 26148864 | tf_op jit(solution)/shard_map/reduce_scatter | solution.py:320
  543.6 1177.3 %all-reduce.16.cloned.1.call-start = ((), (), s32[]{:S(2)}) async-start(), calls=%async_computation.19 | async-start | bytes 59637760 | tf_op jit(solution)/shard_map/psum | solution.py:329
  1196.3 1.6 copy-start.24
  1196.3 1.6 copy-start.33
  1198.3 3.0 copy-start.27
  1198.3 3.0 copy-start.31
  1201.4 42.4 %copy-start.42 = (f32[512]{0:T(512)S(1)}, f32[512]{0:T(512)}, u32[]{:S(2)}) copy-start(f32[512]{0:T(512)} %copy-done.41) | copy-start | bytes 6148
  1243.8 3.4 copy-start.18
  1720.9 4.5 copy-start.35
  1720.9 5.1 copy-start.22
  1727.2 8.6 copy-start.10
  1727.2 13.0 slice-start.6
  1727.2 14.6 slice-start.7
  1735.8 6.1 slice-start.8
  (8 other events, 8.7 us)
Sparse Core Ops, SparseCore 0:
  9.6 32.2 all-gather.5
  43.4 27.6 all-gather.7
  72.6 110.0 all-gather.11
  184.1 110.0 all-gather.9
  295.7 110.0 all-gather.13
  471.3 13.8 reduce-scatter.11
  493.0 13.8 reduce-scatter.9
  509.8 44.0 reduce-scatter.13
  556.8 44.0 reduce-scatter.7
  603.1 196.1 reduce-scatter.19
  801.7 196.1 reduce-scatter.17
  1000.1 196.1 reduce-scatter.15
  1203.1 517.7 all-reduce.15
where the time goes:
time: 1760 us; the launch traced here: 1750 us
  waiting for transfers between devices  1450 us (82%)
  matrix products  169 us (10%)
  blocking collectives  57.3 us (3%)
  local copies, waits for them, and re-layouts  35 us (2%)
  other arithmetic  25 us (1%)
  between operations  17.6 us (1%)
    psum x1, waiting for transfers between devices, shards(): lax.psum((shard_query, shard_key, shard_value, shard_output, shard_gate,...  463 us
    reduce_scatter x1, waiting for transfers between devices, shards(): lax.psum_scatter(grad_up, 'fsdp', scatter_dimension=0, tiled=True)  199 us
    reduce_scatter x1, waiting for transfers between devices, shards(): lax.psum_scatter(grad_gate, 'fsdp', scatter_dimension=0, tiled=True)  198 us
    reduce_scatter x1, waiting for transfers between devices, shards(): lax.psum_scatter(grad_down, 'fsdp', scatter_dimension=0, tiled=True)  198 us
    all_gather x1, waiting for transfers between devices, shards(): lax.all_gather(w_up, 'fsdp', axis=0, tiled=True)  108 us
    all_gather x1, waiting for transfers between devices, shards(): lax.all_gather(w_down, 'fsdp', axis=0, tiled=True)  99.9 us
    all_gather x1, waiting for transfers between devices, shards(): lax.all_gather(w_gate, 'fsdp', axis=0, tiled=True)  99.3 us
    dot_general x7, matrix products, contract_cols(): lax.dot_general(left, right, (((1,), (1,)), ((), ())), preferred_element_...  49.1 us
  transfers between devices with their start and end apart: 13, of which 11 were waited for; matrix products, arithmetic and copies ran while one was open for 8% of the time, Pallas kernels for 0%

commit v1 on v0

--- a/solution.py
+++ b/solution.py
@@ -1,3 +1,5 @@
+import functools
+
 import jax
 import jax.numpy as jnp
 from jax import lax
@@ -127,6 +129,120 @@
     return (query_grads.reshape(length, groups, head_dim), key_grad, value_grad)
 
 
+def swapped(value, axis, bit, size):
+    step = 1 << bit
+    return lax.ppermute(value, axis, [(at, at ^ step) for at in range(size)])
+
+
+def chosen(parts, at):
+    return lax.dynamic_index_in_dim(parts, at, 0, keepdims=False)
+
+
+def added(left, right):
+    return (left.astype(jnp.float32) + right.astype(jnp.float32)).astype(jnp.bfloat16)
+
+
+def ordered(own, other, bit):
+    return jnp.where(bit == 0, jnp.stack([own, other]), jnp.stack([other, own]))
+
+
+class Group:
+    def __init__(self, size, replicas):
+        self.size = size
+        self.replicas = replicas
+        self.at = lax.axis_index("fsdp")
+        self.core = lax.axis_index("rep") & 1
+        self.pair = size == 2 and replicas % 2 == 0
+
+    def swap(self, value):
+        return swapped(value, "fsdp", 0, 2)
+
+    def rows_of_other(self, rows):
+        half = rows.shape[0] // 2
+        mine = lax.dynamic_slice_in_dim(rows, self.core * half, half, 0)
+        got = self.swap(mine)
+        both = ordered(got, swapped(got, "rep", 0, self.replicas), self.core)
+        return both.reshape(rows.shape)
+
+    def whole_rows(self, rows):
+        if not self.pair:
+            return lax.all_gather(rows, "fsdp", axis=0, tiled=True)
+        both = ordered(rows, self.rows_of_other(rows), self.at)
+        return both.reshape((2 * rows.shape[0],) + rows.shape[1:])
+
+    def whole_vector(self, vector):
+        if not self.pair:
+            return lax.all_gather(vector, "fsdp", axis=0, tiled=False)
+        return ordered(vector, self.swap(vector), self.at)
+
+    def my_columns(self, rows):
+        if not self.pair:
+            return lax.all_to_all(rows, "fsdp", 1, 0, tiled=True)
+        width = rows.shape[1] // 2
+        mine = lax.dynamic_slice_in_dim(rows, self.at * width, width, 1)
+        theirs = lax.dynamic_slice_in_dim(rows, (1 - self.at) * width, width, 1)
+        both = ordered(mine, self.rows_of_other(theirs), self.at)
+        return both.reshape(2 * rows.shape[0], width)
+
+    def all_tokens(self, value):
+        if not self.pair:
+            return lax.all_gather(value, "fsdp", axis=0, tiled=True)
+        return jnp.concatenate([value, self.swap(value)])
+
+    def own_tokens(self, partial):
+        if not self.pair:
+            return lax.psum_scatter(partial, "fsdp", scatter_dimension=0, tiled=True)
+        length = partial.shape[0] // 2
+        got = self.swap(partial[length:].astype(jnp.bfloat16))
+        return partial[:length] + got.astype(jnp.float32)
+
+    def sum_parts(self, parts):
+        if not self.pair:
+            return lax.psum_scatter(parts, "fsdp", scatter_dimension=0, tiled=False)
+        got = self.swap(chosen(parts, 1 - self.at))
+        return added(chosen(parts, self.at), got)
+
+    def exchange_parts(self, parts):
+        if not self.pair:
+            return lax.all_to_all(parts, "fsdp", 0, 0, tiled=True)
+        got = self.swap(chosen(parts, 1 - self.at))
+        return ordered(chosen(parts, self.at), got, self.at)
+
+
+class Replicas:
+    def __init__(self, size):
+        self.size = size
+        self.at = lax.axis_index("rep")
+        self.bits = size.bit_length() - 1
+        self.far = list(range(1, self.bits))
+
+    def bit(self, bit):
+        return (self.at >> bit) & 1
+
+    def scatter(self, parts, bit):
+        mine = self.bit(bit)
+        got = swapped(chosen(parts, 1 - mine), "rep", bit, self.size)
+        return added(chosen(parts, mine), got)
+
+    def gather(self, value, bit):
+        return ordered(value, swapped(value, "rep", bit, self.size), self.bit(bit))
+
+    def scatter_all(self, parts, order):
+        for bit in order:
+            parts = self.scatter(parts.reshape((2, parts.shape[0] // 2) + parts.shape[1:]), bit)
+        return parts.reshape(parts.shape[1:])
+
+    def gather_all(self, value, order):
+        value = value[None]
+        for bit in reversed(order):
+            value = self.gather(value, bit)
+            value = value.reshape((value.shape[0] * value.shape[1],) + value.shape[2:])
+        return value
+
+    def both_cores(self, value):
+        return self.gather(value, 0)
+
+
 def shards(
     tokens,
     segments,
@@ -143,48 +259,46 @@
     b_value,
     gain_attn,
     gain_mlp,
+    group_size,
+    replica_count,
 ):
-    (
-        full_query,
-        full_key,
-        full_value,
-        full_output,
-        full_gate,
-        full_up,
-        full_down,
-        bias_query,
-        bias_key,
-        bias_value,
-        full_gain_attn,
-        full_gain_mlp,
-    ) = (
-        lax.all_gather(w_query, "fsdp", axis=0, tiled=True),
-        lax.all_gather(w_key, "fsdp", axis=0, tiled=True),
-        lax.all_gather(w_value, "fsdp", axis=0, tiled=True),
-        lax.all_gather(w_output, "fsdp", axis=0, tiled=True),
-        lax.all_gather(w_gate, "fsdp", axis=0, tiled=True),
-        lax.all_gather(w_up, "fsdp", axis=0, tiled=True),
-        lax.all_gather(w_down, "fsdp", axis=0, tiled=True),
-        lax.all_gather(b_query, "fsdp", axis=0, tiled=True),
-        lax.all_gather(b_key, "fsdp", axis=0, tiled=True),
-        lax.all_gather(b_value, "fsdp", axis=0, tiled=True),
-        lax.all_gather(gain_attn, "fsdp", axis=0, tiled=True),
-        lax.all_gather(gain_mlp, "fsdp", axis=0, tiled=True),
-    )
+    group = Group(group_size, replica_count)
+    replicas = Replicas(replica_count)
+    far = replicas.far
+    near_first = [far[1], far[0]] + far[2:]
+    eighth = 1 << len(far)
+    width = tokens.shape[1]
+    rows_own = w_query.shape[0]
+    qw, kw = w_query.shape[1], w_key.shape[1]
+    vectors = group.whole_vector(
+        jnp.concatenate([b_query, b_key, b_value, gain_attn, gain_mlp])
+    ).astype(jnp.float32)
+    cuts = [0]
+    for part in (b_query, b_key, b_value, gain_attn, gain_mlp):
+        cuts.append(cuts[-1] + part.shape[0])
+    bias_query, bias_key, bias_value, full_gain_attn, full_gain_mlp = (
+        vectors[:, low:high].reshape(-1) for low, high in zip(cuts[:-1], cuts[1:])
+    )
+    full_qkv = group.whole_rows(jnp.concatenate([w_query, w_key, w_value], axis=1))
+    full_output = group.whole_rows(w_output)
+    part_gate = group.my_columns(w_gate)
+    part_up = group.my_columns(w_up)
     length = tokens.shape[0]
-    heads = full_query.shape[1] // HEAD_DIM
-    kv_heads = full_key.shape[1] // HEAD_DIM
+    heads = qw // HEAD_DIM
+    kv_heads = kw // HEAD_DIM
     groups = heads // kv_heads
     block_rows = min(512, length)
     hidden_in = tokens.astype(jnp.float32)
+    grad_in = cotangent.astype(jnp.float32)
     live = (segments >= 0).astype(jnp.float32)[:, None]
+    mlp_grad = (live * grad_in).astype(jnp.bfloat16)
+    mlp_grad_all = group.all_tokens(mlp_grad)
     cosine, sine = rope_tables(segments, HEAD_DIM)
-    normed_low = normed(hidden_in, full_gain_attn.astype(jnp.float32)).astype(jnp.bfloat16)
-    query_pre = forward_product(normed_low, full_query) + bias_query.astype(jnp.float32)
-    key_pre = forward_product(normed_low, full_key) + bias_key.astype(jnp.float32)
-    value_low = (forward_product(normed_low, full_value) + bias_value.astype(jnp.float32)).astype(
-        jnp.bfloat16
-    )
+    normed_low = normed(hidden_in, full_gain_attn).astype(jnp.bfloat16)
+    pre = forward_product(normed_low, full_qkv)
+    query_pre = pre[:, :qw] + bias_query
+    key_pre = pre[:, qw : qw + kw] + bias_key
+    value_low = (pre[:, qw + kw :] + bias_value).astype(jnp.bfloat16)
     query_rot = (
         rotate(query_pre.reshape(length, heads, HEAD_DIM), cosine, sine)
         .astype(jnp.bfloat16)
@@ -208,51 +322,50 @@
         jnp.stack(head_outputs, axis=1).reshape(length, heads * HEAD_DIM).astype(jnp.bfloat16)
     )
     middle = hidden_in + live * forward_product(attended_low, full_output)
-    mid_low = normed(middle, full_gain_mlp.astype(jnp.float32)).astype(jnp.bfloat16)
-    gate = forward_product(mid_low, full_gate)
-    upward = forward_product(mid_low, full_up)
-    activ_low = (jax.nn.silu(gate) * upward).astype(jnp.bfloat16)
-    output = (middle + live * forward_product(activ_low, full_down)).astype(jnp.bfloat16)
-    (
-        back_query,
-        back_key,
-        back_value,
-        back_output,
-        back_gate,
-        back_up,
-        back_down,
-        back_gain_attn,
-        back_gain_mlp,
-    ) = (
-        lax.all_gather(w_query, "fsdp", axis=0, tiled=True),
-        lax.all_gather(w_key, "fsdp", axis=0, tiled=True),
-        lax.all_gather(w_value, "fsdp", axis=0, tiled=True),
-        lax.all_gather(w_output, "fsdp", axis=0, tiled=True),
-        lax.all_gather(w_gate, "fsdp", axis=0, tiled=True),
-        lax.all_gather(w_up, "fsdp", axis=0, tiled=True),
-        lax.all_gather(w_down, "fsdp", axis=0, tiled=True),
-        lax.all_gather(gain_attn, "fsdp", axis=0, tiled=True),
-        lax.all_gather(gain_mlp, "fsdp", axis=0, tiled=True),
-    )
-    grad_in = cotangent.astype(jnp.float32)
-    mlp_grad = (live * grad_in).astype(jnp.bfloat16)
-    grad_down = contract_rows(activ_low, mlp_grad)
-    activ_grad = contract_cols(mlp_grad, back_down)
+    mid_low = normed(middle, full_gain_mlp).astype(jnp.bfloat16)
+
+    mid_all = group.all_tokens(mid_low)
+    gate = forward_product(mid_all, part_gate)
+    upward = forward_product(mid_all, part_up)
+    activ_grad = contract_cols(mlp_grad_all, w_down)
     sigmoid_gate = jax.nn.sigmoid(gate)
+    activ_low = (gate * sigmoid_gate * upward).astype(jnp.bfloat16)
     gate_grad = (activ_grad * upward * sigmoid_gate * (1.0 + gate * (1.0 - sigmoid_gate))).astype(
         jnp.bfloat16
     )
     up_grad = (activ_grad * gate * sigmoid_gate).astype(jnp.bfloat16)
-    grad_gate = contract_rows(mid_low, gate_grad)
-    grad_up = contract_rows(mid_low, up_grad)
-    mid_norm_grad = contract_cols(gate_grad, back_gate) + contract_cols(up_grad, back_up)
-    mid_pull = jax.vjp(normed, middle, back_gain_mlp.astype(jnp.float32))[1]
+
+    grad_down = contract_rows(activ_low, mlp_grad_all).astype(jnp.bfloat16)
+    down_half = replicas.scatter(grad_down.reshape(2, -1, width), 0)
+    down_piece = replicas.scatter_all(down_half.reshape(eighth, -1, width), far)
+    grad_pair = jnp.stack(
+        [
+            contract_rows(mid_all, gate_grad).astype(jnp.bfloat16),
+            contract_rows(mid_all, up_grad).astype(jnp.bfloat16),
+        ]
+    )
+    hidden = grad_pair.shape[2]
+    cut = -(-hidden // 256) * 128
+    pair_pieces = []
+    for low, high, order in ((0, cut, near_first), (cut, hidden, far)):
+        summed = replicas.scatter(grad_pair[:, :, low:high], 0)
+        summed = summed.reshape(group_size, eighth, rows_own // eighth, high - low)
+        piece = replicas.scatter_all(summed.transpose(1, 0, 2, 3), order)
+        piece = group.exchange_parts(piece)
+        pair_pieces.append((piece, order))
+    mid_norm_grad = group.own_tokens(
+        contract_cols(gate_grad, part_gate) + contract_cols(up_grad, part_up)
+    )
+    output = (middle + live * group.own_tokens(forward_product(activ_low, w_down))).astype(
+        jnp.bfloat16
+    )
+    mid_pull = jax.vjp(normed, middle, full_gain_mlp)[1]
     middle_grad, gain_mlp_grad = mid_pull(mid_norm_grad)
     middle_grad = middle_grad + grad_in
     attn_grad = (live * middle_grad).astype(jnp.bfloat16)
     grad_output = contract_rows(attended_low, attn_grad)
     attended_grad = (
-        contract_cols(attn_grad, back_output)
+        contract_cols(attn_grad, full_output)
         .astype(jnp.bfloat16)
         .reshape(length, kv_heads, groups, HEAD_DIM)
     )
@@ -274,32 +387,73 @@
         value_parts.append(value_part)
     query_grad_rot = jnp.stack(query_parts, axis=1).reshape(length, heads, HEAD_DIM)
     key_grad_rot = jnp.stack(key_parts, axis=1)
-    query_grad = (
-        rotate(query_grad_rot, cosine, -sine).reshape(length, heads * HEAD_DIM).astype(jnp.bfloat16)
-    )
-    key_grad = (
-        rotate(key_grad_rot, cosine, -sine)
-        .reshape(length, kv_heads * HEAD_DIM)
-        .astype(jnp.bfloat16)
-    )
-    value_grad = (
-        jnp.stack(value_parts, axis=1).reshape(length, kv_heads * HEAD_DIM).astype(jnp.bfloat16)
-    )
-    grad_query = contract_rows(normed_low, query_grad)
-    grad_key = contract_rows(normed_low, key_grad)
-    grad_value = contract_rows(normed_low, value_grad)
-    bias_query_grad = jnp.sum(query_grad.astype(jnp.float32), axis=0)
-    bias_key_grad = jnp.sum(key_grad.astype(jnp.float32), axis=0)
-    bias_value_grad = jnp.sum(value_grad.astype(jnp.float32), axis=0)
-    in_norm_grad = (
-        contract_cols(query_grad, back_query)
-        + contract_cols(key_grad, back_key)
-        + contract_cols(value_grad, back_value)
-    )
-    in_pull = jax.vjp(normed, hidden_in, back_gain_attn.astype(jnp.float32))[1]
+    qkv_grad = jnp.concatenate(
+        [
+            rotate(query_grad_rot, cosine, -sine).reshape(length, qw),
+            rotate(key_grad_rot, cosine, -sine).reshape(length, kw),
+            jnp.stack(value_parts, axis=1).reshape(length, kw),
+        ],
+        axis=1,
+    ).astype(jnp.bfloat16)
+    grad_qkv = contract_rows(normed_low, qkv_grad)
+    bias_grad = jnp.sum(qkv_grad.astype(jnp.float32), axis=0)
+    in_norm_grad = contract_cols(qkv_grad, full_qkv)
+    in_pull = jax.vjp(normed, hidden_in, full_gain_attn)[1]
     input_grad, gain_attn_grad = in_pull(in_norm_grad)
     input_grad = input_grad + middle_grad
-    (
+
+    small = jnp.concatenate(
+        [
+            part.reshape(group_size, -1)
+            for part in (
+                bias_grad[:qw],
+                bias_grad[qw : qw + kw],
+                bias_grad[qw + kw :],
+                gain_attn_grad,
+                gain_mlp_grad,
+            )
+        ],
+        axis=1,
+    ).astype(jnp.bfloat16)
+    columns = grad_qkv.shape[1] + qw
+    extra = 16
+    small = jnp.pad(small, ((0, 0), (0, extra * columns - small.shape[1])))
+    attn_all = jnp.concatenate(
+        [
+            jnp.concatenate([grad_qkv, grad_output], axis=1)
+            .astype(jnp.bfloat16)
+            .reshape(group_size, rows_own, columns),
+            small.reshape(group_size, extra, columns),
+        ],
+        axis=1,
+    )
+    attn_half = replicas.scatter(
+        attn_all.reshape(group_size, 2, (rows_own + extra) // 2, columns).transpose(1, 0, 2, 3), 0
+    )
+    attn_own = group.sum_parts(attn_half)
+    attn_cols = attn_own.reshape(-1, eighth, columns // eighth).transpose(1, 0, 2)
+    attn_piece = replicas.scatter_all(attn_cols, far)
+
+    down_sum = replicas.both_cores(replicas.gather_all(down_piece, far))
+    shard_down = down_sum.reshape(-1, width).astype(jnp.float32)
+    halves = []
+    for piece, order in pair_pieces:
+        full = replicas.both_cores(replicas.gather_all(piece, order))
+        halves.append(full.transpose(0, 1, 3, 2, 4).reshape(2, rows_own, group_size, -1))
+    shard_pair = jnp.concatenate(halves, axis=3).reshape(2, rows_own, -1)
+    shard_gate = shard_pair[0].astype(jnp.float32)
+    shard_up = shard_pair[1].astype(jnp.float32)
+    attn_sum = replicas.both_cores(replicas.gather_all(attn_piece, far))
+    attn_sum = attn_sum.transpose(0, 2, 1, 3).reshape(rows_own + extra, columns).astype(jnp.float32)
+    shard_query = attn_sum[:rows_own, :qw]
+    shard_key = attn_sum[:rows_own, qw : qw + kw]
+    shard_value = attn_sum[:rows_own, qw + kw : qw + 2 * kw]
+    shard_output = attn_sum[:rows_own, qw + 2 * kw :]
+    vector_sum = attn_sum[rows_own:].reshape(-1)
+    shard_vectors = tuple(vector_sum[low:high] for low, high in zip(cuts[:-1], cuts[1:]))
+    return (
+        output,
+        input_grad,
         shard_query,
         shard_key,
         shard_value,
@@ -307,43 +461,7 @@
         shard_gate,
         shard_up,
         shard_down,
-        shard_bias_query,
-        shard_bias_key,
-        shard_bias_value,
-        shard_gain_attn,
-        shard_gain_mlp,
-    ) = (
-        lax.psum_scatter(grad_query, "fsdp", scatter_dimension=0, tiled=True),
-        lax.psum_scatter(grad_key, "fsdp", scatter_dimension=0, tiled=True),
-        lax.psum_scatter(grad_value, "fsdp", scatter_dimension=0, tiled=True),
-        lax.psum_scatter(grad_output, "fsdp", scatter_dimension=0, tiled=True),
-        lax.psum_scatter(grad_gate, "fsdp", scatter_dimension=0, tiled=True),
-        lax.psum_scatter(grad_up, "fsdp", scatter_dimension=0, tiled=True),
-        lax.psum_scatter(grad_down, "fsdp", scatter_dimension=0, tiled=True),
-        lax.psum_scatter(bias_query_grad, "fsdp", scatter_dimension=0, tiled=True),
-        lax.psum_scatter(bias_key_grad, "fsdp", scatter_dimension=0, tiled=True),
-        lax.psum_scatter(bias_value_grad, "fsdp", scatter_dimension=0, tiled=True),
-        lax.psum_scatter(gain_attn_grad, "fsdp", scatter_dimension=0, tiled=True),
-        lax.psum_scatter(gain_mlp_grad, "fsdp", scatter_dimension=0, tiled=True),
-    )
-    replicas = lax.psum(
-        (
-            shard_query,
-            shard_key,
-            shard_value,
-            shard_output,
-            shard_gate,
-            shard_up,
-            shard_down,
-            shard_bias_query,
-            shard_bias_key,
-            shard_bias_value,
-            shard_gain_attn,
-            shard_gain_mlp,
-        ),
-        "rep",
-    )
-    return (output, input_grad) + tuple(replicas)
+    ) + shard_vectors
 
 
 def solution(mesh):
@@ -365,7 +483,9 @@
         P("fsdp"),
     )
     return jax.shard_map(
-        shards,
+        functools.partial(
+            shards, group_size=mesh.shape["fsdp"], replica_count=mesh.shape["rep"]
+        ),
         mesh=mesh,
         in_specs=placed,
         out_specs=(

time: 1760 us -> 560 us (0.32)
  waiting for transfers between devices: 1450 us -> 172 us
  starting transfers between devices: 1.31 us -> 89.8 us
  blocking collectives: 57.3 us -> 0 us
  local copies, waits for them, and re-layouts: 35 us -> 86.5 us
  other arithmetic: 25 us -> 75.5 us
  matrix products: 169 us -> 126 us
    reduce_scatter x7 -> x0, waiting for transfers between devices: 652 us -> none  [the longest x1 199 us: shards(): lax.psum_scatter(grad_up, 'fsdp', scatter_dimension=0, tiled=True)]
    psum x1 -> x0, waiting for transfers between devices: 463 us -> none  [shards(): lax.psum((shard_query, shard_key, shard_value, shard_output, shard_gate,...]
    all_gather x5 -> x0, waiting for transfers between devices: 328 us -> none  [the longest x1 108 us: shards(): lax.all_gather(w_up, 'fsdp', axis=0, tiled=True)]
    ppermute x0 -> x48, waiting for transfers between devices: none -> 172 us  [swapped(): return lax.ppermute(value, axis, [(at, at ^ step) for at in range(size)])]
    ppermute x0 -> x48, starting transfers between devices: none -> 89.8 us  [swapped(): return lax.ppermute(value, axis, [(at, at ^ step) for at in range(size)])]
    psum x1 -> x0, blocking collectives: 34.6 us -> none  [shards(): lax.psum((shard_query, shard_key, shard_value, shard_output, shard_gate,...]
    convert_element_type x6 -> x25, other arithmetic: 0.24 us -> 24.9 us  [the longest x17 12.9 us: added(): (left.astype(jnp.float32) + right.astype(jnp.float32)).astype(jnp.bfloat16)]
    dot_general x7 -> x5, matrix products: 47 us -> 23.3 us  [contract_rows(): lax.dot_general(left, right, (((0,), (0,)), ((), ())), preferred_element_...]
  transfers between devices with their start and end apart: 13 -> 48, of which waited for: 11 -> 18; matrix products, arithmetic and copies ran while one was open for 8% -> 38% of each run, Pallas kernels for 0% -> 0%
where the time goes in v1:
time: 560 us; the launch traced here: 552 us
  waiting for transfers between devices  172 us (31%)
  matrix products  126 us (22%)
  starting transfers between devices  89.8 us (16%)
  local copies, waits for them, and re-layouts  86.5 us (15%)
  other arithmetic  75.5 us (13%)
    ppermute x48, waiting for transfers between devices, swapped(): return lax.ppermute(value, axis, [(at, at ^ step) for at in range(size)])  172 us
    ppermute x48, starting transfers between devices, swapped(): return lax.ppermute(value, axis, [(at, at ^ step) for at in range(size)])  89.8 us
    dot_general x5, matrix products, contract_cols(): lax.dot_general(left, right, (((1,), (1,)), ((), ())), preferred_element_...  36.3 us
    dot_general x5, matrix products, forward_product(): return jnp.dot(left, right, preferred_element_type=jnp.float32)  26.5 us
    unnamed x179, local copies, waits for them, and re-layouts  25.7 us
    dot_general x5, matrix products, contract_rows(): lax.dot_general(left, right, (((0,), (0,)), ((), ())), preferred_element_...  23.3 us
    select_n x28, other arithmetic, ordered(): return jnp.where(bit == 0, jnp.stack([own, other]), jnp.stack([other, own]))  16.9 us
    convert_element_type x17, other arithmetic, added(): (left.astype(jnp.float32) + right.astype(jnp.float32)).astype(jnp.bfloat16)  12.9 us
  transfers between devices with their start and end apart: 48, of which 18 were waited for; matrix products, arithmetic and copies ran while one was open for 38% of the time, Pallas kernels for 0%

profile of v1, /device:TPU:1, one launch (start us, length us, event | category | flops | bytes accessed | tf_op | source)
XLA Modules:
  0.0 551.8 jit_solution(2697931079044947539)
XLA Ops:
  0.7 4.2 concatenate.213
  13.5 2.9 dynamic_slice.165
  19.6 3.1 dynamic-slice_bitcast_fusion.2
  22.7 3.1 dynamic-slice_bitcast_fusion.3
  28.1 2.8 dynamic_slice.163
  34.5 15.0 %collective-permute-done.1 = bf16[224,1152]{1,0:T(8,128)(2,1)} collective-permute-done((bf16[224,1152]{1,0:T(8,128)(2,1)S(1)}, bf16[224,1152]{1,0:T(8,128)(2,1)}, u32[]{:S(2)}, u32[]{:S(2)}) %collective-permute-start.1) | collective-permute-done | bytes 516128 | tf_op jit(solution)/shard_map/ppermute | solution.py:134
  49.5 3.3 collective-permute-start.2
  71.2 4.3 fusion.124
  75.5 4.3 fusion.125
  80.0 4.3 fusion.7
  90.2 6.1 %collective-permute-done.6 = bf16[224,2432]{1,0:T(8,128)(2,1)} collective-permute-done((bf16[224,2432]{1,0:T(8,128)(2,1)}, bf16[224,2432]{1,0:T(8,128)(2,1)}, u32[]{:S(2)}, u32[]{:S(2)}) %collective-permute-start.6) | collective-permute-done | bytes 1089568 | tf_op jit(solution)/shard_map/ppermute | solution.py:134
  100.7 3.0 maximum_select_fusion.6
  106.1 15.8 %collective-permute-done.5 = bf16[512,896]{1,0:T(8,128)(2,1)S(1)} collective-permute-done((bf16[512,896]{1,0:T(8,128)(2,1)S(1)}, bf16[512,896]{1,0:T(8,128)(2,1)S(1)}, u32[]{:S(2)}, u32[]{:S(2)}) %collective-permute-start.5) | collective-permute-done | bytes 917536 | tf_op jit(solution)/shard_map/ppermute | solution.py:134
  121.8 9.3 %fusion.111 = f32[1024,2432]{1,0:T(8,128)} fusion(bf16[896,2432]{1,0:T(8,128)(2,1)S(1)} %bitcast.436, bf16[512,896]{1,0:T(8,128)(2,1)S(1)} %collective-permute-done.5, bf16[512,896]{1,0:T(8,128)(2,1)S(1)} %multiply_convert_fusion.4), kind=kOutput, calls=%fused_computation.278 | convolution fusion | flops 4466409472 | bytes 16154624 | tf_op jit(solution)/shard_map/dot_general | solution.py:48
  131.1 8.8 %fusion.112 = f32[1024,2432]{1,0:T(8,128)} fusion(bf16[896,2432]{1,0:T(8,128)(2,1)S(1)} %bitcast.434, bf16[512,896]{1,0:T(8,128)(2,1)S(1)} %collective-permute-done.5, bf16[512,896]{1,0:T(8,128)(2,1)S(1)} %multiply_convert_fusion.4), kind=kOutput, calls=%fused_computation.279 | convolution fusion | flops 4466409472 | bytes 16154624 | tf_op jit(solution)/shard_map/dot_general | solution.py:48
  139.9 16.6 %multiply_convert_fusion = (bf16[1024,2432]{1,0:T(8,128)(2,1)}, bf16[1024,2432]{1,0:T(8,128)(2,1)}, bf16[1024,2432]{1,0:T(8,128)(2,1)}) fusion(f32[1024,2432]{1,0:T(8,128)} %fusion.112, f32[1024,2432]{1,0:T(8,128)} %fusion.111, bf16[2432,896]{1,0:T(8,128)(2,1)} %param.24, bf16[512,896]{1,0:T(8,128)(2,1)} %collective-permute-done.11, bf16[512,896]{1,0:T(8,128)(2,1)} %fusion.41), kind=kOutput, calls=%fused_computation | convolution fusion | flops 4506255360 | bytes 41058304 | tf_op jit(solution)/shard_map/dot_general | solution.py:58
  156.5 9.0 %fusion.127 = f32[1024,896]{1,0:T(8,128)S(1)} fusion(bf16[1024,2432]{1,0:T(8,128)(2,1)} %get-tuple-element.101, bf16[896,2432]{1,0:T(8,128)(2,1)} %bitcast.435), kind=kOutput, calls=%fused_computation.292 | convolution fusion | flops 4462739456 | bytes 13008896 | tf_op jit(solution)/shard_map/dot_general | solution.py:58
  165.6 5.5 %convolution_add_fusion = f32[1024,896]{1,0:T(8,128)S(1)} fusion(f32[1024,896]{1,0:T(8,128)S(1)} %fusion.127, bf16[1024,2432]{1,0:T(8,128)(2,1)S(1)} %copy-done.64, bf16[896,2432]{1,0:T(8,128)(2,1)S(1)} %bitcast.437), kind=kOutput, calls=%fused_computation.125 | convolution fusion | flops 4463656960 | bytes 16678912 | tf_op jit(solution)/shard_map/dot_general | solution.py:58
  171.3 5.3 fusion.11
  176.7 5.3 fusion.10
  190.4 5.5 fusion.126
  197.5 7.4 %convolution_convert_fusion = bf16[2432,896]{1,0:T(8,128)(2,1)S(1)} fusion(bf16[1024,2432]{1,0:T(8,128)(2,1)S(1)} %bitcast.517, bf16[512,896]{1,0:T(8,128)(2,1)} %collective-permute-done.11, bf16[512,896]{1,0:T(8,128)(2,1)} %fusion.41), kind=kOutput, calls=%fused_computation.30 | convolution fusion | flops 4468588544 | bytes 11173888 | tf_op jit(solution)/shard_map/dot_general | solution.py:52
  208.7 8.1 %collective-permute-done.10 = bf16[512,896]{1,0:T(8,128)(2,1)S(1)} collective-permute-done((bf16[512,896]{1,0:T(8,128)(2,1)S(1)}, bf16[512,896]{1,0:T(8,128)(2,1)S(1)}, u32[]{:S(2)}, u32[]{:S(2)}) %collective-permute-start.10) | collective-permute-done | bytes 917536 | tf_op jit(solution)/shard_map/ppermute | solution.py:134
  222.1 2.6 copy.113
  224.7 4.5 fusion.73
  229.4 4.4 fusion
  233.8 7.0 %fusion.2 = bf16[7,512,512]{1,2,0:T(8,128)(2,1)} fusion(f32[512,512,7]{1,0,2:T(8,128)} %get-tuple-element.173, f32[7,512,512]{1,2,0:T(8,128)S(1)} %bitcast.378, f32[7,512]{1,0:T(8,128)S(1)} %get-tuple-element.172, f32[7,512]{1,0:T(8,128)S(1)} %log_add_fusion), kind=kLoop, calls=%fused_computation.12 | loop fusion | flops 7340032 | bytes 18378752 | tf_op jit(solution)/shard_map/while/body/eval_jaxpr/convert_element_type | solution.py:114
  240.8 4.1 fusion.63
  244.9 3.9 fusion.50
  248.8 5.0 fusion.70
  253.7 4.4 fusion.3
  258.1 5.2 fusion.5
  270.9 2.9 convolution_convert_fusion.3
  274.1 2.9 fusion.40
  277.7 2.4 pad_maximum_fusion.1
  284.2 2.8 fusion.18
  297.7 12.1 %collective-permute-done.32 = bf16[4,2,56,1152]{3,2,1,0:T(8,128)(2,1)S(1)} collective-permute-done((bf16[4,2,56,1152]{3,2,1,0:T(8,128)(2,1)S(1)}, bf16[4,2,56,1152]{3,2,1,0:T(8,128)(2,1)S(1)}, u32[]{:S(2)}, u32[]{:S(2)}) %collective-permute-start.32) | collective-permute-done | bytes 1032224 | tf_op jit(solution)/shard_map/ppermute | solution.py:134
  311.6 21.5 %collective-permute-done.41 = bf16[4,152,896]{2,1,0:T(8,128)(2,1)S(1)} collective-permute-done((bf16[4,152,896]{2,1,0:T(8,128)(2,1)S(1)}, bf16[4,152,896]{2,1,0:T(8,128)(2,1)S(1)}, u32[]{:S(2)}, u32[]{:S(2)}) %collective-permute-start.41) | collective-permute-done | bytes 1089568 | tf_op jit(solution)/shard_map/ppermute | solution.py:134
  344.9 5.3 collective-permute-done.34
  353.8 3.0 collective-permute-start.43
  360.7 18.3 %collective-permute-done.43 = bf16[1,152,896]{2,1,0:T(8,128)(2,1)S(1)} collective-permute-done((bf16[1,152,896]{2,1,0:T(8,128)(2,1)S(1)}, bf16[1,152,896]{2,1,0:T(8,128)(2,1)S(1)}, u32[]{:S(2)}, u32[]{:S(2)}) %collective-permute-start.43) | collective-permute-done | bytes 272416 | tf_op jit(solution)/shard_map/ppermute | solution.py:134
  379.3 3.7 collective-permute-start.16
  382.9 4.5 collective-permute-done.36
  387.5 3.4 collective-permute-start.37
  391.0 5.5 collective-permute-done.25
  397.1 5.3 collective-permute-done.44
  403.3 3.2 collective-permute-start.17
  406.7 8.7 %collective-permute-done.17 = bf16[1,232,256]{2,1,0:T(8,128)(2,1)S(1)} collective-permute-done((bf16[1,232,256]{2,1,0:T(8,128)(2,1)S(1)}, bf16[1,232,256]{2,1,0:T(8,128)(2,1)S(1)}, u32[]{:S(2)}, u32[]{:S(2)}) %collective-permute-start.17) | collective-permute-done | bytes 118816 | tf_op jit(solution)/shard_map/ppermute | solution.py:134
  415.5 2.9 collective-permute-start.18
  418.5 3.5 collective-permute-done.18
  422.0 9.3 %collective-permute-start.19 = (bf16[2,232,256]{2,1,0:T(8,128)(2,1)S(1)}, bf16[2,232,256]{2,1,0:T(8,128)(2,1)S(1)}, u32[]{:S(2)}, u32[]{:S(2)}) collective-permute-start(bf16[2,232,256]{2,1,0:T(8,128)(2,1)S(1)} %maximum_select_fusion.29), channel_id=1, source_target_pairs={{0,8},{2,10},{4,12},{6,14},{8,0},{10,2},{12,4},{14,6},{16,24},{18,... | collective-permute-start | bytes 712712 | tf_op jit(solution)/shard_map/ppermute | solution.py:134
  432.9 10.7 %collective-permute-done.19 = bf16[2,232,256]{2,1,0:T(8,128)(2,1)S(1)} collective-permute-done((bf16[2,232,256]{2,1,0:T(8,128)(2,1)S(1)}, bf16[2,232,256]{2,1,0:T(8,128)(2,1)S(1)}, u32[]{:S(2)}, u32[]{:S(2)}) %collective-permute-start.19) | collective-permute-done | bytes 237600 | tf_op jit(solution)/shard_map/ppermute | solution.py:134
  446.9 15.6 %collective-permute-done.20 = bf16[4,232,256]{2,1,0:T(8,128)(2,1)S(1)} collective-permute-done((bf16[4,232,256]{2,1,0:T(8,128)(2,1)S(1)}, bf16[4,232,256]{2,1,0:T(8,128)(2,1)S(1)}, u32[]{:S(2)}, u32[]{:S(2)}) %collective-permute-start.20) | collective-permute-done | bytes 475168 | tf_op jit(solution)/shard_map/ppermute | solution.py:134
  462.9 8.7 %collective-permute-start.21 = (bf16[8,232,256]{2,0,1:T(8,128)(2,1)S(1)}, bf16[8,232,256]{2,0,1:T(8,128)(2,1)S(1)}, u32[]{:S(2)}, u32[]{:S(2)}) collective-permute-start(bf16[8,232,256]{2,0,1:T(8,128)(2,1)S(1)} %copy.122), channel_id=1, source_target_pairs={{0,2},{2,0},{4,6},{6,4},{8,10},{10,8},{12,14},{14,12},{16,18},{18,... | collective-permute-start | bytes 2850824 | tf_op jit(solution)/shard_map/ppermute | solution.py:134
  471.6 3.2 collective-permute-done.28
  475.8 10.6 %collective-permute-start.39 = (bf16[8,2,56,1152]{3,2,0,1:T(8,128)(2,1)S(1)}, bf16[8,2,56,1152]{3,2,0,1:T(8,128)(2,1)S(1)}, u32[]{:S(2)}, u32[]{:S(2)}) collective-permute-start(bf16[8,2,56,1152]{3,2,0,1:T(8,128)(2,1)S(1)} %copy.132), channel_id=1, source_target_pairs={{0,2},{2,0},{4,6},{6,4},{8,10},{10,8},{12,14},{14,12},{16,18},{18,... | collective-permute-start | bytes 6193160 | tf_op jit(solution)/shard_map/ppermute | solution.py:134
  486.5 11.7 %collective-permute-done.46 = bf16[4,152,896]{2,1,0:T(8,128)(2,1)S(1)} collective-permute-done((bf16[4,152,896]{2,1,0:T(8,128)(2,1)S(1)}, bf16[4,152,896]{2,1,0:T(8,128)(2,1)S(1)}, u32[]{:S(2)}, u32[]{:S(2)}) %collective-permute-start.46) | collective-permute-done | bytes 1089568 | tf_op jit(solution)/shard_map/ppermute | solution.py:134
  498.5 4.6 collective-permute-start.47
  513.4 4.4 bitcast_convert_fusion
  518.7 2.7 fusion.16
  521.4 11.2 %copy.136 = f32[1,448,2,2432]{3,2,1,0:T(2,128)} copy(f32[1,448,2,2432]{3,1,2,0:T(8,128)S(1)} %get-tuple-element.103) | data formatting | bytes 17432576 | tf_op jit(solution)/shard_map/convert_element_type | solution.py:445
  532.6 7.5 %copy.152 = f32[56,8,2,2432]{3,1,2,0:T(8,128)} copy(f32[56,8,2,2432]{3,2,1,0:T(2,128)} %bitcast.387) | data formatting | bytes 17432576
  540.1 7.3 %copy.135 = f32[1,448,2,2432]{3,2,1,0:T(2,128)S(1)} copy(f32[1,448,2,2432]{3,1,2,0:T(8,128)S(1)} %get-tuple-element.104) | data formatting | bytes 17432576 | tf_op jit(solution)/shard_map/convert_element_type | solution.py:444
  547.5 4.1 copy.151
  (404 shorter events, 131.6 us)
Async XLA Ops:
  0.6 12.5 %copy-start.41 = (bf16[448,896]{1,0:T(8,128)(2,1)S(1)}, bf16[448,896]{1,0:T(8,128)(2,1)}, u32[]{:S(2)}) copy-start(bf16[448,896]{1,0:T(8,128)(2,1)} %param.18) | copy-start | bytes 2408452
  0.7 12.6 %copy-start.47 = (bf16[448,128]{1,0:T(8,128)(2,1)S(1)}, bf16[448,128]{1,0:T(8,128)(2,1)}, u32[]{:S(2)}) copy-start(bf16[448,128]{1,0:T(8,128)(2,1)} %param.19) | copy-start | bytes 344068
  0.7 12.6 %copy-start.48 = (bf16[448,128]{1,0:T(8,128)(2,1)S(1)}, bf16[448,128]{1,0:T(8,128)(2,1)}, u32[]{:S(2)}) copy-start(bf16[448,128]{1,0:T(8,128)(2,1)} %param.20) | copy-start | bytes 344068
  4.8 26.0 %collective-permute-start = (bf16[1472]{0:T(1024)(128)(2,1)}, bf16[1472]{0:T(1024)(128)(2,1)}, u32[]{:S(2)}, u32[]{:S(2)}) collective-permute-start(bf16[1472]{0:T(1024)(128)(2,1)} %concatenate.213), channel_id=1, source_target_pairs={{0,1},{1,0},{2,3},{3,2},{4,5},{5,4},{6,7},{7,6},{8,9},{9,8},{10,11... | collective-permute-start | bytes 8840 | tf_op jit(solution)/shard_map/ppermute | solution.py:134
  8.7 23.0 %collective-permute-start.3 = (bf16[224,896]{1,0:T(8,128)(2,1)}, bf16[224,896]{1,0:T(8,128)(2,1)}, u32[]{:S(2)}, u32[]{:S(2)}) collective-permute-start(bf16[224,896]{1,0:T(8,128)(2,1)} %constant_dynamic-slice_fusion.12), channel_id=1, source_target_pairs={{0,1},{1,0},{2,3},{3,2},{4,5},{5,4},{6,7},{7,6},{8,9},{9,8},{10,11... | collective-permute-start | bytes 1204232 | tf_op jit(solution)/shard_map/ppermute | solution.py:134
  11.7 128.2 %collective-permute-start.11 = (bf16[512,896]{1,0:T(8,128)(2,1)}, bf16[512,896]{1,0:T(8,128)(2,1)}, u32[]{:S(2)}, u32[]{:S(2)}) collective-permute-start(bf16[512,896]{1,0:T(8,128)(2,1)} %fusion.41), channel_id=1, source_target_pairs={{0,1},{1,0},{2,3},{3,2},{4,5},{5,4},{6,7},{7,6},{8,9},{9,8},{10,11... | collective-permute-start | bytes 2752520 | tf_op jit(solution)/shard_map/ppermute | solution.py:134
  13.4 36.2 %collective-permute-start.1 = (bf16[224,1152]{1,0:T(8,128)(2,1)S(1)}, bf16[224,1152]{1,0:T(8,128)(2,1)}, u32[]{:S(2)}, u32[]{:S(2)}) collective-permute-start(bf16[224,1152]{1,0:T(8,128)(2,1)S(1)} %constant_dynamic-slice_fusion.13), channel_id=1, source_target_pairs={{0,1},{1,0},{2,3},{3,2},{4,5},{5,4},{6,7},{7,6},{8,9},{9,8},{10,11... | collective-permute-start | bytes 1548296 | tf_op jit(solution)/shard_map/ppermute | solution.py:134
  16.3 73.7 %collective-permute-start.8 = (bf16[224,2432]{1,0:T(8,128)(2,1)}, bf16[224,2432]{1,0:T(8,128)(2,1)}, u32[]{:S(2)}, u32[]{:S(2)}) collective-permute-start(bf16[224,2432]{1,0:T(8,128)(2,1)} %dynamic_slice.165), channel_id=1, source_target_pairs={{0,1},{1,0},{2,3},{3,2},{4,5},{5,4},{6,7},{7,6},{8,9},{9,8},{10,11... | collective-permute-start | bytes 3268616 | tf_op jit(solution)/shard_map/ppermute | solution.py:134
  25.8 31.3 %copy-start.30 = (bf16[448,896]{1,0:T(8,128)(2,1)S(1)}, bf16[448,896]{1,0:T(8,128)(2,1)}, u32[]{:S(2)}) copy-start(bf16[448,896]{1,0:T(8,128)(2,1)} %param.21) | copy-start | bytes 2408452
  30.9 65.4 %collective-permute-start.6 = (bf16[224,2432]{1,0:T(8,128)(2,1)}, bf16[224,2432]{1,0:T(8,128)(2,1)}, u32[]{:S(2)}, u32[]{:S(2)}) collective-permute-start(bf16[224,2432]{1,0:T(8,128)(2,1)} %dynamic_slice.163), channel_id=1, source_target_pairs={{0,1},{1,0},{2,3},{3,2},{4,5},{5,4},{6,7},{7,6},{8,9},{9,8},{10,11... | collective-permute-start | bytes 3268616 | tf_op jit(solution)/shard_map/ppermute | solution.py:134
  31.7 23.9 %collective-permute-start.4 = (bf16[224,896]{1,0:T(8,128)(2,1)}, bf16[224,896]{1,0:T(8,128)(2,1)}, u32[]{:S(2)}, u32[]{:S(2)}) collective-permute-start(bf16[224,896]{1,0:T(8,128)(2,1)} %collective-permute-done.3), channel_id=1, source_target_pairs={{0,2},{2,0},{4,6},{6,4},{8,10},{10,8},{12,14},{14,12},{16,18},{18,... | collective-permute-start | bytes 1204232 | tf_op jit(solution)/shard_map/ppermute | solution.py:134
  49.5 9.1 %collective-permute-start.2 = (bf16[224,1152]{1,0:T(8,128)(2,1)}, bf16[224,1152]{1,0:T(8,128)(2,1)}, u32[]{:S(2)}, u32[]{:S(2)}) collective-permute-start(bf16[224,1152]{1,0:T(8,128)(2,1)} %collective-permute-done.1), channel_id=1, source_target_pairs={{0,2},{2,0},{4,6},{6,4},{8,10},{10,8},{12,14},{14,12},{16,18},{18,... | collective-permute-start | bytes 1548296 | tf_op jit(solution)/shard_map/ppermute | solution.py:134
  88.5 9.6 %copy-start.33 = (bf16[2,448,896]{2,1,0:T(8,128)(2,1)S(1)}, bf16[2,448,896]{2,1,0:T(8,128)(2,1)}, u32[]{:S(2)}) copy-start(bf16[2,448,896]{2,1,0:T(8,128)(2,1)} %maximum_select_fusion.12) | copy-start | bytes 4816900
  88.6 9.5 %copy-start.54 = (f32[512]{0:T(512)S(1)}, f32[512]{0:T(512)}, u32[]{:S(2)}) copy-start(f32[512]{0:T(512)} %copy-done.53) | copy-start | bytes 6148
  90.1 9.5 %copy-start.37 = (bf16[512,2,7,64]{0,3,2,1:T(8,128)(2,1)}, bf16[512,2,7,64]{0,3,2,1:T(8,128)(2,1)S(1)}, u32[]{:S(2)}) copy-start(bf16[512,2,7,64]{0,3,2,1:T(8,128)(2,1)S(1)} %maximum_convert_fusion) | copy-start | bytes 2752516
  90.1 9.8 %collective-permute-start.9 = (bf16[224,2432]{1,0:T(8,128)(2,1)}, bf16[224,2432]{1,0:T(8,128)(2,1)S(1)}, u32[]{:S(2)}, u32[]{:S(2)}) collective-permute-start(bf16[224,2432]{1,0:T(8,128)(2,1)} %collective-permute-done.8), channel_id=1, source_target_pairs={{0,2},{2,0},{4,6},{6,4},{8,10},{10,8},{12,14},{14,12},{16,18},{18,... | collective-permute-start | bytes 3268616 | tf_op jit(solution)/shard_map/ppermute | solution.py:134
  96.2 4.4 collective-permute-start.7
  99.8 31.3 %copy-start.39 = (bf16[512,896]{1,0:T(8,128)(2,1)}, bf16[512,896]{1,0:T(8,128)(2,1)S(1)}, u32[]{:S(2)}) copy-start(bf16[512,896]{1,0:T(8,128)(2,1)S(1)} %multiply_convert_fusion.4) | copy-start | bytes 2752516
  99.8 22.0 %collective-permute-start.5 = (bf16[512,896]{1,0:T(8,128)(2,1)S(1)}, bf16[512,896]{1,0:T(8,128)(2,1)S(1)}, u32[]{:S(2)}, u32[]{:S(2)}) collective-permute-start(bf16[512,896]{1,0:T(8,128)(2,1)S(1)} %multiply_convert_fusion.4), channel_id=1, source_target_pairs={{0,1},{1,0},{2,3},{3,2},{4,5},{5,4},{6,7},{7,6},{8,9},{9,8},{10,11... | collective-permute-start | bytes 2752520 | tf_op jit(solution)/shard_map/ppermute | solution.py:134
  104.5 26.6 %copy-start.16 = (bf16[2,448,2432]{2,1,0:T(8,128)(2,1)}, bf16[2,448,2432]{2,1,0:T(8,128)(2,1)S(1)}, u32[]{:S(2)}) copy-start(bf16[2,448,2432]{2,1,0:T(8,128)(2,1)S(1)} %maximum_select_fusion.1) | copy-start | bytes 13074436
  106.0 25.0 %copy-start.17 = (bf16[2,448,2432]{2,1,0:T(8,128)(2,1)}, bf16[2,448,2432]{2,1,0:T(8,128)(2,1)S(1)}, u32[]{:S(2)}) copy-start(bf16[2,448,2432]{2,1,0:T(8,128)(2,1)S(1)} %maximum_select_fusion.2) | copy-start | bytes 13074436
  121.8 9.3 %copy-start.62 = (bf16[512,896]{1,0:T(8,128)(2,1)}, bf16[512,896]{1,0:T(8,128)(2,1)S(1)}, u32[]{:S(2)}) copy-start(bf16[512,896]{1,0:T(8,128)(2,1)S(1)} %collective-permute-done.5) | copy-start | bytes 2752516
  156.5 9.1 %copy-start.64 = (bf16[1024,2432]{1,0:T(8,128)(2,1)S(1)}, bf16[1024,2432]{1,0:T(8,128)(2,1)}, u32[]{:S(2)}) copy-start(bf16[1024,2432]{1,0:T(8,128)(2,1)} %get-tuple-element.100) | copy-start | bytes 14942212
  171.2 36.8 %collective-permute-start.12 = (bf16[512,896]{1,0:T(8,128)(2,1)S(1)}, bf16[512,896]{1,0:T(8,128)(2,1)S(1)}, u32[]{:S(2)}, u32[]{:S(2)}) collective-permute-start(bf16[512,896]{1,0:T(8,128)(2,1)S(1)} %slice.366), channel_id=1, source_target_pairs={{0,1},{1,0},{2,3},{3,2},{4,5},{5,4},{6,7},{7,6},{8,9},{9,8},{10,11... | collective-permute-start | bytes 2752520 | tf_op jit(solution)/shard_map/ppermute | solution.py:134
  186.3 97.8 %collective-permute-start.31 = (bf16[896,1152]{1,0:T(8,128)(2,1)}, bf16[896,1152]{1,0:T(8,128)(2,1)}, u32[]{:S(2)}, u32[]{:S(2)}) collective-permute-start(bf16[896,1152]{1,0:T(8,128)(2,1)} %fusion.33), channel_id=1, source_target_pairs={{0,2},{2,0},{4,6},{6,4},{8,10},{10,8},{12,14},{14,12},{16,18},{18,... | collective-permute-start | bytes 6193160 | tf_op jit(solution)/shard_map/ppermute | solution.py:134
  189.1 102.4 %collective-permute-start.22 = (bf16[896,1280]{1,0:T(8,128)(2,1)}, bf16[896,1280]{1,0:T(8,128)(2,1)}, u32[]{:S(2)}, u32[]{:S(2)}) collective-permute-start(bf16[896,1280]{1,0:T(8,128)(2,1)} %dynamic-slice_bitcast_fusion), channel_id=1, source_target_pairs={{0,2},{2,0},{4,6},{6,4},{8,10},{10,8},{12,14},{14,12},{16,18},{18,... | collective-permute-start | bytes 6881288 | tf_op jit(solution)/shard_map/ppermute | solution.py:134
  196.0 20.9 %collective-permute-start.10 = (bf16[512,896]{1,0:T(8,128)(2,1)S(1)}, bf16[512,896]{1,0:T(8,128)(2,1)S(1)}, u32[]{:S(2)}, u32[]{:S(2)}) collective-permute-start(bf16[512,896]{1,0:T(8,128)(2,1)S(1)} %slice.367), channel_id=1, source_target_pairs={{0,1},{1,0},{2,3},{3,2},{4,5},{5,4},{6,7},{7,6},{8,9},{9,8},{10,11... | collective-permute-start | bytes 2752520 | tf_op jit(solution)/shard_map/ppermute | solution.py:134
  206.6 10.2 %copy-start.23 = (bf16[512,896]{1,0:T(8,128)(2,1)S(1)}, bf16[512,896]{1,0:T(8,128)(2,1)}, u32[]{:S(2)}) copy-start(bf16[512,896]{1,0:T(8,128)(2,1)} %param.17) | copy-start | bytes 2752516
  206.6 82.2 %collective-permute-start.40 = (bf16[1216,896]{1,0:T(8,128)(2,1)}, bf16[1216,896]{1,0:T(8,128)(2,1)}, u32[]{:S(2)}, u32[]{:S(2)}) collective-permute-start(bf16[1216,896]{1,0:T(8,128)(2,1)} %dynamic-slice_bitcast_fusion.1), channel_id=1, source_target_pairs={{0,2},{2,0},{4,6},{6,4},{8,10},{10,8},{12,14},{14,12},{16,18},{18,... | collective-permute-start | bytes 6537224 | tf_op jit(solution)/shard_map/ppermute | solution.py:134
  208.7 11.2 %copy-start.34 = (bf16[2,448,896]{2,1,0:T(8,128)(2,1)S(1)}, bf16[2,448,896]{2,1,0:T(8,128)(2,1)}, u32[]{:S(2)}) copy-start(bf16[2,448,896]{2,1,0:T(8,128)(2,1)} %maximum_select_fusion.12) | copy-start | bytes 4816900
  219.9 9.3 %slice-start = ((s8[7340032]{0:T(1024)(128)(4,1)}), s8[3145728]{0:T(1024)(128)(4,1)S(1)}, s32[]{:S(2)}) async-start(s8[7340032]{0:T(1024)(128)(4,1)} %bitcast.377), calls=%async_computation | async-start | bytes 6291456
  240.8 12.9 %slice-start.4 = ((s8[7340032]{0:T(1024)(128)(4,1)}), s8[4194304]{0:T(1024)(128)(4,1)S(1)}, s32[]{:S(2)}) async-start(s8[7340032]{0:T(1024)(128)(4,1)} %bitcast.381), calls=%async_computation.4 | async-start | bytes 8388608
  280.3 15.2 %collective-permute-start.13 = (bf16[2,232,2048]{2,1,0:T(8,128)(2,1)S(1)}, bf16[2,232,2048]{2,1,0:T(8,128)(2,1)S(1)}, u32[]{:S(2)}, u32[]{:S(2)}) collective-permute-start(bf16[2,232,2048]{2,1,0:T(8,128)(2,1)S(1)} %dynamic-slice_bitcast_fusion.4), channel_id=1, source_target_pairs={{0,2},{2,0},{4,6},{6,4},{8,10},{10,8},{12,14},{14,12},{16,18},{18,... | collective-permute-start | bytes 5701640 | tf_op jit(solution)/shard_map/ppermute | solution.py:134
  287.3 22.4 %collective-permute-start.32 = (bf16[4,2,56,1152]{3,2,1,0:T(8,128)(2,1)S(1)}, bf16[4,2,56,1152]{3,2,1,0:T(8,128)(2,1)S(1)}, u32[]{:S(2)}, u32[]{:S(2)}) collective-permute-start(bf16[4,2,56,1152]{3,2,1,0:T(8,128)(2,1)S(1)} %bitcast.482), channel_id=1, source_target_pairs={{0,4},{2,6},{4,0},{6,2},{8,12},{10,14},{12,8},{14,10},{16,20},{18,... | collective-permute-start | bytes 3096584 | tf_op jit(solution)/shard_map/ppermute | solution.py:134
  291.1 42.0 %collective-permute-start.41 = (bf16[4,152,896]{2,1,0:T(8,128)(2,1)S(1)}, bf16[4,152,896]{2,1,0:T(8,128)(2,1)S(1)}, u32[]{:S(2)}, u32[]{:S(2)}) collective-permute-start(bf16[4,152,896]{2,1,0:T(8,128)(2,1)S(1)} %dynamic-slice_bitcast_fusion.5), channel_id=1, source_target_pairs={{0,4},{2,6},{4,0},{6,2},{8,12},{10,14},{12,8},{14,10},{16,20},{18,... | collective-permute-start | bytes 3268616 | tf_op jit(solution)/shard_map/ppermute | solution.py:134
  294.0 41.8 %collective-permute-start.23 = (bf16[4,2,56,1280]{3,2,1,0:T(8,128)(2,1)S(1)}, bf16[4,2,56,1280]{3,2,1,0:T(8,128)(2,1)S(1)}, u32[]{:S(2)}, u32[]{:S(2)}) collective-permute-start(bf16[4,2,56,1280]{3,2,1,0:T(8,128)(2,1)S(1)} %bitcast.472), channel_id=1, source_target_pairs={{0,8},{2,10},{4,12},{6,14},{8,0},{10,2},{12,4},{14,6},{16,24},{18,... | collective-permute-start | bytes 3440648 | tf_op jit(solution)/shard_map/ppermute | solution.py:134
  296.4 44.2 %collective-permute-start.14 = (bf16[232,2048]{1,0:T(8,128)(2,1)S(1)}, bf16[232,2048]{1,0:T(8,128)(2,1)S(1)}, u32[]{:S(2)}, u32[]{:S(2)}) collective-permute-start(bf16[232,2048]{1,0:T(8,128)(2,1)S(1)} %dynamic-slice_bitcast_fusion.6), channel_id=1, source_target_pairs={{0,1},{1,0},{2,3},{3,2},{4,5},{5,4},{6,7},{7,6},{8,9},{9,8},{10,11... | collective-permute-start | bytes 2850824 | tf_op jit(solution)/shard_map/ppermute | solution.py:134
  310.1 28.0 %collective-permute-start.33 = (bf16[2,2,56,1152]{3,2,1,0:T(8,128)(2,1)S(1)}, bf16[2,2,56,1152]{3,2,1,0:T(8,128)(2,1)S(1)}, u32[]{:S(2)}, u32[]{:S(2)}) collective-permute-start(bf16[2,2,56,1152]{3,2,1,0:T(8,128)(2,1)S(1)} %dynamic-slice_bitcast_fusion.9), channel_id=1, source_target_pairs={{0,8},{2,10},{4,12},{6,14},{8,0},{10,2},{12,4},{14,6},{16,24},{18,... | collective-permute-start | bytes 1548296 | tf_op jit(solution)/shard_map/ppermute | solution.py:134
  334.3 18.3 %collective-permute-start.42 = (bf16[2,152,896]{2,1,0:T(8,128)(2,1)}, bf16[2,152,896]{2,1,0:T(8,128)(2,1)}, u32[]{:S(2)}, u32[]{:S(2)}) collective-permute-start(bf16[2,152,896]{2,1,0:T(8,128)(2,1)} %dynamic-slice_bitcast_fusion.8), channel_id=1, source_target_pairs={{0,8},{2,10},{4,12},{6,14},{8,0},{10,2},{12,4},{14,6},{16,24},{18,... | collective-permute-start | bytes 1634312 | tf_op jit(solution)/shard_map/ppermute | solution.py:134
  336.9 21.7 %collective-permute-start.24 = (bf16[2,2,56,1280]{3,2,1,0:T(8,128)(2,1)}, bf16[2,2,56,1280]{3,2,1,0:T(8,128)(2,1)}, u32[]{:S(2)}, u32[]{:S(2)}) collective-permute-start(bf16[2,2,56,1280]{3,2,1,0:T(8,128)(2,1)} %dynamic-slice_bitcast_fusion.7), channel_id=1, source_target_pairs={{0,4},{2,6},{4,0},{6,2},{8,12},{10,14},{12,8},{14,10},{16,20},{18,... | collective-permute-start | bytes 1720328 | tf_op jit(solution)/shard_map/ppermute | solution.py:134
  338.2 12.0 %collective-permute-start.34 = (bf16[1,2,56,1152]{3,2,1,0:T(8,128)(2,1)S(1)}, bf16[1,2,56,1152]{3,2,1,0:T(8,128)(2,1)}, u32[]{:S(2)}, u32[]{:S(2)}) collective-permute-start(bf16[1,2,56,1152]{3,2,1,0:T(8,128)(2,1)S(1)} %constant_dynamic-slice_fusion.2), channel_id=1, source_target_pairs={{0,16},{2,18},{4,20},{6,22},{8,24},{10,26},{12,28},{14,30},{16,0},... | collective-permute-start | bytes 774152 | tf_op jit(solution)/shard_map/ppermute | solution.py:134
  344.6 34.6 %collective-permute-start.15 = (bf16[4,232,256]{2,1,0:T(8,128)(2,1)S(1)}, bf16[4,232,256]{2,1,0:T(8,128)(2,1)S(1)}, u32[]{:S(2)}, u32[]{:S(2)}) collective-permute-start(bf16[4,232,256]{2,1,0:T(8,128)(2,1)S(1)} %bitcast.507), channel_id=1, source_target_pairs={{0,4},{2,6},{4,0},{6,2},{8,12},{10,14},{12,8},{14,10},{16,20},{18,... | collective-permute-start | bytes 1425416 | tf_op jit(solution)/shard_map/ppermute | solution.py:134
  351.3 5.5 collective-permute-start.35
  353.8 25.2 %collective-permute-start.43 = (bf16[1,152,896]{2,1,0:T(8,128)(2,1)S(1)}, bf16[1,152,896]{2,1,0:T(8,128)(2,1)S(1)}, u32[]{:S(2)}, u32[]{:S(2)}) collective-permute-start(bf16[1,152,896]{2,1,0:T(8,128)(2,1)S(1)} %constant_dynamic-slice_fusion), channel_id=1, source_target_pairs={{0,16},{2,18},{4,20},{6,22},{8,24},{10,26},{12,28},{14,30},{16,0},... | collective-permute-start | bytes 817160 | tf_op jit(solution)/shard_map/ppermute | solution.py:134
  356.8 30.6 %collective-permute-start.36 = (bf16[1,2,56,1152]{3,2,1,0:T(8,128)(2,1)S(1)}, bf16[1,2,56,1152]{3,2,1,0:T(8,128)(2,1)S(1)}, u32[]{:S(2)}, u32[]{:S(2)}) collective-permute-start(bf16[1,2,56,1152]{3,2,1,0:T(8,128)(2,1)S(1)} %maximum_select_fusion.27), channel_id=1, source_target_pairs={{0,16},{2,18},{4,20},{6,22},{8,24},{10,26},{12,28},{14,30},{16,0},... | collective-permute-start | bytes 774152 | tf_op jit(solution)/shard_map/ppermute | solution.py:134
  359.8 36.7 %collective-permute-start.25 = (bf16[1,2,56,1280]{3,2,1,0:T(8,128)(2,1)S(1)}, bf16[1,2,56,1280]{3,2,1,0:T(8,128)(2,1)S(1)}, u32[]{:S(2)}, u32[]{:S(2)}) collective-permute-start(bf16[1,2,56,1280]{3,2,1,0:T(8,128)(2,1)S(1)} %constant_dynamic-slice_fusion.6), channel_id=1, source_target_pairs={{0,16},{2,18},{4,20},{6,22},{8,24},{10,26},{12,28},{14,30},{16,0},... | collective-permute-start | bytes 860168 | tf_op jit(solution)/shard_map/ppermute | solution.py:134
  379.1 23.3 %collective-permute-start.44 = (bf16[1,152,896]{2,1,0:T(8,128)(2,1)S(1)}, bf16[1,152,896]{2,1,0:T(8,128)(2,1)S(1)}, u32[]{:S(2)}, u32[]{:S(2)}) collective-permute-start(bf16[1,152,896]{2,1,0:T(8,128)(2,1)S(1)} %add_convert_fusion.3), channel_id=1, source_target_pairs={{0,16},{2,18},{4,20},{6,22},{8,24},{10,26},{12,28},{14,30},{16,0},... | collective-permute-start | bytes 817160 | tf_op jit(solution)/shard_map/ppermute | solution.py:134
  379.3 23.9 %collective-permute-start.16 = (bf16[2,232,256]{2,1,0:T(8,128)(2,1)S(1)}, bf16[2,232,256]{2,1,0:T(8,128)(2,1)S(1)}, u32[]{:S(2)}, u32[]{:S(2)}) collective-permute-start(bf16[2,232,256]{2,1,0:T(8,128)(2,1)S(1)} %dynamic-slice_bitcast_fusion.10), channel_id=1, source_target_pairs={{0,8},{2,10},{4,12},{6,14},{8,0},{10,2},{12,4},{14,6},{16,24},{18,... | collective-permute-start | bytes 712712 | tf_op jit(solution)/shard_map/ppermute | solution.py:134
  387.5 43.8 %collective-permute-start.37 = (bf16[2,2,56,1152]{3,2,1,0:T(8,128)(2,1)S(1)}, bf16[2,2,56,1152]{3,2,1,0:T(8,128)(2,1)S(1)}, u32[]{:S(2)}, u32[]{:S(2)}) collective-permute-start(bf16[2,2,56,1152]{3,2,1,0:T(8,128)(2,1)S(1)} %maximum_select_fusion.24), channel_id=1, source_target_pairs={{0,8},{2,10},{4,12},{6,14},{8,0},{10,2},{12,4},{14,6},{16,24},{18,... | collective-permute-start | bytes 1548296 | tf_op jit(solution)/shard_map/ppermute | solution.py:134
  396.7 21.7 %collective-permute-start.26 = (bf16[56,1280]{1,0:T(8,128)(2,1)S(1)}, bf16[56,1280]{1,0:T(8,128)(2,1)S(1)}, u32[]{:S(2)}, u32[]{:S(2)}) collective-permute-start(bf16[56,1280]{1,0:T(8,128)(2,1)S(1)} %get-tuple-element.148), channel_id=1, source_target_pairs={{0,1},{1,0},{2,3},{3,2},{4,5},{5,4},{6,7},{7,6},{8,9},{9,8},{10,11... | collective-permute-start | bytes 430088 | tf_op jit(solution)/shard_map/ppermute | solution.py:134
  402.6 42.7 %collective-permute-start.45 = (bf16[2,152,896]{2,1,0:T(8,128)(2,1)S(1)}, bf16[2,152,896]{2,1,0:T(8,128)(2,1)S(1)}, u32[]{:S(2)}, u32[]{:S(2)}) collective-permute-start(bf16[2,152,896]{2,1,0:T(8,128)(2,1)S(1)} %maximum_select_fusion.22), channel_id=1, source_target_pairs={{0,8},{2,10},{4,12},{6,14},{8,0},{10,2},{12,4},{14,6},{16,24},{18,... | collective-permute-start | bytes 1634312 | tf_op jit(solution)/shard_map/ppermute | solution.py:134
  403.3 12.1 %collective-permute-start.17 = (bf16[1,232,256]{2,1,0:T(8,128)(2,1)S(1)}, bf16[1,232,256]{2,1,0:T(8,128)(2,1)S(1)}, u32[]{:S(2)}, u32[]{:S(2)}) collective-permute-start(bf16[1,232,256]{2,1,0:T(8,128)(2,1)S(1)} %constant_dynamic-slice_fusion.9), channel_id=1, source_target_pairs={{0,16},{2,18},{4,20},{6,22},{8,24},{10,26},{12,28},{14,30},{16,0},... | collective-permute-start | bytes 356360 | tf_op jit(solution)/shard_map/ppermute | solution.py:134
  415.5 6.5 %collective-permute-start.18 = (bf16[1,232,256]{2,1,0:T(8,128)(2,1)S(1)}, bf16[1,232,256]{2,1,0:T(8,128)(2,1)S(1)}, u32[]{:S(2)}, u32[]{:S(2)}) collective-permute-start(bf16[1,232,256]{2,1,0:T(8,128)(2,1)S(1)} %add_convert_fusion.5), channel_id=1, source_target_pairs={{0,16},{2,18},{4,20},{6,22},{8,24},{10,26},{12,28},{14,30},{16,0},... | collective-permute-start | bytes 356360 | tf_op jit(solution)/shard_map/ppermute | solution.py:134
  418.4 26.6 %collective-permute-start.27 = (bf16[1,2,56,1280]{3,2,1,0:T(8,128)(2,1)S(1)}, bf16[1,2,56,1280]{3,2,1,0:T(8,128)(2,1)S(1)}, u32[]{:S(2)}, u32[]{:S(2)}) collective-permute-start(bf16[1,2,56,1280]{3,2,1,0:T(8,128)(2,1)S(1)} %maximum_select_fusion.26), channel_id=1, source_target_pairs={{0,16},{2,18},{4,20},{6,22},{8,24},{10,26},{12,28},{14,30},{16,0},... | collective-permute-start | bytes 860168 | tf_op jit(solution)/shard_map/ppermute | solution.py:134
  422.0 21.6 %collective-permute-start.19 = (bf16[2,232,256]{2,1,0:T(8,128)(2,1)S(1)}, bf16[2,232,256]{2,1,0:T(8,128)(2,1)S(1)}, u32[]{:S(2)}, u32[]{:S(2)}) collective-permute-start(bf16[2,232,256]{2,1,0:T(8,128)(2,1)S(1)} %maximum_select_fusion.29), channel_id=1, source_target_pairs={{0,8},{2,10},{4,12},{6,14},{8,0},{10,2},{12,4},{14,6},{16,24},{18,... | collective-permute-start | bytes 712712 | tf_op jit(solution)/shard_map/ppermute | solution.py:134
  431.5 43.7 %collective-permute-start.38 = (bf16[4,2,56,1152]{3,2,1,0:T(8,128)(2,1)S(1)}, bf16[4,2,56,1152]{3,2,1,0:T(8,128)(2,1)S(1)}, u32[]{:S(2)}, u32[]{:S(2)}) collective-permute-start(bf16[4,2,56,1152]{3,2,1,0:T(8,128)(2,1)S(1)} %bitcast.448), channel_id=1, source_target_pairs={{0,4},{2,6},{4,0},{6,2},{8,12},{10,14},{12,8},{14,10},{16,20},{18,... | collective-permute-start | bytes 3096584 | tf_op jit(solution)/shard_map/ppermute | solution.py:134
  443.6 18.9 %collective-permute-start.20 = (bf16[4,232,256]{2,1,0:T(8,128)(2,1)S(1)}, bf16[4,232,256]{2,1,0:T(8,128)(2,1)S(1)}, u32[]{:S(2)}, u32[]{:S(2)}) collective-permute-start(bf16[4,232,256]{2,1,0:T(8,128)(2,1)S(1)} %bitcast.466), channel_id=1, source_target_pairs={{0,4},{2,6},{4,0},{6,2},{8,12},{10,14},{12,8},{14,10},{16,20},{18,... | collective-permute-start | bytes 1425416 | tf_op jit(solution)/shard_map/ppermute | solution.py:134
  445.0 29.8 %collective-permute-start.28 = (bf16[2,2,56,1280]{3,2,1,0:T(8,128)(2,1)S(1)}, bf16[2,2,56,1280]{3,2,1,0:T(8,128)(2,1)S(1)}, u32[]{:S(2)}, u32[]{:S(2)}) collective-permute-start(bf16[2,2,56,1280]{3,2,1,0:T(8,128)(2,1)S(1)} %maximum_select_fusion.20), channel_id=1, source_target_pairs={{0,4},{2,6},{4,0},{6,2},{8,12},{10,14},{12,8},{14,10},{16,20},{18,... | collective-permute-start | bytes 1720328 | tf_op jit(solution)/shard_map/ppermute | solution.py:134
  445.5 52.6 %collective-permute-start.46 = (bf16[4,152,896]{2,1,0:T(8,128)(2,1)S(1)}, bf16[4,152,896]{2,1,0:T(8,128)(2,1)S(1)}, u32[]{:S(2)}, u32[]{:S(2)}) collective-permute-start(bf16[4,152,896]{2,1,0:T(8,128)(2,1)S(1)} %bitcast.438), channel_id=1, source_target_pairs={{0,4},{2,6},{4,0},{6,2},{8,12},{10,14},{12,8},{14,10},{16,20},{18,... | collective-permute-start | bytes 3268616 | tf_op jit(solution)/shard_map/ppermute | solution.py:134
  462.9 40.2 %collective-permute-start.21 = (bf16[8,232,256]{2,0,1:T(8,128)(2,1)S(1)}, bf16[8,232,256]{2,0,1:T(8,128)(2,1)S(1)}, u32[]{:S(2)}, u32[]{:S(2)}) collective-permute-start(bf16[8,232,256]{2,0,1:T(8,128)(2,1)S(1)} %copy.122), channel_id=1, source_target_pairs={{0,2},{2,0},{4,6},{6,4},{8,10},{10,8},{12,14},{14,12},{16,18},{18,... | collective-permute-start | bytes 2850824 | tf_op jit(solution)/shard_map/ppermute | solution.py:134
  475.0 34.3 %collective-permute-start.29 = (bf16[4,2,56,1280]{3,2,1,0:T(8,128)(2,1)S(1)}, bf16[4,2,56,1280]{3,2,1,0:T(8,128)(2,1)S(1)}, u32[]{:S(2)}, u32[]{:S(2)}) collective-permute-start(bf16[4,2,56,1280]{3,2,1,0:T(8,128)(2,1)S(1)} %bitcast.430), channel_id=1, source_target_pairs={{0,8},{2,10},{4,12},{6,14},{8,0},{10,2},{12,4},{14,6},{16,24},{18,... | collective-permute-start | bytes 3440648 | tf_op jit(solution)/shard_map/ppermute | solution.py:134
  475.8 34.1 %collective-permute-start.39 = (bf16[8,2,56,1152]{3,2,0,1:T(8,128)(2,1)S(1)}, bf16[8,2,56,1152]{3,2,0,1:T(8,128)(2,1)S(1)}, u32[]{:S(2)}, u32[]{:S(2)}) collective-permute-start(bf16[8,2,56,1152]{3,2,0,1:T(8,128)(2,1)S(1)} %copy.132), channel_id=1, source_target_pairs={{0,2},{2,0},{4,6},{6,4},{8,10},{10,8},{12,14},{14,12},{16,18},{18,... | collective-permute-start | bytes 6193160 | tf_op jit(solution)/shard_map/ppermute | solution.py:134
  498.5 13.8 %collective-permute-start.47 = (bf16[8,152,896]{2,1,0:T(8,128)(2,1)S(1)}, bf16[8,152,896]{2,1,0:T(8,128)(2,1)S(1)}, u32[]{:S(2)}, u32[]{:S(2)}) collective-permute-start(bf16[8,152,896]{2,1,0:T(8,128)(2,1)S(1)} %bitcast.406), channel_id=1, source_target_pairs={{0,2},{2,0},{4,6},{6,4},{8,10},{10,8},{12,14},{14,12},{16,18},{18,... | collective-permute-start | bytes 6537224 | tf_op jit(solution)/shard_map/ppermute | solution.py:134
  509.8 7.9 %collective-permute-start.30 = (bf16[8,2,56,1280]{3,2,0,1:T(8,128)(2,1)S(1)}, bf16[8,2,56,1280]{3,2,0,1:T(8,128)(2,1)S(1)}, u32[]{:S(2)}, u32[]{:S(2)}) collective-permute-start(bf16[8,2,56,1280]{3,2,0,1:T(8,128)(2,1)S(1)} %copy.127), channel_id=1, source_target_pairs={{0,2},{2,0},{4,6},{6,4},{8,10},{10,8},{12,14},{14,12},{16,18},{18,... | collective-permute-start | bytes 6881288 | tf_op jit(solution)/shard_map/ppermute | solution.py:134
  (69 other events, 275.0 us)

commit v2 on v1

v2 whole, which is shorter than its diff:
```python
import functools

import jax
import jax.numpy as jnp
from jax import lax
from jax.experimental import pallas as pl
from jax.experimental.pallas import tpu as pltpu
from jax.sharding import PartitionSpec as P

HEAD_DIM = 64


EPSILON = 1e-06
THETA = 1000000.0
NEGATIVE = -1e30


def positions(segs):
    length = segs.shape[0]
    index = jnp.arange(length, dtype=jnp.int32)
    before = jnp.concatenate([jnp.full((1,), -2, dtype=jnp.int32), segs[:-1]])
    starts = lax.cummax(jnp.where(segs != before, index, jnp.zeros_like(index)), axis=0)
    return (index - starts).astype(jnp.float32)


def rope_tables(segs, head_dim):
    halfway = head_dim // 2
    inverse = THETA ** (-(jnp.arange(halfway, dtype=jnp.float32) * 2.0 / head_dim))
    angles = positions(segs)[:, None] * inverse[None, :]
    return (jnp.cos(angles), jnp.sin(angles))


def normed(values, gain):
    scale = lax.rsqrt(jnp.mean(values * values, axis=-1, keepdims=True) + EPSILON)
    return values * scale * gain


def forward_product(left, right):
    return jnp.dot(left, right, preferred_element_type=jnp.float32)


def contract_rows(left, right):
    return lax.dot_general(
        left, right, (((0,), (0,)), ((), ())), preferred_element_type=jnp.float32
    )


def contract_cols(left, right):
    return lax.dot_general(
        left, right, (((1,), (1,)), ((), ())), preferred_element_type=jnp.float32
    )


LANES = 128


def lane_index(shape):
    return lax.broadcasted_iota(jnp.int32, shape, len(shape) - 1)


def swapped_halves(values):
    half = HEAD_DIM // 2
    lanes = lane_index(values.shape)
    return jnp.where(
        lanes % HEAD_DIM < half,
        pltpu.roll(values, LANES - half, 1),
        pltpu.roll(values, half, 1),
    )


def doubled(pair, head):
    lanes = lane_index(pair.shape)
    wide = pair.astype(jnp.float32)
    other = pltpu.roll(wide, HEAD_DIM, 1)
    return jnp.where((lanes < HEAD_DIM) == (head == 0), wide, other).astype(jnp.bfloat16)


def one_head(pair, parity):
    lanes = lane_index(pair.shape)
    return jnp.where((lanes < HEAD_DIM) == (parity == 0), pair, jnp.zeros_like(pair))


def mask_bias(segs_col, segs_row, row_start):
    rows, keys = segs_col.shape[0], segs_row.shape[1]
    row_index = row_start + lax.broadcasted_iota(jnp.int32, (rows, keys), 0)
    col_index = lax.broadcasted_iota(jnp.int32, (rows, keys), 1)
    allowed = (segs_col == segs_row) & (row_index >= col_index)
    return jnp.where(allowed, 0.0, NEGATIVE).astype(jnp.float32)


def is_live(segs):
    return jnp.where(segs >= 0, 1.0, 0.0)


def double_keys(key_rot, value_low, keys_two, values_two):
    for kv_head in range(2):
        keys_two[kv_head] = doubled(key_rot[...], kv_head)
        values_two[kv_head] = doubled(value_low[...], kv_head)


def attend_rows(
    row_start, key_count, groups, pairs, segs_col, segs_row, query_rot, keys_two, values_two,
    bias, attended, logs, tokens, w_output, gain, middle, mid_low,
):
    rows = attended.shape[0]
    bias[...] = mask_bias(
        segs_col[row_start : row_start + rows], segs_row[:, :key_count], row_start
    )
    logs[...] = jnp.zeros_like(logs)

    def one_pair(pair, carry):
        cols = pl.ds(pl.multiple_of(pair * LANES, LANES), LANES)
        queries = query_rot[row_start : row_start + rows, cols]
        results = []
        log_all = logs[...]
        lanes = lane_index(log_all.shape)
        for parity in range(2):
            head = 2 * pair + parity
            kv_head = head // groups
            query = one_head(queries, parity) * jnp.asarray(HEAD_DIM**-0.5, jnp.bfloat16)
            scores = contract_cols(query, keys_two[kv_head, :key_count]) + bias[...]
            row_max = jnp.max(scores, axis=-1, keepdims=True)
            exponent = jnp.exp(scores - row_max)
            row_total = jnp.sum(exponent, axis=-1, keepdims=True)
            probs = (exponent * (1.0 / row_total)).astype(jnp.bfloat16)
            results.append(forward_product(probs, values_two[kv_head, :key_count]))
            log_all = jnp.where(lanes == head, row_max + jnp.log(row_total), log_all)
        logs[...] = log_all
        attended[:, cols] = jnp.where(
            lane_index(results[0].shape) < HEAD_DIM, results[0], results[1]
        ).astype(jnp.bfloat16)
        return carry

    lax.fori_loop(0, pairs, one_pair, 0)
    mixed = forward_product(attended[...], w_output[...])
    here = slice(row_start, row_start + rows)
    total = tokens[here, :].astype(jnp.float32) + is_live(segs_col[here, :]) * mixed
    middle[...] = total
    mid_low[...] = normed(total, gain[...]).astype(jnp.bfloat16)


def early_kernel(
    groups, pairs, normed_low, w_qkv, bias_qkv, cosine, sine, segs_col, segs_row, tokens,
    w_output, gain, query_rot, key_rot, value_low, attended, logs, middle, mid_low,
    bias, keys_two, values_two,
):
    def project(pair):
        cols = pl.ds(pl.multiple_of(pair * LANES, LANES), LANES)
        return forward_product(normed_low[...], w_qkv[:, cols]) + bias_qkv[:, cols]

    def turned(values):
        return (values * cosine[...] + swapped_halves(values) * sine[...]).astype(jnp.bfloat16)

    def query_pair(pair, carry):
        cols = pl.ds(pl.multiple_of(pair * LANES, LANES), LANES)
        query_rot[:, cols] = turned(project(pair))
        return carry

    lax.fori_loop(0, pairs, query_pair, 0)
    key_rot[...] = turned(project(pairs))
    value_low[...] = project(pairs + 1).astype(jnp.bfloat16)
    double_keys(key_rot, value_low, keys_two, values_two)
    attend_rows(
        0, attended.shape[0], groups, pairs, segs_col, segs_row, query_rot, keys_two, values_two,
        bias, attended, logs, tokens, w_output, gain, middle, mid_low,
    )


def late_kernel(
    groups, pairs, query_rot, key_rot, value_low, segs_col, segs_row, tokens,
    w_output, gain, attended, logs, middle, mid_low, bias, keys_two, values_two,
):
    double_keys(key_rot, value_low, keys_two, values_two)
    rows = attended.shape[0]
    attend_rows(
        rows, 2 * rows, groups, pairs, segs_col, segs_row, query_rot, keys_two, values_two,
        bias, attended, logs, tokens, w_output, gain, middle, mid_low,
    )


def call(kernel, out_shape, scratch, cost, operands):
    return pl.pallas_call(
        kernel,
        out_shape=[jax.ShapeDtypeStruct(shape, kind) for shape, kind in out_shape],
        in_specs=[pl.BlockSpec(memory_space=pltpu.VMEM)] * len(operands),
        out_specs=[pl.BlockSpec(memory_space=pltpu.VMEM)] * len(out_shape),
        scratch_shapes=[pltpu.VMEM(shape, kind) for shape, kind in scratch],
        compiler_params=pltpu.CompilerParams(vmem_limit_bytes=56 * 2**20),
        cost_estimate=pl.CostEstimate(flops=cost, bytes_accessed=cost // 300, transcendentals=0),
    )(*operands)


def attention_shapes(length, w_output, kw):
    queries, width = w_output.shape
    rows = length // 2
    low, wide = jnp.bfloat16, jnp.float32
    half_out = [
        ((rows, queries), low), ((rows, LANES), wide), ((rows, width), wide), ((rows, width), low)
    ]
    return rows, queries, queries // kw, queries // LANES, half_out, [((2, length, LANES), low)] * 2


def attention_early(
    normed_low, w_qkv, bias_qkv, cosine, sine, segs_col, segs_row, tokens, w_output, gain
):
    length = tokens.shape[0]
    kw = (w_qkv.shape[1] - w_output.shape[0]) // 2
    rows, queries, groups, pairs, half_out, scratch = attention_shapes(length, w_output, kw)
    whole = [((length, columns), jnp.bfloat16) for columns in (queries, kw, kw)]
    query_rot, key_rot, value_low, *early = call(
        functools.partial(early_kernel, groups, pairs),
        whole + half_out,
        [((rows, rows), jnp.float32)] + scratch,
        2 * 10**9,
        (normed_low, w_qkv, bias_qkv, cosine, sine, segs_col, segs_row, tokens, w_output, gain),
    )
    return query_rot, key_rot, value_low, early


def attention_late(query_rot, key_rot, value_low, segs_col, segs_row, tokens, w_output, gain):
    length = tokens.shape[0]
    rows, _, groups, pairs, half_out, scratch = attention_shapes(
        length, w_output, key_rot.shape[1]
    )
    return call(
        functools.partial(late_kernel, groups, pairs),
        half_out,
        [((rows, length), jnp.float32)] + scratch,
        2 * 10**9,
        (query_rot, key_rot, value_low, segs_col, segs_row, tokens, w_output, gain),
    )


def norm_pull(values, gain, grad):
    scale = lax.rsqrt(jnp.mean(values * values, axis=-1, keepdims=True) + EPSILON)
    unit = values * scale
    inner = grad * gain
    pull = scale * (inner - unit * jnp.mean(inner * unit, axis=-1, keepdims=True))
    return pull, jnp.sum(grad * unit, axis=0, keepdims=True)


def backward_kernel(
    groups, pairs, mid_early, mid_late, norm_grad, cotangent, gain_mlp, w_output,
    att_early, att_late, log_early, log_late, query_rot, key_rot, value_low, segs_col, segs_row,
    cosine, sine, normed_low, w_qkv, tokens, gain_attn,
    grad_qkv, grad_output, bias_grad, attn_gain_grad, mlp_gain_grad, input_grad,
    attn_grad, attended_grad, low_grads, bias, keys_two, values_two, key_grad, value_grad,
):
    rows = mid_early.shape[0]
    length = 2 * rows
    parts = ((0, mid_early, att_early, log_early), (rows, mid_late, att_late, log_late))
    gain_sum = jnp.zeros(mlp_gain_grad.shape, jnp.float32)
    for start, middle, _, _ in parts:
        here = slice(start, start + rows)
        pull, gain_part = norm_pull(middle[...], gain_mlp[...], norm_grad[here, :])
        gain_sum = gain_sum + gain_part
        total = cotangent[here, :].astype(jnp.float32) + pull
        input_grad[here, :] = total
        attn_grad[here, :] = (is_live(segs_col[here, :]) * total).astype(jnp.bfloat16)
        bias[here, :] = mask_bias(segs_col[here], segs_row[...], start)
    mlp_gain_grad[...] = gain_sum
    double_keys(key_rot, value_low, keys_two, values_two)
    key_grad[...] = jnp.zeros_like(key_grad)
    value_grad[...] = jnp.zeros_like(value_grad)
    bias_grad[...] = jnp.zeros_like(bias_grad)
    for start in range(0, length, rows):
        here = slice(start, start + rows)
        attended_grad[here, :] = contract_cols(attn_grad[here, :], w_output[...]).astype(
            jnp.bfloat16
        )

    def turned_back(values, here):
        return values * cosine[here, :] - swapped_halves(values) * sine[here, :]

    def one_pair(pair, carry):
        cols = pl.ds(pl.multiple_of(pair * LANES, LANES), LANES)
        column_sum = jnp.zeros((1, LANES), jnp.float32)
        out_grad = jnp.zeros((LANES, attn_grad.shape[1]), jnp.float32)
        for start, _, attended, logs in parts:
            here = slice(start, start + rows)
            keys = start + rows
            out_grad = out_grad + contract_rows(attended[:, cols], attn_grad[here, :])
            queries = query_rot[here, cols]
            grads = attended_grad[here, cols]
            log_all = logs[...]
            lanes = lane_index(log_all.shape)
            results = []
            for parity in range(2):
                head = 2 * pair + parity
                kv_head = head // groups
                query = one_head(queries, parity) * jnp.asarray(HEAD_DIM**-0.5, jnp.bfloat16)
                grad = one_head(grads, parity)
                log_total = jnp.sum(
                    jnp.where(lanes == head, log_all, 0.0), axis=-1, keepdims=True
                )
                scores = contract_cols(query, keys_two[kv_head, :keys]) + bias[here, :keys]
                probs = jnp.exp(scores - log_total)
                prob_grad = contract_cols(grad, values_two[kv_head, :keys])
                inner = jnp.sum(prob_grad * probs, axis=-1, keepdims=True)
                score_grad = (probs * (prob_grad - inner)).astype(jnp.bfloat16)
                value_grad[kv_head, :keys] += contract_rows(probs.astype(jnp.bfloat16), grad)
                key_grad[kv_head, :keys] += contract_rows(score_grad, query)
                results.append(
                    forward_product(score_grad, keys_two[kv_head, :keys]) * HEAD_DIM**-0.5
                )
            query_grad = jnp.where(
                lane_index(results[0].shape) < HEAD_DIM, results[0], results[1]
            )
            low = turned_back(query_grad, here).astype(jnp.bfloat16)
            low_grads[here, cols] = low
            column_sum = column_sum + jnp.sum(low.astype(jnp.float32), axis=0, keepdims=True)
        bias_grad[:, cols] = column_sum
        grad_output[cols, :] = out_grad.astype(jnp.bfloat16)
        return carry

    lax.fori_loop(0, pairs, one_pair, 0)

    def folded(pair_sums):
        both = [pair_sums[at] + pltpu.roll(pair_sums[at], HEAD_DIM, 1) for at in range(2)]
        return jnp.where(lane_index(both[0].shape) < HEAD_DIM, both[0], both[1])

    everywhere = slice(0, length)
    key_low = turned_back(folded(key_grad), everywhere).astype(jnp.bfloat16)
    value_grad_low = folded(value_grad).astype(jnp.bfloat16)
    for at, low in ((pairs, key_low), (pairs + 1, value_grad_low)):
        cols = slice(at * LANES, (at + 1) * LANES)
        low_grads[:, cols] = low
        bias_grad[:, cols] = jnp.sum(low.astype(jnp.float32), axis=0, keepdims=True)

    def weight_rows(block, carry):
        cols = pl.ds(pl.multiple_of(block * LANES, LANES), LANES)
        grad_qkv[cols, :] = contract_rows(normed_low[:, cols], low_grads[...]).astype(jnp.bfloat16)
        return carry

    lax.fori_loop(0, normed_low.shape[1] // LANES, weight_rows, 0)
    gain_sum = jnp.zeros(attn_gain_grad.shape, jnp.float32)
    for start in range(0, length, rows):
        here = slice(start, start + rows)
        norm_in = contract_cols(low_grads[here, :], w_qkv[...])
        pull, gain_part = norm_pull(tokens[here, :].astype(jnp.float32), gain_attn[...], norm_in)
        gain_sum = gain_sum + gain_part
        input_grad[here, :] += pull
    attn_gain_grad[...] = gain_sum


def attention_backward(
    early, late, norm_grad, cotangent, gain_mlp, w_output, query_rot, key_rot, value_low,
    segs_col, segs_row, cosine, sine, normed_low, w_qkv, tokens, gain_attn,
):
    length, width = tokens.shape
    queries = w_output.shape[0]
    columns = w_qkv.shape[1]
    kw = (columns - queries) // 2
    low, wide = jnp.bfloat16, jnp.float32
    return call(
        functools.partial(backward_kernel, queries // kw, queries // LANES),
        [
            ((width, columns), low),
            ((queries, width), low),
            ((1, columns), wide),
            ((1, width), wide),
            ((1, width), wide),
            ((length, width), wide),
        ],
        [
            ((length, width), low),
            ((length, queries), low),
            ((length, columns), low),
            ((length, length), wide),
            ((2, length, LANES), low),
            ((2, length, LANES), low),
            ((2, length, LANES), wide),
            ((2, length, LANES), wide),
        ],
        10**9,
        (early[2], late[2], norm_grad, cotangent, gain_mlp, w_output, early[0], late[0],
         early[1], late[1], query_rot, key_rot, value_low, segs_col, segs_row, cosine, sine,
         normed_low, w_qkv, tokens, gain_attn),
    )


def swapped(value, axis, bit, size):
    step = 1 << bit
    return lax.ppermute(value, axis, [(at, at ^ step) for at in range(size)])


def chosen(parts, at):
    return lax.dynamic_index_in_dim(parts, at, 0, keepdims=False)


def added(left, right):
    return (left.astype(jnp.float32) + right.astype(jnp.float32)).astype(jnp.bfloat16)


def ordered(own, other, bit):
    return jnp.where(bit == 0, jnp.stack([own, other]), jnp.stack([other, own]))


def column_cuts(columns):
    step = 4 * LANES
    return [(low, min(low + step, columns)) for low in range(0, columns, step)]


def hidden_kernel(carries, mid_low, mlp_grad, w_gate, w_up, w_down, *refs):
    activ, gate_grad, up_grad = refs[carries:]
    for low, high in column_cuts(w_gate.shape[1]):
        gate = forward_product(mid_low[...], w_gate[:, low:high])
        upward = forward_product(mid_low[...], w_up[:, low:high])
        grad = contract_cols(mlp_grad[...], w_down[low:high, :])
        sigmoid = jax.nn.sigmoid(gate)
        silu = gate * sigmoid
        activ[:, low:high] = (silu * upward).astype(jnp.bfloat16)
        gate_grad[:, low:high] = (grad * upward * (sigmoid + silu * (1.0 - sigmoid))).astype(
            jnp.bfloat16
        )
        up_grad[:, low:high] = (grad * silu).astype(jnp.bfloat16)


def whole_block(array):
    return pl.BlockSpec(array.shape, lambda at: (0,) * array.ndim)


def row_block(array, rows, start=0):
    return pl.BlockSpec((rows, array.shape[1]), lambda at: (at + start, 0))


def grid_call(kernel, grid, operands, in_specs, out_shape, out_specs, flops, aliases=None):
    return pl.pallas_call(
        kernel,
        grid=(grid,),
        out_shape=out_shape,
        in_specs=in_specs,
        out_specs=out_specs,
        input_output_aliases=aliases or {},
        compiler_params=pltpu.CompilerParams(vmem_limit_bytes=56 * 2**20),
        cost_estimate=pl.CostEstimate(flops=flops, bytes_accessed=10**6, transcendentals=0),
    )(*operands)


def hidden_part(mid_low, mlp_grad, w_gate, w_up, w_down, total, start, carried):
    rows = 256
    count = mid_low.shape[0] // rows
    first = start // rows
    shapes = [jax.ShapeDtypeStruct((total, w_gate.shape[1]), jnp.bfloat16)] * 3
    return grid_call(
        functools.partial(hidden_kernel, len(carried)),
        count,
        [mid_low, mlp_grad, w_gate, w_up, w_down] + list(carried),
        [row_block(mid_low, rows), row_block(mlp_grad, rows)]
        + [whole_block(weight) for weight in (w_gate, w_up, w_down)]
        + [pl.BlockSpec(memory_space=pl.ANY)] * len(carried),
        shapes,
        [row_block(shape, rows, first) for shape in shapes],
        10**9,
        {5 + at: at for at in range(len(carried))},
    )


def norm_part_kernel(gate_grad, up_grad, w_gate, w_up, out):
    out[...] = (
        contract_cols(gate_grad[...], w_gate[...]) + contract_cols(up_grad[...], w_up[...])
    ).astype(out.dtype)


def out_part_kernel(activ, w_down, out):
    out[...] = forward_product(activ[...], w_down[...]).astype(out.dtype)


def token_product(kernel, activs, weights, width, start, count, kind):
    rows = 256
    out = jax.ShapeDtypeStruct((count, width), kind)
    return grid_call(
        kernel,
        count // rows,
        list(activs) + list(weights),
        [row_block(activ, rows, start // rows) for activ in activs]
        + [whole_block(weight) for weight in weights],
        out,
        row_block(out, rows),
        10**9,
    )


def together(*values):
    return lax.optimization_barrier(values)


class Group:
    def __init__(self, size, replicas):
        self.size = size
        self.replicas = replicas
        self.at = lax.axis_index("fsdp")
        self.replica = lax.axis_index("rep")
        self.pair = size == 2 and replicas % 2 == 0

    def swap(self, value):
        return swapped(value, "fsdp", 0, 2)

    def fetched(self, rows, bits):
        start, count = 0, rows.shape[0]
        for bit in bits:
            count //= 2
            start = start + ((self.replica >> bit) & 1) * count
        return self.swap(lax.dynamic_slice_in_dim(rows, start, count, 0))

    def shared(self, part, bits):
        for bit in reversed(bits):
            other = swapped(part, "rep", bit, self.replicas)
            part = ordered(part, other, (self.replica >> bit) & 1)
            part = part.reshape((-1,) + part.shape[2:])
        return part

    def joined(self, own, other):
        return ordered(own, other, self.at).reshape((-1,) + own.shape[1:])

    def whole_vector(self, vector):
        if not self.pair:
            return lax.all_gather(vector, "fsdp", axis=0, tiled=False)
        return ordered(vector, self.swap(vector), self.at)

    def columns(self, rows, owner):
        width = rows.shape[1] // 2
        return lax.dynamic_slice_in_dim(rows, owner * width, width, 1)

    def plain_weights(self, qkv, w_output, w_gate, w_up):
        return (
            lax.all_gather(qkv, "fsdp", axis=0, tiled=True),
            lax.all_gather(w_output, "fsdp", axis=0, tiled=True),
            lax.all_to_all(w_gate, "fsdp", 1, 0, tiled=True),
            lax.all_to_all(w_up, "fsdp", 1, 0, tiled=True),
        )

    def all_tokens(self, value):
        return lax.all_gather(value, "fsdp", axis=0, tiled=True)

    def own_tokens(self, partial):
        return lax.psum_scatter(partial, "fsdp", scatter_dimension=0, tiled=True)

    def sum_parts(self, parts):
        if not self.pair:
            return lax.psum_scatter(parts, "fsdp", scatter_dimension=0, tiled=False)
        got = self.swap(chosen(parts, 1 - self.at))
        return added(chosen(parts, self.at), got)

    def exchange_parts(self, parts):
        if not self.pair:
            return lax.all_to_all(parts, "fsdp", 0, 0, tiled=True)
        got = self.swap(chosen(parts, 1 - self.at))
        return ordered(chosen(parts, self.at), got, self.at)


class Replicas:
    def __init__(self, size):
        self.size = size
        self.at = lax.axis_index("rep")
        self.bits = size.bit_length() - 1
        self.far = list(range(1, self.bits))

    def bit(self, bit):
        return (self.at >> bit) & 1

    def swap_core(self, value):
        return swapped(value, "rep", 0, self.size)

    def scatter(self, parts, bit):
        mine = self.bit(bit)
        got = swapped(chosen(parts, 1 - mine), "rep", bit, self.size)
        return added(chosen(parts, mine), got)

    def gather(self, value, bit):
        return ordered(value, swapped(value, "rep", bit, self.size), self.bit(bit))

    def first(self, parts, order):
        if not order:
            return parts
        return self.scatter(parts.reshape((2, -1) + parts.shape[1:]), order[0])

    def scatter_all(self, parts, order):
        for at in range(len(order)):
            parts = self.first(parts, order[at:])
        return parts.reshape(parts.shape[1:])

    def gather_all(self, value, order):
        value = value[None]
        for bit in reversed(order):
            value = self.gather(value, bit)
            value = value.reshape((value.shape[0] * value.shape[1],) + value.shape[2:])
        return value


def shards(
    tokens,
    segments,
    cotangent,
    w_query,
    w_key,
    w_value,
    w_output,
    w_gate,
    w_up,
    w_down,
    b_query,
    b_key,
    b_value,
    gain_attn,
    gain_mlp,
    group_size,
    replica_count,
):
    group = Group(group_size, replica_count)
    replicas = Replicas(replica_count)
    far = replicas.far
    near_first = [far[1], far[0]] + far[2:]
    eighth = 1 << len(far)
    width = tokens.shape[1]
    rows_own = w_query.shape[0]
    qw, kw = w_query.shape[1], w_key.shape[1]
    vectors = group.whole_vector(
        jnp.concatenate([b_query, b_key, b_value, gain_attn, gain_mlp])
    ).astype(jnp.float32)
    cuts = [0]
    for part in (b_query, b_key, b_value, gain_attn, gain_mlp):
        cuts.append(cuts[-1] + part.shape[0])
    bias_query, bias_key, bias_value, full_gain_attn, full_gain_mlp = (
        vectors[:, low:high].reshape(-1) for low, high in zip(cuts[:-1], cuts[1:])
    )
    qkv = jnp.concatenate([w_query, w_key, w_value], axis=1)
    live = (segments >= 0).astype(jnp.float32)[:, None]
    mlp_grad = (live * cotangent.astype(jnp.float32)).astype(jnp.bfloat16)
    cosine, sine = rope_tables(segments, HEAD_DIM)
    copies = LANES // HEAD_DIM
    cosine = jnp.concatenate([cosine, cosine] * copies, axis=1)
    sine = jnp.concatenate([-sine, sine] * copies, axis=1)
    segs_col, segs_row = segments[:, None], segments[None, :]
    normed_low = normed(tokens.astype(jnp.float32), full_gain_attn).astype(jnp.bfloat16)
    gain_attn_row, gain_mlp_row = full_gain_attn[None, :], full_gain_mlp[None, :]
    bias_row = jnp.concatenate([bias_query, bias_key, bias_value])[None, :]
    if group.pair:
        cores = [0]
        chips = [0, 1] if replica_count % 4 == 0 else [0]
        got_qkv, got_output = group.fetched(qkv, cores), group.fetched(w_output, cores)
        got_qkv, got_output, w_gate, w_up = together(got_qkv, got_output, w_gate, w_up)
        full_qkv = group.joined(qkv, group.shared(got_qkv, cores))
        full_output = group.joined(w_output, group.shared(got_output, cores))
        got_gate = group.fetched(group.columns(w_gate, 1 - group.at), chips)
        got_up = group.fetched(group.columns(w_up, 1 - group.at), chips)
    else:
        full_qkv, full_output, part_gate, part_up = group.plain_weights(
            qkv, w_output, w_gate, w_up
        )
    query_rot, key_rot, value_low, early = attention_early(
        normed_low, full_qkv, bias_row, cosine, sine, segs_col, segs_row, tokens, full_output,
        gain_mlp_row,
    )
    if group.pair:
        query_rot, early, got_gate, got_up, mlp_grad = together(
            query_rot, early, got_gate, got_up, mlp_grad
        )
        got_gate, got_up = group.shared(got_gate, chips[1:]), group.shared(got_up, chips[1:])
        others = [group.swap(early[3])]
        mlp_other = group.swap(mlp_grad)
    late = attention_late(
        query_rot, key_rot, value_low, segs_col, segs_row, tokens, full_output, gain_mlp_row
    )
    mid_own = jnp.concatenate([early[3], late[3]])
    length = tokens.shape[0]
    if group.pair:
        late, got_gate, got_up, others = together(late, got_gate, got_up, others)
        others.append(group.swap(late[3]))
        got_gate, got_up = group.shared(got_gate, cores), group.shared(got_up, cores)
        part_gate = group.joined(group.columns(w_gate, group.at), got_gate)
        part_up = group.joined(group.columns(w_up, group.at), got_up)
        hidden = hidden_part(
            mid_own, mlp_grad, part_gate, part_up, w_down, group_size * length, 0, ()
        )
        hidden, others, mlp_other = together(hidden, others, mlp_other)
        mid_other = jnp.concatenate(others)
        activ_low, gate_grad, up_grad = hidden_part(
            mid_other, mlp_other, part_gate, part_up, w_down, group_size * length, length, hidden
        )
        mid_all = jnp.concatenate([mid_own, mid_other])
        mlp_grad_all = jnp.concatenate([mlp_grad, mlp_other])
    else:
        mid_all = group.all_tokens(mid_own)
        mlp_grad_all = group.all_tokens(mlp_grad)
        activ_low, gate_grad, up_grad = hidden_part(
            mid_all, mlp_grad_all, part_gate, part_up, w_down, group_size * length, 0, ()
        )
    middle = jnp.concatenate([early[2], late[2]])

    back_weights, out_weights = (part_gate, part_up), (w_down,)
    back = (gate_grad, up_grad)
    everyone = group_size * length
    if group.pair:
        norm_other = token_product(
            norm_part_kernel, back, back_weights, width, length, length, jnp.bfloat16
        )
        norm_other, activ_low, back = together(norm_other, activ_low, back)
    grad_down = contract_rows(activ_low, mlp_grad_all).astype(jnp.bfloat16)
    grad_down, back = together(grad_down, back)
    gate_grad, up_grad = back
    grad_gate = contract_rows(mid_all, gate_grad).astype(jnp.bfloat16)
    grad_up = contract_rows(mid_all, up_grad).astype(jnp.bfloat16)
    down = replicas.scatter(grad_down.reshape(2, -1, width), 0).reshape(eighth, -1, width)
    grad_gate, grad_up, down, back, activ_low = together(
        grad_gate, grad_up, down, back, activ_low
    )
    hidden_units = grad_gate.shape[1]
    cut = -(-hidden_units // 256) * 128
    core = replicas.bit(0)
    pair_parts = []
    for low, high in ((0, cut), (cut, hidden_units)):
        gate_range, up_range = grad_gate[:, low:high], grad_up[:, low:high]
        got = replicas.swap_core(jnp.where(core == 0, up_range, gate_range))
        summed = added(jnp.where(core == 0, gate_range, up_range), got)
        summed = summed.reshape(group_size, eighth, rows_own // eighth, high - low)
        pair_parts.append(summed.transpose(1, 0, 2, 3))
    first, second = pair_parts
    down = replicas.first(down, far)
    if group.pair:
        norm_grad = token_product(
            norm_part_kernel, back, back_weights, width, 0, length, jnp.float32
        )
        norm_grad = norm_grad + group.swap(norm_other).astype(jnp.float32)
        out_other = token_product(
            out_part_kernel, (activ_low,), out_weights, width, length, length, jnp.bfloat16
        )
    else:
        norm_grad = group.own_tokens(
            token_product(norm_part_kernel, back, back_weights, width, 0, everyone, jnp.float32)
        )
        out_other = token_product(
            out_part_kernel, (activ_low,), out_weights, width, 0, everyone, jnp.float32
        )
    norm_grad, down, first, second, out_other, activ_low = together(
        norm_grad, down, first, second, out_other, activ_low
    )
    grad_qkv, grad_output, bias_grad, gain_attn_grad, gain_mlp_grad, input_grad = (
        attention_backward(
            early, late, norm_grad, cotangent, gain_mlp_row, full_output, query_rot, key_rot,
            value_low, segs_col, segs_row, cosine, sine, normed_low, full_qkv, tokens,
            gain_attn_row,
        )
    )
    down = replicas.first(down, far[1:])
    first = replicas.first(first, near_first)
    second = replicas.first(second, far)
    if group.pair:
        out_sum = token_product(
            out_part_kernel, (activ_low,), out_weights, width, 0, length, jnp.float32
        )
        out_sum = out_sum + group.swap(out_other).astype(jnp.float32)
    else:
        out_sum = group.own_tokens(out_other)
    grad_qkv, grad_output, bias_grad, gain_attn_grad, gain_mlp_grad, down, first, second = together(
        grad_qkv, grad_output, bias_grad, gain_attn_grad, gain_mlp_grad, down, first, second
    )
    output = (middle + live * out_sum).astype(jnp.bfloat16)

    small = jnp.concatenate(
        [
            part.reshape(group_size, -1)
            for part in (
                bias_grad[0, :qw],
                bias_grad[0, qw : qw + kw],
                bias_grad[0, qw + kw :],
                gain_attn_grad,
                gain_mlp_grad,
            )
        ],
        axis=1,
    ).astype(jnp.bfloat16)
    columns = grad_qkv.shape[1] + qw
    unit = 16 * eighth
    extra = -(-(rows_own + 16) // unit) * unit - rows_own
    small = jnp.pad(small, ((0, 0), (0, extra * columns - small.shape[1])))
    attn_all = jnp.concatenate(
        [
            jnp.concatenate([grad_qkv, grad_output], axis=1)
            .astype(jnp.bfloat16)
            .reshape(group_size, rows_own, columns),
            small.reshape(group_size, extra, columns),
        ],
        axis=1,
    )
    attn = replicas.scatter(
        attn_all.reshape(group_size, 2, (rows_own + extra) // 2, columns).transpose(1, 0, 2, 3), 0
    )
    down = replicas.scatter_all(down, far[2:])
    first = group.exchange_parts(replicas.scatter_all(first, near_first[1:]))
    second = group.exchange_parts(replicas.scatter_all(second, far[1:]))
    attn = group.sum_parts(attn).reshape(eighth, -1, columns)
    attn = replicas.scatter_all(attn, far)
    down = replicas.gather(replicas.gather_all(down, far), 0)
    first = replicas.gather_all(first, near_first)
    second = replicas.gather_all(second, far)
    attn = replicas.gather_all(attn, far)
    shard_down = down.reshape(-1, width).astype(jnp.float32)
    gate_parts = [[] for _ in range(group_size)]
    up_parts = [[] for _ in range(group_size)]
    for mine in (first, second):
        got = replicas.swap_core(mine)
        for matrix, parts in (
            (jnp.where(core == 0, mine, got), gate_parts),
            (jnp.where(core == 0, got, mine), up_parts),
        ):
            for sender in range(group_size):
                parts[sender].append(matrix[:, sender].reshape(rows_own, -1))
    shard_gate, shard_up = (
        jnp.concatenate(sum(parts, []), axis=1).astype(jnp.float32)
        for parts in (gate_parts, up_parts)
    )
    attn_sum = replicas.gather(attn, 0).reshape(rows_own + extra, columns).astype(jnp.float32)
    shard_query = attn_sum[:rows_own, :qw]
    shard_key = attn_sum[:rows_own, qw : qw + kw]
    shard_value = attn_sum[:rows_own, qw + kw : qw + 2 * kw]
    shard_output = attn_sum[:rows_own, qw + 2 * kw :]
    vector_sum = attn_sum[rows_own:].reshape(-1)
    shard_vectors = tuple(vector_sum[low:high] for low, high in zip(cuts[:-1], cuts[1:]))
    return (
        output,
        input_grad,
        shard_query,
        shard_key,
        shard_value,
        shard_output,
        shard_gate,
        shard_up,
        shard_down,
    ) + shard_vectors


def solution(mesh):
    placed = (
        P(("rep", "fsdp"), None),
        P(("rep", "fsdp")),
        P(("rep", "fsdp"), None),
        P("fsdp", None),
        P("fsdp", None),
        P("fsdp", None),
        P("fsdp", None),
        P("fsdp", None),
        P("fsdp", None),
        P("fsdp", None),
        P("fsdp"),
        P("fsdp"),
        P("fsdp"),
        P("fsdp"),
        P("fsdp"),
    )
    return jax.shard_map(
        functools.partial(
            shards, group_size=mesh.shape["fsdp"], replica_count=mesh.shape["rep"]
        ),
        mesh=mesh,
        in_specs=placed,
        out_specs=(
            P(("rep", "fsdp"), None),
            P(("rep", "fsdp"), None),
            P("fsdp", None),
            P("fsdp", None),
            P("fsdp", None),
            P("fsdp", None),
            P("fsdp", None),
            P("fsdp", None),
            P("fsdp", None),
            P("fsdp"),
            P("fsdp"),
            P("fsdp"),
            P("fsdp"),
            P("fsdp"),
        ),
        check_vma=False,
    )
```

time: 560 us -> 445 us (0.79)
  Pallas kernels: 0 us -> 126 us
  matrix products: 126 us -> 16.6 us
  waiting for transfers between devices: 172 us -> 102 us
  local copies, waits for them, and re-layouts: 86.5 us -> 25.5 us
  starting transfers between devices: 89.8 us -> 96.3 us
    pallas_call x0 -> x9, Pallas kernels: none -> 126 us  [the longest x6 67.4 us: grid_call(): pl.pallas_call(kernel, grid=(grid,), out_shape=out_shape, in_specs=in_spe...]
    dot_general x22 -> x0, matrix products: 102 us -> none  [the longest x5 36.3 us: contract_cols(): lax.dot_general(left, right, (((1,), (1,)), ((), ())), preferred_element_...]
    ppermute x48 -> x51, waiting for transfers between devices: 172 us -> 102 us  [swapped(): return lax.ppermute(value, axis, [(at, at ^ step) for at in range(size)])]
    unnamed x179 -> x98, local copies, waits for them, and re-layouts: 25.7 us -> 2.93 us
    convert_element_type x4 -> x0, local copies, waits for them, and re-layouts: 21.2 us -> none  [the longest x1 11.2 us: shards(): shard_up = shard_pair[1].astype(jnp.float32)]
    dot_general x5 -> x3, matrix products: 23.3 us -> 16.6 us  [contract_rows(): lax.dot_general(left, right, (((0,), (0,)), ((), ())), preferred_element_...]
    ppermute x48 -> x51, starting transfers between devices: 89.8 us -> 96.3 us  [swapped(): return lax.ppermute(value, axis, [(at, at ^ step) for at in range(size)])]
    convert_element_type x9 -> x7, other arithmetic: 24.2 us -> 17.9 us  [the longest x2 7.62 us: shards(): jnp.concatenate(sum(parts, []), axis=1).astype(jnp.float32)]
  transfers between devices with their start and end apart: 48 -> 51, of which waited for: 18 -> 16; matrix products, arithmetic and copies ran while one was open for 38% -> 20% of each run, Pallas kernels for 0% -> 23%
where the time goes in v2:
time: 445 us; the launch traced here: 440 us
  Pallas kernels  126 us (28%)
  waiting for transfers between devices  102 us (23%)
  starting transfers between devices  96.3 us (22%)
  other arithmetic  70.3 us (16%)
  local copies, waits for them, and re-layouts  25.5 us (6%)
  matrix products  16.6 us (4%)
    ppermute x51, waiting for transfers between devices, swapped(): return lax.ppermute(value, axis, [(at, at ^ step) for at in range(size)])  102 us
    ppermute x51, starting transfers between devices, swapped(): return lax.ppermute(value, axis, [(at, at ^ step) for at in range(size)])  96.3 us
    pallas_call x6, Pallas kernels, grid_call(): pl.pallas_call(kernel, grid=(grid,), out_shape=out_shape, in_specs=in_spe...  67.4 us
    pallas_call x3, Pallas kernels, call(): pl.pallas_call(kernel, out_shape=[jax.ShapeDtypeStruct(shape, kind) for s...  59 us
    select_n x31, other arithmetic, ordered(): return jnp.where(bit == 0, jnp.stack([own, other]), jnp.stack([other, own]))  18.1 us
    convert_element_type x17, other arithmetic, added(): (left.astype(jnp.float32) + right.astype(jnp.float32)).astype(jnp.bfloat16)  18 us
    dot_general x3, matrix products, contract_rows(): lax.dot_general(left, right, (((0,), (0,)), ((), ())), preferred_element_...  16.6 us
  transfers between devices with their start and end apart: 51, of which 16 were waited for; matrix products, arithmetic and copies ran while one was open for 20% of the time, Pallas kernels for 23%

profile of v2, /device:TPU:1, one launch (start us, length us, event | category | flops | bytes accessed | tf_op | source)
XLA Modules:
  0.0 439.9 jit_solution(18162340745362356628)
XLA Ops:
  4.8 2.0 collective-permute-start.1
  15.5 11.8 %collective-permute-done = bf16[1472]{0:T(1024)(128)(2,1)S(1)} collective-permute-done((bf16[1472]{0:T(1024)(128)(2,1)S(1)}, bf16[1472]{0:T(1024)(128)(2,1)S(1)}, u32[]{:S(2)}, u32[]{:S(2)}) %collective-permute-start) | collective-permute-done | bytes 2976 | tf_op jit(solution)/shard_map/ppermute | solution.py:384
  32.9 1.5 collective-permute-start.5
  35.9 1.5 maximum_select_fusion.18
  39.1 1.7 maximum_select_fusion.8
  40.8 16.3 %shard_map.254 = (bf16[512,896]{1,0:T(8,128)(2,1)}, bf16[512,128]{1,0:T(8,128)(2,1)}, bf16[512,128]{1,0:T(8,128)(2,1)}, bf16[256,896]{1,0:T(8,128)(2,1)}, f32[25...) custom-call(bf16[512,896]{1,0:T(8,128)(2,1)} %fusion.8.normed_low, bf16[896,1152]{1,0:T(8,128)(2,1)} %bitcast.217, ...), custom_call_target="tpu_custom_call" | custom-call | flops 2000000000 | bytes 6666666 | tf_op jit(solution)/shard_map/pallas_call | solution.py:182
  61.2 11.5 %shard_map.255 = (bf16[256,896]{1,0:T(8,128)(2,1)}, f32[256,128]{1,0:T(8,128)}, f32[256,896]{1,0:T(8,128)}, bf16[256,896]{1,0:T(8,128)(2,1)}) custom-call(bf16[512,896]{1,0:T(8,128)(2,1)} %get-tuple-element.99.query_rot, bf16[512,128]{1,0:T(8,128)(2,1)} %get-tuple-element.100.key_rot, bf16[512,128]{1,0:T(8,128)(2,1)} %get-tuple-element.101.value_low, ...), custom_call_target="tpu_custom_call" | custom-call | flops 2000000000 | bytes 6666666 | tf_op jit(solution)/shard_map/pallas_call | solution.py:182
  74.0 8.6 %collective-permute-done.7 = bf16[112,2432]{1,0:T(8,128)(2,1)S(1)} collective-permute-done((bf16[112,2432]{1,0:T(8,128)(2,1)}, bf16[112,2432]{1,0:T(8,128)(2,1)S(1)}, u32[]{:S(2)}, u32[]{:S(2)}) %collective-permute-start.7) | collective-permute-done | bytes 544800 | tf_op jit(solution)/shard_map/ppermute | solution.py:384
  84.1 2.3 collective-permute-start.11
  86.7 1.8 dynamic-slice_bitcast_fusion.2
  88.5 1.5 collective-permute-start.13
  92.1 5.1 %maximum_select_fusion = (bf16[2,448,2432]{2,1,0:T(8,128)(2,1)}, bf16[2,448,2432]{2,1,0:T(8,128)(2,1)}) fusion(bf16[1,448,2432]{2,1,0:T(8,128)(2,1)S(1)} %bitcast.208, bf16[1,448,2432]{2,1,0:T(8,128)(2,1)S(1)} %dynamic-slice_bitcast_fusion.2, pred[]{:T(512)S(6)} %eq.10, bf16[1,448,2432]{2,1,0:T(8,128)(2,1)S(1)} %dynamic-slice_bitcast_fusion.1, ...), kind=kLoop, calls=%fused_computation.4 | loop fusion | flops 13074432 | bytes 17432576 | tf_op jit(solution)/shard_map/jit(_where)/select_n | solution.py:396
  97.2 15.9 %shard_map.256 = (bf16[1024,2432]{1,0:T(8,128)(2,1)}, bf16[1024,2432]{1,0:T(8,128)(2,1)}, bf16[1024,2432]{1,0:T(8,128)(2,1)}) custom-call(bf16[512,896]{1,0:T(8,128)(2,1)} %pad_maximum_fusion.2.mid_low, bf16[512,896]{1,0:T(8,128)(2,1)} %copy-done.9, bf16[896,2432]{1,0:T(8,128)(2,1)} %bitcast.184, bf16[896,2432]{1,0:T(8,128)(2,1)} %bitcast.188, ...), custom_call_target="tpu_custom_call" | custom-call | flops 1000000000 | bytes 1000000 | tf_op jit(solution)/shard_map/pallas_call | solution.py:428
  113.1 6.9 %collective-permute-done.12 = bf16[256,896]{1,0:T(8,128)(2,1)S(1)} collective-permute-done((bf16[256,896]{1,0:T(8,128)(2,1)S(1)}, bf16[256,896]{1,0:T(8,128)(2,1)S(1)}, u32[]{:S(2)}, u32[]{:S(2)}) %collective-permute-start.12) | collective-permute-done | bytes 458784 | tf_op jit(solution)/shard_map/ppermute | solution.py:384
  121.1 16.3 %shard_map.257 = (bf16[1024,2432]{1,0:T(8,128)(2,1)}, bf16[1024,2432]{1,0:T(8,128)(2,1)}, bf16[1024,2432]{1,0:T(8,128)(2,1)}) custom-call(bf16[512,896]{1,0:T(8,128)(2,1)} %pad_maximum_fusion.3.mid_low, bf16[512,896]{1,0:T(8,128)(2,1)} %copy-done.22, bf16[896,2432]{1,0:T(8,128)(2,1)} %bitcast.185, ...), custom_call_target="tpu_custom_call", output_to_operand_aliasing={{0}: (5, {}), {1}: (6, {}), {2}: (7, {})} | custom-call | flops 1000000000 | bytes 1000000 | tf_op jit(solution)/shard_map/pallas_call | solution.py:428
  137.4 11.0 %shard_map.258 = bf16[512,896]{1,0:T(8,128)(2,1)} custom-call(bf16[1024,2432]{1,0:T(8,128)(2,1)} %get-tuple-element.133.gate_grad, bf16[1024,2432]{1,0:T(8,128)(2,1)} %get-tuple-element.134.up_grad, bf16[896,2432]{1,0:T(8,128)(2,1)} %bitcast.186, bf16[896,2432]{1,0:T(8,128)(2,1)} %bitcast.190), custom_call_target="tpu_custom_call" | custom-call | flops 1000000000 | bytes 1000000 | tf_op jit(solution)/shard_map/pallas_call | solution.py:428
  148.5 5.9 %convolution_convert_fusion.2 = bf16[2432,896]{1,0:T(8,128)(2,1)S(1)} fusion(bf16[1024,2432]{1,0:T(8,128)(2,1)S(1)} %copy-done, bf16[512,896]{1,0:T(8,128)(2,1)S(1)} %copy-done.23, bf16[512,896]{1,0:T(8,128)(2,1)S(1)} %copy-done.10), kind=kOutput, calls=%fused_computation.2 | convolution fusion | flops 4468588544 | bytes 11173888 | tf_op jit(solution)/shard_map/dot_general | solution.py:43
  156.0 1.5 collective-permute-start.15
  157.6 5.2 %convolution_convert_fusion = bf16[896,2432]{1,0:T(8,128)(2,1)S(1)} fusion(bf16[1024,896]{1,0:T(8,128)(2,1)S(1)} %constant_dynamic-update-slice_fusion.3, bf16[1024,2432]{1,0:T(8,128)(2,1)S(1)} %bitcast.195), kind=kOutput, calls=%fused_computation | convolution fusion | flops 4464918528 | bytes 11173888 | tf_op jit(solution)/shard_map/dot_general | solution.py:43
  162.9 5.4 %convolution_convert_fusion.1 = bf16[896,2432]{1,0:T(8,128)(2,1)S(1)} fusion(bf16[1024,896]{1,0:T(8,128)(2,1)S(1)} %constant_dynamic-update-slice_fusion.3, bf16[1024,2432]{1,0:T(8,128)(2,1)S(1)} %bitcast.193), kind=kOutput, calls=%fused_computation.1 | convolution fusion | flops 4464918528 | bytes 11173888 | tf_op jit(solution)/shard_map/dot_general | solution.py:43
  168.9 2.2 broadcast_select_fusion.5
  171.1 1.5 collective-permute-start.18
  172.6 1.7 broadcast_select_fusion.2
  175.6 6.6 %shard_map.260 = bf16[512,896]{1,0:T(8,128)(2,1)} custom-call(bf16[1024,2432]{1,0:T(8,128)(2,1)} %get-tuple-element.140.activ, bf16[2432,896]{1,0:T(8,128)(2,1)} %w_down.7), custom_call_target="tpu_custom_call" | custom-call | flops 1000000000 | bytes 1000000 | tf_op jit(solution)/shard_map/pallas_call | solution.py:428
  182.2 11.0 %shard_map.259 = f32[512,896]{1,0:T(8,128)} custom-call(bf16[1024,2432]{1,0:T(8,128)(2,1)} %get-tuple-element.133.gate_grad, bf16[1024,2432]{1,0:T(8,128)(2,1)} %get-tuple-element.134.up_grad, bf16[896,2432]{1,0:T(8,128)(2,1)} %bitcast.187, bf16[896,2432]{1,0:T(8,128)(2,1)} %bitcast.191), custom_call_target="tpu_custom_call" | custom-call | flops 1000000000 | bytes 1000000 | tf_op jit(solution)/shard_map/pallas_call | solution.py:428
  193.3 3.1 convert_add_fusion.6.norm_grad
  196.4 3.3 collective-permute-done.16
  199.7 1.6 fusion.3
  201.4 3.0 add_convert_fusion.1
  204.4 3.2 add_convert_fusion
  214.2 6.6 %shard_map.261 = f32[512,896]{1,0:T(8,128)} custom-call(bf16[1024,2432]{1,0:T(8,128)(2,1)} %get-tuple-element.140.activ, bf16[2432,896]{1,0:T(8,128)(2,1)} %w_down.7), custom_call_target="tpu_custom_call" | custom-call | flops 1000000000 | bytes 1000000 | tf_op jit(solution)/shard_map/pallas_call | solution.py:428
  220.8 31.2 %shard_map.262 = (bf16[896,1152]{1,0:T(8,128)(2,1)}, bf16[896,896]{1,0:T(8,128)(2,1)}, f32[1,1152]{1,0:T(1,128)}, f32[1,896]{1,0:T(1,128)}, f32[1,896]{1,0:T(1,128)}, /*index=5*/f32[512,896]{1,0:T(8,128)}) custom-call(f32[256,896]{1,0:T(8,128)} %get-tuple-element.98.mid_early, f32[256,896]{1,0:T(8,128)} %get-tuple-element.109.mid_late, ...), custom_call_target="tpu_custom_call" | custom-call | flops 1000000000 | bytes 3333333 | tf_op jit(solution)/shard_map/pallas_call | solution.py:182
  253.4 2.6 fusion.9
  257.5 1.9 fusion.2
  260.3 2.3 collective-permute-start.46
  266.8 1.9 pad_maximum_fusion.1
  269.5 3.3 collective-permute-start.23
  272.8 1.8 collective-permute-done.46
  275.8 8.0 %collective-permute-done.39 = bf16[2,2,56,1152]{3,2,0,1:T(8,128)(2,1)} collective-permute-done((bf16[2,2,56,1152]{3,2,0,1:T(8,128)(2,1)}, bf16[2,2,56,1152]{3,2,0,1:T(8,128)(2,1)}, u32[]{:S(2)}, u32[]{:S(2)}) %collective-permute-start.39) | collective-permute-done | bytes 516128 | tf_op jit(solution)/shard_map/ppermute | solution.py:384
  285.1 9.4 %collective-permute-done.47 = bf16[1,152,896]{2,1,0:T(8,128)(2,1)S(1)} collective-permute-done((bf16[1,152,896]{2,1,0:T(8,128)(2,1)S(1)}, bf16[1,152,896]{2,1,0:T(8,128)(2,1)S(1)}, u32[]{:S(2)}, u32[]{:S(2)}) %collective-permute-start.47) | collective-permute-done | bytes 272416 | tf_op jit(solution)/shard_map/ppermute | solution.py:384
  294.7 2.0 collective-permute-start.48
  298.2 3.2 collective-permute-start.33
  302.8 9.4 %collective-permute-done.33 = bf16[1,2,56,1280]{3,2,0,1:T(8,128)(2,1)S(1)} collective-permute-done((bf16[1,2,56,1280]{3,2,0,1:T(8,128)(2,1)S(1)}, bf16[1,2,56,1280]{3,2,0,1:T(8,128)(2,1)S(1)}, u32[]{:S(2)}, u32[]{:S(2)}) %collective-permute-start.33) | collective-permute-done | bytes 286752 | tf_op jit(solution)/shard_map/ppermute | solution.py:384
  313.7 3.2 collective-permute-start.42
  317.1 2.4 collective-permute-start.35
  323.8 12.1 %collective-permute-start.43 = (bf16[2,2,56,1152]{3,2,0,1:T(8,128)(2,1)S(1)}, bf16[2,2,56,1152]{3,2,0,1:T(8,128)(2,1)S(1)}, u32[]{:S(2)}, u32[]{:S(2)}) collective-permute-start(bf16[2,2,56,1152]{3,2,0,1:T(8,128)(2,1)S(1)} %maximum_select_fusion.25), channel_id=1, source_target_pairs={{0,8},{2,10},{4,12},{6,14},{8,0},{10,2},{12,4},{14,6},{16,24},{18,... | collective-permute-start | bytes 1548296 | tf_op jit(solution)/shard_map/ppermute | solution.py:384
  336.0 4.2 collective-permute-done.24
  340.6 2.9 collective-permute-start.25
  343.8 8.5 %collective-permute-done.43 = bf16[2,2,56,1152]{3,2,0,1:T(8,128)(2,1)S(1)} collective-permute-done((bf16[2,2,56,1152]{3,2,0,1:T(8,128)(2,1)S(1)}, bf16[2,2,56,1152]{3,2,0,1:T(8,128)(2,1)S(1)}, u32[]{:S(2)}, u32[]{:S(2)}) %collective-permute-start.43) | collective-permute-done | bytes 516128 | tf_op jit(solution)/shard_map/ppermute | solution.py:384
  353.7 2.4 collective-permute-done.25
  356.2 2.5 collective-permute-start.26
  358.7 9.6 %collective-permute-done.36 = bf16[2,2,56,1280]{3,2,0,1:T(8,128)(2,1)S(1)} collective-permute-done((bf16[2,2,56,1280]{3,2,0,1:T(8,128)(2,1)S(1)}, bf16[2,2,56,1280]{3,2,0,1:T(8,128)(2,1)S(1)}, u32[]{:S(2)}, u32[]{:S(2)}) %collective-permute-start.36) | collective-permute-done | bytes 573472 | tf_op jit(solution)/shard_map/ppermute | solution.py:384
  368.6 2.5 collective-permute-start.37
  371.5 7.2 %collective-permute-start.50 = (bf16[8,152,896]{2,1,0:T(8,128)(2,1)S(1)}, bf16[8,152,896]{2,1,0:T(8,128)(2,1)S(1)}, u32[]{:S(2)}, u32[]{:S(2)}) collective-permute-start(bf16[8,152,896]{2,1,0:T(8,128)(2,1)S(1)} %bitcast.209), channel_id=1, source_target_pairs={{0,2},{2,0},{4,6},{6,4},{8,10},{10,8},{12,14},{14,12},{16,18},{18,... | collective-permute-start | bytes 6537224 | tf_op jit(solution)/shard_map/ppermute | solution.py:384
  378.8 2.2 collective-permute-start.27
  381.0 9.5 %collective-permute-done.44 = bf16[4,2,56,1152]{3,2,0,1:T(8,128)(2,1)S(1)} collective-permute-done((bf16[4,2,56,1152]{3,2,0,1:T(8,128)(2,1)S(1)}, bf16[4,2,56,1152]{3,2,0,1:T(8,128)(2,1)S(1)}, u32[]{:S(2)}, u32[]{:S(2)}) %collective-permute-start.44) | collective-permute-done | bytes 1032224 | tf_op jit(solution)/shard_map/ppermute | solution.py:384
  390.9 5.0 %collective-permute-start.45 = (bf16[8,2,56,1152]{3,2,0,1:T(8,128)(2,1)S(1)}, bf16[8,2,56,1152]{3,2,0,1:T(8,128)(2,1)S(1)}, u32[]{:S(2)}, u32[]{:S(2)}) collective-permute-start(bf16[8,2,56,1152]{3,2,0,1:T(8,128)(2,1)S(1)} %bitcast.215), channel_id=1, source_target_pairs={{0,2},{2,0},{4,6},{6,4},{8,10},{10,8},{12,14},{14,12},{16,18},{18,... | collective-permute-start | bytes 6193160 | tf_op jit(solution)/shard_map/ppermute | solution.py:384
  396.4 8.4 %collective-permute-start.38 = (bf16[8,2,56,1280]{3,2,0,1:T(8,128)(2,1)S(1)}, bf16[8,2,56,1280]{3,2,0,1:T(8,128)(2,1)S(1)}, u32[]{:S(2)}, u32[]{:S(2)}) collective-permute-start(bf16[8,2,56,1280]{3,2,0,1:T(8,128)(2,1)S(1)} %bitcast.205), channel_id=1, source_target_pairs={{0,2},{2,0},{4,6},{6,4},{8,10},{10,8},{12,14},{14,12},{16,18},{18,... | collective-permute-start | bytes 6881288 | tf_op jit(solution)/shard_map/ppermute | solution.py:384
  406.0 4.4 %bitcast_convert_fusion = f32[2432,896]{1,0:T(8,128)} fusion(bf16[2,8,152,896]{3,2,1,0:T(8,128)(2,1)S(1)} %maximum_select_fusion.2), kind=kLoop, calls=%fused_computation.9 | loop fusion | flops 2179072 | bytes 13074432 | tf_op jit(solution)/shard_map/convert_element_type | solution.py:798
  412.0 6.6 %collective-permute-done.30 = bf16[4,32,2048]{2,1,0:T(8,128)(2,1)S(1)} collective-permute-done((bf16[4,32,2048]{2,1,0:T(8,128)(2,1)S(1)}, bf16[4,32,2048]{2,1,0:T(8,128)(2,1)S(1)}, u32[]{:S(2)}, u32[]{:S(2)}) %collective-permute-start.30) | collective-permute-done | bytes 524320 | tf_op jit(solution)/shard_map/ppermute | solution.py:384
  418.8 7.3 %collective-permute-start.31 = (bf16[8,32,2048]{2,1,0:T(8,128)(2,1)S(1)}, bf16[8,32,2048]{2,1,0:T(8,128)(2,1)S(1)}, u32[]{:S(2)}, u32[]{:S(2)}) collective-permute-start(bf16[8,32,2048]{2,1,0:T(8,128)(2,1)S(1)} %bitcast.241), channel_id=1, source_target_pairs={{0,2},{2,0},{4,6},{6,4},{8,10},{10,8},{12,14},{14,12},{16,18},{18,... | collective-permute-start | bytes 3145736 | tf_op jit(solution)/shard_map/ppermute | solution.py:384
  426.5 3.8 maximum_convert_fusion.1
  430.5 3.8 maximum_convert_fusion
  435.3 1.9 fusion.22
  (294 shorter events, 72.4 us)
Async XLA Ops:
  4.8 22.6 %collective-permute-start.1 = (bf16[224,1152]{1,0:T(8,128)(2,1)}, bf16[224,1152]{1,0:T(8,128)(2,1)S(1)}, u32[]{:S(2)}, u32[]{:S(2)}) collective-permute-start(bf16[224,1152]{1,0:T(8,128)(2,1)} %constant_dynamic-slice_fusion.7), channel_id=1, source_target_pairs={{0,1},{1,0},{2,3},{3,2},{4,5},{5,4},{6,7},{7,6},{8,9},{9,8},{10,11... | collective-permute-start | bytes 1548296 | tf_op jit(solution)/shard_map/ppermute | solution.py:384
  7.6 19.8 %collective-permute-start.2 = (bf16[224,896]{1,0:T(8,128)(2,1)}, bf16[224,896]{1,0:T(8,128)(2,1)}, u32[]{:S(2)}, u32[]{:S(2)}) collective-permute-start(bf16[224,896]{1,0:T(8,128)(2,1)} %constant_dynamic-slice_fusion.6), channel_id=1, source_target_pairs={{0,1},{1,0},{2,3},{3,2},{4,5},{5,4},{6,7},{7,6},{8,9},{9,8},{10,11... | collective-permute-start | bytes 1204232 | tf_op jit(solution)/shard_map/ppermute | solution.py:384
  7.7 19.6 %collective-permute-start = (bf16[1472]{0:T(1024)(128)(2,1)S(1)}, bf16[1472]{0:T(1024)(128)(2,1)S(1)}, u32[]{:S(2)}, u32[]{:S(2)}) collective-permute-start(bf16[1472]{0:T(1024)(128)(2,1)S(1)} %concatenate.206), channel_id=1, source_target_pairs={{0,1},{1,0},{2,3},{3,2},{4,5},{5,4},{6,7},{7,6},{8,9},{9,8},{10,11... | collective-permute-start | bytes 8840 | tf_op jit(solution)/shard_map/ppermute | solution.py:384
  13.5 75.0 %copy-start.9 = (bf16[512,896]{1,0:T(8,128)(2,1)}, bf16[512,896]{1,0:T(8,128)(2,1)S(1)}, u32[]{:S(2)}) copy-start(bf16[512,896]{1,0:T(8,128)(2,1)S(1)} %multiply_convert_fusion.mlp_grad) | copy-start | bytes 2752516
  27.4 8.5 %collective-permute-start.4 = (bf16[224,896]{1,0:T(8,128)(2,1)}, bf16[224,896]{1,0:T(8,128)(2,1)}, u32[]{:S(2)}, u32[]{:S(2)}) collective-permute-start(bf16[224,896]{1,0:T(8,128)(2,1)} %collective-permute-done.2), channel_id=1, source_target_pairs={{0,2},{2,0},{4,6},{6,4},{8,10},{10,8},{12,14},{14,12},{16,18},{18,... | collective-permute-start | bytes 1204232 | tf_op jit(solution)/shard_map/ppermute | solution.py:384
  30.3 8.6 %collective-permute-start.3 = (bf16[224,1152]{1,0:T(8,128)(2,1)S(1)}, bf16[224,1152]{1,0:T(8,128)(2,1)S(1)}, u32[]{:S(2)}, u32[]{:S(2)}) collective-permute-start(bf16[224,1152]{1,0:T(8,128)(2,1)S(1)} %collective-permute-done.1), channel_id=1, source_target_pairs={{0,2},{2,0},{4,6},{6,4},{8,10},{10,8},{12,14},{14,12},{16,18},{18,... | collective-permute-start | bytes 1548296 | tf_op jit(solution)/shard_map/ppermute | solution.py:384
  32.9 24.2 %collective-permute-start.5 = (bf16[112,2432]{1,0:T(8,128)(2,1)S(1)}, bf16[112,2432]{1,0:T(8,128)(2,1)}, u32[]{:S(2)}, u32[]{:S(2)}) collective-permute-start(bf16[112,2432]{1,0:T(8,128)(2,1)S(1)} %dynamic_slice.121), channel_id=1, source_target_pairs={{0,1},{1,0},{2,3},{3,2},{4,5},{5,4},{6,7},{7,6},{8,9},{9,8},{10,11... | collective-permute-start | bytes 1634312 | tf_op jit(solution)/shard_map/ppermute | solution.py:384
  35.8 22.4 %collective-permute-start.6 = (bf16[112,2432]{1,0:T(8,128)(2,1)S(1)}, bf16[112,2432]{1,0:T(8,128)(2,1)}, u32[]{:S(2)}, u32[]{:S(2)}) collective-permute-start(bf16[112,2432]{1,0:T(8,128)(2,1)S(1)} %dynamic_slice.122), channel_id=1, source_target_pairs={{0,1},{1,0},{2,3},{3,2},{4,5},{5,4},{6,7},{7,6},{8,9},{9,8},{10,11... | collective-permute-start | bytes 1634312 | tf_op jit(solution)/shard_map/ppermute | solution.py:384
  40.8 45.6 %slice-start.8 = ((s8[4358144]{0:T(1024)(128)(4,1)}), s8[163840]{0:T(1024)(128)(4,1)S(1)}, s32[]{:S(2)}) async-start(s8[4358144]{0:T(1024)(128)(4,1)} %bitcast.268), calls=%async_computation.8 | async-start | bytes 327680
  58.2 14.4 %collective-permute-start.8 = (bf16[112,2432]{1,0:T(8,128)(2,1)}, bf16[112,2432]{1,0:T(8,128)(2,1)S(1)}, u32[]{:S(2)}, u32[]{:S(2)}) collective-permute-start(bf16[112,2432]{1,0:T(8,128)(2,1)} %collective-permute-done.6), channel_id=1, source_target_pairs={{0,4},{2,6},{4,0},{6,2},{8,12},{10,14},{12,8},{14,10},{16,20},{18,... | collective-permute-start | bytes 1634312 | tf_op jit(solution)/shard_map/ppermute | solution.py:384
  59.7 23.0 %collective-permute-start.7 = (bf16[112,2432]{1,0:T(8,128)(2,1)}, bf16[112,2432]{1,0:T(8,128)(2,1)S(1)}, u32[]{:S(2)}, u32[]{:S(2)}) collective-permute-start(bf16[112,2432]{1,0:T(8,128)(2,1)} %collective-permute-done.5), channel_id=1, source_target_pairs={{0,4},{2,6},{4,0},{6,2},{8,12},{10,14},{12,8},{14,10},{16,20},{18,... | collective-permute-start | bytes 1634312 | tf_op jit(solution)/shard_map/ppermute | solution.py:384
  59.7 24.4 %collective-permute-start.9 = (bf16[256,896]{1,0:T(8,128)(2,1)}, bf16[256,896]{1,0:T(8,128)(2,1)S(1)}, u32[]{:S(2)}, u32[]{:S(2)}) collective-permute-start(bf16[256,896]{1,0:T(8,128)(2,1)} %get-tuple-element.108), channel_id=1, source_target_pairs={{0,1},{1,0},{2,3},{3,2},{4,5},{5,4},{6,7},{7,6},{8,9},{9,8},{10,11... | collective-permute-start | bytes 1376264 | tf_op jit(solution)/shard_map/ppermute | solution.py:384
  61.2 25.3 %slice-start.9 = ((s8[4358144]{0:T(1024)(128)(4,1)}), s8[4194304]{0:T(1024)(128)(4,1)S(1)}, s32[]{:S(2)}) async-start(s8[4358144]{0:T(1024)(128)(4,1)} %bitcast.268), calls=%async_computation.9 | async-start | bytes 8388608
  84.1 7.2 %collective-permute-start.11 = (bf16[224,2432]{1,0:T(8,128)(2,1)S(1)}, bf16[224,2432]{1,0:T(8,128)(2,1)S(1)}, u32[]{:S(2)}, u32[]{:S(2)}) collective-permute-start(bf16[224,2432]{1,0:T(8,128)(2,1)S(1)} %bitcast.233), channel_id=1, source_target_pairs={{0,2},{2,0},{4,6},{6,4},{8,10},{10,8},{12,14},{14,12},{16,18},{18,... | collective-permute-start | bytes 3268616 | tf_op jit(solution)/shard_map/ppermute | solution.py:384
  86.6 5.1 %collective-permute-start.10 = (bf16[224,2432]{1,0:T(8,128)(2,1)S(1)}, bf16[224,2432]{1,0:T(8,128)(2,1)S(1)}, u32[]{:S(2)}, u32[]{:S(2)}) collective-permute-start(bf16[224,2432]{1,0:T(8,128)(2,1)S(1)} %bitcast.235), channel_id=1, source_target_pairs={{0,2},{2,0},{4,6},{6,4},{8,10},{10,8},{12,14},{14,12},{16,18},{18,... | collective-permute-start | bytes 3268616 | tf_op jit(solution)/shard_map/ppermute | solution.py:384
  88.5 24.5 %collective-permute-start.13 = (bf16[512,896]{1,0:T(8,128)(2,1)S(1)}, bf16[512,896]{1,0:T(8,128)(2,1)S(1)}, u32[]{:S(2)}, u32[]{:S(2)}) collective-permute-start(bf16[512,896]{1,0:T(8,128)(2,1)S(1)} %multiply_convert_fusion.mlp_grad), channel_id=1, source_target_pairs={{0,1},{1,0},{2,3},{3,2},{4,5},{5,4},{6,7},{7,6},{8,9},{9,8},{10,11... | collective-permute-start | bytes 2752520 | tf_op jit(solution)/shard_map/ppermute | solution.py:384
  91.3 28.7 %collective-permute-start.12 = (bf16[256,896]{1,0:T(8,128)(2,1)S(1)}, bf16[256,896]{1,0:T(8,128)(2,1)S(1)}, u32[]{:S(2)}, u32[]{:S(2)}) collective-permute-start(bf16[256,896]{1,0:T(8,128)(2,1)S(1)} %copy-done.17), channel_id=1, source_target_pairs={{0,1},{1,0},{2,3},{3,2},{4,5},{5,4},{6,7},{7,6},{8,9},{9,8},{10,11... | collective-permute-start | bytes 1376264 | tf_op jit(solution)/shard_map/ppermute | solution.py:384
  120.0 17.4 %copy-start.18 = (bf16[256,896]{1,0:T(8,128)(2,1)}, bf16[256,896]{1,0:T(8,128)(2,1)S(1)}, u32[]{:S(2)}) copy-start(bf16[256,896]{1,0:T(8,128)(2,1)S(1)} %collective-permute-done.12) | copy-start | bytes 1376260
  137.4 11.1 %copy-start = (bf16[1024,2432]{1,0:T(8,128)(2,1)S(1)}, bf16[1024,2432]{1,0:T(8,128)(2,1)}, u32[]{:S(2)}) copy-start(bf16[1024,2432]{1,0:T(8,128)(2,1)} %get-tuple-element.140.activ) | copy-start | bytes 14942212
  137.4 11.0 %copy-start.10 = (bf16[512,896]{1,0:T(8,128)(2,1)S(1)}, bf16[512,896]{1,0:T(8,128)(2,1)}, u32[]{:S(2)}) copy-start(bf16[512,896]{1,0:T(8,128)(2,1)} %copy-done.9) | copy-start | bytes 2752516
  137.4 11.0 %copy-start.23 = (bf16[512,896]{1,0:T(8,128)(2,1)S(1)}, bf16[512,896]{1,0:T(8,128)(2,1)}, u32[]{:S(2)}) copy-start(bf16[512,896]{1,0:T(8,128)(2,1)} %copy-done.22) | copy-start | bytes 2752516
  137.4 20.1 %slice-start.2 = ((s8[4980736]{0:T(1024)(128)(4,1)}), s8[786432]{0:T(1024)(128)(4,1)S(1)}, s32[]{:S(2)}) async-start(s8[4980736]{0:T(1024)(128)(4,1)} %bitcast.194), calls=%async_computation.2 | async-start | bytes 1572864
  154.6 13.7 %collective-permute-start.14 = (bf16[1216,896]{1,0:T(8,128)(2,1)S(1)}, bf16[1216,896]{1,0:T(8,128)(2,1)S(1)}, u32[]{:S(2)}, u32[]{:S(2)}) collective-permute-start(bf16[1216,896]{1,0:T(8,128)(2,1)S(1)} %dynamic-slice_bitcast_fusion), channel_id=1, source_target_pairs={{0,2},{2,0},{4,6},{6,4},{8,10},{10,8},{12,14},{14,12},{16,18},{18,... | collective-permute-start | bytes 6537224 | tf_op jit(solution)/shard_map/ppermute | solution.py:384
  156.0 37.3 %collective-permute-start.15 = (bf16[512,896]{1,0:T(8,128)(2,1)}, bf16[512,896]{1,0:T(8,128)(2,1)}, u32[]{:S(2)}, u32[]{:S(2)}) collective-permute-start(bf16[512,896]{1,0:T(8,128)(2,1)} %shard_map.258), channel_id=1, source_target_pairs={{0,1},{1,0},{2,3},{3,2},{4,5},{5,4},{6,7},{7,6},{8,9},{9,8},{10,11... | collective-permute-start | bytes 2752520 | tf_op jit(solution)/shard_map/ppermute | solution.py:384
  171.1 30.3 %collective-permute-start.18 = (bf16[896,1152]{1,0:T(8,128)(2,1)}, bf16[896,1152]{1,0:T(8,128)(2,1)}, u32[]{:S(2)}, u32[]{:S(2)}) collective-permute-start(bf16[896,1152]{1,0:T(8,128)(2,1)} %broadcast_select_fusion.5), channel_id=1, source_target_pairs={{0,2},{2,0},{4,6},{6,4},{8,10},{10,8},{12,14},{14,12},{16,18},{18,... | collective-permute-start | bytes 6193160 | tf_op jit(solution)/shard_map/ppermute | solution.py:384
  174.2 30.1 %collective-permute-start.17 = (bf16[896,1280]{1,0:T(8,128)(2,1)}, bf16[896,1280]{1,0:T(8,128)(2,1)}, u32[]{:S(2)}, u32[]{:S(2)}) collective-permute-start(bf16[896,1280]{1,0:T(8,128)(2,1)} %broadcast_select_fusion.2), channel_id=1, source_target_pairs={{0,2},{2,0},{4,6},{6,4},{8,10},{10,8},{12,14},{14,12},{16,18},{18,... | collective-permute-start | bytes 6881288 | tf_op jit(solution)/shard_map/ppermute | solution.py:384
  174.4 25.3 %collective-permute-start.16 = (bf16[4,152,896]{2,1,0:T(8,128)(2,1)S(1)}, bf16[4,152,896]{2,1,0:T(8,128)(2,1)}, u32[]{:S(2)}, u32[]{:S(2)}) collective-permute-start(bf16[4,152,896]{2,1,0:T(8,128)(2,1)S(1)} %dynamic-slice_bitcast_fusion.5), channel_id=1, source_target_pairs={{0,4},{2,6},{4,0},{6,2},{8,12},{10,14},{12,8},{14,10},{16,20},{18,... | collective-permute-start | bytes 3268616 | tf_op jit(solution)/shard_map/ppermute | solution.py:384
  175.6 25.7 %slice-start.4 = ((s8[4358144]{0:T(1024)(128)(4,1)}), s8[4194304]{0:T(1024)(128)(4,1)S(1)}, s32[]{:S(2)}) async-start(s8[4358144]{0:T(1024)(128)(4,1)} %bitcast.196), calls=%async_computation.4 | async-start | bytes 8388608
  182.2 19.1 %slice-start.5 = ((s8[4358144]{0:T(1024)(128)(4,1)}), s8[163840]{0:T(1024)(128)(4,1)S(1)}, s32[]{:S(2)}) async-start(s8[4358144]{0:T(1024)(128)(4,1)} %bitcast.196), calls=%async_computation.5 | async-start | bytes 327680
  208.5 43.5 %collective-permute-start.20 = (bf16[2,152,896]{2,1,0:T(8,128)(2,1)}, bf16[2,152,896]{2,1,0:T(8,128)(2,1)}, u32[]{:S(2)}, u32[]{:S(2)}) collective-permute-start(bf16[2,152,896]{2,1,0:T(8,128)(2,1)} %dynamic-slice_bitcast_fusion.9), channel_id=1, source_target_pairs={{0,8},{2,10},{4,12},{6,14},{8,0},{10,2},{12,4},{14,6},{16,24},{18,... | collective-permute-start | bytes 1634312 | tf_op jit(solution)/shard_map/ppermute | solution.py:384
  209.8 43.5 %collective-permute-start.19 = (bf16[512,896]{1,0:T(8,128)(2,1)}, bf16[512,896]{1,0:T(8,128)(2,1)}, u32[]{:S(2)}, u32[]{:S(2)}) collective-permute-start(bf16[512,896]{1,0:T(8,128)(2,1)} %shard_map.260), channel_id=1, source_target_pairs={{0,1},{1,0},{2,3},{3,2},{4,5},{5,4},{6,7},{7,6},{8,9},{9,8},{10,11... | collective-permute-start | bytes 2752520 | tf_op jit(solution)/shard_map/ppermute | solution.py:384
  211.1 44.9 %collective-permute-start.22 = (bf16[4,2,56,1152]{3,2,0,1:T(8,128)(2,1)}, bf16[4,2,56,1152]{3,2,0,1:T(8,128)(2,1)}, u32[]{:S(2)}, u32[]{:S(2)}) collective-permute-start(bf16[4,2,56,1152]{3,2,0,1:T(8,128)(2,1)} %dynamic-slice_bitcast_fusion.7), channel_id=1, source_target_pairs={{0,4},{2,6},{4,0},{6,2},{8,12},{10,14},{12,8},{14,10},{16,20},{18,... | collective-permute-start | bytes 3096584 | tf_op jit(solution)/shard_map/ppermute | solution.py:384
  214.0 43.5 %collective-permute-start.21 = (bf16[4,2,56,1280]{3,2,0,1:T(8,128)(2,1)}, bf16[4,2,56,1280]{3,2,0,1:T(8,128)(2,1)}, u32[]{:S(2)}, u32[]{:S(2)}) collective-permute-start(bf16[4,2,56,1280]{3,2,0,1:T(8,128)(2,1)} %dynamic-slice_bitcast_fusion.4), channel_id=1, source_target_pairs={{0,8},{2,10},{4,12},{6,14},{8,0},{10,2},{12,4},{14,6},{16,24},{18,... | collective-permute-start | bytes 3440648 | tf_op jit(solution)/shard_map/ppermute | solution.py:384
  220.8 32.5 %copy-start.6 = (f32[512,896]{1,0:T(8,128)S(1)}, f32[512,896]{1,0:T(8,128)}, u32[]{:S(2)}) copy-start(f32[512,896]{1,0:T(8,128)} %shard_map.261) | copy-start | bytes 5505028
  220.8 32.5 %copy-start.12 = (f32[256,896]{1,0:T(8,128)S(1)}, f32[256,896]{1,0:T(8,128)}, u32[]{:S(2)}) copy-start(f32[256,896]{1,0:T(8,128)} %get-tuple-element.109.mid_late) | copy-start | bytes 2752516
  260.3 14.4 %collective-permute-start.46 = (bf16[1,152,896]{2,1,0:T(8,128)(2,1)}, bf16[1,152,896]{2,1,0:T(8,128)(2,1)}, u32[]{:S(2)}, u32[]{:S(2)}) collective-permute-start(bf16[1,152,896]{2,1,0:T(8,128)(2,1)} %constant_dynamic-slice_fusion), channel_id=1, source_target_pairs={{0,16},{2,18},{4,20},{6,22},{8,24},{10,26},{12,28},{14,30},{16,0},... | collective-permute-start | bytes 817160 | tf_op jit(solution)/shard_map/ppermute | solution.py:384
  263.4 33.6 %collective-permute-start.32 = (bf16[2,2,56,1280]{3,2,0,1:T(8,128)(2,1)}, bf16[2,2,56,1280]{3,2,0,1:T(8,128)(2,1)}, u32[]{:S(2)}, u32[]{:S(2)}) collective-permute-start(bf16[2,2,56,1280]{3,2,0,1:T(8,128)(2,1)} %dynamic-slice_bitcast_fusion.8), channel_id=1, source_target_pairs={{0,4},{2,6},{4,0},{6,2},{8,12},{10,14},{12,8},{14,10},{16,20},{18,... | collective-permute-start | bytes 1720328 | tf_op jit(solution)/shard_map/ppermute | solution.py:384
  264.5 19.3 %collective-permute-start.39 = (bf16[2,2,56,1152]{3,2,0,1:T(8,128)(2,1)}, bf16[2,2,56,1152]{3,2,0,1:T(8,128)(2,1)}, u32[]{:S(2)}, u32[]{:S(2)}) collective-permute-start(bf16[2,2,56,1152]{3,2,0,1:T(8,128)(2,1)} %dynamic-slice_bitcast_fusion.11), channel_id=1, source_target_pairs={{0,8},{2,10},{4,12},{6,14},{8,0},{10,2},{12,4},{14,6},{16,24},{18,... | collective-permute-start | bytes 1548296 | tf_op jit(solution)/shard_map/ppermute | solution.py:384
  269.3 14.5 %copy-start.8 = (bf16[4,2,56,1152]{3,2,0,1:T(8,128)(2,1)S(1)}, bf16[4,2,56,1152]{3,2,0,1:T(8,128)(2,1)}, u32[]{:S(2)}) copy-start(bf16[4,2,56,1152]{3,2,0,1:T(8,128)(2,1)} %copy-done.7) | copy-start | bytes 3096580
  269.5 50.0 %collective-permute-start.23 = (bf16[2,256,2048]{2,1,0:T(8,128)(2,1)S(1)}, bf16[2,256,2048]{2,1,0:T(8,128)(2,1)S(1)}, u32[]{:S(2)}, u32[]{:S(2)}) collective-permute-start(bf16[2,256,2048]{2,1,0:T(8,128)(2,1)S(1)} %dynamic-slice_bitcast_fusion.3), channel_id=1, source_target_pairs={{0,2},{2,0},{4,6},{6,4},{8,10},{10,8},{12,14},{14,12},{16,18},{18,... | collective-permute-start | bytes 6291464 | tf_op jit(solution)/shard_map/ppermute | solution.py:384
  275.7 18.8 %collective-permute-start.47 = (bf16[1,152,896]{2,1,0:T(8,128)(2,1)S(1)}, bf16[1,152,896]{2,1,0:T(8,128)(2,1)S(1)}, u32[]{:S(2)}, u32[]{:S(2)}) collective-permute-start(bf16[1,152,896]{2,1,0:T(8,128)(2,1)S(1)} %add_convert_fusion.3), channel_id=1, source_target_pairs={{0,16},{2,18},{4,20},{6,22},{8,24},{10,26},{12,28},{14,30},{16,0},... | collective-permute-start | bytes 817160 | tf_op jit(solution)/shard_map/ppermute | solution.py:384
  285.0 16.4 %collective-permute-start.40 = (bf16[1,2,56,1152]{3,2,0,1:T(8,128)(2,1)S(1)}, bf16[1,2,56,1152]{3,2,0,1:T(8,128)(2,1)S(1)}, u32[]{:S(2)}, u32[]{:S(2)}) collective-permute-start(bf16[1,2,56,1152]{3,2,0,1:T(8,128)(2,1)S(1)} %constant_dynamic-slice_fusion.2), channel_id=1, source_target_pairs={{0,16},{2,18},{4,20},{6,22},{8,24},{10,26},{12,28},{14,30},{16,0},... | collective-permute-start | bytes 774152 | tf_op jit(solution)/shard_map/ppermute | solution.py:384
  294.7 28.3 %collective-permute-start.48 = (bf16[2,152,896]{2,1,0:T(8,128)(2,1)S(1)}, bf16[2,152,896]{2,1,0:T(8,128)(2,1)S(1)}, u32[]{:S(2)}, u32[]{:S(2)}) collective-permute-start(bf16[2,152,896]{2,1,0:T(8,128)(2,1)S(1)} %maximum_select_fusion.22), channel_id=1, source_target_pairs={{0,8},{2,10},{4,12},{6,14},{8,0},{10,2},{12,4},{14,6},{16,24},{18,... | collective-permute-start | bytes 1634312 | tf_op jit(solution)/shard_map/ppermute | solution.py:384
  298.2 13.9 %collective-permute-start.33 = (bf16[1,2,56,1280]{3,2,0,1:T(8,128)(2,1)S(1)}, bf16[1,2,56,1280]{3,2,0,1:T(8,128)(2,1)S(1)}, u32[]{:S(2)}, u32[]{:S(2)}) collective-permute-start(bf16[1,2,56,1280]{3,2,0,1:T(8,128)(2,1)S(1)} %constant_dynamic-slice_fusion.4), channel_id=1, source_target_pairs={{0,16},{2,18},{4,20},{6,22},{8,24},{10,26},{12,28},{14,30},{16,0},... | collective-permute-start | bytes 860168 | tf_op jit(solution)/shard_map/ppermute | solution.py:384
  301.5 12.1 %collective-permute-start.41 = (bf16[56,1152]{1,0:T(8,128)(2,1)S(1)}, bf16[56,1152]{1,0:T(8,128)(2,1)S(1)}, u32[]{:S(2)}, u32[]{:S(2)}) collective-permute-start(bf16[56,1152]{1,0:T(8,128)(2,1)S(1)} %get-tuple-element.190), channel_id=1, source_target_pairs={{0,1},{1,0},{2,3},{3,2},{4,5},{5,4},{6,7},{7,6},{8,9},{9,8},{10,11... | collective-permute-start | bytes 387080 | tf_op jit(solution)/shard_map/ppermute | solution.py:384
  312.3 4.7 %collective-permute-start.34 = (bf16[56,1280]{1,0:T(8,128)(2,1)S(1)}, bf16[56,1280]{1,0:T(8,128)(2,1)S(1)}, u32[]{:S(2)}, u32[]{:S(2)}) collective-permute-start(bf16[56,1280]{1,0:T(8,128)(2,1)S(1)} %get-tuple-element.188), channel_id=1, source_target_pairs={{0,1},{1,0},{2,3},{3,2},{4,5},{5,4},{6,7},{7,6},{8,9},{9,8},{10,11... | collective-permute-start | bytes 430088 | tf_op jit(solution)/shard_map/ppermute | solution.py:384
  313.7 9.9 %collective-permute-start.42 = (bf16[1,2,56,1152]{3,2,1,0:T(8,128)(2,1)S(1)}, bf16[1,2,56,1152]{3,2,1,0:T(8,128)(2,1)S(1)}, u32[]{:S(2)}, u32[]{:S(2)}) collective-permute-start(bf16[1,2,56,1152]{3,2,1,0:T(8,128)(2,1)S(1)} %fusion.40), channel_id=1, source_target_pairs={{0,16},{2,18},{4,20},{6,22},{8,24},{10,26},{12,28},{14,30},{16,0},... | collective-permute-start | bytes 774152 | tf_op jit(solution)/shard_map/ppermute | solution.py:384
  317.1 26.4 %collective-permute-start.35 = (bf16[1,2,56,1280]{3,2,1,0:T(8,128)(2,1)S(1)}, bf16[1,2,56,1280]{3,2,1,0:T(8,128)(2,1)S(1)}, u32[]{:S(2)}, u32[]{:S(2)}) collective-permute-start(bf16[1,2,56,1280]{3,2,1,0:T(8,128)(2,1)S(1)} %fusion.38), channel_id=1, source_target_pairs={{0,16},{2,18},{4,20},{6,22},{8,24},{10,26},{12,28},{14,30},{16,0},... | collective-permute-start | bytes 860168 | tf_op jit(solution)/shard_map/ppermute | solution.py:384
  320.4 19.7 %collective-permute-start.24 = (bf16[256,2048]{1,0:T(8,128)(2,1)S(1)}, bf16[256,2048]{1,0:T(8,128)(2,1)S(1)}, u32[]{:S(2)}, u32[]{:S(2)}) collective-permute-start(bf16[256,2048]{1,0:T(8,128)(2,1)S(1)} %dynamic-slice_bitcast_fusion.6), channel_id=1, source_target_pairs={{0,1},{1,0},{2,3},{3,2},{4,5},{5,4},{6,7},{7,6},{8,9},{9,8},{10,11... | collective-permute-start | bytes 3145736 | tf_op jit(solution)/shard_map/ppermute | solution.py:384
  323.2 47.8 %collective-permute-start.49 = (bf16[4,152,896]{2,1,0:T(8,128)(2,1)S(1)}, bf16[4,152,896]{2,1,0:T(8,128)(2,1)S(1)}, u32[]{:S(2)}, u32[]{:S(2)}) collective-permute-start(bf16[4,152,896]{2,1,0:T(8,128)(2,1)S(1)} %bitcast.231), channel_id=1, source_target_pairs={{0,4},{2,6},{4,0},{6,2},{8,12},{10,14},{12,8},{14,10},{16,20},{18,... | collective-permute-start | bytes 3268616 | tf_op jit(solution)/shard_map/ppermute | solution.py:384
  323.8 28.5 %collective-permute-start.43 = (bf16[2,2,56,1152]{3,2,0,1:T(8,128)(2,1)S(1)}, bf16[2,2,56,1152]{3,2,0,1:T(8,128)(2,1)S(1)}, u32[]{:S(2)}, u32[]{:S(2)}) collective-permute-start(bf16[2,2,56,1152]{3,2,0,1:T(8,128)(2,1)S(1)} %maximum_select_fusion.25), channel_id=1, source_target_pairs={{0,8},{2,10},{4,12},{6,14},{8,0},{10,2},{12,4},{14,6},{16,24},{18,... | collective-permute-start | bytes 1548296 | tf_op jit(solution)/shard_map/ppermute | solution.py:384
  340.6 15.4 %collective-permute-start.25 = (bf16[4,32,2048]{2,1,0:T(8,128)(2,1)S(1)}, bf16[4,32,2048]{2,1,0:T(8,128)(2,1)S(1)}, u32[]{:S(2)}, u32[]{:S(2)}) collective-permute-start(bf16[4,32,2048]{2,1,0:T(8,128)(2,1)S(1)} %dynamic-slice_bitcast_fusion.10), channel_id=1, source_target_pairs={{0,4},{2,6},{4,0},{6,2},{8,12},{10,14},{12,8},{14,10},{16,20},{18,... | collective-permute-start | bytes 1572872 | tf_op jit(solution)/shard_map/ppermute | solution.py:384
  343.6 24.7 %collective-permute-start.36 = (bf16[2,2,56,1280]{3,2,0,1:T(8,128)(2,1)S(1)}, bf16[2,2,56,1280]{3,2,0,1:T(8,128)(2,1)S(1)}, u32[]{:S(2)}, u32[]{:S(2)}) collective-permute-start(bf16[2,2,56,1280]{3,2,0,1:T(8,128)(2,1)S(1)} %maximum_select_fusion.20), channel_id=1, source_target_pairs={{0,4},{2,6},{4,0},{6,2},{8,12},{10,14},{12,8},{14,10},{16,20},{18,... | collective-permute-start | bytes 1720328 | tf_op jit(solution)/shard_map/ppermute | solution.py:384
  352.6 37.9 %collective-permute-start.44 = (bf16[4,2,56,1152]{3,2,0,1:T(8,128)(2,1)S(1)}, bf16[4,2,56,1152]{3,2,0,1:T(8,128)(2,1)S(1)}, u32[]{:S(2)}, u32[]{:S(2)}) collective-permute-start(bf16[4,2,56,1152]{3,2,0,1:T(8,128)(2,1)S(1)} %bitcast.251), channel_id=1, source_target_pairs={{0,4},{2,6},{4,0},{6,2},{8,12},{10,14},{12,8},{14,10},{16,20},{18,... | collective-permute-start | bytes 3096584 | tf_op jit(solution)/shard_map/ppermute | solution.py:384
  356.2 22.5 %collective-permute-start.26 = (bf16[2,32,2048]{2,1,0:T(8,128)(2,1)S(1)}, bf16[2,32,2048]{2,1,0:T(8,128)(2,1)S(1)}, u32[]{:S(2)}, u32[]{:S(2)}) collective-permute-start(bf16[2,32,2048]{2,1,0:T(8,128)(2,1)S(1)} %dynamic-slice_bitcast_fusion.12), channel_id=1, source_target_pairs={{0,8},{2,10},{4,12},{6,14},{8,0},{10,2},{12,4},{14,6},{16,24},{18,... | collective-permute-start | bytes 786440 | tf_op jit(solution)/shard_map/ppermute | solution.py:384
  368.6 27.4 %collective-permute-start.37 = (bf16[4,2,56,1280]{3,2,0,1:T(8,128)(2,1)S(1)}, bf16[4,2,56,1280]{3,2,0,1:T(8,128)(2,1)S(1)}, u32[]{:S(2)}, u32[]{:S(2)}) collective-permute-start(bf16[4,2,56,1280]{3,2,0,1:T(8,128)(2,1)S(1)} %bitcast.227), channel_id=1, source_target_pairs={{0,8},{2,10},{4,12},{6,14},{8,0},{10,2},{12,4},{14,6},{16,24},{18,... | collective-permute-start | bytes 3440648 | tf_op jit(solution)/shard_map/ppermute | solution.py:384
  371.5 33.5 %collective-permute-start.50 = (bf16[8,152,896]{2,1,0:T(8,128)(2,1)S(1)}, bf16[8,152,896]{2,1,0:T(8,128)(2,1)S(1)}, u32[]{:S(2)}, u32[]{:S(2)}) collective-permute-start(bf16[8,152,896]{2,1,0:T(8,128)(2,1)S(1)} %bitcast.209), channel_id=1, source_target_pairs={{0,2},{2,0},{4,6},{6,4},{8,10},{10,8},{12,14},{14,12},{16,18},{18,... | collective-permute-start | bytes 6537224 | tf_op jit(solution)/shard_map/ppermute | solution.py:384
  378.8 17.1 %collective-permute-start.27 = (bf16[1,32,2048]{2,1,0:T(8,128)(2,1)S(1)}, bf16[1,32,2048]{2,1,0:T(8,128)(2,1)S(1)}, u32[]{:S(2)}, u32[]{:S(2)}) collective-permute-start(bf16[1,32,2048]{2,1,0:T(8,128)(2,1)S(1)} %constant_dynamic-slice_fusion.5), channel_id=1, source_target_pairs={{0,16},{2,18},{4,20},{6,22},{8,24},{10,26},{12,28},{14,30},{16,0},... | collective-permute-start | bytes 393224 | tf_op jit(solution)/shard_map/ppermute | solution.py:384
  390.9 20.4 %collective-permute-start.45 = (bf16[8,2,56,1152]{3,2,0,1:T(8,128)(2,1)S(1)}, bf16[8,2,56,1152]{3,2,0,1:T(8,128)(2,1)S(1)}, u32[]{:S(2)}, u32[]{:S(2)}) collective-permute-start(bf16[8,2,56,1152]{3,2,0,1:T(8,128)(2,1)S(1)} %bitcast.215), channel_id=1, source_target_pairs={{0,2},{2,0},{4,6},{6,4},{8,10},{10,8},{12,14},{14,12},{16,18},{18,... | collective-permute-start | bytes 6193160 | tf_op jit(solution)/shard_map/ppermute | solution.py:384
  395.9 8.9 %collective-permute-start.28 = (bf16[1,32,2048]{2,1,0:T(8,128)(2,1)S(1)}, bf16[1,32,2048]{2,1,0:T(8,128)(2,1)S(1)}, u32[]{:S(2)}, u32[]{:S(2)}) collective-permute-start(bf16[1,32,2048]{2,1,0:T(8,128)(2,1)S(1)} %add_convert_fusion.5), channel_id=1, source_target_pairs={{0,16},{2,18},{4,20},{6,22},{8,24},{10,26},{12,28},{14,30},{16,0},... | collective-permute-start | bytes 393224 | tf_op jit(solution)/shard_map/ppermute | solution.py:384
  396.4 29.7 %collective-permute-start.38 = (bf16[8,2,56,1280]{3,2,0,1:T(8,128)(2,1)S(1)}, bf16[8,2,56,1280]{3,2,0,1:T(8,128)(2,1)S(1)}, u32[]{:S(2)}, u32[]{:S(2)}) collective-permute-start(bf16[8,2,56,1280]{3,2,0,1:T(8,128)(2,1)S(1)} %bitcast.205), channel_id=1, source_target_pairs={{0,2},{2,0},{4,6},{6,4},{8,10},{10,8},{12,14},{14,12},{16,18},{18,... | collective-permute-start | bytes 6881288 | tf_op jit(solution)/shard_map/ppermute | solution.py:384
  404.8 5.6 %collective-permute-start.29 = (bf16[2,32,2048]{2,1,0:T(8,128)(2,1)S(1)}, bf16[2,32,2048]{2,1,0:T(8,128)(2,1)S(1)}, u32[]{:S(2)}, u32[]{:S(2)}) collective-permute-start(bf16[2,32,2048]{2,1,0:T(8,128)(2,1)S(1)} %maximum_select_fusion.28), channel_id=1, source_target_pairs={{0,8},{2,10},{4,12},{6,14},{8,0},{10,2},{12,4},{14,6},{16,24},{18,... | collective-permute-start | bytes 786440 | tf_op jit(solution)/shard_map/ppermute | solution.py:384
  410.5 8.1 %collective-permute-start.30 = (bf16[4,32,2048]{2,1,0:T(8,128)(2,1)S(1)}, bf16[4,32,2048]{2,1,0:T(8,128)(2,1)S(1)}, u32[]{:S(2)}, u32[]{:S(2)}) collective-permute-start(bf16[4,32,2048]{2,1,0:T(8,128)(2,1)S(1)} %bitcast.262), channel_id=1, source_target_pairs={{0,4},{2,6},{4,0},{6,2},{8,12},{10,14},{12,8},{14,10},{16,20},{18,... | collective-permute-start | bytes 1572872 | tf_op jit(solution)/shard_map/ppermute | solution.py:384
  418.8 15.5 %collective-permute-start.31 = (bf16[8,32,2048]{2,1,0:T(8,128)(2,1)S(1)}, bf16[8,32,2048]{2,1,0:T(8,128)(2,1)S(1)}, u32[]{:S(2)}, u32[]{:S(2)}) collective-permute-start(bf16[8,32,2048]{2,1,0:T(8,128)(2,1)S(1)} %bitcast.241), channel_id=1, source_target_pairs={{0,2},{2,0},{4,6},{6,4},{8,10},{10,8},{12,14},{14,12},{16,18},{18,... | collective-permute-start | bytes 3145736 | tf_op jit(solution)/shard_map/ppermute | solution.py:384
  (32 other events, 176.5 us)

commit v3 on v2

--- a/solution.py
+++ b/solution.py
@@ -80,11 +80,11 @@
     return jnp.where((lanes < HEAD_DIM) == (parity == 0), pair, jnp.zeros_like(pair))
 
 
-def mask_bias(segs_col, segs_row, row_start):
-    rows, keys = segs_col.shape[0], segs_row.shape[1]
-    row_index = row_start + lax.broadcasted_iota(jnp.int32, (rows, keys), 0)
-    col_index = lax.broadcasted_iota(jnp.int32, (rows, keys), 1)
-    allowed = (segs_col == segs_row) & (row_index >= col_index)
+def mask_bias(key_segs, row_segs, row_start):
+    keys, rows = key_segs.shape[0], row_segs.shape[1]
+    key_index = lax.broadcasted_iota(jnp.int32, (keys, rows), 0)
+    row_index = row_start + lax.broadcasted_iota(jnp.int32, (keys, rows), 1)
+    allowed = (key_segs == row_segs) & (row_index >= key_index)
     return jnp.where(allowed, 0.0, NEGATIVE).astype(jnp.float32)
 
 
@@ -92,43 +92,43 @@
     return jnp.where(segs >= 0, 1.0, 0.0)
 
 
-def double_keys(key_rot, value_low, keys_two, values_two):
-    for kv_head in range(2):
-        keys_two[kv_head] = doubled(key_rot[...], kv_head)
-        values_two[kv_head] = doubled(value_low[...], kv_head)
+def turned_over(values):
+    return jnp.transpose(values.astype(jnp.float32)).astype(jnp.bfloat16)
+
+
+def one_of_pair(first, second):
+    rows = lax.broadcasted_iota(jnp.int32, first.shape, 0)
+    return jnp.where(rows < HEAD_DIM, first, second)
 
 
 def attend_rows(
-    row_start, key_count, groups, pairs, segs_col, segs_row, query_rot, keys_two, values_two,
-    bias, attended, logs, tokens, w_output, gain, middle, mid_low,
+    row_start, key_count, groups, pairs, segs_col, segs_row, query_rot, key_rot, value_low,
+    bias, keys_two, values_over, attended, logs, tokens, w_output, gain, middle, mid_low,
 ):
     rows = attended.shape[0]
+    for kv_head in range(2):
+        keys_two[kv_head] = doubled(key_rot[:key_count, :], kv_head)
+        values_over[kv_head] = turned_over(doubled(value_low[:key_count, :], kv_head))
     bias[...] = mask_bias(
-        segs_col[row_start : row_start + rows], segs_row[:, :key_count], row_start
-    )
-    logs[...] = jnp.zeros_like(logs)
+        segs_col[:key_count], segs_row[:, row_start : row_start + rows], row_start
+    )
 
     def one_pair(pair, carry):
         cols = pl.ds(pl.multiple_of(pair * LANES, LANES), LANES)
         queries = query_rot[row_start : row_start + rows, cols]
         results = []
-        log_all = logs[...]
-        lanes = lane_index(log_all.shape)
         for parity in range(2):
             head = 2 * pair + parity
             kv_head = head // groups
             query = one_head(queries, parity) * jnp.asarray(HEAD_DIM**-0.5, jnp.bfloat16)
-            scores = contract_cols(query, keys_two[kv_head, :key_count]) + bias[...]
-            row_max = jnp.max(scores, axis=-1, keepdims=True)
+            scores = contract_cols(keys_two[kv_head], query) + bias[...]
+            row_max = jnp.max(scores, axis=0, keepdims=True)
             exponent = jnp.exp(scores - row_max)
-            row_total = jnp.sum(exponent, axis=-1, keepdims=True)
+            row_total = jnp.sum(exponent, axis=0, keepdims=True)
             probs = (exponent * (1.0 / row_total)).astype(jnp.bfloat16)
-            results.append(forward_product(probs, values_two[kv_head, :key_count]))
-            log_all = jnp.where(lanes == head, row_max + jnp.log(row_total), log_all)
-        logs[...] = log_all
-        attended[:, cols] = jnp.where(
-            lane_index(results[0].shape) < HEAD_DIM, results[0], results[1]
-        ).astype(jnp.bfloat16)
+            results.append(forward_product(values_over[kv_head], probs))
+            logs[pl.ds(head, 1), :] = row_max + jnp.log(row_total)
+        attended[:, cols] = jnp.transpose(one_of_pair(*results)).astype(jnp.bfloat16)
         return carry
 
     lax.fori_loop(0, pairs, one_pair, 0)
@@ -142,7 +142,7 @@
 def early_kernel(
     groups, pairs, normed_low, w_qkv, bias_qkv, cosine, sine, segs_col, segs_row, tokens,
     w_output, gain, query_rot, key_rot, value_low, attended, logs, middle, mid_low,
-    bias, keys_two, values_two,
+    bias, keys_two, values_over,
 ):
     def project(pair):
         cols = pl.ds(pl.multiple_of(pair * LANES, LANES), LANES)
@@ -159,22 +159,20 @@
     lax.fori_loop(0, pairs, query_pair, 0)
     key_rot[...] = turned(project(pairs))
     value_low[...] = project(pairs + 1).astype(jnp.bfloat16)
-    double_keys(key_rot, value_low, keys_two, values_two)
     attend_rows(
-        0, attended.shape[0], groups, pairs, segs_col, segs_row, query_rot, keys_two, values_two,
-        bias, attended, logs, tokens, w_output, gain, middle, mid_low,
+        0, attended.shape[0], groups, pairs, segs_col, segs_row, query_rot, key_rot, value_low,
+        bias, keys_two, values_over, attended, logs, tokens, w_output, gain, middle, mid_low,
     )
 
 
 def late_kernel(
     groups, pairs, query_rot, key_rot, value_low, segs_col, segs_row, tokens,
-    w_output, gain, attended, logs, middle, mid_low, bias, keys_two, values_two,
+    w_output, gain, attended, logs, middle, mid_low, bias, keys_two, values_over,
 ):
-    double_keys(key_rot, value_low, keys_two, values_two)
     rows = attended.shape[0]
     attend_rows(
-        rows, 2 * rows, groups, pairs, segs_col, segs_row, query_rot, keys_two, values_two,
-        bias, attended, logs, tokens, w_output, gain, middle, mid_low,
+        rows, 2 * rows, groups, pairs, segs_col, segs_row, query_rot, key_rot, value_low,
+        bias, keys_two, values_over, attended, logs, tokens, w_output, gain, middle, mid_low,
     )
 
 
@@ -190,14 +188,18 @@
     )(*operands)
 
 
-def attention_shapes(length, w_output, kw):
+def attention_shapes(length, key_count, w_output, kw):
     queries, width = w_output.shape
     rows = length // 2
+    heads = -(-queries // HEAD_DIM // 8) * 8
     low, wide = jnp.bfloat16, jnp.float32
     half_out = [
-        ((rows, queries), low), ((rows, LANES), wide), ((rows, width), wide), ((rows, width), low)
+        ((rows, queries), low), ((heads, rows), wide), ((rows, width), wide), ((rows, width), low)
     ]
-    return rows, queries, queries // kw, queries // LANES, half_out, [((2, length, LANES), low)] * 2
+    scratch = [
+        ((key_count, rows), wide), ((2, key_count, LANES), low), ((2, LANES, key_count), low)
+    ]
+    return queries, queries // kw, queries // LANES, half_out, scratch
 
 
 def attention_early(
@@ -205,12 +207,14 @@
 ):
     length = tokens.shape[0]
     kw = (w_qkv.shape[1] - w_output.shape[0]) // 2
-    rows, queries, groups, pairs, half_out, scratch = attention_shapes(length, w_output, kw)
+    queries, groups, pairs, half_out, scratch = attention_shapes(
+        length, length // 2, w_output, kw
+    )
     whole = [((length, columns), jnp.bfloat16) for columns in (queries, kw, kw)]
     query_rot, key_rot, value_low, *early = call(
         functools.partial(early_kernel, groups, pairs),
         whole + half_out,
-        [((rows, rows), jnp.float32)] + scratch,
+        scratch,
         2 * 10**9,
         (normed_low, w_qkv, bias_qkv, cosine, sine, segs_col, segs_row, tokens, w_output, gain),
     )
@@ -219,13 +223,13 @@
 
 def attention_late(query_rot, key_rot, value_low, segs_col, segs_row, tokens, w_output, gain):
     length = tokens.shape[0]
-    rows, _, groups, pairs, half_out, scratch = attention_shapes(
-        length, w_output, key_rot.shape[1]
+    _, groups, pairs, half_out, scratch = attention_shapes(
+        length, length, w_output, key_rot.shape[1]
     )
     return call(
         functools.partial(late_kernel, groups, pairs),
         half_out,
-        [((rows, length), jnp.float32)] + scratch,
+        scratch,
         2 * 10**9,
         (query_rot, key_rot, value_low, segs_col, segs_row, tokens, w_output, gain),
     )
@@ -240,29 +244,48 @@
 
 
 def backward_kernel(
-    groups, pairs, mid_early, mid_late, norm_grad, cotangent, gain_mlp, w_output,
+    groups, pairs, devices, mid_early, mid_late, norm_own, norm_got, cotangent, gain_mlp, w_output,
     att_early, att_late, log_early, log_late, query_rot, key_rot, value_low, segs_col, segs_row,
     cosine, sine, normed_low, w_qkv, tokens, gain_attn,
-    grad_qkv, grad_output, bias_grad, attn_gain_grad, mlp_gain_grad, input_grad,
-    attn_grad, attended_grad, low_grads, bias, keys_two, values_two, key_grad, value_grad,
+    sums, input_grad, attn_grad, attended_grad, low_grads, bias, keys_two, keys_over, values_two, key_grad, value_grad,
+    qkv_sums, out_sums,
 ):
     rows = mid_early.shape[0]
     length = 2 * rows
     parts = ((0, mid_early, att_early, log_early), (rows, mid_late, att_late, log_late))
-    gain_sum = jnp.zeros(mlp_gain_grad.shape, jnp.float32)
+    width, columns = w_qkv.shape
+    own = width // devices
+    padded = sums.shape[0] // devices
+
+    def sum_row(row, first, value):
+        low = value.astype(jnp.bfloat16)
+        for device in range(devices):
+            at = device * padded + own + row
+            sums[at : at + 1, first : first + low.shape[1]] = low
+
+    for device in range(devices):
+        at = device * padded + own
+        sums[at : at + padded - own, :] = jnp.zeros((padded - own, sums.shape[1]), jnp.bfloat16)
+    gain_sum = jnp.zeros(gain_mlp.shape, jnp.float32)
     for start, middle, _, _ in parts:
         here = slice(start, start + rows)
-        pull, gain_part = norm_pull(middle[...], gain_mlp[...], norm_grad[here, :])
+        pull, gain_part = norm_pull(
+            middle[...],
+            gain_mlp[...],
+            norm_own[here, :] + norm_got[here, :].astype(jnp.float32),
+        )
         gain_sum = gain_sum + gain_part
         total = cotangent[here, :].astype(jnp.float32) + pull
         input_grad[here, :] = total
         attn_grad[here, :] = (is_live(segs_col[here, :]) * total).astype(jnp.bfloat16)
-        bias[here, :] = mask_bias(segs_col[here], segs_row[...], start)
-    mlp_gain_grad[...] = gain_sum
-    double_keys(key_rot, value_low, keys_two, values_two)
+        bias[: start + rows, here] = mask_bias(segs_col[: start + rows], segs_row[:, here], start)
+    sum_row(1, 0, gain_sum)
+    for kv_head in range(2):
+        keys_two[kv_head] = doubled(key_rot[...], kv_head)
+        keys_over[kv_head] = turned_over(keys_two[kv_head])
+        values_two[kv_head] = doubled(value_low[...], kv_head)
     key_grad[...] = jnp.zeros_like(key_grad)
     value_grad[...] = jnp.zeros_like(value_grad)
-    bias_grad[...] = jnp.zeros_like(bias_grad)
     for start in range(0, length, rows):
         here = slice(start, start + rows)
         attended_grad[here, :] = contract_cols(attn_grad[here, :], w_output[...]).astype(
@@ -274,7 +297,6 @@
 
     def one_pair(pair, carry):
         cols = pl.ds(pl.multiple_of(pair * LANES, LANES), LANES)
-        column_sum = jnp.zeros((1, LANES), jnp.float32)
         out_grad = jnp.zeros((LANES, attn_grad.shape[1]), jnp.float32)
         for start, _, attended, logs in parts:
             here = slice(start, start + rows)
@@ -282,35 +304,24 @@
             out_grad = out_grad + contract_rows(attended[:, cols], attn_grad[here, :])
             queries = query_rot[here, cols]
             grads = attended_grad[here, cols]
-            log_all = logs[...]
-            lanes = lane_index(log_all.shape)
             results = []
             for parity in range(2):
                 head = 2 * pair + parity
                 kv_head = head // groups
                 query = one_head(queries, parity) * jnp.asarray(HEAD_DIM**-0.5, jnp.bfloat16)
                 grad = one_head(grads, parity)
-                log_total = jnp.sum(
-                    jnp.where(lanes == head, log_all, 0.0), axis=-1, keepdims=True
-                )
-                scores = contract_cols(query, keys_two[kv_head, :keys]) + bias[here, :keys]
-                probs = jnp.exp(scores - log_total)
-                prob_grad = contract_cols(grad, values_two[kv_head, :keys])
-                inner = jnp.sum(prob_grad * probs, axis=-1, keepdims=True)
+                scores = contract_cols(keys_two[kv_head, :keys], query) + bias[:keys, here]
+                probs = jnp.exp(scores - logs[pl.ds(head, 1), :])
+                prob_grad = contract_cols(values_two[kv_head, :keys], grad)
+                inner = jnp.sum(prob_grad * probs, axis=0, keepdims=True)
                 score_grad = (probs * (prob_grad - inner)).astype(jnp.bfloat16)
-                value_grad[kv_head, :keys] += contract_rows(probs.astype(jnp.bfloat16), grad)
-                key_grad[kv_head, :keys] += contract_rows(score_grad, query)
-                results.append(
-                    forward_product(score_grad, keys_two[kv_head, :keys]) * HEAD_DIM**-0.5
-                )
-            query_grad = jnp.where(
-                lane_index(results[0].shape) < HEAD_DIM, results[0], results[1]
-            )
+                value_grad[kv_head, :keys] += forward_product(probs.astype(jnp.bfloat16), grad)
+                key_grad[kv_head, :keys] += forward_product(score_grad, query)
+                results.append(forward_product(keys_over[kv_head, :, :keys], score_grad))
+            query_grad = jnp.transpose(one_of_pair(*results)) * HEAD_DIM**-0.5
             low = turned_back(query_grad, here).astype(jnp.bfloat16)
             low_grads[here, cols] = low
-            column_sum = column_sum + jnp.sum(low.astype(jnp.float32), axis=0, keepdims=True)
-        bias_grad[:, cols] = column_sum
-        grad_output[cols, :] = out_grad.astype(jnp.bfloat16)
+        out_sums[cols, :] = out_grad.astype(jnp.bfloat16)
         return carry
 
     lax.fori_loop(0, pairs, one_pair, 0)
@@ -325,26 +336,31 @@
     for at, low in ((pairs, key_low), (pairs + 1, value_grad_low)):
         cols = slice(at * LANES, (at + 1) * LANES)
         low_grads[:, cols] = low
-        bias_grad[:, cols] = jnp.sum(low.astype(jnp.float32), axis=0, keepdims=True)
+    sum_row(0, 0, jnp.sum(low_grads[...].astype(jnp.float32), axis=0, keepdims=True))
 
     def weight_rows(block, carry):
         cols = pl.ds(pl.multiple_of(block * LANES, LANES), LANES)
-        grad_qkv[cols, :] = contract_rows(normed_low[:, cols], low_grads[...]).astype(jnp.bfloat16)
+        qkv_sums[cols, :] = contract_rows(normed_low[:, cols], low_grads[...]).astype(jnp.bfloat16)
         return carry
 
-    lax.fori_loop(0, normed_low.shape[1] // LANES, weight_rows, 0)
-    gain_sum = jnp.zeros(attn_gain_grad.shape, jnp.float32)
+    lax.fori_loop(0, width // LANES, weight_rows, 0)
+    for device in range(devices):
+        here = slice(device * padded, device * padded + own)
+        there = slice(device * own, (device + 1) * own)
+        sums[here, :columns] = qkv_sums[there, :]
+        sums[here, columns:] = out_sums[there, :]
+    gain_sum = jnp.zeros(gain_attn.shape, jnp.float32)
     for start in range(0, length, rows):
         here = slice(start, start + rows)
         norm_in = contract_cols(low_grads[here, :], w_qkv[...])
         pull, gain_part = norm_pull(tokens[here, :].astype(jnp.float32), gain_attn[...], norm_in)
         gain_sum = gain_sum + gain_part
         input_grad[here, :] += pull
-    attn_gain_grad[...] = gain_sum
+    sum_row(0, columns, gain_sum)
 
 
 def attention_backward(
-    early, late, norm_grad, cotangent, gain_mlp, w_output, query_rot, key_rot, value_low,
+    devices, padded, early, late, norm_own, norm_got, cotangent, gain_mlp, w_output, query_rot, key_rot, value_low,
     segs_col, segs_row, cosine, sine, normed_low, w_qkv, tokens, gain_attn,
 ):
     length, width = tokens.shape
@@ -353,27 +369,23 @@
     kw = (columns - queries) // 2
     low, wide = jnp.bfloat16, jnp.float32
     return call(
-        functools.partial(backward_kernel, queries // kw, queries // LANES),
-        [
-            ((width, columns), low),
-            ((queries, width), low),
-            ((1, columns), wide),
-            ((1, width), wide),
-            ((1, width), wide),
-            ((length, width), wide),
-        ],
+        functools.partial(backward_kernel, queries // kw, queries // LANES, devices),
+        [((devices * padded, columns + width), low), ((length, width), wide)],
         [
             ((length, width), low),
             ((length, queries), low),
             ((length, columns), low),
             ((length, length), wide),
             ((2, length, LANES), low),
+            ((2, LANES, length), low),
             ((2, length, LANES), low),
             ((2, length, LANES), wide),
             ((2, length, LANES), wide),
+            ((width, columns), low),
+            ((queries, width), low),
         ],
         10**9,
-        (early[2], late[2], norm_grad, cotangent, gain_mlp, w_output, early[0], late[0],
+        (early[2], late[2], norm_own, norm_got, cotangent, gain_mlp, w_output, early[0], late[0],
          early[1], late[1], query_rot, key_rot, value_low, segs_col, segs_row, cosine, sine,
          normed_low, w_qkv, tokens, gain_attn),
     )
@@ -456,27 +468,41 @@
     )
 
 
-def norm_part_kernel(gate_grad, up_grad, w_gate, w_up, out):
-    out[...] = (
-        contract_cols(gate_grad[...], w_gate[...]) + contract_cols(up_grad[...], w_up[...])
-    ).astype(out.dtype)
-
-
-def out_part_kernel(activ, w_down, out):
-    out[...] = forward_product(activ[...], w_down[...]).astype(out.dtype)
-
-
-def token_product(kernel, activs, weights, width, start, count, kind):
+def norm_part_kernel(gate_grad, up_grad, w_gate, w_up, first, second):
+    value = contract_cols(gate_grad[...], w_gate[...]) + contract_cols(up_grad[...], w_up[...])
+    two_parts(value, first, second)
+
+
+def out_part_kernel(activ, w_down, first, second):
+    two_parts(forward_product(activ[...], w_down[...]), first, second)
+
+
+def two_parts(value, first, second):
+    at, half = pl.program_id(0), pl.num_programs(0) // 2
+
+    @pl.when(at < half)
+    def _():
+        first[...] = value.astype(first.dtype)
+
+    @pl.when(at >= half)
+    def _():
+        second[...] = value.astype(second.dtype)
+
+
+def token_product(kernel, activs, weights, width, kinds):
     rows = 256
-    out = jax.ShapeDtypeStruct((count, width), kind)
+    total, hidden = activs[0].shape
+    half = total // rows // 2
     return grid_call(
         kernel,
-        count // rows,
+        2 * half,
         list(activs) + list(weights),
-        [row_block(activ, rows, start // rows) for activ in activs]
-        + [whole_block(weight) for weight in weights],
-        out,
-        row_block(out, rows),
+        [row_block(activ, rows) for activ in activs] + [whole_block(weight) for weight in weights],
+        [jax.ShapeDtypeStruct((total // 2, width), kind) for kind in kinds],
+        [
+            pl.BlockSpec((rows, width), lambda at: (jnp.minimum(at, half - 1), 0)),
+            pl.BlockSpec((rows, width), lambda at: (jnp.maximum(at - half, 0), 0)),
+        ],
         10**9,
     )
 
@@ -690,12 +716,9 @@
 
     back_weights, out_weights = (part_gate, part_up), (w_down,)
     back = (gate_grad, up_grad)
-    everyone = group_size * length
-    if group.pair:
-        norm_other = token_product(
-            norm_part_kernel, back, back_weights, width, length, length, jnp.bfloat16
-        )
-        norm_other, activ_low, back = together(norm_other, activ_low, back)
+    kinds = (jnp.float32, jnp.bfloat16) if group.pair else (jnp.float32, jnp.float32)
+    norm_own, norm_other = token_product(norm_part_kernel, back, back_weights, width, kinds)
+    norm_own, norm_other, activ_low, back = together(norm_own, norm_other, activ_low, back)
     grad_down = contract_rows(activ_low, mlp_grad_all).astype(jnp.bfloat16)
     grad_down, back = together(grad_down, back)
     gate_grad, up_grad = back
@@ -717,84 +740,46 @@
         pair_parts.append(summed.transpose(1, 0, 2, 3))
     first, second = pair_parts
     down = replicas.first(down, far)
+    out_own, out_other = token_product(
+        out_part_kernel, (activ_low,), out_weights, width, kinds
+    )
     if group.pair:
-        norm_grad = token_product(
-            norm_part_kernel, back, back_weights, width, 0, length, jnp.float32
-        )
-        norm_grad = norm_grad + group.swap(norm_other).astype(jnp.float32)
-        out_other = token_product(
-            out_part_kernel, (activ_low,), out_weights, width, length, length, jnp.bfloat16
-        )
+        norm_got = group.swap(norm_other)
     else:
-        norm_grad = group.own_tokens(
-            token_product(norm_part_kernel, back, back_weights, width, 0, everyone, jnp.float32)
-        )
-        out_other = token_product(
-            out_part_kernel, (activ_low,), out_weights, width, 0, everyone, jnp.float32
-        )
-    norm_grad, down, first, second, out_other, activ_low = together(
-        norm_grad, down, first, second, out_other, activ_low
-    )
-    grad_qkv, grad_output, bias_grad, gain_attn_grad, gain_mlp_grad, input_grad = (
-        attention_backward(
-            early, late, norm_grad, cotangent, gain_mlp_row, full_output, query_rot, key_rot,
-            value_low, segs_col, segs_row, cosine, sine, normed_low, full_qkv, tokens,
-            gain_attn_row,
-        )
+        norm_own = group.own_tokens(jnp.concatenate([norm_own, norm_other]))
+        norm_got = jnp.zeros((length, width), jnp.bfloat16)
+    norm_own, norm_got, out_own, out_other, down, first, second = together(
+        norm_own, norm_got, out_own, out_other, down, first, second
+    )
+    columns = full_qkv.shape[1] + width
+    unit = 16 * eighth
+    padded = -(-(rows_own + 16) // unit) * unit
+    attn, input_grad = attention_backward(
+        group_size, padded, early, late, norm_own, norm_got, cotangent, gain_mlp_row, full_output,
+        query_rot, key_rot, value_low, segs_col, segs_row, cosine, sine, normed_low, full_qkv,
+        tokens, gain_attn_row,
     )
     down = replicas.first(down, far[1:])
     first = replicas.first(first, near_first)
     second = replicas.first(second, far)
     if group.pair:
-        out_sum = token_product(
-            out_part_kernel, (activ_low,), out_weights, width, 0, length, jnp.float32
-        )
-        out_sum = out_sum + group.swap(out_other).astype(jnp.float32)
+        out_sum = out_own + group.swap(out_other).astype(jnp.float32)
     else:
-        out_sum = group.own_tokens(out_other)
-    grad_qkv, grad_output, bias_grad, gain_attn_grad, gain_mlp_grad, down, first, second = together(
-        grad_qkv, grad_output, bias_grad, gain_attn_grad, gain_mlp_grad, down, first, second
-    )
+        out_sum = group.own_tokens(jnp.concatenate([out_own, out_other]))
+    attn, down, first, second = together(attn, down, first, second)
     output = (middle + live * out_sum).astype(jnp.bfloat16)
-
-    small = jnp.concatenate(
-        [
-            part.reshape(group_size, -1)
-            for part in (
-                bias_grad[0, :qw],
-                bias_grad[0, qw : qw + kw],
-                bias_grad[0, qw + kw :],
-                gain_attn_grad,
-                gain_mlp_grad,
-            )
-        ],
-        axis=1,
-    ).astype(jnp.bfloat16)
-    columns = grad_qkv.shape[1] + qw
-    unit = 16 * eighth
-    extra = -(-(rows_own + 16) // unit) * unit - rows_own
-    small = jnp.pad(small, ((0, 0), (0, extra * columns - small.shape[1])))
-    attn_all = jnp.concatenate(
-        [
-            jnp.concatenate([grad_qkv, grad_output], axis=1)
-            .astype(jnp.bfloat16)
-            .reshape(group_size, rows_own, columns),
-            small.reshape(group_size, extra, columns),
-        ],
-        axis=1,
-    )
     attn = replicas.scatter(
-        attn_all.reshape(group_size, 2, (rows_own + extra) // 2, columns).transpose(1, 0, 2, 3), 0
-    )
+        attn.reshape(group_size, 2, padded // 2, columns).transpose(1, 0, 2, 3), 0
+    )
+    attn = group.sum_parts(attn).reshape(eighth, -1, columns)
+    attn = replicas.scatter_all(attn, near_first)
     down = replicas.scatter_all(down, far[2:])
     first = group.exchange_parts(replicas.scatter_all(first, near_first[1:]))
     second = group.exchange_parts(replicas.scatter_all(second, far[1:]))
-    attn = group.sum_parts(attn).reshape(eighth, -1, columns)
-    attn = replicas.scatter_all(attn, far)
     down = replicas.gather(replicas.gather_all(down, far), 0)
     first = replicas.gather_all(first, near_first)
     second = replicas.gather_all(second, far)
-    attn = replicas.gather_all(attn, far)
+    attn = replicas.gather_all(attn, near_first)
     shard_down = down.reshape(-1, width).astype(jnp.float32)
     gate_parts = [[] for _ in range(group_size)]
     up_parts = [[] for _ in range(group_size)]
@@ -810,13 +795,22 @@
         jnp.concatenate(sum(parts, []), axis=1).astype(jnp.float32)
         for parts in (gate_parts, up_parts)
     )
-    attn_sum = replicas.gather(attn, 0).reshape(rows_own + extra, columns).astype(jnp.float32)
+    attn_sum = replicas.gather(attn, 0).reshape(padded, columns).astype(jnp.float32)
     shard_query = attn_sum[:rows_own, :qw]
     shard_key = attn_sum[:rows_own, qw : qw + kw]
     shard_value = attn_sum[:rows_own, qw + kw : qw + 2 * kw]
     shard_output = attn_sum[:rows_own, qw + 2 * kw :]
-    vector_sum = attn_sum[rows_own:].reshape(-1)
-    shard_vectors = tuple(vector_sum[low:high] for low, high in zip(cuts[:-1], cuts[1:]))
+    bias_sum = attn_sum[rows_own, : columns - width]
+    shard_vectors = tuple(
+        chosen(vector.reshape(group_size, -1), group.at)
+        for vector in (
+            bias_sum[:qw],
+            bias_sum[qw : qw + kw],
+            bias_sum[qw + kw :],
+            attn_sum[rows_own, columns - width :],
+            attn_sum[rows_own + 1, :width],
+        )
+    )
     return (
         output,
         input_grad,

time: 445 us -> 435 us (0.978)
  waiting for transfers between devices: 102 us -> 130 us
  starting transfers between devices: 96.3 us -> 79.1 us
  other arithmetic: 70.3 us -> 59.5 us
  Pallas kernels: 126 us -> 118 us
    ppermute x51, waiting for transfers between devices: 102 us -> 130 us  [swapped(): return lax.ppermute(value, axis, [(at, at ^ step) for at in range(size)])]
    ppermute x51, starting transfers between devices: 96.3 us -> 79.1 us  [swapped(): return lax.ppermute(value, axis, [(at, at ^ step) for at in range(size)])]
    pallas_call x6 -> x4, Pallas kernels: 67.4 us -> 59.4 us  [grid_call(): pl.pallas_call(kernel, grid=(grid,), out_shape=out_shape, in_specs=in_spe...]
  transfers between devices with their start and end apart: 51 -> 51, of which waited for: 16 -> 19; matrix products, arithmetic and copies ran while one was open for 20% -> 18% of each run, Pallas kernels for 23% -> 20%
where the time goes in v3:
time: 435 us; the launch traced here: 430 us
  waiting for transfers between devices  130 us (30%)
  Pallas kernels  118 us (27%)
  starting transfers between devices  79.1 us (18%)
  other arithmetic  59.5 us (14%)
  local copies, waits for them, and re-layouts  24.2 us (6%)
  matrix products  18 us (4%)
    ppermute x51, waiting for transfers between devices, swapped(): return lax.ppermute(value, axis, [(at, at ^ step) for at in range(size)])  130 us
    ppermute x51, starting transfers between devices, swapped(): return lax.ppermute(value, axis, [(at, at ^ step) for at in range(size)])  79.1 us
    pallas_call x4, Pallas kernels, grid_call(): pl.pallas_call(kernel, grid=(grid,), out_shape=out_shape, in_specs=in_spe...  59.4 us
    pallas_call x3, Pallas kernels, call(): pl.pallas_call(kernel, out_shape=[jax.ShapeDtypeStruct(shape, kind) for s...  58.4 us
    dot_general x3, matrix products, contract_rows(): lax.dot_general(left, right, (((0,), (0,)), ((), ())), preferred_element_...  18 us
    select_n x31, other arithmetic, ordered(): return jnp.where(bit == 0, jnp.stack([own, other]), jnp.stack([other, own]))  16.6 us
    convert_element_type x17, other arithmetic, added(): (left.astype(jnp.float32) + right.astype(jnp.float32)).astype(jnp.bfloat16)  14.8 us
  transfers between devices with their start and end apart: 51, of which 19 were waited for; matrix products, arithmetic and copies ran while one was open for 18% of the time, Pallas kernels for 20%

profile of v3, /device:TPU:1, one launch (start us, length us, event | category | flops | bytes accessed | tf_op | source)
XLA Modules:
  0.0 430.4 jit_solution(3137963621971047624)
XLA Ops:
  4.8 2.0 collective-permute-start.1
  7.7 1.4 collective-permute-start
  12.1 1.4 multiply_convert_fusion.mlp_grad
  15.4 11.8 %collective-permute-done = bf16[1472]{0:T(1024)(128)(2,1)S(1)} collective-permute-done((bf16[1472]{0:T(1024)(128)(2,1)S(1)}, bf16[1472]{0:T(1024)(128)(2,1)S(1)}, u32[]{:S(2)}, u32[]{:S(2)}) %collective-permute-start) | collective-permute-done | bytes 2976 | tf_op jit(solution)/shard_map/ppermute | solution.py:396
  31.5 1.4 dynamic_slice.138
  32.9 1.5 collective-permute-start.5
  37.2 1.4 maximum_select_fusion.10
  38.6 1.5 maximum_select_fusion.16
  40.1 1.7 maximum_select_fusion.8
  41.7 16.3 %shard_map.254 = (bf16[512,896]{1,0:T(8,128)(2,1)}, bf16[512,128]{1,0:T(8,128)(2,1)}, bf16[512,128]{1,0:T(8,128)(2,1)}, bf16[256,896]{1,0:T(8,128)(2,1)}, f32[16...) custom-call(bf16[512,896]{1,0:T(8,128)(2,1)} %fusion.8.normed_low, bf16[896,1152]{1,0:T(8,128)(2,1)} %bitcast.205, ...), custom_call_target="tpu_custom_call" | custom-call | flops 2000000000 | bytes 6666666 | tf_op jit(solution)/shard_map/pallas_call | solution.py:180
  58.1 1.4 collective-permute-start.8
  61.0 12.9 %shard_map.255 = (bf16[256,896]{1,0:T(8,128)(2,1)}, f32[16,256]{1,0:T(8,128)}, f32[256,896]{1,0:T(8,128)}, bf16[256,896]{1,0:T(8,128)(2,1)}) custom-call(bf16[512,896]{1,0:T(8,128)(2,1)} %get-tuple-element.95.query_rot, bf16[512,128]{1,0:T(8,128)(2,1)} %get-tuple-element.96.key_rot, bf16[512,128]{1,0:T(8,128)(2,1)} %get-tuple-element.97.value_low, ...), custom_call_target="tpu_custom_call" | custom-call | flops 2000000000 | bytes 6666666 | tf_op jit(solution)/shard_map/pallas_call | solution.py:180
  74.1 8.2 %collective-permute-done.7 = bf16[112,2432]{1,0:T(8,128)(2,1)S(1)} collective-permute-done((bf16[112,2432]{1,0:T(8,128)(2,1)S(1)}, bf16[112,2432]{1,0:T(8,128)(2,1)S(1)}, u32[]{:S(2)}, u32[]{:S(2)}) %collective-permute-start.7) | collective-permute-done | bytes 544800 | tf_op jit(solution)/shard_map/ppermute | solution.py:396
  82.6 2.3 collective-permute-start.11
  85.2 1.8 dynamic-slice_bitcast_fusion.2
  87.0 1.5 collective-permute-start.13
  91.0 5.0 %maximum_select_fusion = (bf16[2,448,2432]{2,1,0:T(8,128)(2,1)}, bf16[2,448,2432]{2,1,0:T(8,128)(2,1)}) fusion(bf16[1,448,2432]{2,1,0:T(8,128)(2,1)S(1)} %bitcast.200, bf16[1,448,2432]{2,1,0:T(8,128)(2,1)S(1)} %dynamic-slice_bitcast_fusion.2, pred[]{:T(512)S(6)} %eq.10, bf16[1,448,2432]{2,1,0:T(8,128)(2,1)S(1)} %dynamic-slice_bitcast_fusion.1, ...), kind=kLoop, calls=%fused_computation.4 | loop fusion | flops 13074432 | bytes 17432576 | tf_op jit(solution)/shard_map/jit(_where)/select_n | solution.py:408
  96.0 15.8 %shard_map.256 = (bf16[1024,2432]{1,0:T(8,128)(2,1)}, bf16[1024,2432]{1,0:T(8,128)(2,1)}, bf16[1024,2432]{1,0:T(8,128)(2,1)}) custom-call(bf16[512,896]{1,0:T(8,128)(2,1)} %pad_maximum_fusion.mid_low, bf16[512,896]{1,0:T(8,128)(2,1)} %copy-done.8, bf16[896,2432]{1,0:T(8,128)(2,1)} %bitcast.183, bf16[896,2432]{1,0:T(8,128)(2,1)} %bitcast.186, ...), custom_call_target="tpu_custom_call" | custom-call | flops 1000000000 | bytes 1000000 | tf_op jit(solution)/shard_map/pallas_call | solution.py:440
  111.9 6.6 %collective-permute-done.12 = bf16[256,896]{1,0:T(8,128)(2,1)S(1)} collective-permute-done((bf16[256,896]{1,0:T(8,128)(2,1)S(1)}, bf16[256,896]{1,0:T(8,128)(2,1)S(1)}, u32[]{:S(2)}, u32[]{:S(2)}) %collective-permute-start.12) | collective-permute-done | bytes 458784 | tf_op jit(solution)/shard_map/ppermute | solution.py:396
  119.4 16.0 %shard_map.257 = (bf16[1024,2432]{1,0:T(8,128)(2,1)}, bf16[1024,2432]{1,0:T(8,128)(2,1)}, bf16[1024,2432]{1,0:T(8,128)(2,1)}) custom-call(bf16[512,896]{1,0:T(8,128)(2,1)} %pad_maximum_fusion.1.mid_low, bf16[512,896]{1,0:T(8,128)(2,1)} %copy-done.17, bf16[896,2432]{1,0:T(8,128)(2,1)} %bitcast.184, ...), custom_call_target="tpu_custom_call", output_to_operand_aliasing={{0}: (5, {}), {1}: (6, {}), {2}: (7, {})} | custom-call | flops 1000000000 | bytes 1000000 | tf_op jit(solution)/shard_map/pallas_call | solution.py:440
  135.5 17.4 %shard_map.258 = (f32[512,896]{1,0:T(8,128)}, bf16[512,896]{1,0:T(8,128)(2,1)}) custom-call(bf16[1024,2432]{1,0:T(8,128)(2,1)} %get-tuple-element.130.gate_grad, bf16[1024,2432]{1,0:T(8,128)(2,1)} %get-tuple-element.131.up_grad, bf16[896,2432]{1,0:T(8,128)(2,1)} %bitcast.185, bf16[896,2432]{1,0:T(8,128)(2,1)} %bitcast.188), custom_call_target="tpu_custom_call" | custom-call | flops 1000000000 | bytes 1000000 | tf_op jit(solution)/shard_map/pallas_call | solution.py:440
  152.9 7.3 %convolution_convert_fusion.2 = bf16[2432,896]{1,0:T(8,128)(2,1)S(1)} fusion(bf16[1024,2432]{1,0:T(8,128)(2,1)S(1)} %copy-done, bf16[512,896]{1,0:T(8,128)(2,1)} %copy-done.17, bf16[512,896]{1,0:T(8,128)(2,1)S(1)} %copy-done.9), kind=kOutput, calls=%fused_computation.2 | convolution fusion | flops 4468588544 | bytes 11173888 | tf_op jit(solution)/shard_map/dot_general | solution.py:43
  162.6 5.3 %convolution_convert_fusion = bf16[896,2432]{1,0:T(8,128)(2,1)S(1)} fusion(bf16[1024,896]{1,0:T(8,128)(2,1)S(1)} %constant_dynamic-update-slice_fusion.3, bf16[1024,2432]{1,0:T(8,128)(2,1)S(1)} %copy-done.1), kind=kOutput, calls=%fused_computation | convolution fusion | flops 4464918528 | bytes 11173888 | tf_op jit(solution)/shard_map/dot_general | solution.py:43
  167.9 5.5 %convolution_convert_fusion.1 = bf16[896,2432]{1,0:T(8,128)(2,1)S(1)} fusion(bf16[1024,896]{1,0:T(8,128)(2,1)S(1)} %constant_dynamic-update-slice_fusion.3, bf16[1024,2432]{1,0:T(8,128)(2,1)S(1)} %bitcast.190), kind=kOutput, calls=%fused_computation.1 | convolution fusion | flops 4464918528 | bytes 11173888 | tf_op jit(solution)/shard_map/dot_general | solution.py:43
  174.0 2.0 broadcast_select_fusion.5
  177.2 1.6 broadcast_select_fusion.2
  179.0 1.5 collective-permute-start.16
  181.7 10.1 %shard_map.259 = (f32[512,896]{1,0:T(8,128)}, bf16[512,896]{1,0:T(8,128)(2,1)}) custom-call(bf16[1024,2432]{1,0:T(8,128)(2,1)} %get-tuple-element.133.activ, bf16[2432,896]{1,0:T(8,128)(2,1)} %w_down.5), custom_call_target="tpu_custom_call" | custom-call | flops 1000000000 | bytes 1000000 | tf_op jit(solution)/shard_map/pallas_call | solution.py:440
  191.8 12.5 %collective-permute-done.16 = bf16[4,152,896]{2,1,0:T(8,128)(2,1)} collective-permute-done((bf16[4,152,896]{2,1,0:T(8,128)(2,1)S(1)}, bf16[4,152,896]{2,1,0:T(8,128)(2,1)}, u32[]{:S(2)}, u32[]{:S(2)}) %collective-permute-start.16) | collective-permute-done | bytes 1089568 | tf_op jit(solution)/shard_map/ppermute | solution.py:396
  204.4 1.6 fusion.3
  206.1 3.0 add_convert_fusion.1
  209.1 3.2 add_convert_fusion
  213.2 1.5 collective-permute-start.20
  219.2 29.2 %shard_map.260 = (bf16[1024,2048]{1,0:T(8,128)(2,1)}, f32[512,896]{1,0:T(8,128)}) custom-call(f32[256,896]{1,0:T(8,128)} %get-tuple-element.94.mid_early, f32[256,896]{1,0:T(8,128)} %get-tuple-element.105.mid_late, f32[512,896]{1,0:T(8,128)} %get-tuple-element.141.norm_own, bf16[512,896]{1,0:T(8,128)(2,1)} %collective-permute-done.14.norm_got, ...), custom_call_target="tpu_custom_call" | custom-call | flops 1000000000 | bytes 3333333 | tf_op jit(solution)/shard_map/pallas_call | solution.py:180
  249.7 2.6 fusion.9
  252.3 1.5 fusion.5
  253.8 1.7 fusion.2
  255.6 2.4 collective-permute-start.46
  259.9 3.3 collective-permute-start.23
  263.1 6.6 %collective-permute-done.46 = bf16[1,152,896]{2,1,0:T(8,128)(2,1)S(1)} collective-permute-done((bf16[1,152,896]{2,1,0:T(8,128)(2,1)S(1)}, bf16[1,152,896]{2,1,0:T(8,128)(2,1)S(1)}, u32[]{:S(2)}, u32[]{:S(2)}) %collective-permute-start.46) | collective-permute-done | bytes 272416 | tf_op jit(solution)/shard_map/ppermute | solution.py:396
  269.9 5.8 %collective-permute-done.39 = bf16[2,2,56,1152]{3,2,0,1:T(8,128)(2,1)S(1)} collective-permute-done((bf16[2,2,56,1152]{3,2,0,1:T(8,128)(2,1)S(1)}, bf16[2,2,56,1152]{3,2,0,1:T(8,128)(2,1)S(1)}, u32[]{:S(2)}, u32[]{:S(2)}) %collective-permute-start.39) | collective-permute-done | bytes 516128 | tf_op jit(solution)/shard_map/ppermute | solution.py:396
  275.9 3.0 collective-permute-done.47
  279.1 12.2 %collective-permute-start.48 = (bf16[2,152,896]{2,1,0:T(8,128)(2,1)S(1)}, bf16[2,152,896]{2,1,0:T(8,128)(2,1)S(1)}, u32[]{:S(2)}, u32[]{:S(2)}) collective-permute-start(bf16[2,152,896]{2,1,0:T(8,128)(2,1)S(1)} %maximum_select_fusion.22), channel_id=1, source_target_pairs={{0,8},{2,10},{4,12},{6,14},{8,0},{10,2},{12,4},{14,6},{16,24},{18,... | collective-permute-start | bytes 1634312 | tf_op jit(solution)/shard_map/ppermute | solution.py:396
  291.7 3.2 collective-permute-start.33
  295.3 12.0 %collective-permute-done.33 = bf16[1,2,56,1280]{3,2,0,1:T(8,128)(2,1)S(1)} collective-permute-done((bf16[1,2,56,1280]{3,2,0,1:T(8,128)(2,1)S(1)}, bf16[1,2,56,1280]{3,2,0,1:T(8,128)(2,1)S(1)}, u32[]{:S(2)}, u32[]{:S(2)}) %collective-permute-start.33) | collective-permute-done | bytes 286752 | tf_op jit(solution)/shard_map/ppermute | solution.py:396
  307.8 3.2 collective-permute-start.42
  311.8 2.9 collective-permute-start.35
  317.1 11.1 %collective-permute-done.42 = bf16[1,2,56,1152]{3,2,1,0:T(8,128)(2,1)S(1)} collective-permute-done((bf16[1,2,56,1152]{3,2,1,0:T(8,128)(2,1)S(1)}, bf16[1,2,56,1152]{3,2,1,0:T(8,128)(2,1)S(1)}, u32[]{:S(2)}, u32[]{:S(2)}) %collective-permute-start.42) | collective-permute-done | bytes 258080 | tf_op jit(solution)/shard_map/ppermute | solution.py:396
  328.3 1.7 collective-permute-start.43
  330.2 6.0 %collective-permute-done.24 = bf16[256,2048]{1,0:T(8,128)(2,1)S(1)} collective-permute-done((bf16[256,2048]{1,0:T(8,128)(2,1)S(1)}, bf16[256,2048]{1,0:T(8,128)(2,1)S(1)}, u32[]{:S(2)}, u32[]{:S(2)}) %collective-permute-start.24) | collective-permute-done | bytes 1048608 | tf_op jit(solution)/shard_map/ppermute | solution.py:396
  336.6 2.3 collective-permute-start.25
  339.5 8.1 %collective-permute-done.43 = bf16[2,2,56,1152]{3,2,0,1:T(8,128)(2,1)S(1)} collective-permute-done((bf16[2,2,56,1152]{3,2,0,1:T(8,128)(2,1)S(1)}, bf16[2,2,56,1152]{3,2,0,1:T(8,128)(2,1)S(1)}, u32[]{:S(2)}, u32[]{:S(2)}) %collective-permute-start.43) | collective-permute-done | bytes 516128 | tf_op jit(solution)/shard_map/ppermute | solution.py:396
  348.2 10.6 %collective-permute-done.25 = bf16[4,32,2048]{2,1,0:T(8,128)(2,1)S(1)} collective-permute-done((bf16[4,32,2048]{2,1,0:T(8,128)(2,1)S(1)}, bf16[4,32,2048]{2,1,0:T(8,128)(2,1)S(1)}, u32[]{:S(2)}, u32[]{:S(2)}) %collective-permute-start.25) | collective-permute-done | bytes 524320 | tf_op jit(solution)/shard_map/ppermute | solution.py:396
  360.9 18.0 %collective-permute-done.26 = bf16[2,32,2048]{2,1,0:T(8,128)(2,1)S(1)} collective-permute-done((bf16[2,32,2048]{2,1,0:T(8,128)(2,1)S(1)}, bf16[2,32,2048]{2,1,0:T(8,128)(2,1)S(1)}, u32[]{:S(2)}, u32[]{:S(2)}) %collective-permute-start.26) | collective-permute-done | bytes 262176 | tf_op jit(solution)/shard_map/ppermute | solution.py:396
  379.5 5.8 %collective-permute-start.45 = (bf16[8,2,56,1152]{3,2,0,1:T(8,128)(2,1)S(1)}, bf16[8,2,56,1152]{3,2,0,1:T(8,128)(2,1)S(1)}, u32[]{:S(2)}, u32[]{:S(2)}) collective-permute-start(bf16[8,2,56,1152]{3,2,0,1:T(8,128)(2,1)S(1)} %bitcast.209), channel_id=1, source_target_pairs={{0,2},{2,0},{4,6},{6,4},{8,10},{10,8},{12,14},{14,12},{16,18},{18,... | collective-permute-start | bytes 6193160 | tf_op jit(solution)/shard_map/ppermute | solution.py:396
  386.6 3.2 collective-permute-start.28
  390.2 1.9 collective-permute-start.38
  394.5 4.4 %bitcast_convert_fusion = f32[2432,896]{1,0:T(8,128)} fusion(bf16[2,8,152,896]{3,2,1,0:T(8,128)(2,1)S(1)} %maximum_select_fusion.2), kind=kLoop, calls=%fused_computation.9 | loop fusion | flops 2179072 | bytes 13074432 | tf_op jit(solution)/shard_map/convert_element_type | solution.py:783
  399.0 2.6 collective-permute-start.30
  402.3 6.8 %collective-permute-done.30 = bf16[4,32,2048]{2,1,0:T(8,128)(2,1)S(1)} collective-permute-done((bf16[4,32,2048]{2,1,0:T(8,128)(2,1)S(1)}, bf16[4,32,2048]{2,1,0:T(8,128)(2,1)S(1)}, u32[]{:S(2)}, u32[]{:S(2)}) %collective-permute-start.30) | collective-permute-done | bytes 524320 | tf_op jit(solution)/shard_map/ppermute | solution.py:396
  409.2 5.7 %collective-permute-start.31 = (bf16[8,32,2048]{2,1,0:T(8,128)(2,1)S(1)}, bf16[8,32,2048]{2,1,0:T(8,128)(2,1)S(1)}, u32[]{:S(2)}, u32[]{:S(2)}) collective-permute-start(bf16[8,32,2048]{2,1,0:T(8,128)(2,1)S(1)} %bitcast.233), channel_id=1, source_target_pairs={{0,2},{2,0},{4,6},{6,4},{8,10},{10,8},{12,14},{14,12},{16,18},{18,... | collective-permute-start | bytes 3145736 | tf_op jit(solution)/shard_map/ppermute | solution.py:396
  415.5 3.8 maximum_convert_fusion.1
  419.4 3.8 maximum_convert_fusion
  424.2 1.9 fusion.24
  (261 shorter events, 56.7 us)
Async XLA Ops:
  0.7 8.5 %copy-start.4 = (bf16[512,896]{1,0:T(8,128)(2,1)S(1)}, bf16[512,896]{1,0:T(8,128)(2,1)}, u32[]{:S(2)}) copy-start(bf16[512,896]{1,0:T(8,128)(2,1)} %tokens.5) | copy-start | bytes 2752516
  0.7 8.7 %copy-start.20 = (s32[512]{0:T(512)S(1)}, s32[512]{0:T(512)}, u32[]{:S(2)}) copy-start(s32[512]{0:T(512)} %param.16) | copy-start | bytes 6148
  4.8 22.6 %collective-permute-start.1 = (bf16[224,1152]{1,0:T(8,128)(2,1)}, bf16[224,1152]{1,0:T(8,128)(2,1)}, u32[]{:S(2)}, u32[]{:S(2)}) collective-permute-start(bf16[224,1152]{1,0:T(8,128)(2,1)} %constant_dynamic-slice_fusion.12), channel_id=1, source_target_pairs={{0,1},{1,0},{2,3},{3,2},{4,5},{5,4},{6,7},{7,6},{8,9},{9,8},{10,11... | collective-permute-start | bytes 1548296 | tf_op jit(solution)/shard_map/ppermute | solution.py:396
  7.6 19.8 %collective-permute-start.2 = (bf16[224,896]{1,0:T(8,128)(2,1)}, bf16[224,896]{1,0:T(8,128)(2,1)}, u32[]{:S(2)}, u32[]{:S(2)}) collective-permute-start(bf16[224,896]{1,0:T(8,128)(2,1)} %constant_dynamic-slice_fusion.11), channel_id=1, source_target_pairs={{0,1},{1,0},{2,3},{3,2},{4,5},{5,4},{6,7},{7,6},{8,9},{9,8},{10,11... | collective-permute-start | bytes 1204232 | tf_op jit(solution)/shard_map/ppermute | solution.py:396
  7.7 19.6 %collective-permute-start = (bf16[1472]{0:T(1024)(128)(2,1)S(1)}, bf16[1472]{0:T(1024)(128)(2,1)S(1)}, u32[]{:S(2)}, u32[]{:S(2)}) collective-permute-start(bf16[1472]{0:T(1024)(128)(2,1)S(1)} %concatenate.196), channel_id=1, source_target_pairs={{0,1},{1,0},{2,3},{3,2},{4,5},{5,4},{6,7},{7,6},{8,9},{9,8},{10,11... | collective-permute-start | bytes 8840 | tf_op jit(solution)/shard_map/ppermute | solution.py:396
  13.5 73.5 %copy-start.8 = (bf16[512,896]{1,0:T(8,128)(2,1)}, bf16[512,896]{1,0:T(8,128)(2,1)S(1)}, u32[]{:S(2)}) copy-start(bf16[512,896]{1,0:T(8,128)(2,1)S(1)} %multiply_convert_fusion.mlp_grad) | copy-start | bytes 2752516
  27.4 8.5 %collective-permute-start.4 = (bf16[224,896]{1,0:T(8,128)(2,1)}, bf16[224,896]{1,0:T(8,128)(2,1)S(1)}, u32[]{:S(2)}, u32[]{:S(2)}) collective-permute-start(bf16[224,896]{1,0:T(8,128)(2,1)} %collective-permute-done.2), channel_id=1, source_target_pairs={{0,2},{2,0},{4,6},{6,4},{8,10},{10,8},{12,14},{14,12},{16,18},{18,... | collective-permute-start | bytes 1204232 | tf_op jit(solution)/shard_map/ppermute | solution.py:396
  30.3 8.3 %collective-permute-start.3 = (bf16[224,1152]{1,0:T(8,128)(2,1)}, bf16[224,1152]{1,0:T(8,128)(2,1)S(1)}, u32[]{:S(2)}, u32[]{:S(2)}) collective-permute-start(bf16[224,1152]{1,0:T(8,128)(2,1)} %collective-permute-done.1), channel_id=1, source_target_pairs={{0,2},{2,0},{4,6},{6,4},{8,10},{10,8},{12,14},{14,12},{16,18},{18,... | collective-permute-start | bytes 1548296 | tf_op jit(solution)/shard_map/ppermute | solution.py:396
  32.9 25.1 %collective-permute-start.5 = (bf16[112,2432]{1,0:T(8,128)(2,1)S(1)}, bf16[112,2432]{1,0:T(8,128)(2,1)S(1)}, u32[]{:S(2)}, u32[]{:S(2)}) collective-permute-start(bf16[112,2432]{1,0:T(8,128)(2,1)S(1)} %dynamic_slice.138), channel_id=1, source_target_pairs={{0,1},{1,0},{2,3},{3,2},{4,5},{5,4},{6,7},{7,6},{8,9},{9,8},{10,11... | collective-permute-start | bytes 1634312 | tf_op jit(solution)/shard_map/ppermute | solution.py:396
  35.8 22.3 %collective-permute-start.6 = (bf16[112,2432]{1,0:T(8,128)(2,1)S(1)}, bf16[112,2432]{1,0:T(8,128)(2,1)S(1)}, u32[]{:S(2)}, u32[]{:S(2)}) collective-permute-start(bf16[112,2432]{1,0:T(8,128)(2,1)S(1)} %dynamic_slice.139), channel_id=1, source_target_pairs={{0,1},{1,0},{2,3},{3,2},{4,5},{5,4},{6,7},{7,6},{8,9},{9,8},{10,11... | collective-permute-start | bytes 1634312 | tf_op jit(solution)/shard_map/ppermute | solution.py:396
  41.7 43.1 %slice-start.6 = ((s8[4358144]{0:T(1024)(128)(4,1)}), s8[163840]{0:T(1024)(128)(4,1)S(1)}, s32[]{:S(2)}) async-start(s8[4358144]{0:T(1024)(128)(4,1)} %bitcast.260), calls=%async_computation.6 | async-start | bytes 327680
  58.1 15.8 %collective-permute-start.8 = (bf16[112,2432]{1,0:T(8,128)(2,1)S(1)}, bf16[112,2432]{1,0:T(8,128)(2,1)S(1)}, u32[]{:S(2)}, u32[]{:S(2)}) collective-permute-start(bf16[112,2432]{1,0:T(8,128)(2,1)S(1)} %collective-permute-done.6), channel_id=1, source_target_pairs={{0,4},{2,6},{4,0},{6,2},{8,12},{10,14},{12,8},{14,10},{16,20},{18,... | collective-permute-start | bytes 1634312 | tf_op jit(solution)/shard_map/ppermute | solution.py:396
  59.6 22.8 %collective-permute-start.7 = (bf16[112,2432]{1,0:T(8,128)(2,1)S(1)}, bf16[112,2432]{1,0:T(8,128)(2,1)S(1)}, u32[]{:S(2)}, u32[]{:S(2)}) collective-permute-start(bf16[112,2432]{1,0:T(8,128)(2,1)S(1)} %collective-permute-done.5), channel_id=1, source_target_pairs={{0,4},{2,6},{4,0},{6,2},{8,12},{10,14},{12,8},{14,10},{16,20},{18,... | collective-permute-start | bytes 1634312 | tf_op jit(solution)/shard_map/ppermute | solution.py:396
  59.7 22.9 %collective-permute-start.9 = (bf16[256,896]{1,0:T(8,128)(2,1)}, bf16[256,896]{1,0:T(8,128)(2,1)S(1)}, u32[]{:S(2)}, u32[]{:S(2)}) collective-permute-start(bf16[256,896]{1,0:T(8,128)(2,1)} %get-tuple-element.104), channel_id=1, source_target_pairs={{0,1},{1,0},{2,3},{3,2},{4,5},{5,4},{6,7},{7,6},{8,9},{9,8},{10,11... | collective-permute-start | bytes 1376264 | tf_op jit(solution)/shard_map/ppermute | solution.py:396
  61.0 23.8 %slice-start.7 = ((s8[4358144]{0:T(1024)(128)(4,1)}), s8[4194304]{0:T(1024)(128)(4,1)S(1)}, s32[]{:S(2)}) async-start(s8[4358144]{0:T(1024)(128)(4,1)} %bitcast.260), calls=%async_computation.7 | async-start | bytes 8388608
  82.6 7.2 %collective-permute-start.11 = (bf16[224,2432]{1,0:T(8,128)(2,1)S(1)}, bf16[224,2432]{1,0:T(8,128)(2,1)S(1)}, u32[]{:S(2)}, u32[]{:S(2)}) collective-permute-start(bf16[224,2432]{1,0:T(8,128)(2,1)S(1)} %bitcast.225), channel_id=1, source_target_pairs={{0,2},{2,0},{4,6},{6,4},{8,10},{10,8},{12,14},{14,12},{16,18},{18,... | collective-permute-start | bytes 3268616 | tf_op jit(solution)/shard_map/ppermute | solution.py:396
  85.0 5.5 %collective-permute-start.10 = (bf16[224,2432]{1,0:T(8,128)(2,1)S(1)}, bf16[224,2432]{1,0:T(8,128)(2,1)S(1)}, u32[]{:S(2)}, u32[]{:S(2)}) collective-permute-start(bf16[224,2432]{1,0:T(8,128)(2,1)S(1)} %bitcast.227), channel_id=1, source_target_pairs={{0,2},{2,0},{4,6},{6,4},{8,10},{10,8},{12,14},{14,12},{16,18},{18,... | collective-permute-start | bytes 3268616 | tf_op jit(solution)/shard_map/ppermute | solution.py:396
  87.0 24.9 %collective-permute-start.13 = (bf16[512,896]{1,0:T(8,128)(2,1)S(1)}, bf16[512,896]{1,0:T(8,128)(2,1)S(1)}, u32[]{:S(2)}, u32[]{:S(2)}) collective-permute-start(bf16[512,896]{1,0:T(8,128)(2,1)S(1)} %multiply_convert_fusion.mlp_grad), channel_id=1, source_target_pairs={{0,1},{1,0},{2,3},{3,2},{4,5},{5,4},{6,7},{7,6},{8,9},{9,8},{10,11... | collective-permute-start | bytes 2752520 | tf_op jit(solution)/shard_map/ppermute | solution.py:396
  89.7 28.7 %collective-permute-start.12 = (bf16[256,896]{1,0:T(8,128)(2,1)S(1)}, bf16[256,896]{1,0:T(8,128)(2,1)S(1)}, u32[]{:S(2)}, u32[]{:S(2)}) collective-permute-start(bf16[256,896]{1,0:T(8,128)(2,1)S(1)} %copy-done.13), channel_id=1, source_target_pairs={{0,1},{1,0},{2,3},{3,2},{4,5},{5,4},{6,7},{7,6},{8,9},{9,8},{10,11... | collective-permute-start | bytes 1376264 | tf_op jit(solution)/shard_map/ppermute | solution.py:396
  135.5 17.4 %copy-start = (bf16[1024,2432]{1,0:T(8,128)(2,1)S(1)}, bf16[1024,2432]{1,0:T(8,128)(2,1)}, u32[]{:S(2)}) copy-start(bf16[1024,2432]{1,0:T(8,128)(2,1)} %get-tuple-element.133.activ) | copy-start | bytes 14942212
  135.5 17.4 %copy-start.9 = (bf16[512,896]{1,0:T(8,128)(2,1)S(1)}, bf16[512,896]{1,0:T(8,128)(2,1)}, u32[]{:S(2)}) copy-start(bf16[512,896]{1,0:T(8,128)(2,1)} %copy-done.8) | copy-start | bytes 2752516
  152.9 8.8 %copy-start.19 = (bf16[1024,896]{1,0:T(8,128)(2,1)S(1)}, bf16[1024,896]{1,0:T(8,128)(2,1)}, u32[]{:S(2)}) copy-start(bf16[1024,896]{1,0:T(8,128)(2,1)} %copy-done.18) | copy-start | bytes 5505028
  160.4 13.0 %collective-permute-start.15 = (bf16[1216,896]{1,0:T(8,128)(2,1)S(1)}, bf16[1216,896]{1,0:T(8,128)(2,1)S(1)}, u32[]{:S(2)}, u32[]{:S(2)}) collective-permute-start(bf16[1216,896]{1,0:T(8,128)(2,1)S(1)} %dynamic-slice_bitcast_fusion), channel_id=1, source_target_pairs={{0,2},{2,0},{4,6},{6,4},{8,10},{10,8},{12,14},{14,12},{16,18},{18,... | collective-permute-start | bytes 6537224 | tf_op jit(solution)/shard_map/ppermute | solution.py:396
  167.9 9.3 %copy-start.2 = (bf16[896,2432]{1,0:T(8,128)(2,1)}, bf16[896,2432]{1,0:T(8,128)(2,1)S(1)}, u32[]{:S(2)}) copy-start(bf16[896,2432]{1,0:T(8,128)(2,1)S(1)} %convolution_convert_fusion) | copy-start | bytes 13074436
  176.0 30.1 %collective-permute-start.18 = (bf16[896,1152]{1,0:T(8,128)(2,1)}, bf16[896,1152]{1,0:T(8,128)(2,1)}, u32[]{:S(2)}, u32[]{:S(2)}) collective-permute-start(bf16[896,1152]{1,0:T(8,128)(2,1)} %broadcast_select_fusion.5), channel_id=1, source_target_pairs={{0,2},{2,0},{4,6},{6,4},{8,10},{10,8},{12,14},{14,12},{16,18},{18,... | collective-permute-start | bytes 6193160 | tf_op jit(solution)/shard_map/ppermute | solution.py:396
  178.8 30.2 %collective-permute-start.17 = (bf16[896,1280]{1,0:T(8,128)(2,1)}, bf16[896,1280]{1,0:T(8,128)(2,1)}, u32[]{:S(2)}, u32[]{:S(2)}) collective-permute-start(bf16[896,1280]{1,0:T(8,128)(2,1)} %broadcast_select_fusion.2), channel_id=1, source_target_pairs={{0,2},{2,0},{4,6},{6,4},{8,10},{10,8},{12,14},{14,12},{16,18},{18,... | collective-permute-start | bytes 6881288 | tf_op jit(solution)/shard_map/ppermute | solution.py:396
  178.9 27.1 %slice-start.2 = ((s8[4358144]{0:T(1024)(128)(4,1)}), s8[163840]{0:T(1024)(128)(4,1)S(1)}, s32[]{:S(2)}) async-start(s8[4358144]{0:T(1024)(128)(4,1)} %bitcast.191), calls=%async_computation.2 | async-start | bytes 327680
  179.0 25.4 %collective-permute-start.16 = (bf16[4,152,896]{2,1,0:T(8,128)(2,1)S(1)}, bf16[4,152,896]{2,1,0:T(8,128)(2,1)}, u32[]{:S(2)}, u32[]{:S(2)}) collective-permute-start(bf16[4,152,896]{2,1,0:T(8,128)(2,1)S(1)} %dynamic-slice_bitcast_fusion.5), channel_id=1, source_target_pairs={{0,4},{2,6},{4,0},{6,2},{8,12},{10,14},{12,8},{14,10},{16,20},{18,... | collective-permute-start | bytes 3268616 | tf_op jit(solution)/shard_map/ppermute | solution.py:396
  180.5 25.6 %slice-start.3 = ((s8[4358144]{0:T(1024)(128)(4,1)}), s8[4194304]{0:T(1024)(128)(4,1)S(1)}, s32[]{:S(2)}) async-start(s8[4358144]{0:T(1024)(128)(4,1)} %bitcast.191), calls=%async_computation.3 | async-start | bytes 8388608
  180.5 31.8 %collective-permute-start.14 = (bf16[512,896]{1,0:T(8,128)(2,1)}, bf16[512,896]{1,0:T(8,128)(2,1)}, u32[]{:S(2)}, u32[]{:S(2)}) collective-permute-start(bf16[512,896]{1,0:T(8,128)(2,1)} %get-tuple-element.126), channel_id=1, source_target_pairs={{0,1},{1,0},{2,3},{3,2},{4,5},{5,4},{6,7},{7,6},{8,9},{9,8},{10,11... | collective-permute-start | bytes 2752520 | tf_op jit(solution)/shard_map/ppermute | solution.py:396
  213.2 35.2 %collective-permute-start.20 = (bf16[2,152,896]{2,1,0:T(8,128)(2,1)}, bf16[2,152,896]{2,1,0:T(8,128)(2,1)}, u32[]{:S(2)}, u32[]{:S(2)}) collective-permute-start(bf16[2,152,896]{2,1,0:T(8,128)(2,1)} %dynamic-slice_bitcast_fusion.9), channel_id=1, source_target_pairs={{0,8},{2,10},{4,12},{6,14},{8,0},{10,2},{12,4},{14,6},{16,24},{18,... | collective-permute-start | bytes 1634312 | tf_op jit(solution)/shard_map/ppermute | solution.py:396
  214.7 35.0 %collective-permute-start.19 = (bf16[512,896]{1,0:T(8,128)(2,1)}, bf16[512,896]{1,0:T(8,128)(2,1)}, u32[]{:S(2)}, u32[]{:S(2)}) collective-permute-start(bf16[512,896]{1,0:T(8,128)(2,1)} %get-tuple-element.140), channel_id=1, source_target_pairs={{0,1},{1,0},{2,3},{3,2},{4,5},{5,4},{6,7},{7,6},{8,9},{9,8},{10,11... | collective-permute-start | bytes 2752520 | tf_op jit(solution)/shard_map/ppermute | solution.py:396
  216.9 35.4 %collective-permute-start.22 = (bf16[4,2,56,1152]{3,2,0,1:T(8,128)(2,1)}, bf16[4,2,56,1152]{3,2,0,1:T(8,128)(2,1)}, u32[]{:S(2)}, u32[]{:S(2)}) collective-permute-start(bf16[4,2,56,1152]{3,2,0,1:T(8,128)(2,1)} %dynamic-slice_bitcast_fusion.7), channel_id=1, source_target_pairs={{0,4},{2,6},{4,0},{6,2},{8,12},{10,14},{12,8},{14,10},{16,20},{18,... | collective-permute-start | bytes 3096584 | tf_op jit(solution)/shard_map/ppermute | solution.py:396
  218.9 34.9 %collective-permute-start.21 = (bf16[4,2,56,1280]{3,2,0,1:T(8,128)(2,1)S(1)}, bf16[4,2,56,1280]{3,2,0,1:T(8,128)(2,1)}, u32[]{:S(2)}, u32[]{:S(2)}) collective-permute-start(bf16[4,2,56,1280]{3,2,0,1:T(8,128)(2,1)S(1)} %dynamic-slice_bitcast_fusion.4), channel_id=1, source_target_pairs={{0,8},{2,10},{4,12},{6,14},{8,0},{10,2},{12,4},{14,6},{16,24},{18,... | collective-permute-start | bytes 3440648 | tf_op jit(solution)/shard_map/ppermute | solution.py:396
  219.2 30.5 %copy-start.11 = (f32[256,896]{1,0:T(8,128)S(1)}, f32[256,896]{1,0:T(8,128)}, u32[]{:S(2)}) copy-start(f32[256,896]{1,0:T(8,128)} %get-tuple-element.105.mid_late) | copy-start | bytes 2752516
  219.2 30.6 %copy-start.14 = (f32[512,896]{1,0:T(8,128)S(1)}, f32[512,896]{1,0:T(8,128)}, u32[]{:S(2)}) copy-start(f32[512,896]{1,0:T(8,128)} %get-tuple-element.139) | copy-start | bytes 5505028
  255.6 14.2 %collective-permute-start.46 = (bf16[1,152,896]{2,1,0:T(8,128)(2,1)S(1)}, bf16[1,152,896]{2,1,0:T(8,128)(2,1)S(1)}, u32[]{:S(2)}, u32[]{:S(2)}) collective-permute-start(bf16[1,152,896]{2,1,0:T(8,128)(2,1)S(1)} %constant_dynamic-slice_fusion.5), channel_id=1, source_target_pairs={{0,16},{2,18},{4,20},{6,22},{8,24},{10,26},{12,28},{14,30},{16,0},... | collective-permute-start | bytes 817160 | tf_op jit(solution)/shard_map/ppermute | solution.py:396
  258.0 17.7 %collective-permute-start.39 = (bf16[2,2,56,1152]{3,2,0,1:T(8,128)(2,1)S(1)}, bf16[2,2,56,1152]{3,2,0,1:T(8,128)(2,1)S(1)}, u32[]{:S(2)}, u32[]{:S(2)}) collective-permute-start(bf16[2,2,56,1152]{3,2,0,1:T(8,128)(2,1)S(1)} %dynamic-slice_bitcast_fusion.11), channel_id=1, source_target_pairs={{0,8},{2,10},{4,12},{6,14},{8,0},{10,2},{12,4},{14,6},{16,24},{18,... | collective-permute-start | bytes 1548296 | tf_op jit(solution)/shard_map/ppermute | solution.py:396
  259.4 32.1 %collective-permute-start.32 = (bf16[2,2,56,1280]{3,2,0,1:T(8,128)(2,1)S(1)}, bf16[2,2,56,1280]{3,2,0,1:T(8,128)(2,1)S(1)}, u32[]{:S(2)}, u32[]{:S(2)}) collective-permute-start(bf16[2,2,56,1280]{3,2,0,1:T(8,128)(2,1)S(1)} %dynamic-slice_bitcast_fusion.8), channel_id=1, source_target_pairs={{0,4},{2,6},{4,0},{6,2},{8,12},{10,14},{12,8},{14,10},{16,20},{18,... | collective-permute-start | bytes 1720328 | tf_op jit(solution)/shard_map/ppermute | solution.py:396
  259.9 54.8 %collective-permute-start.23 = (bf16[2,256,2048]{2,1,0:T(8,128)(2,1)S(1)}, bf16[2,256,2048]{2,1,0:T(8,128)(2,1)S(1)}, u32[]{:S(2)}, u32[]{:S(2)}) collective-permute-start(bf16[2,256,2048]{2,1,0:T(8,128)(2,1)S(1)} %dynamic-slice_bitcast_fusion.3), channel_id=1, source_target_pairs={{0,2},{2,0},{4,6},{6,4},{8,10},{10,8},{12,14},{14,12},{16,18},{18,... | collective-permute-start | bytes 6291464 | tf_op jit(solution)/shard_map/ppermute | solution.py:396
  269.8 9.1 %collective-permute-start.47 = (bf16[1,152,896]{2,1,0:T(8,128)(2,1)S(1)}, bf16[1,152,896]{2,1,0:T(8,128)(2,1)S(1)}, u32[]{:S(2)}, u32[]{:S(2)}) collective-permute-start(bf16[1,152,896]{2,1,0:T(8,128)(2,1)S(1)} %add_convert_fusion.3), channel_id=1, source_target_pairs={{0,16},{2,18},{4,20},{6,22},{8,24},{10,26},{12,28},{14,30},{16,0},... | collective-permute-start | bytes 817160 | tf_op jit(solution)/shard_map/ppermute | solution.py:396
  275.8 19.0 %collective-permute-start.40 = (bf16[1,2,56,1152]{3,2,0,1:T(8,128)(2,1)S(1)}, bf16[1,2,56,1152]{3,2,0,1:T(8,128)(2,1)S(1)}, u32[]{:S(2)}, u32[]{:S(2)}) collective-permute-start(bf16[1,2,56,1152]{3,2,0,1:T(8,128)(2,1)S(1)} %constant_dynamic-slice_fusion.7), channel_id=1, source_target_pairs={{0,16},{2,18},{4,20},{6,22},{8,24},{10,26},{12,28},{14,30},{16,0},... | collective-permute-start | bytes 774152 | tf_op jit(solution)/shard_map/ppermute | solution.py:396
  279.1 37.4 %collective-permute-start.48 = (bf16[2,152,896]{2,1,0:T(8,128)(2,1)S(1)}, bf16[2,152,896]{2,1,0:T(8,128)(2,1)S(1)}, u32[]{:S(2)}, u32[]{:S(2)}) collective-permute-start(bf16[2,152,896]{2,1,0:T(8,128)(2,1)S(1)} %maximum_select_fusion.22), channel_id=1, source_target_pairs={{0,8},{2,10},{4,12},{6,14},{8,0},{10,2},{12,4},{14,6},{16,24},{18,... | collective-permute-start | bytes 1634312 | tf_op jit(solution)/shard_map/ppermute | solution.py:396
  291.7 15.6 %collective-permute-start.33 = (bf16[1,2,56,1280]{3,2,0,1:T(8,128)(2,1)S(1)}, bf16[1,2,56,1280]{3,2,0,1:T(8,128)(2,1)S(1)}, u32[]{:S(2)}, u32[]{:S(2)}) collective-permute-start(bf16[1,2,56,1280]{3,2,0,1:T(8,128)(2,1)S(1)} %constant_dynamic-slice_fusion.9), channel_id=1, source_target_pairs={{0,16},{2,18},{4,20},{6,22},{8,24},{10,26},{12,28},{14,30},{16,0},... | collective-permute-start | bytes 860168 | tf_op jit(solution)/shard_map/ppermute | solution.py:396
  295.0 12.8 %collective-permute-start.41 = (bf16[56,1152]{1,0:T(8,128)(2,1)S(1)}, bf16[56,1152]{1,0:T(8,128)(2,1)S(1)}, u32[]{:S(2)}, u32[]{:S(2)}) collective-permute-start(bf16[56,1152]{1,0:T(8,128)(2,1)S(1)} %get-tuple-element.180), channel_id=1, source_target_pairs={{0,1},{1,0},{2,3},{3,2},{4,5},{5,4},{6,7},{7,6},{8,9},{9,8},{10,11... | collective-permute-start | bytes 387080 | tf_op jit(solution)/shard_map/ppermute | solution.py:396
  307.5 4.3 %collective-permute-start.34 = (bf16[56,1280]{1,0:T(8,128)(2,1)S(1)}, bf16[56,1280]{1,0:T(8,128)(2,1)S(1)}, u32[]{:S(2)}, u32[]{:S(2)}) collective-permute-start(bf16[56,1280]{1,0:T(8,128)(2,1)S(1)} %get-tuple-element.178), channel_id=1, source_target_pairs={{0,1},{1,0},{2,3},{3,2},{4,5},{5,4},{6,7},{7,6},{8,9},{9,8},{10,11... | collective-permute-start | bytes 430088 | tf_op jit(solution)/shard_map/ppermute | solution.py:396
  307.8 20.4 %collective-permute-start.42 = (bf16[1,2,56,1152]{3,2,1,0:T(8,128)(2,1)S(1)}, bf16[1,2,56,1152]{3,2,1,0:T(8,128)(2,1)S(1)}, u32[]{:S(2)}, u32[]{:S(2)}) collective-permute-start(bf16[1,2,56,1152]{3,2,1,0:T(8,128)(2,1)S(1)} %fusion.40), channel_id=1, source_target_pairs={{0,16},{2,18},{4,20},{6,22},{8,24},{10,26},{12,28},{14,30},{16,0},... | collective-permute-start | bytes 774152 | tf_op jit(solution)/shard_map/ppermute | solution.py:396
  311.8 27.2 %collective-permute-start.35 = (bf16[1,2,56,1280]{3,2,1,0:T(8,128)(2,1)S(1)}, bf16[1,2,56,1280]{3,2,1,0:T(8,128)(2,1)S(1)}, u32[]{:S(2)}, u32[]{:S(2)}) collective-permute-start(bf16[1,2,56,1280]{3,2,1,0:T(8,128)(2,1)S(1)} %fusion.38), channel_id=1, source_target_pairs={{0,16},{2,18},{4,20},{6,22},{8,24},{10,26},{12,28},{14,30},{16,0},... | collective-permute-start | bytes 860168 | tf_op jit(solution)/shard_map/ppermute | solution.py:396
  315.6 20.6 %collective-permute-start.24 = (bf16[256,2048]{1,0:T(8,128)(2,1)S(1)}, bf16[256,2048]{1,0:T(8,128)(2,1)S(1)}, u32[]{:S(2)}, u32[]{:S(2)}) collective-permute-start(bf16[256,2048]{1,0:T(8,128)(2,1)S(1)} %dynamic-slice_bitcast_fusion.6), channel_id=1, source_target_pairs={{0,1},{1,0},{2,3},{3,2},{4,5},{5,4},{6,7},{7,6},{8,9},{9,8},{10,11... | collective-permute-start | bytes 3145736 | tf_op jit(solution)/shard_map/ppermute | solution.py:396
  316.8 42.8 %collective-permute-start.49 = (bf16[4,152,896]{2,1,0:T(8,128)(2,1)S(1)}, bf16[4,152,896]{2,1,0:T(8,128)(2,1)S(1)}, u32[]{:S(2)}, u32[]{:S(2)}) collective-permute-start(bf16[4,152,896]{2,1,0:T(8,128)(2,1)S(1)} %bitcast.223), channel_id=1, source_target_pairs={{0,4},{2,6},{4,0},{6,2},{8,12},{10,14},{12,8},{14,10},{16,20},{18,... | collective-permute-start | bytes 3268616 | tf_op jit(solution)/shard_map/ppermute | solution.py:396
  328.3 19.2 %collective-permute-start.43 = (bf16[2,2,56,1152]{3,2,0,1:T(8,128)(2,1)S(1)}, bf16[2,2,56,1152]{3,2,0,1:T(8,128)(2,1)S(1)}, u32[]{:S(2)}, u32[]{:S(2)}) collective-permute-start(bf16[2,2,56,1152]{3,2,0,1:T(8,128)(2,1)S(1)} %maximum_select_fusion.25), channel_id=1, source_target_pairs={{0,8},{2,10},{4,12},{6,14},{8,0},{10,2},{12,4},{14,6},{16,24},{18,... | collective-permute-start | bytes 1548296 | tf_op jit(solution)/shard_map/ppermute | solution.py:396
  336.6 22.1 %collective-permute-start.25 = (bf16[4,32,2048]{2,1,0:T(8,128)(2,1)S(1)}, bf16[4,32,2048]{2,1,0:T(8,128)(2,1)S(1)}, u32[]{:S(2)}, u32[]{:S(2)}) collective-permute-start(bf16[4,32,2048]{2,1,0:T(8,128)(2,1)S(1)} %dynamic-slice_bitcast_fusion.10), channel_id=1, source_target_pairs={{0,8},{2,10},{4,12},{6,14},{8,0},{10,2},{12,4},{14,6},{16,24},{18,... | collective-permute-start | bytes 1572872 | tf_op jit(solution)/shard_map/ppermute | solution.py:396
  339.1 20.2 %collective-permute-start.36 = (bf16[2,2,56,1280]{3,2,0,1:T(8,128)(2,1)S(1)}, bf16[2,2,56,1280]{3,2,0,1:T(8,128)(2,1)S(1)}, u32[]{:S(2)}, u32[]{:S(2)}) collective-permute-start(bf16[2,2,56,1280]{3,2,0,1:T(8,128)(2,1)S(1)} %maximum_select_fusion.20), channel_id=1, source_target_pairs={{0,4},{2,6},{4,0},{6,2},{8,12},{10,14},{12,8},{14,10},{16,20},{18,... | collective-permute-start | bytes 1720328 | tf_op jit(solution)/shard_map/ppermute | solution.py:396
  347.9 31.2 %collective-permute-start.44 = (bf16[4,2,56,1152]{3,2,0,1:T(8,128)(2,1)S(1)}, bf16[4,2,56,1152]{3,2,0,1:T(8,128)(2,1)S(1)}, u32[]{:S(2)}, u32[]{:S(2)}) collective-permute-start(bf16[4,2,56,1152]{3,2,0,1:T(8,128)(2,1)S(1)} %bitcast.245), channel_id=1, source_target_pairs={{0,4},{2,6},{4,0},{6,2},{8,12},{10,14},{12,8},{14,10},{16,20},{18,... | collective-permute-start | bytes 3096584 | tf_op jit(solution)/shard_map/ppermute | solution.py:396
  359.0 20.0 %collective-permute-start.26 = (bf16[2,32,2048]{2,1,0:T(8,128)(2,1)S(1)}, bf16[2,32,2048]{2,1,0:T(8,128)(2,1)S(1)}, u32[]{:S(2)}, u32[]{:S(2)}) collective-permute-start(bf16[2,32,2048]{2,1,0:T(8,128)(2,1)S(1)} %dynamic-slice_bitcast_fusion.12), channel_id=1, source_target_pairs={{0,4},{2,6},{4,0},{6,2},{8,12},{10,14},{12,8},{14,10},{16,20},{18,... | collective-permute-start | bytes 786440 | tf_op jit(solution)/shard_map/ppermute | solution.py:396
  359.5 30.2 %collective-permute-start.37 = (bf16[4,2,56,1280]{3,2,0,1:T(8,128)(2,1)S(1)}, bf16[4,2,56,1280]{3,2,0,1:T(8,128)(2,1)S(1)}, u32[]{:S(2)}, u32[]{:S(2)}) collective-permute-start(bf16[4,2,56,1280]{3,2,0,1:T(8,128)(2,1)S(1)} %bitcast.219), channel_id=1, source_target_pairs={{0,8},{2,10},{4,12},{6,14},{8,0},{10,2},{12,4},{14,6},{16,24},{18,... | collective-permute-start | bytes 3440648 | tf_op jit(solution)/shard_map/ppermute | solution.py:396
  360.1 33.4 %collective-permute-start.50 = (bf16[8,152,896]{2,1,0:T(8,128)(2,1)S(1)}, bf16[8,152,896]{2,1,0:T(8,128)(2,1)S(1)}, u32[]{:S(2)}, u32[]{:S(2)}) collective-permute-start(bf16[8,152,896]{2,1,0:T(8,128)(2,1)S(1)} %bitcast.201), channel_id=1, source_target_pairs={{0,2},{2,0},{4,6},{6,4},{8,10},{10,8},{12,14},{14,12},{16,18},{18,... | collective-permute-start | bytes 6537224 | tf_op jit(solution)/shard_map/ppermute | solution.py:396
  379.0 7.6 %collective-permute-start.27 = (bf16[1,32,2048]{2,1,0:T(8,128)(2,1)S(1)}, bf16[1,32,2048]{2,1,0:T(8,128)(2,1)S(1)}, u32[]{:S(2)}, u32[]{:S(2)}) collective-permute-start(bf16[1,32,2048]{2,1,0:T(8,128)(2,1)S(1)} %constant_dynamic-slice_fusion.10), channel_id=1, source_target_pairs={{0,16},{2,18},{4,20},{6,22},{8,24},{10,26},{12,28},{14,30},{16,0},... | collective-permute-start | bytes 393224 | tf_op jit(solution)/shard_map/ppermute | solution.py:396
  379.5 22.1 %collective-permute-start.45 = (bf16[8,2,56,1152]{3,2,0,1:T(8,128)(2,1)S(1)}, bf16[8,2,56,1152]{3,2,0,1:T(8,128)(2,1)S(1)}, u32[]{:S(2)}, u32[]{:S(2)}) collective-permute-start(bf16[8,2,56,1152]{3,2,0,1:T(8,128)(2,1)S(1)} %bitcast.209), channel_id=1, source_target_pairs={{0,2},{2,0},{4,6},{6,4},{8,10},{10,8},{12,14},{14,12},{16,18},{18,... | collective-permute-start | bytes 6193160 | tf_op jit(solution)/shard_map/ppermute | solution.py:396
  386.6 5.6 %collective-permute-start.28 = (bf16[1,32,2048]{2,1,0:T(8,128)(2,1)S(1)}, bf16[1,32,2048]{2,1,0:T(8,128)(2,1)S(1)}, u32[]{:S(2)}, u32[]{:S(2)}) collective-permute-start(bf16[1,32,2048]{2,1,0:T(8,128)(2,1)S(1)} %add_convert_fusion.5), channel_id=1, source_target_pairs={{0,16},{2,18},{4,20},{6,22},{8,24},{10,26},{12,28},{14,30},{16,0},... | collective-permute-start | bytes 393224 | tf_op jit(solution)/shard_map/ppermute | solution.py:396
  390.2 24.8 %collective-permute-start.38 = (bf16[8,2,56,1280]{3,2,0,1:T(8,128)(2,1)S(1)}, bf16[8,2,56,1280]{3,2,0,1:T(8,128)(2,1)S(1)}, u32[]{:S(2)}, u32[]{:S(2)}) collective-permute-start(bf16[8,2,56,1280]{3,2,0,1:T(8,128)(2,1)S(1)} %bitcast.197), channel_id=1, source_target_pairs={{0,2},{2,0},{4,6},{6,4},{8,10},{10,8},{12,14},{14,12},{16,18},{18,... | collective-permute-start | bytes 6881288 | tf_op jit(solution)/shard_map/ppermute | solution.py:396
  392.2 6.6 %collective-permute-start.29 = (bf16[2,32,2048]{2,1,0:T(8,128)(2,1)S(1)}, bf16[2,32,2048]{2,1,0:T(8,128)(2,1)S(1)}, u32[]{:S(2)}, u32[]{:S(2)}) collective-permute-start(bf16[2,32,2048]{2,1,0:T(8,128)(2,1)S(1)} %maximum_select_fusion.28), channel_id=1, source_target_pairs={{0,4},{2,6},{4,0},{6,2},{8,12},{10,14},{12,8},{14,10},{16,20},{18,... | collective-permute-start | bytes 786440 | tf_op jit(solution)/shard_map/ppermute | solution.py:396
  399.0 10.1 %collective-permute-start.30 = (bf16[4,32,2048]{2,1,0:T(8,128)(2,1)S(1)}, bf16[4,32,2048]{2,1,0:T(8,128)(2,1)S(1)}, u32[]{:S(2)}, u32[]{:S(2)}) collective-permute-start(bf16[4,32,2048]{2,1,0:T(8,128)(2,1)S(1)} %bitcast.255), channel_id=1, source_target_pairs={{0,8},{2,10},{4,12},{6,14},{8,0},{10,2},{12,4},{14,6},{16,24},{18,... | collective-permute-start | bytes 1572872 | tf_op jit(solution)/shard_map/ppermute | solution.py:396
  409.2 14.0 %collective-permute-start.31 = (bf16[8,32,2048]{2,1,0:T(8,128)(2,1)S(1)}, bf16[8,32,2048]{2,1,0:T(8,128)(2,1)S(1)}, u32[]{:S(2)}, u32[]{:S(2)}) collective-permute-start(bf16[8,32,2048]{2,1,0:T(8,128)(2,1)S(1)} %bitcast.233), channel_id=1, source_target_pairs={{0,2},{2,0},{4,6},{6,4},{8,10},{10,8},{12,14},{14,12},{16,18},{18,... | collective-permute-start | bytes 3145736 | tf_op jit(solution)/shard_map/ppermute | solution.py:396
  (21 other events, 104.7 us)

commit v4 on v3

--- a/solution.py
+++ b/solution.py
@@ -215,7 +215,7 @@
         functools.partial(early_kernel, groups, pairs),
         whole + half_out,
         scratch,
-        2 * 10**9,
+        10**6,
         (normed_low, w_qkv, bias_qkv, cosine, sine, segs_col, segs_row, tokens, w_output, gain),
     )
     return query_rot, key_rot, value_low, early
@@ -230,7 +230,7 @@
         functools.partial(late_kernel, groups, pairs),
         half_out,
         scratch,
-        2 * 10**9,
+        10**6,
         (query_rot, key_rot, value_low, segs_col, segs_row, tokens, w_output, gain),
     )
 
@@ -384,7 +384,7 @@
             ((width, columns), low),
             ((queries, width), low),
         ],
-        10**9,
+        10**6,
         (early[2], late[2], norm_own, norm_got, cotangent, gain_mlp, w_output, early[0], late[0],
          early[1], late[1], query_rot, key_rot, value_low, segs_col, segs_row, cosine, sine,
          normed_low, w_qkv, tokens, gain_attn),
@@ -445,7 +445,7 @@
         out_specs=out_specs,
         input_output_aliases=aliases or {},
         compiler_params=pltpu.CompilerParams(vmem_limit_bytes=56 * 2**20),
-        cost_estimate=pl.CostEstimate(flops=flops, bytes_accessed=10**6, transcendentals=0),
+        cost_estimate=pl.CostEstimate(flops=flops, bytes_accessed=10**3, transcendentals=0),
     )(*operands)
 
 
@@ -463,7 +463,7 @@
         + [pl.BlockSpec(memory_space=pl.ANY)] * len(carried),
         shapes,
         [row_block(shape, rows, first) for shape in shapes],
-        10**9,
+        10**6,
         {5 + at: at for at in range(len(carried))},
     )
 
@@ -503,7 +503,7 @@
             pl.BlockSpec((rows, width), lambda at: (jnp.minimum(at, half - 1), 0)),
             pl.BlockSpec((rows, width), lambda at: (jnp.maximum(at - half, 0), 0)),
         ],
-        10**9,
+        10**6,
     )
 
 
@@ -669,7 +669,7 @@
         full_qkv = group.joined(qkv, group.shared(got_qkv, cores))
         full_output = group.joined(w_output, group.shared(got_output, cores))
         got_gate = group.fetched(group.columns(w_gate, 1 - group.at), chips)
-        got_up = group.fetched(group.columns(w_up, 1 - group.at), chips)
+        got_up = group.fetched(group.columns(w_up, 1 - group.at), cores)
     else:
         full_qkv, full_output, part_gate, part_up = group.plain_weights(
             qkv, w_output, w_gate, w_up
@@ -679,10 +679,8 @@
         gain_mlp_row,
     )
     if group.pair:
-        query_rot, early, got_gate, got_up, mlp_grad = together(
-            query_rot, early, got_gate, got_up, mlp_grad
-        )
-        got_gate, got_up = group.shared(got_gate, chips[1:]), group.shared(got_up, chips[1:])
+        query_rot, early, got_gate, mlp_grad = together(query_rot, early, got_gate, mlp_grad)
+        got_gate = group.shared(got_gate, chips[1:])
         others = [group.swap(early[3])]
         mlp_other = group.swap(mlp_grad)
     late = attention_late(

time: 435 us -> 430 us (0.989)
  waiting for transfers between devices: 130 us -> 122 us
    ppermute x51 -> x50, waiting for transfers between devices: 130 us -> 122 us  [swapped(): return lax.ppermute(value, axis, [(at, at ^ step) for at in range(size)])]
    select_n x31 -> x30, other arithmetic: 16.6 us -> 18.2 us  [ordered(): return jnp.where(bit == 0, jnp.stack([own, other]), jnp.stack([other, own]))]
    ppermute x51 -> x50, starting transfers between devices: 79.1 us -> 80.4 us  [swapped(): return lax.ppermute(value, axis, [(at, at ^ step) for at in range(size)])]
  transfers between devices with their start and end apart: 51 -> 50, of which waited for: 19 -> 18; matrix products, arithmetic and copies ran while one was open for 18% -> 19% of each run, Pallas kernels for 20% -> 20%
where the time goes in v4:
time: 430 us; the launch traced here: 425 us
  waiting for transfers between devices  122 us (28%)
  Pallas kernels  118 us (27%)
  starting transfers between devices  80.4 us (19%)
  other arithmetic  61.1 us (14%)
  local copies, waits for them, and re-layouts  25.2 us (6%)
  matrix products  16.7 us (4%)
    ppermute x50, waiting for transfers between devices, swapped(): return lax.ppermute(value, axis, [(at, at ^ step) for at in range(size)])  122 us
    ppermute x50, starting transfers between devices, swapped(): return lax.ppermute(value, axis, [(at, at ^ step) for at in range(size)])  80.4 us
    pallas_call x4, Pallas kernels, grid_call(): pl.pallas_call(kernel, grid=(grid,), out_shape=out_shape, in_specs=in_spe...  59.4 us
    pallas_call x3, Pallas kernels, call(): pl.pallas_call(kernel, out_shape=[jax.ShapeDtypeStruct(shape, kind) for s...  58.5 us
    select_n x30, other arithmetic, ordered(): return jnp.where(bit == 0, jnp.stack([own, other]), jnp.stack([other, own]))  18.2 us
    dot_general x3, matrix products, contract_rows(): lax.dot_general(left, right, (((0,), (0,)), ((), ())), preferred_element_...  16.7 us
    convert_element_type x17, other arithmetic, added(): (left.astype(jnp.float32) + right.astype(jnp.float32)).astype(jnp.bfloat16)  14.8 us
  transfers between devices with their start and end apart: 50, of which 18 were waited for; matrix products, arithmetic and copies ran while one was open for 19% of the time, Pallas kernels for 20%

profile of v4, /device:TPU:1, one launch (start us, length us, event | category | flops | bytes accessed | tf_op | source)
XLA Modules:
  0.0 425.2 jit_solution(12409048849661631348)
XLA Ops:
  4.0 2.1 collective-permute-start.1
  7.0 1.4 collective-permute-start
  14.7 11.6 %collective-permute-done = bf16[1472]{0:T(1024)(128)(2,1)S(1)} collective-permute-done((bf16[1472]{0:T(1024)(128)(2,1)S(1)}, bf16[1472]{0:T(1024)(128)(2,1)S(1)}, u32[]{:S(2)}, u32[]{:S(2)}) %collective-permute-start) | collective-permute-done | bytes 2976 | tf_op jit(solution)/shard_map/ppermute | solution.py:396
  31.9 1.5 collective-permute-start.5
  33.5 2.8 dynamic_slice.139
  36.3 1.5 maximum_select_fusion.17
  37.9 1.4 maximum_select_fusion.10
  39.3 1.4 maximum_select_fusion.15
  40.8 1.7 maximum_select_fusion.8
  42.5 16.3 %shard_map.254 = (bf16[512,896]{1,0:T(8,128)(2,1)}, bf16[512,128]{1,0:T(8,128)(2,1)}, bf16[512,128]{1,0:T(8,128)(2,1)}, bf16[256,896]{1,0:T(8,128)(2,1)}, f32[16...) custom-call(bf16[512,896]{1,0:T(8,128)(2,1)} %fusion.8.normed_low, bf16[896,1152]{1,0:T(8,128)(2,1)} %bitcast.191, ...), custom_call_target="tpu_custom_call" | custom-call | flops 1000000 | bytes 3333 | tf_op jit(solution)/shard_map/pallas_call | solution.py:180
  58.8 1.5 collective-permute-start.6
  61.5 12.9 %shard_map.255 = (bf16[256,896]{1,0:T(8,128)(2,1)}, f32[16,256]{1,0:T(8,128)}, f32[256,896]{1,0:T(8,128)}, bf16[256,896]{1,0:T(8,128)(2,1)}) custom-call(bf16[512,896]{1,0:T(8,128)(2,1)} %get-tuple-element.93.query_rot, bf16[512,128]{1,0:T(8,128)(2,1)} %get-tuple-element.94.key_rot, bf16[512,128]{1,0:T(8,128)(2,1)} %get-tuple-element.95.value_low, ...), custom_call_target="tpu_custom_call" | custom-call | flops 1000000 | bytes 3333 | tf_op jit(solution)/shard_map/pallas_call | solution.py:180
  74.5 4.1 collective-permute-done.8
  80.0 1.8 dynamic-slice_bitcast_fusion.1
  82.1 1.5 collective-permute-start.12
  85.5 1.9 maximum_select_fusion.5
  87.9 5.0 %maximum_select_fusion = (bf16[2,448,2432]{2,1,0:T(8,128)(2,1)}, bf16[2,448,2432]{2,1,0:T(8,128)(2,1)}) fusion(bf16[1,448,2432]{2,1,0:T(8,128)(2,1)S(1)} %bitcast.202, bf16[1,448,2432]{2,1,0:T(8,128)(2,1)S(1)} %dynamic-slice_bitcast_fusion.2, pred[]{:T(512)S(6)} %eq.10, bf16[1,448,2432]{2,1,0:T(8,128)(2,1)S(1)} %dynamic-slice_bitcast_fusion.1, ...), kind=kLoop, calls=%fused_computation.4 | loop fusion | flops 13074432 | bytes 17432576 | tf_op jit(solution)/shard_map/jit(_where)/select_n | solution.py:408
  92.9 15.8 %shard_map.256 = (bf16[1024,2432]{1,0:T(8,128)(2,1)}, bf16[1024,2432]{1,0:T(8,128)(2,1)}, bf16[1024,2432]{1,0:T(8,128)(2,1)}) custom-call(bf16[512,896]{1,0:T(8,128)(2,1)} %pad_maximum_fusion.mid_low, bf16[512,896]{1,0:T(8,128)(2,1)} %copy-done.8, bf16[896,2432]{1,0:T(8,128)(2,1)} %bitcast.180, bf16[896,2432]{1,0:T(8,128)(2,1)} %bitcast.183, ...), custom_call_target="tpu_custom_call" | custom-call | flops 1000000 | bytes 1000 | tf_op jit(solution)/shard_map/pallas_call | solution.py:440
  108.8 4.6 %collective-permute-done.11 = bf16[256,896]{1,0:T(8,128)(2,1)S(1)} collective-permute-done((bf16[256,896]{1,0:T(8,128)(2,1)S(1)}, bf16[256,896]{1,0:T(8,128)(2,1)S(1)}, u32[]{:S(2)}, u32[]{:S(2)}) %collective-permute-start.11) | collective-permute-done | bytes 458784 | tf_op jit(solution)/shard_map/ppermute | solution.py:396
  114.4 16.0 %shard_map.257 = (bf16[1024,2432]{1,0:T(8,128)(2,1)}, bf16[1024,2432]{1,0:T(8,128)(2,1)}, bf16[1024,2432]{1,0:T(8,128)(2,1)}) custom-call(bf16[512,896]{1,0:T(8,128)(2,1)} %pad_maximum_fusion.1.mid_low, bf16[512,896]{1,0:T(8,128)(2,1)} %copy-done.17, bf16[896,2432]{1,0:T(8,128)(2,1)} %bitcast.181, ...), custom_call_target="tpu_custom_call", output_to_operand_aliasing={{0}: (5, {}), {1}: (6, {}), {2}: (7, {})} | custom-call | flops 1000000 | bytes 1000 | tf_op jit(solution)/shard_map/pallas_call | solution.py:440
  130.5 17.4 %shard_map.258 = (f32[512,896]{1,0:T(8,128)}, bf16[512,896]{1,0:T(8,128)(2,1)}) custom-call(bf16[1024,2432]{1,0:T(8,128)(2,1)} %get-tuple-element.128.gate_grad, bf16[1024,2432]{1,0:T(8,128)(2,1)} %get-tuple-element.129.up_grad, bf16[896,2432]{1,0:T(8,128)(2,1)} %bitcast.182, bf16[896,2432]{1,0:T(8,128)(2,1)} %bitcast.185), custom_call_target="tpu_custom_call" | custom-call | flops 1000000 | bytes 1000 | tf_op jit(solution)/shard_map/pallas_call | solution.py:440
  147.9 5.9 %convolution_convert_fusion.2 = bf16[2432,896]{1,0:T(8,128)(2,1)S(1)} fusion(bf16[1024,2432]{1,0:T(8,128)(2,1)S(1)} %copy-done.1, bf16[512,896]{1,0:T(8,128)(2,1)S(1)} %copy-done.18, bf16[512,896]{1,0:T(8,128)(2,1)S(1)} %copy-done.9), kind=kOutput, calls=%fused_computation.2 | convolution fusion | flops 4468588544 | bytes 11173888 | tf_op jit(solution)/shard_map/dot_general | solution.py:43
  156.2 5.3 %convolution_convert_fusion = bf16[896,2432]{1,0:T(8,128)(2,1)S(1)} fusion(bf16[1024,896]{1,0:T(8,128)(2,1)S(1)} %constant_dynamic-update-slice_fusion.3, bf16[1024,2432]{1,0:T(8,128)(2,1)S(1)} %copy-done.2), kind=kOutput, calls=%fused_computation | convolution fusion | flops 4464918528 | bytes 11173888 | tf_op jit(solution)/shard_map/dot_general | solution.py:43
  161.5 5.5 %convolution_convert_fusion.1 = bf16[896,2432]{1,0:T(8,128)(2,1)S(1)} fusion(bf16[1024,896]{1,0:T(8,128)(2,1)S(1)} %constant_dynamic-update-slice_fusion.3, bf16[1024,2432]{1,0:T(8,128)(2,1)S(1)} %bitcast.190), kind=kOutput, calls=%fused_computation.1 | convolution fusion | flops 4464918528 | bytes 11173888 | tf_op jit(solution)/shard_map/dot_general | solution.py:43
  167.6 2.0 broadcast_select_fusion.5
  170.9 1.6 broadcast_select_fusion.2
  172.7 1.5 collective-permute-start.15
  175.5 10.1 %shard_map.259 = (f32[512,896]{1,0:T(8,128)}, bf16[512,896]{1,0:T(8,128)(2,1)}) custom-call(bf16[1024,2432]{1,0:T(8,128)(2,1)} %get-tuple-element.131.activ, bf16[2432,896]{1,0:T(8,128)(2,1)} %w_down.5), custom_call_target="tpu_custom_call" | custom-call | flops 1000000 | bytes 1000 | tf_op jit(solution)/shard_map/pallas_call | solution.py:440
  185.6 12.5 %collective-permute-done.15 = bf16[4,152,896]{2,1,0:T(8,128)(2,1)} collective-permute-done((bf16[4,152,896]{2,1,0:T(8,128)(2,1)S(1)}, bf16[4,152,896]{2,1,0:T(8,128)(2,1)}, u32[]{:S(2)}, u32[]{:S(2)}) %collective-permute-start.15) | collective-permute-done | bytes 1089568 | tf_op jit(solution)/shard_map/ppermute | solution.py:396
  198.1 1.6 fusion.3
  199.8 3.0 add_convert_fusion.1
  202.8 3.2 add_convert_fusion
  206.9 1.5 collective-permute-start.19
  213.9 29.3 %shard_map.260 = (bf16[1024,2048]{1,0:T(8,128)(2,1)}, f32[512,896]{1,0:T(8,128)}) custom-call(f32[256,896]{1,0:T(8,128)} %get-tuple-element.92.mid_early, f32[256,896]{1,0:T(8,128)} %get-tuple-element.103.mid_late, f32[512,896]{1,0:T(8,128)} %get-tuple-element.139.norm_own, bf16[512,896]{1,0:T(8,128)(2,1)} %collective-permute-done.13.norm_got, ...), custom_call_target="tpu_custom_call" | custom-call | flops 1000000 | bytes 3333 | tf_op jit(solution)/shard_map/pallas_call | solution.py:180
  244.5 2.6 fusion.9
  247.1 1.5 fusion.5
  248.6 1.7 fusion.2
  250.3 2.4 collective-permute-start.45
  254.6 3.3 collective-permute-start.22
  257.9 6.6 %collective-permute-done.45 = bf16[1,152,896]{2,1,0:T(8,128)(2,1)S(1)} collective-permute-done((bf16[1,152,896]{2,1,0:T(8,128)(2,1)S(1)}, bf16[1,152,896]{2,1,0:T(8,128)(2,1)S(1)}, u32[]{:S(2)}, u32[]{:S(2)}) %collective-permute-start.45) | collective-permute-done | bytes 272416 | tf_op jit(solution)/shard_map/ppermute | solution.py:396
  264.6 3.7 collective-permute-done.38
  269.6 4.1 collective-permute-done.46
  273.9 12.2 %collective-permute-start.47 = (bf16[2,152,896]{2,1,0:T(8,128)(2,1)S(1)}, bf16[2,152,896]{2,1,0:T(8,128)(2,1)S(1)}, u32[]{:S(2)}, u32[]{:S(2)}) collective-permute-start(bf16[2,152,896]{2,1,0:T(8,128)(2,1)S(1)} %maximum_select_fusion.21), channel_id=1, source_target_pairs={{0,8},{2,10},{4,12},{6,14},{8,0},{10,2},{12,4},{14,6},{16,24},{18,... | collective-permute-start | bytes 1634312 | tf_op jit(solution)/shard_map/ppermute | solution.py:396
  286.5 3.2 collective-permute-start.32
  290.1 11.9 %collective-permute-done.32 = bf16[1,2,56,1280]{3,2,0,1:T(8,128)(2,1)S(1)} collective-permute-done((bf16[1,2,56,1280]{3,2,0,1:T(8,128)(2,1)S(1)}, bf16[1,2,56,1280]{3,2,0,1:T(8,128)(2,1)S(1)}, u32[]{:S(2)}, u32[]{:S(2)}) %collective-permute-start.32) | collective-permute-done | bytes 286752 | tf_op jit(solution)/shard_map/ppermute | solution.py:396
  302.6 3.2 collective-permute-start.41
  306.4 2.9 collective-permute-start.34
  311.8 11.1 %collective-permute-done.41 = bf16[1,2,56,1152]{3,2,1,0:T(8,128)(2,1)S(1)} collective-permute-done((bf16[1,2,56,1152]{3,2,1,0:T(8,128)(2,1)S(1)}, bf16[1,2,56,1152]{3,2,1,0:T(8,128)(2,1)S(1)}, u32[]{:S(2)}, u32[]{:S(2)}) %collective-permute-start.41) | collective-permute-done | bytes 258080 | tf_op jit(solution)/shard_map/ppermute | solution.py:396
  323.1 1.7 collective-permute-start.42
  324.9 5.7 %collective-permute-done.23 = bf16[256,2048]{1,0:T(8,128)(2,1)S(1)} collective-permute-done((bf16[256,2048]{1,0:T(8,128)(2,1)S(1)}, bf16[256,2048]{1,0:T(8,128)(2,1)S(1)}, u32[]{:S(2)}, u32[]{:S(2)}) %collective-permute-start.23) | collective-permute-done | bytes 1048608 | tf_op jit(solution)/shard_map/ppermute | solution.py:396
  331.0 2.6 collective-permute-start.24
  334.2 8.1 %collective-permute-done.42 = bf16[2,2,56,1152]{3,2,0,1:T(8,128)(2,1)S(1)} collective-permute-done((bf16[2,2,56,1152]{3,2,0,1:T(8,128)(2,1)S(1)}, bf16[2,2,56,1152]{3,2,0,1:T(8,128)(2,1)S(1)}, u32[]{:S(2)}, u32[]{:S(2)}) %collective-permute-start.42) | collective-permute-done | bytes 516128 | tf_op jit(solution)/shard_map/ppermute | solution.py:396
  342.9 10.6 %collective-permute-done.24 = bf16[4,32,2048]{2,1,0:T(8,128)(2,1)S(1)} collective-permute-done((bf16[4,32,2048]{2,1,0:T(8,128)(2,1)S(1)}, bf16[4,32,2048]{2,1,0:T(8,128)(2,1)S(1)}, u32[]{:S(2)}, u32[]{:S(2)}) %collective-permute-start.24) | collective-permute-done | bytes 524320 | tf_op jit(solution)/shard_map/ppermute | solution.py:396
  355.7 18.1 %collective-permute-done.25 = bf16[2,32,2048]{2,1,0:T(8,128)(2,1)S(1)} collective-permute-done((bf16[2,32,2048]{2,1,0:T(8,128)(2,1)S(1)}, bf16[2,32,2048]{2,1,0:T(8,128)(2,1)S(1)}, u32[]{:S(2)}, u32[]{:S(2)}) %collective-permute-start.25) | collective-permute-done | bytes 262176 | tf_op jit(solution)/shard_map/ppermute | solution.py:396
  374.3 5.7 %collective-permute-start.44 = (bf16[8,2,56,1152]{3,2,0,1:T(8,128)(2,1)S(1)}, bf16[8,2,56,1152]{3,2,0,1:T(8,128)(2,1)S(1)}, u32[]{:S(2)}, u32[]{:S(2)}) collective-permute-start(bf16[8,2,56,1152]{3,2,0,1:T(8,128)(2,1)S(1)} %bitcast.209), channel_id=1, source_target_pairs={{0,2},{2,0},{4,6},{6,4},{8,10},{10,8},{12,14},{14,12},{16,18},{18,... | collective-permute-start | bytes 6193160 | tf_op jit(solution)/shard_map/ppermute | solution.py:396
  381.4 3.2 collective-permute-start.27
  384.9 1.9 collective-permute-start.37
  389.2 4.4 %bitcast_convert_fusion = f32[2432,896]{1,0:T(8,128)} fusion(bf16[2,8,152,896]{3,2,1,0:T(8,128)(2,1)S(1)} %maximum_select_fusion.2), kind=kLoop, calls=%fused_computation.9 | loop fusion | flops 2179072 | bytes 13074432 | tf_op jit(solution)/shard_map/convert_element_type | solution.py:781
  393.7 2.6 collective-permute-start.29
  397.0 6.8 %collective-permute-done.29 = bf16[4,32,2048]{2,1,0:T(8,128)(2,1)S(1)} collective-permute-done((bf16[4,32,2048]{2,1,0:T(8,128)(2,1)S(1)}, bf16[4,32,2048]{2,1,0:T(8,128)(2,1)S(1)}, u32[]{:S(2)}, u32[]{:S(2)}) %collective-permute-start.29) | collective-permute-done | bytes 524320 | tf_op jit(solution)/shard_map/ppermute | solution.py:396
  404.0 5.7 %collective-permute-start.30 = (bf16[8,32,2048]{2,1,0:T(8,128)(2,1)S(1)}, bf16[8,32,2048]{2,1,0:T(8,128)(2,1)S(1)}, u32[]{:S(2)}, u32[]{:S(2)}) collective-permute-start(bf16[8,32,2048]{2,1,0:T(8,128)(2,1)S(1)} %bitcast.228), channel_id=1, source_target_pairs={{0,2},{2,0},{4,6},{6,4},{8,10},{10,8},{12,14},{14,12},{16,18},{18,... | collective-permute-start | bytes 3145736 | tf_op jit(solution)/shard_map/ppermute | solution.py:396
  410.2 3.8 maximum_convert_fusion.1
  414.2 3.8 maximum_convert_fusion
  419.0 1.9 fusion.24
  (260 shorter events, 59.0 us)
Async XLA Ops:
  0.7 7.8 %copy-start = (bf16[512,896]{1,0:T(8,128)(2,1)S(1)}, bf16[512,896]{1,0:T(8,128)(2,1)}, u32[]{:S(2)}) copy-start(bf16[512,896]{1,0:T(8,128)(2,1)} %tokens.5) | copy-start | bytes 2752516
  0.7 8.0 %copy-start.21 = (s32[512]{0:T(512)S(1)}, s32[512]{0:T(512)}, u32[]{:S(2)}) copy-start(s32[512]{0:T(512)} %param.16) | copy-start | bytes 6148
  4.0 22.5 %collective-permute-start.1 = (bf16[224,1152]{1,0:T(8,128)(2,1)S(1)}, bf16[224,1152]{1,0:T(8,128)(2,1)}, u32[]{:S(2)}, u32[]{:S(2)}) collective-permute-start(bf16[224,1152]{1,0:T(8,128)(2,1)S(1)} %constant_dynamic-slice_fusion.12), channel_id=1, source_target_pairs={{0,1},{1,0},{2,3},{3,2},{4,5},{5,4},{6,7},{7,6},{8,9},{9,8},{10,11... | collective-permute-start | bytes 1548296 | tf_op jit(solution)/shard_map/ppermute | solution.py:396
  6.9 19.6 %collective-permute-start.2 = (bf16[224,896]{1,0:T(8,128)(2,1)}, bf16[224,896]{1,0:T(8,128)(2,1)}, u32[]{:S(2)}, u32[]{:S(2)}) collective-permute-start(bf16[224,896]{1,0:T(8,128)(2,1)} %constant_dynamic-slice_fusion.11), channel_id=1, source_target_pairs={{0,1},{1,0},{2,3},{3,2},{4,5},{5,4},{6,7},{7,6},{8,9},{9,8},{10,11... | collective-permute-start | bytes 1204232 | tf_op jit(solution)/shard_map/ppermute | solution.py:396
  7.0 19.3 %collective-permute-start = (bf16[1472]{0:T(1024)(128)(2,1)S(1)}, bf16[1472]{0:T(1024)(128)(2,1)S(1)}, u32[]{:S(2)}, u32[]{:S(2)}) collective-permute-start(bf16[1472]{0:T(1024)(128)(2,1)S(1)} %concatenate.196), channel_id=1, source_target_pairs={{0,1},{1,0},{2,3},{3,2},{4,5},{5,4},{6,7},{7,6},{8,9},{9,8},{10,11... | collective-permute-start | bytes 8840 | tf_op jit(solution)/shard_map/ppermute | solution.py:396
  12.8 69.2 %copy-start.8 = (bf16[512,896]{1,0:T(8,128)(2,1)}, bf16[512,896]{1,0:T(8,128)(2,1)S(1)}, u32[]{:S(2)}) copy-start(bf16[512,896]{1,0:T(8,128)(2,1)S(1)} %multiply_convert_fusion.mlp_grad) | copy-start | bytes 2752516
  26.5 9.9 %collective-permute-start.4 = (bf16[224,896]{1,0:T(8,128)(2,1)}, bf16[224,896]{1,0:T(8,128)(2,1)}, u32[]{:S(2)}, u32[]{:S(2)}) collective-permute-start(bf16[224,896]{1,0:T(8,128)(2,1)} %collective-permute-done.2), channel_id=1, source_target_pairs={{0,2},{2,0},{4,6},{6,4},{8,10},{10,8},{12,14},{14,12},{16,18},{18,... | collective-permute-start | bytes 1204232 | tf_op jit(solution)/shard_map/ppermute | solution.py:396
  29.4 10.0 %collective-permute-start.3 = (bf16[224,1152]{1,0:T(8,128)(2,1)}, bf16[224,1152]{1,0:T(8,128)(2,1)S(1)}, u32[]{:S(2)}, u32[]{:S(2)}) collective-permute-start(bf16[224,1152]{1,0:T(8,128)(2,1)} %collective-permute-done.1), channel_id=1, source_target_pairs={{0,2},{2,0},{4,6},{6,4},{8,10},{10,8},{12,14},{14,12},{16,18},{18,... | collective-permute-start | bytes 1548296 | tf_op jit(solution)/shard_map/ppermute | solution.py:396
  31.9 26.9 %collective-permute-start.5 = (bf16[112,2432]{1,0:T(8,128)(2,1)S(1)}, bf16[112,2432]{1,0:T(8,128)(2,1)S(1)}, u32[]{:S(2)}, u32[]{:S(2)}) collective-permute-start(bf16[112,2432]{1,0:T(8,128)(2,1)S(1)} %dynamic_slice.138), channel_id=1, source_target_pairs={{0,1},{1,0},{2,3},{3,2},{4,5},{5,4},{6,7},{7,6},{8,9},{9,8},{10,11... | collective-permute-start | bytes 1634312 | tf_op jit(solution)/shard_map/ppermute | solution.py:396
  36.2 42.4 %collective-permute-start.7 = (bf16[224,2432]{1,0:T(8,128)(2,1)}, bf16[224,2432]{1,0:T(8,128)(2,1)}, u32[]{:S(2)}, u32[]{:S(2)}) collective-permute-start(bf16[224,2432]{1,0:T(8,128)(2,1)} %dynamic_slice.139), channel_id=1, source_target_pairs={{0,1},{1,0},{2,3},{3,2},{4,5},{5,4},{6,7},{7,6},{8,9},{9,8},{10,11... | collective-permute-start | bytes 3268616 | tf_op jit(solution)/shard_map/ppermute | solution.py:396
  42.5 39.4 %slice-start.6 = ((s8[4358144]{0:T(1024)(128)(4,1)}), s8[163840]{0:T(1024)(128)(4,1)S(1)}, s32[]{:S(2)}) async-start(s8[4358144]{0:T(1024)(128)(4,1)} %bitcast.255), calls=%async_computation.6 | async-start | bytes 327680
  58.8 15.5 %collective-permute-start.6 = (bf16[112,2432]{1,0:T(8,128)(2,1)S(1)}, bf16[112,2432]{1,0:T(8,128)(2,1)S(1)}, u32[]{:S(2)}, u32[]{:S(2)}) collective-permute-start(bf16[112,2432]{1,0:T(8,128)(2,1)S(1)} %collective-permute-done.5), channel_id=1, source_target_pairs={{0,4},{2,6},{4,0},{6,2},{8,12},{10,14},{12,8},{14,10},{16,20},{18,... | collective-permute-start | bytes 1634312 | tf_op jit(solution)/shard_map/ppermute | solution.py:396
  60.2 18.4 %collective-permute-start.8 = (bf16[256,896]{1,0:T(8,128)(2,1)}, bf16[256,896]{1,0:T(8,128)(2,1)S(1)}, u32[]{:S(2)}, u32[]{:S(2)}) collective-permute-start(bf16[256,896]{1,0:T(8,128)(2,1)} %get-tuple-element.102), channel_id=1, source_target_pairs={{0,1},{1,0},{2,3},{3,2},{4,5},{5,4},{6,7},{7,6},{8,9},{9,8},{10,11... | collective-permute-start | bytes 1376264 | tf_op jit(solution)/shard_map/ppermute | solution.py:396
  61.4 20.4 %slice-start.7 = ((s8[4358144]{0:T(1024)(128)(4,1)}), s8[4194304]{0:T(1024)(128)(4,1)S(1)}, s32[]{:S(2)}) async-start(s8[4358144]{0:T(1024)(128)(4,1)} %bitcast.255), calls=%async_computation.7 | async-start | bytes 8388608
  78.6 6.9 %collective-permute-start.10 = (bf16[224,2432]{1,0:T(8,128)(2,1)}, bf16[224,2432]{1,0:T(8,128)(2,1)S(1)}, u32[]{:S(2)}, u32[]{:S(2)}) collective-permute-start(bf16[224,2432]{1,0:T(8,128)(2,1)} %collective-permute-done.7), channel_id=1, source_target_pairs={{0,2},{2,0},{4,6},{6,4},{8,10},{10,8},{12,14},{14,12},{16,18},{18,... | collective-permute-start | bytes 3268616 | tf_op jit(solution)/shard_map/ppermute | solution.py:396
  81.8 5.7 %collective-permute-start.9 = (bf16[224,2432]{1,0:T(8,128)(2,1)S(1)}, bf16[224,2432]{1,0:T(8,128)(2,1)S(1)}, u32[]{:S(2)}, u32[]{:S(2)}) collective-permute-start(bf16[224,2432]{1,0:T(8,128)(2,1)S(1)} %bitcast.222), channel_id=1, source_target_pairs={{0,2},{2,0},{4,6},{6,4},{8,10},{10,8},{12,14},{14,12},{16,18},{18,... | collective-permute-start | bytes 3268616 | tf_op jit(solution)/shard_map/ppermute | solution.py:396
  82.1 26.7 %collective-permute-start.12 = (bf16[512,896]{1,0:T(8,128)(2,1)S(1)}, bf16[512,896]{1,0:T(8,128)(2,1)S(1)}, u32[]{:S(2)}, u32[]{:S(2)}) collective-permute-start(bf16[512,896]{1,0:T(8,128)(2,1)S(1)} %multiply_convert_fusion.mlp_grad), channel_id=1, source_target_pairs={{0,1},{1,0},{2,3},{3,2},{4,5},{5,4},{6,7},{7,6},{8,9},{9,8},{10,11... | collective-permute-start | bytes 2752520 | tf_op jit(solution)/shard_map/ppermute | solution.py:396
  84.8 28.6 %collective-permute-start.11 = (bf16[256,896]{1,0:T(8,128)(2,1)S(1)}, bf16[256,896]{1,0:T(8,128)(2,1)S(1)}, u32[]{:S(2)}, u32[]{:S(2)}) collective-permute-start(bf16[256,896]{1,0:T(8,128)(2,1)S(1)} %copy-done.13), channel_id=1, source_target_pairs={{0,1},{1,0},{2,3},{3,2},{4,5},{5,4},{6,7},{7,6},{8,9},{9,8},{10,11... | collective-permute-start | bytes 1376264 | tf_op jit(solution)/shard_map/ppermute | solution.py:396
  130.4 17.4 %copy-start.1 = (bf16[1024,2432]{1,0:T(8,128)(2,1)S(1)}, bf16[1024,2432]{1,0:T(8,128)(2,1)}, u32[]{:S(2)}) copy-start(bf16[1024,2432]{1,0:T(8,128)(2,1)} %get-tuple-element.131.activ) | copy-start | bytes 14942212
  130.4 17.4 %copy-start.9 = (bf16[512,896]{1,0:T(8,128)(2,1)S(1)}, bf16[512,896]{1,0:T(8,128)(2,1)}, u32[]{:S(2)}) copy-start(bf16[512,896]{1,0:T(8,128)(2,1)} %copy-done.8) | copy-start | bytes 2752516
  130.5 17.4 %copy-start.18 = (bf16[512,896]{1,0:T(8,128)(2,1)S(1)}, bf16[512,896]{1,0:T(8,128)(2,1)}, u32[]{:S(2)}) copy-start(bf16[512,896]{1,0:T(8,128)(2,1)} %copy-done.17) | copy-start | bytes 2752516
  147.9 7.5 %copy-start.20 = (bf16[1024,896]{1,0:T(8,128)(2,1)S(1)}, bf16[1024,896]{1,0:T(8,128)(2,1)}, u32[]{:S(2)}) copy-start(bf16[1024,896]{1,0:T(8,128)(2,1)} %copy-done.19) | copy-start | bytes 5505028
  154.0 13.0 %collective-permute-start.14 = (bf16[1216,896]{1,0:T(8,128)(2,1)S(1)}, bf16[1216,896]{1,0:T(8,128)(2,1)S(1)}, u32[]{:S(2)}, u32[]{:S(2)}) collective-permute-start(bf16[1216,896]{1,0:T(8,128)(2,1)S(1)} %dynamic-slice_bitcast_fusion), channel_id=1, source_target_pairs={{0,2},{2,0},{4,6},{6,4},{8,10},{10,8},{12,14},{14,12},{16,18},{18,... | collective-permute-start | bytes 6537224 | tf_op jit(solution)/shard_map/ppermute | solution.py:396
  161.5 9.4 %copy-start.3 = (bf16[896,2432]{1,0:T(8,128)(2,1)}, bf16[896,2432]{1,0:T(8,128)(2,1)S(1)}, u32[]{:S(2)}) copy-start(bf16[896,2432]{1,0:T(8,128)(2,1)S(1)} %convolution_convert_fusion) | copy-start | bytes 13074436
  169.6 30.2 %collective-permute-start.17 = (bf16[896,1152]{1,0:T(8,128)(2,1)}, bf16[896,1152]{1,0:T(8,128)(2,1)}, u32[]{:S(2)}, u32[]{:S(2)}) collective-permute-start(bf16[896,1152]{1,0:T(8,128)(2,1)} %broadcast_select_fusion.5), channel_id=1, source_target_pairs={{0,2},{2,0},{4,6},{6,4},{8,10},{10,8},{12,14},{14,12},{16,18},{18,... | collective-permute-start | bytes 6193160 | tf_op jit(solution)/shard_map/ppermute | solution.py:396
  172.5 30.2 %collective-permute-start.16 = (bf16[896,1280]{1,0:T(8,128)(2,1)}, bf16[896,1280]{1,0:T(8,128)(2,1)}, u32[]{:S(2)}, u32[]{:S(2)}) collective-permute-start(bf16[896,1280]{1,0:T(8,128)(2,1)} %broadcast_select_fusion.2), channel_id=1, source_target_pairs={{0,2},{2,0},{4,6},{6,4},{8,10},{10,8},{12,14},{14,12},{16,18},{18,... | collective-permute-start | bytes 6881288 | tf_op jit(solution)/shard_map/ppermute | solution.py:396
  172.6 27.2 %slice-start.2 = ((s8[4358144]{0:T(1024)(128)(4,1)}), s8[163840]{0:T(1024)(128)(4,1)S(1)}, s32[]{:S(2)}) async-start(s8[4358144]{0:T(1024)(128)(4,1)} %bitcast.193), calls=%async_computation.2 | async-start | bytes 327680
  172.7 25.4 %collective-permute-start.15 = (bf16[4,152,896]{2,1,0:T(8,128)(2,1)S(1)}, bf16[4,152,896]{2,1,0:T(8,128)(2,1)}, u32[]{:S(2)}, u32[]{:S(2)}) collective-permute-start(bf16[4,152,896]{2,1,0:T(8,128)(2,1)S(1)} %dynamic-slice_bitcast_fusion.5), channel_id=1, source_target_pairs={{0,4},{2,6},{4,0},{6,2},{8,12},{10,14},{12,8},{14,10},{16,20},{18,... | collective-permute-start | bytes 3268616 | tf_op jit(solution)/shard_map/ppermute | solution.py:396
  174.3 25.5 %slice-start.3 = ((s8[4358144]{0:T(1024)(128)(4,1)}), s8[4194304]{0:T(1024)(128)(4,1)S(1)}, s32[]{:S(2)}) async-start(s8[4358144]{0:T(1024)(128)(4,1)} %bitcast.193), calls=%async_computation.3 | async-start | bytes 8388608
  174.3 31.8 %collective-permute-start.13 = (bf16[512,896]{1,0:T(8,128)(2,1)}, bf16[512,896]{1,0:T(8,128)(2,1)}, u32[]{:S(2)}, u32[]{:S(2)}) collective-permute-start(bf16[512,896]{1,0:T(8,128)(2,1)} %get-tuple-element.124), channel_id=1, source_target_pairs={{0,1},{1,0},{2,3},{3,2},{4,5},{5,4},{6,7},{7,6},{8,9},{9,8},{10,11... | collective-permute-start | bytes 2752520 | tf_op jit(solution)/shard_map/ppermute | solution.py:396
  206.9 36.2 %collective-permute-start.19 = (bf16[2,152,896]{2,1,0:T(8,128)(2,1)}, bf16[2,152,896]{2,1,0:T(8,128)(2,1)}, u32[]{:S(2)}, u32[]{:S(2)}) collective-permute-start(bf16[2,152,896]{2,1,0:T(8,128)(2,1)} %dynamic-slice_bitcast_fusion.9), channel_id=1, source_target_pairs={{0,8},{2,10},{4,12},{6,14},{8,0},{10,2},{12,4},{14,6},{16,24},{18,... | collective-permute-start | bytes 1634312 | tf_op jit(solution)/shard_map/ppermute | solution.py:396
  208.5 36.0 %collective-permute-start.18 = (bf16[512,896]{1,0:T(8,128)(2,1)}, bf16[512,896]{1,0:T(8,128)(2,1)}, u32[]{:S(2)}, u32[]{:S(2)}) collective-permute-start(bf16[512,896]{1,0:T(8,128)(2,1)} %get-tuple-element.138), channel_id=1, source_target_pairs={{0,1},{1,0},{2,3},{3,2},{4,5},{5,4},{6,7},{7,6},{8,9},{9,8},{10,11... | collective-permute-start | bytes 2752520 | tf_op jit(solution)/shard_map/ppermute | solution.py:396
  210.7 36.4 %collective-permute-start.21 = (bf16[4,2,56,1152]{3,2,0,1:T(8,128)(2,1)}, bf16[4,2,56,1152]{3,2,0,1:T(8,128)(2,1)}, u32[]{:S(2)}, u32[]{:S(2)}) collective-permute-start(bf16[4,2,56,1152]{3,2,0,1:T(8,128)(2,1)} %dynamic-slice_bitcast_fusion.7), channel_id=1, source_target_pairs={{0,4},{2,6},{4,0},{6,2},{8,12},{10,14},{12,8},{14,10},{16,20},{18,... | collective-permute-start | bytes 3096584 | tf_op jit(solution)/shard_map/ppermute | solution.py:396
  213.0 35.5 %collective-permute-start.20 = (bf16[4,2,56,1280]{3,2,0,1:T(8,128)(2,1)}, bf16[4,2,56,1280]{3,2,0,1:T(8,128)(2,1)}, u32[]{:S(2)}, u32[]{:S(2)}) collective-permute-start(bf16[4,2,56,1280]{3,2,0,1:T(8,128)(2,1)} %dynamic-slice_bitcast_fusion.4), channel_id=1, source_target_pairs={{0,8},{2,10},{4,12},{6,14},{8,0},{10,2},{12,4},{14,6},{16,24},{18,... | collective-permute-start | bytes 3440648 | tf_op jit(solution)/shard_map/ppermute | solution.py:396
  213.9 30.6 %copy-start.11 = (f32[256,896]{1,0:T(8,128)S(1)}, f32[256,896]{1,0:T(8,128)}, u32[]{:S(2)}) copy-start(f32[256,896]{1,0:T(8,128)} %get-tuple-element.103.mid_late) | copy-start | bytes 2752516
  213.9 30.6 %copy-start.14 = (f32[512,896]{1,0:T(8,128)S(1)}, f32[512,896]{1,0:T(8,128)}, u32[]{:S(2)}) copy-start(f32[512,896]{1,0:T(8,128)} %get-tuple-element.137) | copy-start | bytes 5505028
  250.3 14.2 %collective-permute-start.45 = (bf16[1,152,896]{2,1,0:T(8,128)(2,1)S(1)}, bf16[1,152,896]{2,1,0:T(8,128)(2,1)S(1)}, u32[]{:S(2)}, u32[]{:S(2)}) collective-permute-start(bf16[1,152,896]{2,1,0:T(8,128)(2,1)S(1)} %constant_dynamic-slice_fusion.5), channel_id=1, source_target_pairs={{0,16},{2,18},{4,20},{6,22},{8,24},{10,26},{12,28},{14,30},{16,0},... | collective-permute-start | bytes 817160 | tf_op jit(solution)/shard_map/ppermute | solution.py:396
  252.7 15.6 %collective-permute-start.38 = (bf16[2,2,56,1152]{3,2,0,1:T(8,128)(2,1)S(1)}, bf16[2,2,56,1152]{3,2,0,1:T(8,128)(2,1)S(1)}, u32[]{:S(2)}, u32[]{:S(2)}) collective-permute-start(bf16[2,2,56,1152]{3,2,0,1:T(8,128)(2,1)S(1)} %dynamic-slice_bitcast_fusion.11), channel_id=1, source_target_pairs={{0,8},{2,10},{4,12},{6,14},{8,0},{10,2},{12,4},{14,6},{16,24},{18,... | collective-permute-start | bytes 1548296 | tf_op jit(solution)/shard_map/ppermute | solution.py:396
  254.1 32.1 %collective-permute-start.31 = (bf16[2,2,56,1280]{3,2,0,1:T(8,128)(2,1)S(1)}, bf16[2,2,56,1280]{3,2,0,1:T(8,128)(2,1)S(1)}, u32[]{:S(2)}, u32[]{:S(2)}) collective-permute-start(bf16[2,2,56,1280]{3,2,0,1:T(8,128)(2,1)S(1)} %dynamic-slice_bitcast_fusion.8), channel_id=1, source_target_pairs={{0,4},{2,6},{4,0},{6,2},{8,12},{10,14},{12,8},{14,10},{16,20},{18,... | collective-permute-start | bytes 1720328 | tf_op jit(solution)/shard_map/ppermute | solution.py:396
  254.6 54.6 %collective-permute-start.22 = (bf16[2,256,2048]{2,1,0:T(8,128)(2,1)S(1)}, bf16[2,256,2048]{2,1,0:T(8,128)(2,1)S(1)}, u32[]{:S(2)}, u32[]{:S(2)}) collective-permute-start(bf16[2,256,2048]{2,1,0:T(8,128)(2,1)S(1)} %dynamic-slice_bitcast_fusion.3), channel_id=1, source_target_pairs={{0,2},{2,0},{4,6},{6,4},{8,10},{10,8},{12,14},{14,12},{16,18},{18,... | collective-permute-start | bytes 6291464 | tf_op jit(solution)/shard_map/ppermute | solution.py:396
  264.6 9.1 %collective-permute-start.46 = (bf16[1,152,896]{2,1,0:T(8,128)(2,1)S(1)}, bf16[1,152,896]{2,1,0:T(8,128)(2,1)S(1)}, u32[]{:S(2)}, u32[]{:S(2)}) collective-permute-start(bf16[1,152,896]{2,1,0:T(8,128)(2,1)S(1)} %add_convert_fusion.3), channel_id=1, source_target_pairs={{0,16},{2,18},{4,20},{6,22},{8,24},{10,26},{12,28},{14,30},{16,0},... | collective-permute-start | bytes 817160 | tf_op jit(solution)/shard_map/ppermute | solution.py:396
  268.5 21.1 %collective-permute-start.39 = (bf16[1,2,56,1152]{3,2,0,1:T(8,128)(2,1)S(1)}, bf16[1,2,56,1152]{3,2,0,1:T(8,128)(2,1)S(1)}, u32[]{:S(2)}, u32[]{:S(2)}) collective-permute-start(bf16[1,2,56,1152]{3,2,0,1:T(8,128)(2,1)S(1)} %constant_dynamic-slice_fusion.7), channel_id=1, source_target_pairs={{0,16},{2,18},{4,20},{6,22},{8,24},{10,26},{12,28},{14,30},{16,0},... | collective-permute-start | bytes 774152 | tf_op jit(solution)/shard_map/ppermute | solution.py:396
  273.9 37.4 %collective-permute-start.47 = (bf16[2,152,896]{2,1,0:T(8,128)(2,1)S(1)}, bf16[2,152,896]{2,1,0:T(8,128)(2,1)S(1)}, u32[]{:S(2)}, u32[]{:S(2)}) collective-permute-start(bf16[2,152,896]{2,1,0:T(8,128)(2,1)S(1)} %maximum_select_fusion.21), channel_id=1, source_target_pairs={{0,8},{2,10},{4,12},{6,14},{8,0},{10,2},{12,4},{14,6},{16,24},{18,... | collective-permute-start | bytes 1634312 | tf_op jit(solution)/shard_map/ppermute | solution.py:396
  286.5 15.5 %collective-permute-start.32 = (bf16[1,2,56,1280]{3,2,0,1:T(8,128)(2,1)S(1)}, bf16[1,2,56,1280]{3,2,0,1:T(8,128)(2,1)S(1)}, u32[]{:S(2)}, u32[]{:S(2)}) collective-permute-start(bf16[1,2,56,1280]{3,2,0,1:T(8,128)(2,1)S(1)} %constant_dynamic-slice_fusion.9), channel_id=1, source_target_pairs={{0,16},{2,18},{4,20},{6,22},{8,24},{10,26},{12,28},{14,30},{16,0},... | collective-permute-start | bytes 860168 | tf_op jit(solution)/shard_map/ppermute | solution.py:396
  289.7 12.8 %collective-permute-start.40 = (bf16[56,1152]{1,0:T(8,128)(2,1)S(1)}, bf16[56,1152]{1,0:T(8,128)(2,1)S(1)}, u32[]{:S(2)}, u32[]{:S(2)}) collective-permute-start(bf16[56,1152]{1,0:T(8,128)(2,1)S(1)} %get-tuple-element.178), channel_id=1, source_target_pairs={{0,1},{1,0},{2,3},{3,2},{4,5},{5,4},{6,7},{7,6},{8,9},{9,8},{10,11... | collective-permute-start | bytes 387080 | tf_op jit(solution)/shard_map/ppermute | solution.py:396
  302.0 4.3 %collective-permute-start.33 = (bf16[56,1280]{1,0:T(8,128)(2,1)S(1)}, bf16[56,1280]{1,0:T(8,128)(2,1)S(1)}, u32[]{:S(2)}, u32[]{:S(2)}) collective-permute-start(bf16[56,1280]{1,0:T(8,128)(2,1)S(1)} %get-tuple-element.176), channel_id=1, source_target_pairs={{0,1},{1,0},{2,3},{3,2},{4,5},{5,4},{6,7},{7,6},{8,9},{9,8},{10,11... | collective-permute-start | bytes 430088 | tf_op jit(solution)/shard_map/ppermute | solution.py:396
  302.6 20.4 %collective-permute-start.41 = (bf16[1,2,56,1152]{3,2,1,0:T(8,128)(2,1)S(1)}, bf16[1,2,56,1152]{3,2,1,0:T(8,128)(2,1)S(1)}, u32[]{:S(2)}, u32[]{:S(2)}) collective-permute-start(bf16[1,2,56,1152]{3,2,1,0:T(8,128)(2,1)S(1)} %fusion.40), channel_id=1, source_target_pairs={{0,16},{2,18},{4,20},{6,22},{8,24},{10,26},{12,28},{14,30},{16,0},... | collective-permute-start | bytes 774152 | tf_op jit(solution)/shard_map/ppermute | solution.py:396
  306.4 27.3 %collective-permute-start.34 = (bf16[1,2,56,1280]{3,2,1,0:T(8,128)(2,1)S(1)}, bf16[1,2,56,1280]{3,2,1,0:T(8,128)(2,1)S(1)}, u32[]{:S(2)}, u32[]{:S(2)}) collective-permute-start(bf16[1,2,56,1280]{3,2,1,0:T(8,128)(2,1)S(1)} %fusion.38), channel_id=1, source_target_pairs={{0,16},{2,18},{4,20},{6,22},{8,24},{10,26},{12,28},{14,30},{16,0},... | collective-permute-start | bytes 860168 | tf_op jit(solution)/shard_map/ppermute | solution.py:396
  310.2 20.4 %collective-permute-start.23 = (bf16[256,2048]{1,0:T(8,128)(2,1)S(1)}, bf16[256,2048]{1,0:T(8,128)(2,1)S(1)}, u32[]{:S(2)}, u32[]{:S(2)}) collective-permute-start(bf16[256,2048]{1,0:T(8,128)(2,1)S(1)} %dynamic-slice_bitcast_fusion.6), channel_id=1, source_target_pairs={{0,1},{1,0},{2,3},{3,2},{4,5},{5,4},{6,7},{7,6},{8,9},{9,8},{10,11... | collective-permute-start | bytes 3145736 | tf_op jit(solution)/shard_map/ppermute | solution.py:396
  311.6 42.8 %collective-permute-start.48 = (bf16[4,152,896]{2,1,0:T(8,128)(2,1)S(1)}, bf16[4,152,896]{2,1,0:T(8,128)(2,1)S(1)}, u32[]{:S(2)}, u32[]{:S(2)}) collective-permute-start(bf16[4,152,896]{2,1,0:T(8,128)(2,1)S(1)} %bitcast.220), channel_id=1, source_target_pairs={{0,4},{2,6},{4,0},{6,2},{8,12},{10,14},{12,8},{14,10},{16,20},{18,... | collective-permute-start | bytes 3268616 | tf_op jit(solution)/shard_map/ppermute | solution.py:396
  323.1 19.2 %collective-permute-start.42 = (bf16[2,2,56,1152]{3,2,0,1:T(8,128)(2,1)S(1)}, bf16[2,2,56,1152]{3,2,0,1:T(8,128)(2,1)S(1)}, u32[]{:S(2)}, u32[]{:S(2)}) collective-permute-start(bf16[2,2,56,1152]{3,2,0,1:T(8,128)(2,1)S(1)} %maximum_select_fusion.24), channel_id=1, source_target_pairs={{0,8},{2,10},{4,12},{6,14},{8,0},{10,2},{12,4},{14,6},{16,24},{18,... | collective-permute-start | bytes 1548296 | tf_op jit(solution)/shard_map/ppermute | solution.py:396
  331.0 22.5 %collective-permute-start.24 = (bf16[4,32,2048]{2,1,0:T(8,128)(2,1)S(1)}, bf16[4,32,2048]{2,1,0:T(8,128)(2,1)S(1)}, u32[]{:S(2)}, u32[]{:S(2)}) collective-permute-start(bf16[4,32,2048]{2,1,0:T(8,128)(2,1)S(1)} %dynamic-slice_bitcast_fusion.10), channel_id=1, source_target_pairs={{0,8},{2,10},{4,12},{6,14},{8,0},{10,2},{12,4},{14,6},{16,24},{18,... | collective-permute-start | bytes 1572872 | tf_op jit(solution)/shard_map/ppermute | solution.py:396
  333.8 20.2 %collective-permute-start.35 = (bf16[2,2,56,1280]{3,2,0,1:T(8,128)(2,1)S(1)}, bf16[2,2,56,1280]{3,2,0,1:T(8,128)(2,1)S(1)}, u32[]{:S(2)}, u32[]{:S(2)}) collective-permute-start(bf16[2,2,56,1280]{3,2,0,1:T(8,128)(2,1)S(1)} %maximum_select_fusion.19), channel_id=1, source_target_pairs={{0,4},{2,6},{4,0},{6,2},{8,12},{10,14},{12,8},{14,10},{16,20},{18,... | collective-permute-start | bytes 1720328 | tf_op jit(solution)/shard_map/ppermute | solution.py:396
  342.6 31.3 %collective-permute-start.43 = (bf16[4,2,56,1152]{3,2,0,1:T(8,128)(2,1)S(1)}, bf16[4,2,56,1152]{3,2,0,1:T(8,128)(2,1)S(1)}, u32[]{:S(2)}, u32[]{:S(2)}) collective-permute-start(bf16[4,2,56,1152]{3,2,0,1:T(8,128)(2,1)S(1)} %bitcast.240), channel_id=1, source_target_pairs={{0,4},{2,6},{4,0},{6,2},{8,12},{10,14},{12,8},{14,10},{16,20},{18,... | collective-permute-start | bytes 3096584 | tf_op jit(solution)/shard_map/ppermute | solution.py:396
  353.7 20.0 %collective-permute-start.25 = (bf16[2,32,2048]{2,1,0:T(8,128)(2,1)S(1)}, bf16[2,32,2048]{2,1,0:T(8,128)(2,1)S(1)}, u32[]{:S(2)}, u32[]{:S(2)}) collective-permute-start(bf16[2,32,2048]{2,1,0:T(8,128)(2,1)S(1)} %dynamic-slice_bitcast_fusion.12), channel_id=1, source_target_pairs={{0,4},{2,6},{4,0},{6,2},{8,12},{10,14},{12,8},{14,10},{16,20},{18,... | collective-permute-start | bytes 786440 | tf_op jit(solution)/shard_map/ppermute | solution.py:396
  354.3 30.2 %collective-permute-start.36 = (bf16[4,2,56,1280]{3,2,0,1:T(8,128)(2,1)S(1)}, bf16[4,2,56,1280]{3,2,0,1:T(8,128)(2,1)S(1)}, u32[]{:S(2)}, u32[]{:S(2)}) collective-permute-start(bf16[4,2,56,1280]{3,2,0,1:T(8,128)(2,1)S(1)} %bitcast.216), channel_id=1, source_target_pairs={{0,8},{2,10},{4,12},{6,14},{8,0},{10,2},{12,4},{14,6},{16,24},{18,... | collective-permute-start | bytes 3440648 | tf_op jit(solution)/shard_map/ppermute | solution.py:396
  354.8 33.4 %collective-permute-start.49 = (bf16[8,152,896]{2,1,0:T(8,128)(2,1)S(1)}, bf16[8,152,896]{2,1,0:T(8,128)(2,1)S(1)}, u32[]{:S(2)}, u32[]{:S(2)}) collective-permute-start(bf16[8,152,896]{2,1,0:T(8,128)(2,1)S(1)} %bitcast.203), channel_id=1, source_target_pairs={{0,2},{2,0},{4,6},{6,4},{8,10},{10,8},{12,14},{14,12},{16,18},{18,... | collective-permute-start | bytes 6537224 | tf_op jit(solution)/shard_map/ppermute | solution.py:396
  373.8 7.5 %collective-permute-start.26 = (bf16[1,32,2048]{2,1,0:T(8,128)(2,1)S(1)}, bf16[1,32,2048]{2,1,0:T(8,128)(2,1)S(1)}, u32[]{:S(2)}, u32[]{:S(2)}) collective-permute-start(bf16[1,32,2048]{2,1,0:T(8,128)(2,1)S(1)} %constant_dynamic-slice_fusion.10), channel_id=1, source_target_pairs={{0,16},{2,18},{4,20},{6,22},{8,24},{10,26},{12,28},{14,30},{16,0},... | collective-permute-start | bytes 393224 | tf_op jit(solution)/shard_map/ppermute | solution.py:396
  374.3 22.0 %collective-permute-start.44 = (bf16[8,2,56,1152]{3,2,0,1:T(8,128)(2,1)S(1)}, bf16[8,2,56,1152]{3,2,0,1:T(8,128)(2,1)S(1)}, u32[]{:S(2)}, u32[]{:S(2)}) collective-permute-start(bf16[8,2,56,1152]{3,2,0,1:T(8,128)(2,1)S(1)} %bitcast.209), channel_id=1, source_target_pairs={{0,2},{2,0},{4,6},{6,4},{8,10},{10,8},{12,14},{14,12},{16,18},{18,... | collective-permute-start | bytes 6193160 | tf_op jit(solution)/shard_map/ppermute | solution.py:396
  381.4 5.6 %collective-permute-start.27 = (bf16[1,32,2048]{2,1,0:T(8,128)(2,1)S(1)}, bf16[1,32,2048]{2,1,0:T(8,128)(2,1)S(1)}, u32[]{:S(2)}, u32[]{:S(2)}) collective-permute-start(bf16[1,32,2048]{2,1,0:T(8,128)(2,1)S(1)} %add_convert_fusion.5), channel_id=1, source_target_pairs={{0,16},{2,18},{4,20},{6,22},{8,24},{10,26},{12,28},{14,30},{16,0},... | collective-permute-start | bytes 393224 | tf_op jit(solution)/shard_map/ppermute | solution.py:396
  384.9 24.8 %collective-permute-start.37 = (bf16[8,2,56,1280]{3,2,0,1:T(8,128)(2,1)S(1)}, bf16[8,2,56,1280]{3,2,0,1:T(8,128)(2,1)S(1)}, u32[]{:S(2)}, u32[]{:S(2)}) collective-permute-start(bf16[8,2,56,1280]{3,2,0,1:T(8,128)(2,1)S(1)} %bitcast.199), channel_id=1, source_target_pairs={{0,2},{2,0},{4,6},{6,4},{8,10},{10,8},{12,14},{14,12},{16,18},{18,... | collective-permute-start | bytes 6881288 | tf_op jit(solution)/shard_map/ppermute | solution.py:396
  387.0 6.6 %collective-permute-start.28 = (bf16[2,32,2048]{2,1,0:T(8,128)(2,1)S(1)}, bf16[2,32,2048]{2,1,0:T(8,128)(2,1)S(1)}, u32[]{:S(2)}, u32[]{:S(2)}) collective-permute-start(bf16[2,32,2048]{2,1,0:T(8,128)(2,1)S(1)} %maximum_select_fusion.27), channel_id=1, source_target_pairs={{0,4},{2,6},{4,0},{6,2},{8,12},{10,14},{12,8},{14,10},{16,20},{18,... | collective-permute-start | bytes 786440 | tf_op jit(solution)/shard_map/ppermute | solution.py:396
  393.7 10.1 %collective-permute-start.29 = (bf16[4,32,2048]{2,1,0:T(8,128)(2,1)S(1)}, bf16[4,32,2048]{2,1,0:T(8,128)(2,1)S(1)}, u32[]{:S(2)}, u32[]{:S(2)}) collective-permute-start(bf16[4,32,2048]{2,1,0:T(8,128)(2,1)S(1)} %bitcast.250), channel_id=1, source_target_pairs={{0,8},{2,10},{4,12},{6,14},{8,0},{10,2},{12,4},{14,6},{16,24},{18,... | collective-permute-start | bytes 1572872 | tf_op jit(solution)/shard_map/ppermute | solution.py:396
  404.0 14.0 %collective-permute-start.30 = (bf16[8,32,2048]{2,1,0:T(8,128)(2,1)S(1)}, bf16[8,32,2048]{2,1,0:T(8,128)(2,1)S(1)}, u32[]{:S(2)}, u32[]{:S(2)}) collective-permute-start(bf16[8,32,2048]{2,1,0:T(8,128)(2,1)S(1)} %bitcast.228), channel_id=1, source_target_pairs={{0,2},{2,0},{4,6},{6,4},{8,10},{10,8},{12,14},{14,12},{16,18},{18,... | collective-permute-start | bytes 3145736 | tf_op jit(solution)/shard_map/ppermute | solution.py:396
  (21 other events, 95.9 us)

commit v5 on v4

--- a/solution.py
+++ b/solution.py
@@ -408,24 +408,16 @@
     return jnp.where(bit == 0, jnp.stack([own, other]), jnp.stack([other, own]))
 
 
-def column_cuts(columns):
-    step = 4 * LANES
-    return [(low, min(low + step, columns)) for low in range(0, columns, step)]
-
-
 def hidden_kernel(carries, mid_low, mlp_grad, w_gate, w_up, w_down, *refs):
     activ, gate_grad, up_grad = refs[carries:]
-    for low, high in column_cuts(w_gate.shape[1]):
-        gate = forward_product(mid_low[...], w_gate[:, low:high])
-        upward = forward_product(mid_low[...], w_up[:, low:high])
-        grad = contract_cols(mlp_grad[...], w_down[low:high, :])
-        sigmoid = jax.nn.sigmoid(gate)
-        silu = gate * sigmoid
-        activ[:, low:high] = (silu * upward).astype(jnp.bfloat16)
-        gate_grad[:, low:high] = (grad * upward * (sigmoid + silu * (1.0 - sigmoid))).astype(
-            jnp.bfloat16
-        )
-        up_grad[:, low:high] = (grad * silu).astype(jnp.bfloat16)
+    gate = forward_product(mid_low[...], w_gate[...])
+    upward = forward_product(mid_low[...], w_up[...])
+    grad = contract_cols(mlp_grad[...], w_down[...])
+    sigmoid = jax.nn.sigmoid(gate)
+    silu = gate * sigmoid
+    activ[...] = (silu * upward).astype(jnp.bfloat16)
+    gate_grad[...] = (grad * upward * (sigmoid + silu * (1.0 - sigmoid))).astype(jnp.bfloat16)
+    up_grad[...] = (grad * silu).astype(jnp.bfloat16)
 
 
 def whole_block(array):
@@ -439,7 +431,7 @@
 def grid_call(kernel, grid, operands, in_specs, out_shape, out_specs, flops, aliases=None):
     return pl.pallas_call(
         kernel,
-        grid=(grid,),
+        grid=grid,
         out_shape=out_shape,
         in_specs=in_specs,
         out_specs=out_specs,
@@ -450,19 +442,21 @@
 
 
 def hidden_part(mid_low, mlp_grad, w_gate, w_up, w_down, total, start, carried):
-    rows = 256
-    count = mid_low.shape[0] // rows
+    rows, columns = 512, 4 * LANES
+    width, hidden = w_gate.shape
     first = start // rows
-    shapes = [jax.ShapeDtypeStruct((total, w_gate.shape[1]), jnp.bfloat16)] * 3
+    shapes = [jax.ShapeDtypeStruct((total, hidden), jnp.bfloat16)] * 3
+    tokens = pl.BlockSpec((rows, width), lambda token, unit: (token, 0))
+    across = pl.BlockSpec((width, columns), lambda token, unit: (0, unit))
     return grid_call(
         functools.partial(hidden_kernel, len(carried)),
-        count,
+        (mid_low.shape[0] // rows, pl.cdiv(hidden, columns)),
         [mid_low, mlp_grad, w_gate, w_up, w_down] + list(carried),
-        [row_block(mid_low, rows), row_block(mlp_grad, rows)]
-        + [whole_block(weight) for weight in (w_gate, w_up, w_down)]
+        [tokens, tokens, across, across]
+        + [pl.BlockSpec((columns, width), lambda token, unit: (unit, 0))]
         + [pl.BlockSpec(memory_space=pl.ANY)] * len(carried),
         shapes,
-        [row_block(shape, rows, first) for shape in shapes],
+        [pl.BlockSpec((rows, columns), lambda token, unit: (token + first, unit))] * 3,
         10**6,
         {5 + at: at for at in range(len(carried))},
     )
@@ -495,7 +489,7 @@
     half = total // rows // 2
     return grid_call(
         kernel,
-        2 * half,
+        (2 * half,),
         list(activs) + list(weights),
         [row_block(activ, rows) for activ in activs] + [whole_block(weight) for weight in weights],
         [jax.ShapeDtypeStruct((total // 2, width), kind) for kind in kinds],

time: 430 us -> 428 us (level)
  waiting for transfers between devices: 122 us -> 128 us
  Pallas kernels: 118 us -> 113 us
    ppermute x50, waiting for transfers between devices: 122 us -> 128 us  [swapped(): return lax.ppermute(value, axis, [(at, at ^ step) for at in range(size)])]
    pallas_call x4, Pallas kernels: 59.4 us -> 54.9 us  [grid_call(): pl.pallas_call(kernel, grid=grid, out_shape=out_shape, in_specs=in_specs,...]
  transfers between devices with their start and end apart: 50 -> 50, of which waited for: 18 -> 18; matrix products, arithmetic and copies ran while one was open for 19% -> 19% of each run, Pallas kernels for 20% -> 19%
where the time goes in v5:
time: 428 us; the launch traced here: 423 us
  waiting for transfers between devices  128 us (30%)
  Pallas kernels  113 us (26%)
  starting transfers between devices  76.6 us (18%)
  other arithmetic  61.1 us (14%)
  local copies, waits for them, and re-layouts  25.2 us (6%)
  matrix products  16.7 us (4%)
    ppermute x50, waiting for transfers between devices, swapped(): return lax.ppermute(value, axis, [(at, at ^ step) for at in range(size)])  128 us
    ppermute x50, starting transfers between devices, swapped(): return lax.ppermute(value, axis, [(at, at ^ step) for at in range(size)])  76.6 us
    pallas_call x3, Pallas kernels, call(): pl.pallas_call(kernel, out_shape=[jax.ShapeDtypeStruct(shape, kind) for s...  58.5 us
    pallas_call x4, Pallas kernels, grid_call(): pl.pallas_call(kernel, grid=grid, out_shape=out_shape, in_specs=in_specs,...  54.9 us
    select_n x30, other arithmetic, ordered(): return jnp.where(bit == 0, jnp.stack([own, other]), jnp.stack([other, own]))  18.2 us
    dot_general x3, matrix products, contract_rows(): lax.dot_general(left, right, (((0,), (0,)), ((), ())), preferred_element_...  16.7 us
    convert_element_type x17, other arithmetic, added(): (left.astype(jnp.float32) + right.astype(jnp.float32)).astype(jnp.bfloat16)  14.8 us
  transfers between devices with their start and end apart: 50, of which 18 were waited for; matrix products, arithmetic and copies ran while one was open for 19% of the time, Pallas kernels for 19%

profile of v5, /device:TPU:1, one launch (start us, length us, event | category | flops | bytes accessed | tf_op | source)
XLA Modules:
  0.0 422.8 jit_solution(4989737543714536244)
XLA Ops:
  4.0 2.1 collective-permute-start.1
  7.0 1.4 collective-permute-start
  14.7 11.6 %collective-permute-done = bf16[1472]{0:T(1024)(128)(2,1)S(1)} collective-permute-done((bf16[1472]{0:T(1024)(128)(2,1)S(1)}, bf16[1472]{0:T(1024)(128)(2,1)S(1)}, u32[]{:S(2)}, u32[]{:S(2)}) %collective-permute-start) | collective-permute-done | bytes 2976 | tf_op jit(solution)/shard_map/ppermute | solution.py:396
  31.9 1.5 collective-permute-start.5
  33.5 2.8 dynamic_slice.139
  36.3 1.5 maximum_select_fusion.17
  39.3 1.4 maximum_select_fusion.15
  40.8 1.7 maximum_select_fusion.8
  42.5 16.3 %shard_map.254 = (bf16[512,896]{1,0:T(8,128)(2,1)}, bf16[512,128]{1,0:T(8,128)(2,1)}, bf16[512,128]{1,0:T(8,128)(2,1)}, bf16[256,896]{1,0:T(8,128)(2,1)}, f32[16...) custom-call(bf16[512,896]{1,0:T(8,128)(2,1)} %fusion.8.normed_low, bf16[896,1152]{1,0:T(8,128)(2,1)} %bitcast.191, ...), custom_call_target="tpu_custom_call" | custom-call | flops 1000000 | bytes 3333 | tf_op jit(solution)/shard_map/pallas_call | solution.py:180
  58.8 1.5 collective-permute-start.6
  61.5 12.9 %shard_map.255 = (bf16[256,896]{1,0:T(8,128)(2,1)}, f32[16,256]{1,0:T(8,128)}, f32[256,896]{1,0:T(8,128)}, bf16[256,896]{1,0:T(8,128)(2,1)}) custom-call(bf16[512,896]{1,0:T(8,128)(2,1)} %get-tuple-element.93.query_rot, bf16[512,128]{1,0:T(8,128)(2,1)} %get-tuple-element.94.key_rot, bf16[512,128]{1,0:T(8,128)(2,1)} %get-tuple-element.95.value_low, ...), custom_call_target="tpu_custom_call" | custom-call | flops 1000000 | bytes 3333 | tf_op jit(solution)/shard_map/pallas_call | solution.py:180
  74.5 4.1 collective-permute-done.8
  80.0 1.8 dynamic-slice_bitcast_fusion.1
  82.1 1.5 collective-permute-start.12
  85.5 1.9 maximum_select_fusion.5
  87.9 5.0 %maximum_select_fusion = (bf16[2,448,2432]{2,1,0:T(8,128)(2,1)}, bf16[2,448,2432]{2,1,0:T(8,128)(2,1)}) fusion(bf16[1,448,2432]{2,1,0:T(8,128)(2,1)S(1)} %bitcast.202, bf16[1,448,2432]{2,1,0:T(8,128)(2,1)S(1)} %dynamic-slice_bitcast_fusion.2, pred[]{:T(512)S(6)} %eq.10, bf16[1,448,2432]{2,1,0:T(8,128)(2,1)S(1)} %dynamic-slice_bitcast_fusion.1, ...), kind=kLoop, calls=%fused_computation.4 | loop fusion | flops 13074432 | bytes 17432576 | tf_op jit(solution)/shard_map/jit(_where)/select_n | solution.py:408
  92.9 13.6 %shard_map.256 = (bf16[1024,2432]{1,0:T(8,128)(2,1)}, bf16[1024,2432]{1,0:T(8,128)(2,1)}, bf16[1024,2432]{1,0:T(8,128)(2,1)}) custom-call(bf16[512,896]{1,0:T(8,128)(2,1)} %pad_maximum_fusion.mid_low, bf16[512,896]{1,0:T(8,128)(2,1)} %copy-done.8, bf16[896,2432]{1,0:T(8,128)(2,1)} %bitcast.180, bf16[896,2432]{1,0:T(8,128)(2,1)} %bitcast.183, ...), custom_call_target="tpu_custom_call" | custom-call | flops 1000000 | bytes 1000 | tf_op jit(solution)/shard_map/pallas_call | solution.py:432
  106.5 6.9 %collective-permute-done.11 = bf16[256,896]{1,0:T(8,128)(2,1)S(1)} collective-permute-done((bf16[256,896]{1,0:T(8,128)(2,1)S(1)}, bf16[256,896]{1,0:T(8,128)(2,1)S(1)}, u32[]{:S(2)}, u32[]{:S(2)}) %collective-permute-start.11) | collective-permute-done | bytes 458784 | tf_op jit(solution)/shard_map/ppermute | solution.py:396
  114.4 13.6 %shard_map.257 = (bf16[1024,2432]{1,0:T(8,128)(2,1)}, bf16[1024,2432]{1,0:T(8,128)(2,1)}, bf16[1024,2432]{1,0:T(8,128)(2,1)}) custom-call(bf16[512,896]{1,0:T(8,128)(2,1)} %pad_maximum_fusion.1.mid_low, bf16[512,896]{1,0:T(8,128)(2,1)} %copy-done.17, bf16[896,2432]{1,0:T(8,128)(2,1)} %bitcast.181, ...), custom_call_target="tpu_custom_call", output_to_operand_aliasing={{0}: (5, {}), {1}: (6, {}), {2}: (7, {})} | custom-call | flops 1000000 | bytes 1000 | tf_op jit(solution)/shard_map/pallas_call | solution.py:432
  128.1 17.6 %shard_map.258 = (f32[512,896]{1,0:T(8,128)}, bf16[512,896]{1,0:T(8,128)(2,1)}) custom-call(bf16[1024,2432]{1,0:T(8,128)(2,1)} %get-tuple-element.128.gate_grad, bf16[1024,2432]{1,0:T(8,128)(2,1)} %get-tuple-element.129.up_grad, bf16[896,2432]{1,0:T(8,128)(2,1)} %bitcast.182, bf16[896,2432]{1,0:T(8,128)(2,1)} %bitcast.185), custom_call_target="tpu_custom_call" | custom-call | flops 1000000 | bytes 1000 | tf_op jit(solution)/shard_map/pallas_call | solution.py:432
  145.6 5.9 %convolution_convert_fusion.2 = bf16[2432,896]{1,0:T(8,128)(2,1)S(1)} fusion(bf16[1024,2432]{1,0:T(8,128)(2,1)S(1)} %copy-done.1, bf16[512,896]{1,0:T(8,128)(2,1)S(1)} %copy-done.18, bf16[512,896]{1,0:T(8,128)(2,1)S(1)} %copy-done.9), kind=kOutput, calls=%fused_computation.2 | convolution fusion | flops 4468588544 | bytes 11173888 | tf_op jit(solution)/shard_map/dot_general | solution.py:43
  154.0 5.3 %convolution_convert_fusion = bf16[896,2432]{1,0:T(8,128)(2,1)S(1)} fusion(bf16[1024,896]{1,0:T(8,128)(2,1)S(1)} %constant_dynamic-update-slice_fusion.3, bf16[1024,2432]{1,0:T(8,128)(2,1)S(1)} %copy-done.2), kind=kOutput, calls=%fused_computation | convolution fusion | flops 4464918528 | bytes 11173888 | tf_op jit(solution)/shard_map/dot_general | solution.py:43
  159.3 5.5 %convolution_convert_fusion.1 = bf16[896,2432]{1,0:T(8,128)(2,1)S(1)} fusion(bf16[1024,896]{1,0:T(8,128)(2,1)S(1)} %constant_dynamic-update-slice_fusion.3, bf16[1024,2432]{1,0:T(8,128)(2,1)S(1)} %bitcast.190), kind=kOutput, calls=%fused_computation.1 | convolution fusion | flops 4464918528 | bytes 11173888 | tf_op jit(solution)/shard_map/dot_general | solution.py:43
  165.4 2.0 broadcast_select_fusion.5
  168.7 1.6 broadcast_select_fusion.2
  170.5 1.5 collective-permute-start.15
  173.2 10.1 %shard_map.259 = (f32[512,896]{1,0:T(8,128)}, bf16[512,896]{1,0:T(8,128)(2,1)}) custom-call(bf16[1024,2432]{1,0:T(8,128)(2,1)} %get-tuple-element.131.activ, bf16[2432,896]{1,0:T(8,128)(2,1)} %w_down.5), custom_call_target="tpu_custom_call" | custom-call | flops 1000000 | bytes 1000 | tf_op jit(solution)/shard_map/pallas_call | solution.py:432
  183.4 12.5 %collective-permute-done.15 = bf16[4,152,896]{2,1,0:T(8,128)(2,1)} collective-permute-done((bf16[4,152,896]{2,1,0:T(8,128)(2,1)S(1)}, bf16[4,152,896]{2,1,0:T(8,128)(2,1)}, u32[]{:S(2)}, u32[]{:S(2)}) %collective-permute-start.15) | collective-permute-done | bytes 1089568 | tf_op jit(solution)/shard_map/ppermute | solution.py:396
  195.9 1.6 fusion.3
  197.6 3.0 add_convert_fusion.1
  200.6 3.2 add_convert_fusion
  204.7 1.5 collective-permute-start.19
  211.7 29.3 %shard_map.260 = (bf16[1024,2048]{1,0:T(8,128)(2,1)}, f32[512,896]{1,0:T(8,128)}) custom-call(f32[256,896]{1,0:T(8,128)} %get-tuple-element.92.mid_early, f32[256,896]{1,0:T(8,128)} %get-tuple-element.103.mid_late, f32[512,896]{1,0:T(8,128)} %get-tuple-element.139.norm_own, bf16[512,896]{1,0:T(8,128)(2,1)} %collective-permute-done.13.norm_got, ...), custom_call_target="tpu_custom_call" | custom-call | flops 1000000 | bytes 3333 | tf_op jit(solution)/shard_map/pallas_call | solution.py:180
  242.3 2.6 fusion.9
  244.9 1.5 fusion.5
  246.4 1.7 fusion.2
  248.1 2.4 collective-permute-start.45
  252.4 3.3 collective-permute-start.22
  255.6 6.6 %collective-permute-done.45 = bf16[1,152,896]{2,1,0:T(8,128)(2,1)S(1)} collective-permute-done((bf16[1,152,896]{2,1,0:T(8,128)(2,1)S(1)}, bf16[1,152,896]{2,1,0:T(8,128)(2,1)S(1)}, u32[]{:S(2)}, u32[]{:S(2)}) %collective-permute-start.45) | collective-permute-done | bytes 272416 | tf_op jit(solution)/shard_map/ppermute | solution.py:396
  262.4 5.8 %collective-permute-done.38 = bf16[2,2,56,1152]{3,2,0,1:T(8,128)(2,1)S(1)} collective-permute-done((bf16[2,2,56,1152]{3,2,0,1:T(8,128)(2,1)S(1)}, bf16[2,2,56,1152]{3,2,0,1:T(8,128)(2,1)S(1)}, u32[]{:S(2)}, u32[]{:S(2)}) %collective-permute-start.38) | collective-permute-done | bytes 516128 | tf_op jit(solution)/shard_map/ppermute | solution.py:396
  268.4 3.0 collective-permute-done.46
  271.6 12.2 %collective-permute-start.47 = (bf16[2,152,896]{2,1,0:T(8,128)(2,1)S(1)}, bf16[2,152,896]{2,1,0:T(8,128)(2,1)S(1)}, u32[]{:S(2)}, u32[]{:S(2)}) collective-permute-start(bf16[2,152,896]{2,1,0:T(8,128)(2,1)S(1)} %maximum_select_fusion.21), channel_id=1, source_target_pairs={{0,8},{2,10},{4,12},{6,14},{8,0},{10,2},{12,4},{14,6},{16,24},{18,... | collective-permute-start | bytes 1634312 | tf_op jit(solution)/shard_map/ppermute | solution.py:396
  284.2 3.2 collective-permute-start.32
  287.8 12.1 %collective-permute-done.32 = bf16[1,2,56,1280]{3,2,0,1:T(8,128)(2,1)S(1)} collective-permute-done((bf16[1,2,56,1280]{3,2,0,1:T(8,128)(2,1)S(1)}, bf16[1,2,56,1280]{3,2,0,1:T(8,128)(2,1)S(1)}, u32[]{:S(2)}, u32[]{:S(2)}) %collective-permute-start.32) | collective-permute-done | bytes 286752 | tf_op jit(solution)/shard_map/ppermute | solution.py:396
  300.2 3.2 collective-permute-start.41
  304.3 2.9 collective-permute-start.34
  309.6 11.1 %collective-permute-done.41 = bf16[1,2,56,1152]{3,2,1,0:T(8,128)(2,1)S(1)} collective-permute-done((bf16[1,2,56,1152]{3,2,1,0:T(8,128)(2,1)S(1)}, bf16[1,2,56,1152]{3,2,1,0:T(8,128)(2,1)S(1)}, u32[]{:S(2)}, u32[]{:S(2)}) %collective-permute-start.41) | collective-permute-done | bytes 258080 | tf_op jit(solution)/shard_map/ppermute | solution.py:396
  320.9 1.4 collective-permute-start.42
  322.5 6.2 %collective-permute-done.23 = bf16[256,2048]{1,0:T(8,128)(2,1)S(1)} collective-permute-done((bf16[256,2048]{1,0:T(8,128)(2,1)S(1)}, bf16[256,2048]{1,0:T(8,128)(2,1)S(1)}, u32[]{:S(2)}, u32[]{:S(2)}) %collective-permute-start.23) | collective-permute-done | bytes 1048608 | tf_op jit(solution)/shard_map/ppermute | solution.py:396
  329.2 2.3 collective-permute-start.24
  332.0 8.1 %collective-permute-done.42 = bf16[2,2,56,1152]{3,2,0,1:T(8,128)(2,1)S(1)} collective-permute-done((bf16[2,2,56,1152]{3,2,0,1:T(8,128)(2,1)S(1)}, bf16[2,2,56,1152]{3,2,0,1:T(8,128)(2,1)S(1)}, u32[]{:S(2)}, u32[]{:S(2)}) %collective-permute-start.42) | collective-permute-done | bytes 516128 | tf_op jit(solution)/shard_map/ppermute | solution.py:396
  340.7 10.6 %collective-permute-done.24 = bf16[4,32,2048]{2,1,0:T(8,128)(2,1)S(1)} collective-permute-done((bf16[4,32,2048]{2,1,0:T(8,128)(2,1)S(1)}, bf16[4,32,2048]{2,1,0:T(8,128)(2,1)S(1)}, u32[]{:S(2)}, u32[]{:S(2)}) %collective-permute-start.24) | collective-permute-done | bytes 524320 | tf_op jit(solution)/shard_map/ppermute | solution.py:396
  353.4 18.0 %collective-permute-done.25 = bf16[2,32,2048]{2,1,0:T(8,128)(2,1)S(1)} collective-permute-done((bf16[2,32,2048]{2,1,0:T(8,128)(2,1)S(1)}, bf16[2,32,2048]{2,1,0:T(8,128)(2,1)S(1)}, u32[]{:S(2)}, u32[]{:S(2)}) %collective-permute-start.25) | collective-permute-done | bytes 262176 | tf_op jit(solution)/shard_map/ppermute | solution.py:396
  372.0 5.8 %collective-permute-start.44 = (bf16[8,2,56,1152]{3,2,0,1:T(8,128)(2,1)S(1)}, bf16[8,2,56,1152]{3,2,0,1:T(8,128)(2,1)S(1)}, u32[]{:S(2)}, u32[]{:S(2)}) collective-permute-start(bf16[8,2,56,1152]{3,2,0,1:T(8,128)(2,1)S(1)} %bitcast.209), channel_id=1, source_target_pairs={{0,2},{2,0},{4,6},{6,4},{8,10},{10,8},{12,14},{14,12},{16,18},{18,... | collective-permute-start | bytes 6193160 | tf_op jit(solution)/shard_map/ppermute | solution.py:396
  379.1 3.2 collective-permute-start.27
  382.7 1.8 collective-permute-start.37
  384.5 1.6 collective-permute-done.27
  387.2 4.4 %bitcast_convert_fusion = f32[2432,896]{1,0:T(8,128)} fusion(bf16[2,8,152,896]{3,2,1,0:T(8,128)(2,1)S(1)} %maximum_select_fusion.2), kind=kLoop, calls=%fused_computation.9 | loop fusion | flops 2179072 | bytes 13074432 | tf_op jit(solution)/shard_map/convert_element_type | solution.py:775
  391.7 2.3 collective-permute-start.29
  394.6 6.8 %collective-permute-done.29 = bf16[4,32,2048]{2,1,0:T(8,128)(2,1)S(1)} collective-permute-done((bf16[4,32,2048]{2,1,0:T(8,128)(2,1)S(1)}, bf16[4,32,2048]{2,1,0:T(8,128)(2,1)S(1)}, u32[]{:S(2)}, u32[]{:S(2)}) %collective-permute-start.29) | collective-permute-done | bytes 524320 | tf_op jit(solution)/shard_map/ppermute | solution.py:396
  401.6 5.7 %collective-permute-start.30 = (bf16[8,32,2048]{2,1,0:T(8,128)(2,1)S(1)}, bf16[8,32,2048]{2,1,0:T(8,128)(2,1)S(1)}, u32[]{:S(2)}, u32[]{:S(2)}) collective-permute-start(bf16[8,32,2048]{2,1,0:T(8,128)(2,1)S(1)} %bitcast.228), channel_id=1, source_target_pairs={{0,2},{2,0},{4,6},{6,4},{8,10},{10,8},{12,14},{14,12},{16,18},{18,... | collective-permute-start | bytes 3145736 | tf_op jit(solution)/shard_map/ppermute | solution.py:396
  407.8 3.8 maximum_convert_fusion.1
  411.8 3.8 maximum_convert_fusion
  416.6 1.9 fusion.24
  (260 shorter events, 57.9 us)
Async XLA Ops:
  0.7 7.8 %copy-start = (bf16[512,896]{1,0:T(8,128)(2,1)S(1)}, bf16[512,896]{1,0:T(8,128)(2,1)}, u32[]{:S(2)}) copy-start(bf16[512,896]{1,0:T(8,128)(2,1)} %tokens.5) | copy-start | bytes 2752516
  0.7 8.0 %copy-start.21 = (s32[512]{0:T(512)S(1)}, s32[512]{0:T(512)}, u32[]{:S(2)}) copy-start(s32[512]{0:T(512)} %param.16) | copy-start | bytes 6148
  4.0 22.5 %collective-permute-start.1 = (bf16[224,1152]{1,0:T(8,128)(2,1)S(1)}, bf16[224,1152]{1,0:T(8,128)(2,1)}, u32[]{:S(2)}, u32[]{:S(2)}) collective-permute-start(bf16[224,1152]{1,0:T(8,128)(2,1)S(1)} %constant_dynamic-slice_fusion.12), channel_id=1, source_target_pairs={{0,1},{1,0},{2,3},{3,2},{4,5},{5,4},{6,7},{7,6},{8,9},{9,8},{10,11... | collective-permute-start | bytes 1548296 | tf_op jit(solution)/shard_map/ppermute | solution.py:396
  6.9 19.6 %collective-permute-start.2 = (bf16[224,896]{1,0:T(8,128)(2,1)}, bf16[224,896]{1,0:T(8,128)(2,1)}, u32[]{:S(2)}, u32[]{:S(2)}) collective-permute-start(bf16[224,896]{1,0:T(8,128)(2,1)} %constant_dynamic-slice_fusion.11), channel_id=1, source_target_pairs={{0,1},{1,0},{2,3},{3,2},{4,5},{5,4},{6,7},{7,6},{8,9},{9,8},{10,11... | collective-permute-start | bytes 1204232 | tf_op jit(solution)/shard_map/ppermute | solution.py:396
  7.0 19.3 %collective-permute-start = (bf16[1472]{0:T(1024)(128)(2,1)S(1)}, bf16[1472]{0:T(1024)(128)(2,1)S(1)}, u32[]{:S(2)}, u32[]{:S(2)}) collective-permute-start(bf16[1472]{0:T(1024)(128)(2,1)S(1)} %concatenate.196), channel_id=1, source_target_pairs={{0,1},{1,0},{2,3},{3,2},{4,5},{5,4},{6,7},{7,6},{8,9},{9,8},{10,11... | collective-permute-start | bytes 8840 | tf_op jit(solution)/shard_map/ppermute | solution.py:396
  12.8 69.2 %copy-start.8 = (bf16[512,896]{1,0:T(8,128)(2,1)}, bf16[512,896]{1,0:T(8,128)(2,1)S(1)}, u32[]{:S(2)}) copy-start(bf16[512,896]{1,0:T(8,128)(2,1)S(1)} %multiply_convert_fusion.mlp_grad) | copy-start | bytes 2752516
  26.5 9.9 %collective-permute-start.4 = (bf16[224,896]{1,0:T(8,128)(2,1)}, bf16[224,896]{1,0:T(8,128)(2,1)}, u32[]{:S(2)}, u32[]{:S(2)}) collective-permute-start(bf16[224,896]{1,0:T(8,128)(2,1)} %collective-permute-done.2), channel_id=1, source_target_pairs={{0,2},{2,0},{4,6},{6,4},{8,10},{10,8},{12,14},{14,12},{16,18},{18,... | collective-permute-start | bytes 1204232 | tf_op jit(solution)/shard_map/ppermute | solution.py:396
  29.4 10.0 %collective-permute-start.3 = (bf16[224,1152]{1,0:T(8,128)(2,1)}, bf16[224,1152]{1,0:T(8,128)(2,1)S(1)}, u32[]{:S(2)}, u32[]{:S(2)}) collective-permute-start(bf16[224,1152]{1,0:T(8,128)(2,1)} %collective-permute-done.1), channel_id=1, source_target_pairs={{0,2},{2,0},{4,6},{6,4},{8,10},{10,8},{12,14},{14,12},{16,18},{18,... | collective-permute-start | bytes 1548296 | tf_op jit(solution)/shard_map/ppermute | solution.py:396
  31.9 26.9 %collective-permute-start.5 = (bf16[112,2432]{1,0:T(8,128)(2,1)S(1)}, bf16[112,2432]{1,0:T(8,128)(2,1)S(1)}, u32[]{:S(2)}, u32[]{:S(2)}) collective-permute-start(bf16[112,2432]{1,0:T(8,128)(2,1)S(1)} %dynamic_slice.138), channel_id=1, source_target_pairs={{0,1},{1,0},{2,3},{3,2},{4,5},{5,4},{6,7},{7,6},{8,9},{9,8},{10,11... | collective-permute-start | bytes 1634312 | tf_op jit(solution)/shard_map/ppermute | solution.py:396
  36.2 42.4 %collective-permute-start.7 = (bf16[224,2432]{1,0:T(8,128)(2,1)}, bf16[224,2432]{1,0:T(8,128)(2,1)}, u32[]{:S(2)}, u32[]{:S(2)}) collective-permute-start(bf16[224,2432]{1,0:T(8,128)(2,1)} %dynamic_slice.139), channel_id=1, source_target_pairs={{0,1},{1,0},{2,3},{3,2},{4,5},{5,4},{6,7},{7,6},{8,9},{9,8},{10,11... | collective-permute-start | bytes 3268616 | tf_op jit(solution)/shard_map/ppermute | solution.py:396
  42.5 39.4 %slice-start.6 = ((s8[4358144]{0:T(1024)(128)(4,1)}), s8[163840]{0:T(1024)(128)(4,1)S(1)}, s32[]{:S(2)}) async-start(s8[4358144]{0:T(1024)(128)(4,1)} %bitcast.255), calls=%async_computation.6 | async-start | bytes 327680
  58.8 15.5 %collective-permute-start.6 = (bf16[112,2432]{1,0:T(8,128)(2,1)S(1)}, bf16[112,2432]{1,0:T(8,128)(2,1)S(1)}, u32[]{:S(2)}, u32[]{:S(2)}) collective-permute-start(bf16[112,2432]{1,0:T(8,128)(2,1)S(1)} %collective-permute-done.5), channel_id=1, source_target_pairs={{0,4},{2,6},{4,0},{6,2},{8,12},{10,14},{12,8},{14,10},{16,20},{18,... | collective-permute-start | bytes 1634312 | tf_op jit(solution)/shard_map/ppermute | solution.py:396
  60.2 18.4 %collective-permute-start.8 = (bf16[256,896]{1,0:T(8,128)(2,1)}, bf16[256,896]{1,0:T(8,128)(2,1)S(1)}, u32[]{:S(2)}, u32[]{:S(2)}) collective-permute-start(bf16[256,896]{1,0:T(8,128)(2,1)} %get-tuple-element.102), channel_id=1, source_target_pairs={{0,1},{1,0},{2,3},{3,2},{4,5},{5,4},{6,7},{7,6},{8,9},{9,8},{10,11... | collective-permute-start | bytes 1376264 | tf_op jit(solution)/shard_map/ppermute | solution.py:396
  61.4 20.4 %slice-start.7 = ((s8[4358144]{0:T(1024)(128)(4,1)}), s8[4194304]{0:T(1024)(128)(4,1)S(1)}, s32[]{:S(2)}) async-start(s8[4358144]{0:T(1024)(128)(4,1)} %bitcast.255), calls=%async_computation.7 | async-start | bytes 8388608
  78.6 6.9 %collective-permute-start.10 = (bf16[224,2432]{1,0:T(8,128)(2,1)}, bf16[224,2432]{1,0:T(8,128)(2,1)S(1)}, u32[]{:S(2)}, u32[]{:S(2)}) collective-permute-start(bf16[224,2432]{1,0:T(8,128)(2,1)} %collective-permute-done.7), channel_id=1, source_target_pairs={{0,2},{2,0},{4,6},{6,4},{8,10},{10,8},{12,14},{14,12},{16,18},{18,... | collective-permute-start | bytes 3268616 | tf_op jit(solution)/shard_map/ppermute | solution.py:396
  81.8 5.7 %collective-permute-start.9 = (bf16[224,2432]{1,0:T(8,128)(2,1)S(1)}, bf16[224,2432]{1,0:T(8,128)(2,1)S(1)}, u32[]{:S(2)}, u32[]{:S(2)}) collective-permute-start(bf16[224,2432]{1,0:T(8,128)(2,1)S(1)} %bitcast.222), channel_id=1, source_target_pairs={{0,2},{2,0},{4,6},{6,4},{8,10},{10,8},{12,14},{14,12},{16,18},{18,... | collective-permute-start | bytes 3268616 | tf_op jit(solution)/shard_map/ppermute | solution.py:396
  82.1 24.5 %collective-permute-start.12 = (bf16[512,896]{1,0:T(8,128)(2,1)S(1)}, bf16[512,896]{1,0:T(8,128)(2,1)S(1)}, u32[]{:S(2)}, u32[]{:S(2)}) collective-permute-start(bf16[512,896]{1,0:T(8,128)(2,1)S(1)} %multiply_convert_fusion.mlp_grad), channel_id=1, source_target_pairs={{0,1},{1,0},{2,3},{3,2},{4,5},{5,4},{6,7},{7,6},{8,9},{9,8},{10,11... | collective-permute-start | bytes 2752520 | tf_op jit(solution)/shard_map/ppermute | solution.py:396
  84.8 28.6 %collective-permute-start.11 = (bf16[256,896]{1,0:T(8,128)(2,1)S(1)}, bf16[256,896]{1,0:T(8,128)(2,1)S(1)}, u32[]{:S(2)}, u32[]{:S(2)}) collective-permute-start(bf16[256,896]{1,0:T(8,128)(2,1)S(1)} %copy-done.13), channel_id=1, source_target_pairs={{0,1},{1,0},{2,3},{3,2},{4,5},{5,4},{6,7},{7,6},{8,9},{9,8},{10,11... | collective-permute-start | bytes 1376264 | tf_op jit(solution)/shard_map/ppermute | solution.py:396
  106.5 7.9 %copy-start.17 = (bf16[512,896]{1,0:T(8,128)(2,1)}, bf16[512,896]{1,0:T(8,128)(2,1)S(1)}, u32[]{:S(2)}) copy-start(bf16[512,896]{1,0:T(8,128)(2,1)S(1)} %collective-permute-done.12.mlp_grad) | copy-start | bytes 2752516
  128.0 17.6 %copy-start.1 = (bf16[1024,2432]{1,0:T(8,128)(2,1)S(1)}, bf16[1024,2432]{1,0:T(8,128)(2,1)}, u32[]{:S(2)}) copy-start(bf16[1024,2432]{1,0:T(8,128)(2,1)} %get-tuple-element.131.activ) | copy-start | bytes 14942212
  128.0 17.6 %copy-start.9 = (bf16[512,896]{1,0:T(8,128)(2,1)S(1)}, bf16[512,896]{1,0:T(8,128)(2,1)}, u32[]{:S(2)}) copy-start(bf16[512,896]{1,0:T(8,128)(2,1)} %copy-done.8) | copy-start | bytes 2752516
  128.0 17.6 %copy-start.18 = (bf16[512,896]{1,0:T(8,128)(2,1)S(1)}, bf16[512,896]{1,0:T(8,128)(2,1)}, u32[]{:S(2)}) copy-start(bf16[512,896]{1,0:T(8,128)(2,1)} %copy-done.17) | copy-start | bytes 2752516
  151.8 13.0 %collective-permute-start.14 = (bf16[1216,896]{1,0:T(8,128)(2,1)S(1)}, bf16[1216,896]{1,0:T(8,128)(2,1)S(1)}, u32[]{:S(2)}, u32[]{:S(2)}) collective-permute-start(bf16[1216,896]{1,0:T(8,128)(2,1)S(1)} %dynamic-slice_bitcast_fusion), channel_id=1, source_target_pairs={{0,2},{2,0},{4,6},{6,4},{8,10},{10,8},{12,14},{14,12},{16,18},{18,... | collective-permute-start | bytes 6537224 | tf_op jit(solution)/shard_map/ppermute | solution.py:396
  159.3 9.4 %copy-start.3 = (bf16[896,2432]{1,0:T(8,128)(2,1)}, bf16[896,2432]{1,0:T(8,128)(2,1)S(1)}, u32[]{:S(2)}) copy-start(bf16[896,2432]{1,0:T(8,128)(2,1)S(1)} %convolution_convert_fusion) | copy-start | bytes 13074436
  167.4 30.2 %collective-permute-start.17 = (bf16[896,1152]{1,0:T(8,128)(2,1)}, bf16[896,1152]{1,0:T(8,128)(2,1)}, u32[]{:S(2)}, u32[]{:S(2)}) collective-permute-start(bf16[896,1152]{1,0:T(8,128)(2,1)} %broadcast_select_fusion.5), channel_id=1, source_target_pairs={{0,2},{2,0},{4,6},{6,4},{8,10},{10,8},{12,14},{14,12},{16,18},{18,... | collective-permute-start | bytes 6193160 | tf_op jit(solution)/shard_map/ppermute | solution.py:396
  170.3 30.2 %collective-permute-start.16 = (bf16[896,1280]{1,0:T(8,128)(2,1)}, bf16[896,1280]{1,0:T(8,128)(2,1)}, u32[]{:S(2)}, u32[]{:S(2)}) collective-permute-start(bf16[896,1280]{1,0:T(8,128)(2,1)} %broadcast_select_fusion.2), channel_id=1, source_target_pairs={{0,2},{2,0},{4,6},{6,4},{8,10},{10,8},{12,14},{14,12},{16,18},{18,... | collective-permute-start | bytes 6881288 | tf_op jit(solution)/shard_map/ppermute | solution.py:396
  170.4 27.2 %slice-start.2 = ((s8[4358144]{0:T(1024)(128)(4,1)}), s8[163840]{0:T(1024)(128)(4,1)S(1)}, s32[]{:S(2)}) async-start(s8[4358144]{0:T(1024)(128)(4,1)} %bitcast.193), calls=%async_computation.2 | async-start | bytes 327680
  170.5 25.4 %collective-permute-start.15 = (bf16[4,152,896]{2,1,0:T(8,128)(2,1)S(1)}, bf16[4,152,896]{2,1,0:T(8,128)(2,1)}, u32[]{:S(2)}, u32[]{:S(2)}) collective-permute-start(bf16[4,152,896]{2,1,0:T(8,128)(2,1)S(1)} %dynamic-slice_bitcast_fusion.5), channel_id=1, source_target_pairs={{0,4},{2,6},{4,0},{6,2},{8,12},{10,14},{12,8},{14,10},{16,20},{18,... | collective-permute-start | bytes 3268616 | tf_op jit(solution)/shard_map/ppermute | solution.py:396
  172.0 25.5 %slice-start.3 = ((s8[4358144]{0:T(1024)(128)(4,1)}), s8[4194304]{0:T(1024)(128)(4,1)S(1)}, s32[]{:S(2)}) async-start(s8[4358144]{0:T(1024)(128)(4,1)} %bitcast.193), calls=%async_computation.3 | async-start | bytes 8388608
  172.0 31.8 %collective-permute-start.13 = (bf16[512,896]{1,0:T(8,128)(2,1)}, bf16[512,896]{1,0:T(8,128)(2,1)}, u32[]{:S(2)}, u32[]{:S(2)}) collective-permute-start(bf16[512,896]{1,0:T(8,128)(2,1)} %get-tuple-element.124), channel_id=1, source_target_pairs={{0,1},{1,0},{2,3},{3,2},{4,5},{5,4},{6,7},{7,6},{8,9},{9,8},{10,11... | collective-permute-start | bytes 2752520 | tf_op jit(solution)/shard_map/ppermute | solution.py:396
  204.7 36.2 %collective-permute-start.19 = (bf16[2,152,896]{2,1,0:T(8,128)(2,1)}, bf16[2,152,896]{2,1,0:T(8,128)(2,1)}, u32[]{:S(2)}, u32[]{:S(2)}) collective-permute-start(bf16[2,152,896]{2,1,0:T(8,128)(2,1)} %dynamic-slice_bitcast_fusion.9), channel_id=1, source_target_pairs={{0,8},{2,10},{4,12},{6,14},{8,0},{10,2},{12,4},{14,6},{16,24},{18,... | collective-permute-start | bytes 1634312 | tf_op jit(solution)/shard_map/ppermute | solution.py:396
  206.2 36.0 %collective-permute-start.18 = (bf16[512,896]{1,0:T(8,128)(2,1)}, bf16[512,896]{1,0:T(8,128)(2,1)}, u32[]{:S(2)}, u32[]{:S(2)}) collective-permute-start(bf16[512,896]{1,0:T(8,128)(2,1)} %get-tuple-element.138), channel_id=1, source_target_pairs={{0,1},{1,0},{2,3},{3,2},{4,5},{5,4},{6,7},{7,6},{8,9},{9,8},{10,11... | collective-permute-start | bytes 2752520 | tf_op jit(solution)/shard_map/ppermute | solution.py:396
  208.5 36.4 %collective-permute-start.21 = (bf16[4,2,56,1152]{3,2,0,1:T(8,128)(2,1)}, bf16[4,2,56,1152]{3,2,0,1:T(8,128)(2,1)}, u32[]{:S(2)}, u32[]{:S(2)}) collective-permute-start(bf16[4,2,56,1152]{3,2,0,1:T(8,128)(2,1)} %dynamic-slice_bitcast_fusion.7), channel_id=1, source_target_pairs={{0,4},{2,6},{4,0},{6,2},{8,12},{10,14},{12,8},{14,10},{16,20},{18,... | collective-permute-start | bytes 3096584 | tf_op jit(solution)/shard_map/ppermute | solution.py:396
  210.8 35.5 %collective-permute-start.20 = (bf16[4,2,56,1280]{3,2,0,1:T(8,128)(2,1)}, bf16[4,2,56,1280]{3,2,0,1:T(8,128)(2,1)}, u32[]{:S(2)}, u32[]{:S(2)}) collective-permute-start(bf16[4,2,56,1280]{3,2,0,1:T(8,128)(2,1)} %dynamic-slice_bitcast_fusion.4), channel_id=1, source_target_pairs={{0,8},{2,10},{4,12},{6,14},{8,0},{10,2},{12,4},{14,6},{16,24},{18,... | collective-permute-start | bytes 3440648 | tf_op jit(solution)/shard_map/ppermute | solution.py:396
  211.7 30.6 %copy-start.11 = (f32[256,896]{1,0:T(8,128)S(1)}, f32[256,896]{1,0:T(8,128)}, u32[]{:S(2)}) copy-start(f32[256,896]{1,0:T(8,128)} %get-tuple-element.103.mid_late) | copy-start | bytes 2752516
  211.7 30.6 %copy-start.14 = (f32[512,896]{1,0:T(8,128)S(1)}, f32[512,896]{1,0:T(8,128)}, u32[]{:S(2)}) copy-start(f32[512,896]{1,0:T(8,128)} %get-tuple-element.137) | copy-start | bytes 5505028
  248.1 14.2 %collective-permute-start.45 = (bf16[1,152,896]{2,1,0:T(8,128)(2,1)S(1)}, bf16[1,152,896]{2,1,0:T(8,128)(2,1)S(1)}, u32[]{:S(2)}, u32[]{:S(2)}) collective-permute-start(bf16[1,152,896]{2,1,0:T(8,128)(2,1)S(1)} %constant_dynamic-slice_fusion.5), channel_id=1, source_target_pairs={{0,16},{2,18},{4,20},{6,22},{8,24},{10,26},{12,28},{14,30},{16,0},... | collective-permute-start | bytes 817160 | tf_op jit(solution)/shard_map/ppermute | solution.py:396
  250.5 17.7 %collective-permute-start.38 = (bf16[2,2,56,1152]{3,2,0,1:T(8,128)(2,1)S(1)}, bf16[2,2,56,1152]{3,2,0,1:T(8,128)(2,1)S(1)}, u32[]{:S(2)}, u32[]{:S(2)}) collective-permute-start(bf16[2,2,56,1152]{3,2,0,1:T(8,128)(2,1)S(1)} %dynamic-slice_bitcast_fusion.11), channel_id=1, source_target_pairs={{0,8},{2,10},{4,12},{6,14},{8,0},{10,2},{12,4},{14,6},{16,24},{18,... | collective-permute-start | bytes 1548296 | tf_op jit(solution)/shard_map/ppermute | solution.py:396
  251.9 32.1 %collective-permute-start.31 = (bf16[2,2,56,1280]{3,2,0,1:T(8,128)(2,1)S(1)}, bf16[2,2,56,1280]{3,2,0,1:T(8,128)(2,1)S(1)}, u32[]{:S(2)}, u32[]{:S(2)}) collective-permute-start(bf16[2,2,56,1280]{3,2,0,1:T(8,128)(2,1)S(1)} %dynamic-slice_bitcast_fusion.8), channel_id=1, source_target_pairs={{0,4},{2,6},{4,0},{6,2},{8,12},{10,14},{12,8},{14,10},{16,20},{18,... | collective-permute-start | bytes 1720328 | tf_op jit(solution)/shard_map/ppermute | solution.py:396
  252.4 54.8 %collective-permute-start.22 = (bf16[2,256,2048]{2,1,0:T(8,128)(2,1)S(1)}, bf16[2,256,2048]{2,1,0:T(8,128)(2,1)S(1)}, u32[]{:S(2)}, u32[]{:S(2)}) collective-permute-start(bf16[2,256,2048]{2,1,0:T(8,128)(2,1)S(1)} %dynamic-slice_bitcast_fusion.3), channel_id=1, source_target_pairs={{0,2},{2,0},{4,6},{6,4},{8,10},{10,8},{12,14},{14,12},{16,18},{18,... | collective-permute-start | bytes 6291464 | tf_op jit(solution)/shard_map/ppermute | solution.py:396
  262.3 9.1 %collective-permute-start.46 = (bf16[1,152,896]{2,1,0:T(8,128)(2,1)S(1)}, bf16[1,152,896]{2,1,0:T(8,128)(2,1)S(1)}, u32[]{:S(2)}, u32[]{:S(2)}) collective-permute-start(bf16[1,152,896]{2,1,0:T(8,128)(2,1)S(1)} %add_convert_fusion.3), channel_id=1, source_target_pairs={{0,16},{2,18},{4,20},{6,22},{8,24},{10,26},{12,28},{14,30},{16,0},... | collective-permute-start | bytes 817160 | tf_op jit(solution)/shard_map/ppermute | solution.py:396
  268.4 19.0 %collective-permute-start.39 = (bf16[1,2,56,1152]{3,2,0,1:T(8,128)(2,1)S(1)}, bf16[1,2,56,1152]{3,2,0,1:T(8,128)(2,1)S(1)}, u32[]{:S(2)}, u32[]{:S(2)}) collective-permute-start(bf16[1,2,56,1152]{3,2,0,1:T(8,128)(2,1)S(1)} %constant_dynamic-slice_fusion.7), channel_id=1, source_target_pairs={{0,16},{2,18},{4,20},{6,22},{8,24},{10,26},{12,28},{14,30},{16,0},... | collective-permute-start | bytes 774152 | tf_op jit(solution)/shard_map/ppermute | solution.py:396
  271.6 37.4 %collective-permute-start.47 = (bf16[2,152,896]{2,1,0:T(8,128)(2,1)S(1)}, bf16[2,152,896]{2,1,0:T(8,128)(2,1)S(1)}, u32[]{:S(2)}, u32[]{:S(2)}) collective-permute-start(bf16[2,152,896]{2,1,0:T(8,128)(2,1)S(1)} %maximum_select_fusion.21), channel_id=1, source_target_pairs={{0,8},{2,10},{4,12},{6,14},{8,0},{10,2},{12,4},{14,6},{16,24},{18,... | collective-permute-start | bytes 1634312 | tf_op jit(solution)/shard_map/ppermute | solution.py:396
  284.2 15.6 %collective-permute-start.32 = (bf16[1,2,56,1280]{3,2,0,1:T(8,128)(2,1)S(1)}, bf16[1,2,56,1280]{3,2,0,1:T(8,128)(2,1)S(1)}, u32[]{:S(2)}, u32[]{:S(2)}) collective-permute-start(bf16[1,2,56,1280]{3,2,0,1:T(8,128)(2,1)S(1)} %constant_dynamic-slice_fusion.9), channel_id=1, source_target_pairs={{0,16},{2,18},{4,20},{6,22},{8,24},{10,26},{12,28},{14,30},{16,0},... | collective-permute-start | bytes 860168 | tf_op jit(solution)/shard_map/ppermute | solution.py:396
  287.5 12.6 %collective-permute-start.40 = (bf16[56,1152]{1,0:T(8,128)(2,1)S(1)}, bf16[56,1152]{1,0:T(8,128)(2,1)S(1)}, u32[]{:S(2)}, u32[]{:S(2)}) collective-permute-start(bf16[56,1152]{1,0:T(8,128)(2,1)S(1)} %get-tuple-element.178), channel_id=1, source_target_pairs={{0,1},{1,0},{2,3},{3,2},{4,5},{5,4},{6,7},{7,6},{8,9},{9,8},{10,11... | collective-permute-start | bytes 387080 | tf_op jit(solution)/shard_map/ppermute | solution.py:396
  300.0 4.3 %collective-permute-start.33 = (bf16[56,1280]{1,0:T(8,128)(2,1)S(1)}, bf16[56,1280]{1,0:T(8,128)(2,1)S(1)}, u32[]{:S(2)}, u32[]{:S(2)}) collective-permute-start(bf16[56,1280]{1,0:T(8,128)(2,1)S(1)} %get-tuple-element.176), channel_id=1, source_target_pairs={{0,1},{1,0},{2,3},{3,2},{4,5},{5,4},{6,7},{7,6},{8,9},{9,8},{10,11... | collective-permute-start | bytes 430088 | tf_op jit(solution)/shard_map/ppermute | solution.py:396
  300.2 20.5 %collective-permute-start.41 = (bf16[1,2,56,1152]{3,2,1,0:T(8,128)(2,1)S(1)}, bf16[1,2,56,1152]{3,2,1,0:T(8,128)(2,1)S(1)}, u32[]{:S(2)}, u32[]{:S(2)}) collective-permute-start(bf16[1,2,56,1152]{3,2,1,0:T(8,128)(2,1)S(1)} %fusion.40), channel_id=1, source_target_pairs={{0,16},{2,18},{4,20},{6,22},{8,24},{10,26},{12,28},{14,30},{16,0},... | collective-permute-start | bytes 774152 | tf_op jit(solution)/shard_map/ppermute | solution.py:396
  304.3 27.2 %collective-permute-start.34 = (bf16[1,2,56,1280]{3,2,1,0:T(8,128)(2,1)S(1)}, bf16[1,2,56,1280]{3,2,1,0:T(8,128)(2,1)S(1)}, u32[]{:S(2)}, u32[]{:S(2)}) collective-permute-start(bf16[1,2,56,1280]{3,2,1,0:T(8,128)(2,1)S(1)} %fusion.38), channel_id=1, source_target_pairs={{0,16},{2,18},{4,20},{6,22},{8,24},{10,26},{12,28},{14,30},{16,0},... | collective-permute-start | bytes 860168 | tf_op jit(solution)/shard_map/ppermute | solution.py:396
  308.1 20.6 %collective-permute-start.23 = (bf16[256,2048]{1,0:T(8,128)(2,1)S(1)}, bf16[256,2048]{1,0:T(8,128)(2,1)S(1)}, u32[]{:S(2)}, u32[]{:S(2)}) collective-permute-start(bf16[256,2048]{1,0:T(8,128)(2,1)S(1)} %dynamic-slice_bitcast_fusion.6), channel_id=1, source_target_pairs={{0,1},{1,0},{2,3},{3,2},{4,5},{5,4},{6,7},{7,6},{8,9},{9,8},{10,11... | collective-permute-start | bytes 3145736 | tf_op jit(solution)/shard_map/ppermute | solution.py:396
  309.3 42.8 %collective-permute-start.48 = (bf16[4,152,896]{2,1,0:T(8,128)(2,1)S(1)}, bf16[4,152,896]{2,1,0:T(8,128)(2,1)S(1)}, u32[]{:S(2)}, u32[]{:S(2)}) collective-permute-start(bf16[4,152,896]{2,1,0:T(8,128)(2,1)S(1)} %bitcast.220), channel_id=1, source_target_pairs={{0,4},{2,6},{4,0},{6,2},{8,12},{10,14},{12,8},{14,10},{16,20},{18,... | collective-permute-start | bytes 3268616 | tf_op jit(solution)/shard_map/ppermute | solution.py:396
  320.9 19.2 %collective-permute-start.42 = (bf16[2,2,56,1152]{3,2,0,1:T(8,128)(2,1)S(1)}, bf16[2,2,56,1152]{3,2,0,1:T(8,128)(2,1)S(1)}, u32[]{:S(2)}, u32[]{:S(2)}) collective-permute-start(bf16[2,2,56,1152]{3,2,0,1:T(8,128)(2,1)S(1)} %maximum_select_fusion.24), channel_id=1, source_target_pairs={{0,8},{2,10},{4,12},{6,14},{8,0},{10,2},{12,4},{14,6},{16,24},{18,... | collective-permute-start | bytes 1548296 | tf_op jit(solution)/shard_map/ppermute | solution.py:396
  329.2 22.1 %collective-permute-start.24 = (bf16[4,32,2048]{2,1,0:T(8,128)(2,1)S(1)}, bf16[4,32,2048]{2,1,0:T(8,128)(2,1)S(1)}, u32[]{:S(2)}, u32[]{:S(2)}) collective-permute-start(bf16[4,32,2048]{2,1,0:T(8,128)(2,1)S(1)} %dynamic-slice_bitcast_fusion.10), channel_id=1, source_target_pairs={{0,8},{2,10},{4,12},{6,14},{8,0},{10,2},{12,4},{14,6},{16,24},{18,... | collective-permute-start | bytes 1572872 | tf_op jit(solution)/shard_map/ppermute | solution.py:396
  331.6 20.2 %collective-permute-start.35 = (bf16[2,2,56,1280]{3,2,0,1:T(8,128)(2,1)S(1)}, bf16[2,2,56,1280]{3,2,0,1:T(8,128)(2,1)S(1)}, u32[]{:S(2)}, u32[]{:S(2)}) collective-permute-start(bf16[2,2,56,1280]{3,2,0,1:T(8,128)(2,1)S(1)} %maximum_select_fusion.19), channel_id=1, source_target_pairs={{0,4},{2,6},{4,0},{6,2},{8,12},{10,14},{12,8},{14,10},{16,20},{18,... | collective-permute-start | bytes 1720328 | tf_op jit(solution)/shard_map/ppermute | solution.py:396
  340.4 31.2 %collective-permute-start.43 = (bf16[4,2,56,1152]{3,2,0,1:T(8,128)(2,1)S(1)}, bf16[4,2,56,1152]{3,2,0,1:T(8,128)(2,1)S(1)}, u32[]{:S(2)}, u32[]{:S(2)}) collective-permute-start(bf16[4,2,56,1152]{3,2,0,1:T(8,128)(2,1)S(1)} %bitcast.240), channel_id=1, source_target_pairs={{0,4},{2,6},{4,0},{6,2},{8,12},{10,14},{12,8},{14,10},{16,20},{18,... | collective-permute-start | bytes 3096584 | tf_op jit(solution)/shard_map/ppermute | solution.py:396
  351.5 19.9 %collective-permute-start.25 = (bf16[2,32,2048]{2,1,0:T(8,128)(2,1)S(1)}, bf16[2,32,2048]{2,1,0:T(8,128)(2,1)S(1)}, u32[]{:S(2)}, u32[]{:S(2)}) collective-permute-start(bf16[2,32,2048]{2,1,0:T(8,128)(2,1)S(1)} %dynamic-slice_bitcast_fusion.12), channel_id=1, source_target_pairs={{0,4},{2,6},{4,0},{6,2},{8,12},{10,14},{12,8},{14,10},{16,20},{18,... | collective-permute-start | bytes 786440 | tf_op jit(solution)/shard_map/ppermute | solution.py:396
  352.1 30.2 %collective-permute-start.36 = (bf16[4,2,56,1280]{3,2,0,1:T(8,128)(2,1)S(1)}, bf16[4,2,56,1280]{3,2,0,1:T(8,128)(2,1)S(1)}, u32[]{:S(2)}, u32[]{:S(2)}) collective-permute-start(bf16[4,2,56,1280]{3,2,0,1:T(8,128)(2,1)S(1)} %bitcast.216), channel_id=1, source_target_pairs={{0,8},{2,10},{4,12},{6,14},{8,0},{10,2},{12,4},{14,6},{16,24},{18,... | collective-permute-start | bytes 3440648 | tf_op jit(solution)/shard_map/ppermute | solution.py:396
  352.6 33.6 %collective-permute-start.49 = (bf16[8,152,896]{2,1,0:T(8,128)(2,1)S(1)}, bf16[8,152,896]{2,1,0:T(8,128)(2,1)S(1)}, u32[]{:S(2)}, u32[]{:S(2)}) collective-permute-start(bf16[8,152,896]{2,1,0:T(8,128)(2,1)S(1)} %bitcast.203), channel_id=1, source_target_pairs={{0,2},{2,0},{4,6},{6,4},{8,10},{10,8},{12,14},{14,12},{16,18},{18,... | collective-permute-start | bytes 6537224 | tf_op jit(solution)/shard_map/ppermute | solution.py:396
  371.5 7.6 %collective-permute-start.26 = (bf16[1,32,2048]{2,1,0:T(8,128)(2,1)S(1)}, bf16[1,32,2048]{2,1,0:T(8,128)(2,1)S(1)}, u32[]{:S(2)}, u32[]{:S(2)}) collective-permute-start(bf16[1,32,2048]{2,1,0:T(8,128)(2,1)S(1)} %constant_dynamic-slice_fusion.10), channel_id=1, source_target_pairs={{0,16},{2,18},{4,20},{6,22},{8,24},{10,26},{12,28},{14,30},{16,0},... | collective-permute-start | bytes 393224 | tf_op jit(solution)/shard_map/ppermute | solution.py:396
  372.0 21.9 %collective-permute-start.44 = (bf16[8,2,56,1152]{3,2,0,1:T(8,128)(2,1)S(1)}, bf16[8,2,56,1152]{3,2,0,1:T(8,128)(2,1)S(1)}, u32[]{:S(2)}, u32[]{:S(2)}) collective-permute-start(bf16[8,2,56,1152]{3,2,0,1:T(8,128)(2,1)S(1)} %bitcast.209), channel_id=1, source_target_pairs={{0,2},{2,0},{4,6},{6,4},{8,10},{10,8},{12,14},{14,12},{16,18},{18,... | collective-permute-start | bytes 6193160 | tf_op jit(solution)/shard_map/ppermute | solution.py:396
  379.1 6.9 %collective-permute-start.27 = (bf16[1,32,2048]{2,1,0:T(8,128)(2,1)S(1)}, bf16[1,32,2048]{2,1,0:T(8,128)(2,1)S(1)}, u32[]{:S(2)}, u32[]{:S(2)}) collective-permute-start(bf16[1,32,2048]{2,1,0:T(8,128)(2,1)S(1)} %add_convert_fusion.5), channel_id=1, source_target_pairs={{0,16},{2,18},{4,20},{6,22},{8,24},{10,26},{12,28},{14,30},{16,0},... | collective-permute-start | bytes 393224 | tf_op jit(solution)/shard_map/ppermute | solution.py:396
  382.7 24.7 %collective-permute-start.37 = (bf16[8,2,56,1280]{3,2,0,1:T(8,128)(2,1)S(1)}, bf16[8,2,56,1280]{3,2,0,1:T(8,128)(2,1)S(1)}, u32[]{:S(2)}, u32[]{:S(2)}) collective-permute-start(bf16[8,2,56,1280]{3,2,0,1:T(8,128)(2,1)S(1)} %bitcast.199), channel_id=1, source_target_pairs={{0,2},{2,0},{4,6},{6,4},{8,10},{10,8},{12,14},{14,12},{16,18},{18,... | collective-permute-start | bytes 6881288 | tf_op jit(solution)/shard_map/ppermute | solution.py:396
  386.1 5.5 %collective-permute-start.28 = (bf16[2,32,2048]{2,1,0:T(8,128)(2,1)S(1)}, bf16[2,32,2048]{2,1,0:T(8,128)(2,1)S(1)}, u32[]{:S(2)}, u32[]{:S(2)}) collective-permute-start(bf16[2,32,2048]{2,1,0:T(8,128)(2,1)S(1)} %maximum_select_fusion.27), channel_id=1, source_target_pairs={{0,4},{2,6},{4,0},{6,2},{8,12},{10,14},{12,8},{14,10},{16,20},{18,... | collective-permute-start | bytes 786440 | tf_op jit(solution)/shard_map/ppermute | solution.py:396
  391.7 9.8 %collective-permute-start.29 = (bf16[4,32,2048]{2,1,0:T(8,128)(2,1)S(1)}, bf16[4,32,2048]{2,1,0:T(8,128)(2,1)S(1)}, u32[]{:S(2)}, u32[]{:S(2)}) collective-permute-start(bf16[4,32,2048]{2,1,0:T(8,128)(2,1)S(1)} %bitcast.250), channel_id=1, source_target_pairs={{0,8},{2,10},{4,12},{6,14},{8,0},{10,2},{12,4},{14,6},{16,24},{18,... | collective-permute-start | bytes 1572872 | tf_op jit(solution)/shard_map/ppermute | solution.py:396
  401.6 14.0 %collective-permute-start.30 = (bf16[8,32,2048]{2,1,0:T(8,128)(2,1)S(1)}, bf16[8,32,2048]{2,1,0:T(8,128)(2,1)S(1)}, u32[]{:S(2)}, u32[]{:S(2)}) collective-permute-start(bf16[8,32,2048]{2,1,0:T(8,128)(2,1)S(1)} %bitcast.228), channel_id=1, source_target_pairs={{0,2},{2,0},{4,6},{6,4},{8,10},{10,8},{12,14},{14,12},{16,18},{18,... | collective-permute-start | bytes 3145736 | tf_op jit(solution)/shard_map/ppermute | solution.py:396
  (21 other events, 97.8 us)
